TPU v7x, 32 devices: a whole 2x2x4 slice. The times are simulated.
32 devices in a mesh: dp: 16 (over z, y, x), tensor: 2 (over core).
Axes of the slice: x: 2, y: 2, z: 4, core: 2. Of those that a mesh axis runs over, the one named last changes fastest.
Arguments:
- inputs: bfloat16 [16416, 1024], P('dp'), may hold values from -6 to 6
- skips: bfloat16 [2, 16416, 1024], P(None, 'dp'), may hold values from -6 to 6
- cotangent: bfloat16 [16416, 1024], P('dp'), may hold values from -6 to 6
- skip_weight: bfloat16 [2, 2, 1024, 1024], P(None, 'tensor'), may hold values from -0.125 to 0.125
- skip_bias: bfloat16 [2, 1024], replicated, may hold values from -3 to 3
- attn_norm_gain: bfloat16 [2, 1024], replicated, may hold values from 0.5 to 1.5
- attn_norm_bias: bfloat16 [2, 1024], replicated, may hold values from -1 to 1
- qkv_weight: bfloat16 [2, 1024, 3, 1024], P(None, None, None, 'tensor'), may hold values from -0.1875 to 0.1875
- proj_weight: bfloat16 [2, 1024, 1024], P(None, None, 'tensor'), may hold values from -6 to 6
- proj_bias: bfloat16 [2, 1024], replicated, may hold values from -3 to 3
- ffn_norm_gain: bfloat16 [2, 1024], replicated, may hold values from 0.5 to 1.5
- ffn_norm_bias: bfloat16 [2, 1024], replicated, may hold values from -1 to 1
- up_weight: bfloat16 [2, 1024, 4096], P(None, None, 'tensor'), may hold values from -0.1875 to 0.1875
- up_bias: bfloat16 [2, 4096], P(None, 'tensor'), may hold values from -3 to 3
- down_weight: bfloat16 [2, 1024, 4096], P(None, None, 'tensor'), may hold values from -0.125 to 0.125
- down_bias: bfloat16 [2, 1024], replicated, may hold values from -3 to 3
Outputs:
- output: bfloat16 [16416, 1024], P('dp')
- input_grad: bfloat16 [16416, 1024], P('dp')
- skip_grad: bfloat16 [2, 16416, 1024], P(None, 'dp')
- skip_weight_grad: float32 [2, 2, 1024, 1024], P(None, 'tensor', 'dp')
- skip_bias_grad: float32 [2, 1024], P(None, 'dp')
- attn_norm_gain_grad: float32 [2, 1024], P(None, 'dp')
- attn_norm_bias_grad: float32 [2, 1024], P(None, 'dp')
- qkv_weight_grad: float32 [2, 1024, 3, 1024], P(None, 'dp', None, 'tensor')
- proj_weight_grad: float32 [2, 1024, 1024], P(None, 'dp', 'tensor')
- proj_bias_grad: float32 [2, 1024], P(None, 'dp')
- ffn_norm_gain_grad: float32 [2, 1024], P(None, 'dp')
- ffn_norm_bias_grad: float32 [2, 1024], P(None, 'dp')
- up_weight_grad: float32 [2, 1024, 4096], P(None, 'dp', 'tensor')
- up_bias_grad: float32 [2, 4096], P(None, ('tensor', 'dp'))
- down_weight_grad: float32 [2, 1024, 4096], P(None, 'dp', 'tensor')
- down_bias_grad: float32 [2, 1024], P(None, 'dp')
All inputs are finite; a program needn't handle non-finite values.
Results may differ from a plain program's by a relative error of at most 0.02.
Values may be sent and summed in bfloat16 or wider, within the bound.
No kernel may reach another device: no remote copies, remote signals or barrier semaphores. Data moves between devices by JAX's collectives and lax.ppermute only.
A program may use at most 512 MiB of HBM per device.

v0:
```python
import jax
import jax.numpy as jnp
from jax import lax
from jax.sharding import PartitionSpec as P

HD = 64
SEQ = 1026


epsilon = 1e-05


def broadcast(value, axis, source):
    kept = jnp.where(lax.axis_index(axis) == source, value, 0).astype(value.dtype)
    return lax.psum(kept, axis)


def block_count(length):
    total = max(1, length // 512)
    while length % total:
        total = total - 1
    return total


def layer_norm(values_in, gain_row, shift_row):
    average = jnp.mean(values_in, axis=-1, keepdims=True)
    centred = values_in - average
    variance = jnp.mean(centred * centred, axis=-1, keepdims=True)
    return centred * lax.rsqrt(variance + epsilon) * gain_row + shift_row


def gelu_exact(values_in):
    return jax.nn.gelu(values_in, approximate=False)


def attend_forward(single):
    queries = single[:, 0]
    key_rows = single[:, 1]
    value_rows = single[:, 2]
    scale = queries.shape[-1] ** (-0.5)
    length = queries.shape[0]
    blocks = block_count(length)
    block_rows = length // blocks
    outputs = []
    totals = []
    for block_index in range(blocks):
        query_block = queries[block_index * block_rows : (block_index + 1) * block_rows]
        scores = (
            jnp.einsum("qhd,khd->hqk", query_block, key_rows, preferred_element_type=jnp.float32)
            * scale
        )
        largest = jnp.max(scores, axis=-1, keepdims=True)
        exponent = jnp.exp(scores - largest)
        denominator = jnp.sum(exponent, axis=-1, keepdims=True)
        probabilities = (exponent / denominator).astype(jnp.bfloat16)
        outputs.append(
            jnp.einsum(
                "hqk,khd->qhd", probabilities, value_rows, preferred_element_type=jnp.float32
            ).astype(jnp.bfloat16)
        )
        totals.append((largest + jnp.log(denominator))[..., 0])
    return (jnp.concatenate(outputs, axis=0), jnp.concatenate(totals, axis=1))


def attend_backward(triple):
    single, out_grad, log_total = triple
    queries = single[:, 0]
    key_rows = single[:, 1]
    value_rows = single[:, 2]
    scale = queries.shape[-1] ** (-0.5)
    length = queries.shape[0]
    blocks = block_count(length)
    block_rows = length // blocks
    query_grads = []
    key_grad = jnp.zeros(key_rows.shape, jnp.float32)
    value_grad = jnp.zeros(value_rows.shape, jnp.float32)
    for block_index in range(blocks):
        start_row = block_index * block_rows
        query_block = queries[start_row : start_row + block_rows]
        grad_block = out_grad[start_row : start_row + block_rows]
        scores = (
            jnp.einsum("qhd,khd->hqk", query_block, key_rows, preferred_element_type=jnp.float32)
            * scale
        )
        probabilities = jnp.exp(scores - log_total[:, start_row : start_row + block_rows, None])
        prob_grad = jnp.einsum(
            "qhd,khd->hqk", grad_block, value_rows, preferred_element_type=jnp.float32
        )
        inner_sum = jnp.sum(prob_grad * probabilities, axis=-1, keepdims=True)
        score_grad = (probabilities * (prob_grad - inner_sum)).astype(jnp.bfloat16)
        query_grads.append(
            (
                jnp.einsum("hqk,khd->qhd", score_grad, key_rows, preferred_element_type=jnp.float32)
                * scale
            ).astype(jnp.bfloat16)
        )
        key_grad = (
            key_grad
            + jnp.einsum(
                "hqk,qhd->khd", score_grad, query_block, preferred_element_type=jnp.float32
            )
            * scale
        )
        value_grad = value_grad + jnp.einsum(
            "hqk,qhd->khd",
            probabilities.astype(jnp.bfloat16),
            grad_block,
            preferred_element_type=jnp.float32,
        )
    return jnp.stack(
        [
            jnp.concatenate(query_grads, axis=0),
            key_grad.astype(jnp.bfloat16),
            value_grad.astype(jnp.bfloat16),
        ],
        axis=1,
    )


def layer_forward(residual, skip_rows, params):
    (
        skip_matrix,
        skip_offset,
        gain_one,
        shift_one,
        qkv_matrix,
        proj_matrix,
        proj_offset,
        gain_two,
        shift_two,
        up_matrix,
        up_offset,
        down_matrix,
        down_offset,
    ) = params
    row_count = residual.shape[0]
    is_first = lax.axis_index("tensor") == 0
    half_input = jnp.where(is_first, residual.astype(jnp.bfloat16), skip_rows)
    hidden = lax.psum(
        jnp.dot(half_input, skip_matrix[0], preferred_element_type=jnp.float32), "tensor"
    ) + skip_offset.astype(jnp.float32)
    normed_one = layer_norm(
        hidden, gain_one.astype(jnp.float32), shift_one.astype(jnp.float32)
    ).astype(jnp.bfloat16)
    head_width = qkv_matrix.shape[2]
    heads_here = head_width // HD
    projected = jnp.dot(
        normed_one,
        qkv_matrix.reshape(qkv_matrix.shape[0], 3 * head_width),
        preferred_element_type=jnp.float32,
    ).astype(jnp.bfloat16)
    grouped = projected.reshape(row_count // SEQ, SEQ, 3, heads_here, HD)
    attended, log_total = lax.map(attend_forward, grouped)
    attended = attended.reshape(row_count, head_width)
    mixed = lax.psum(
        jnp.einsum("rc,dc->rd", attended, proj_matrix, preferred_element_type=jnp.float32), "tensor"
    )
    middle = hidden + mixed + proj_offset.astype(jnp.float32)
    normed_two = layer_norm(
        middle, gain_two.astype(jnp.float32), shift_two.astype(jnp.float32)
    ).astype(jnp.bfloat16)
    up_proj = jnp.dot(normed_two, up_matrix, preferred_element_type=jnp.float32) + up_offset.astype(
        jnp.float32
    )
    activation = gelu_exact(up_proj).astype(jnp.bfloat16)
    ffn_out = lax.psum(
        jnp.einsum("rf,df->rd", activation, down_matrix, preferred_element_type=jnp.float32).astype(
            jnp.bfloat16
        ),
        "tensor",
    ).astype(jnp.float32)
    result = middle + ffn_out + down_offset.astype(jnp.float32)
    kept = (
        half_input,
        hidden,
        normed_one,
        projected,
        attended,
        log_total,
        middle,
        normed_two,
        up_proj,
        activation,
    )
    return (result, kept)


def share_halves(half_grad, is_bottom):
    model_width = half_grad.shape[1]
    if is_bottom:
        joined = lax.all_gather(half_grad.astype(jnp.bfloat16), "tensor", axis=1, tiled=True)
        return (joined[:, :model_width], joined[:, model_width:])
    residual_part = broadcast(half_grad.astype(jnp.bfloat16), "tensor", 0).astype(half_grad.dtype)
    skip_part = broadcast(half_grad.astype(jnp.bfloat16), "tensor", 1)
    return (residual_part, skip_part)


def layer_backward(gradient, kept, params, is_bottom):
    (
        skip_matrix,
        skip_offset,
        gain_one,
        shift_one,
        qkv_matrix,
        proj_matrix,
        proj_offset,
        gain_two,
        shift_two,
        up_matrix,
        up_offset,
        down_matrix,
        down_offset,
    ) = params
    (
        half_input,
        hidden,
        normed_one,
        projected,
        attended,
        log_total,
        middle,
        normed_two,
        up_proj,
        activation,
    ) = kept
    row_count = gradient.shape[0]
    grad_low = gradient.astype(jnp.bfloat16)
    down_offset_grad = jnp.sum(gradient, axis=0)
    down_matrix_grad = jnp.einsum(
        "rd,rf->df", grad_low, activation, preferred_element_type=jnp.float32
    )
    act_grad = jnp.dot(grad_low, down_matrix, preferred_element_type=jnp.float32)
    unused, gelu_pull = jax.vjp(gelu_exact, up_proj)
    up_grad = gelu_pull(act_grad)[0]
    up_offset_grad = jnp.sum(up_grad, axis=0)
    up_low = up_grad.astype(jnp.bfloat16)
    up_matrix_grad = jnp.einsum("rd,rf->df", normed_two, up_low, preferred_element_type=jnp.float32)
    normed_two_grad = lax.psum(
        jnp.einsum("rf,df->rd", up_low, up_matrix, preferred_element_type=jnp.float32).astype(
            jnp.bfloat16
        ),
        "tensor",
    ).astype(jnp.float32)
    unused, norm_pull = jax.vjp(
        layer_norm, middle, gain_two.astype(jnp.float32), shift_two.astype(jnp.float32)
    )
    middle_part, gain_two_grad, shift_two_grad = norm_pull(normed_two_grad)
    middle_grad = gradient + middle_part
    proj_offset_grad = jnp.sum(middle_grad, axis=0)
    middle_low = middle_grad.astype(jnp.bfloat16)
    proj_matrix_grad = jnp.einsum(
        "rd,rc->dc", middle_low, attended, preferred_element_type=jnp.float32
    )
    attended_grad = jnp.dot(middle_low, proj_matrix, preferred_element_type=jnp.float32).astype(
        jnp.bfloat16
    )
    head_width = proj_matrix.shape[1]
    heads_here = head_width // HD
    seq_count = row_count // SEQ
    projected_grad = lax.map(
        attend_backward,
        (
            projected.reshape(seq_count, SEQ, 3, heads_here, HD),
            attended_grad.reshape(seq_count, SEQ, heads_here, HD),
            log_total,
        ),
    ).reshape(row_count, 3 * head_width)
    qkv_flat = qkv_matrix.reshape(qkv_matrix.shape[0], 3 * head_width)
    qkv_matrix_grad = jnp.einsum(
        "rd,rc->dc", normed_one, projected_grad, preferred_element_type=jnp.float32
    ).reshape(qkv_matrix.shape)
    normed_one_grad = lax.psum(
        jnp.einsum(
            "rc,dc->rd", projected_grad, qkv_flat, preferred_element_type=jnp.float32
        ).astype(jnp.bfloat16),
        "tensor",
    ).astype(jnp.float32)
    unused, first_pull = jax.vjp(
        layer_norm, hidden, gain_one.astype(jnp.float32), shift_one.astype(jnp.float32)
    )
    hidden_part, gain_one_grad, shift_one_grad = first_pull(normed_one_grad)
    hidden_grad = middle_grad + hidden_part
    skip_offset_grad = jnp.sum(hidden_grad, axis=0)
    hidden_low = hidden_grad.astype(jnp.bfloat16)
    skip_matrix_grad = jnp.einsum(
        "rd,re->de", half_input, hidden_low, preferred_element_type=jnp.float32
    )
    half_grad = jnp.einsum(
        "re,de->rd", hidden_low, skip_matrix[0], preferred_element_type=jnp.float32
    )
    residual_part, skip_part = share_halves(half_grad, is_bottom)
    grads = (
        skip_matrix_grad,
        skip_offset_grad,
        gain_one_grad,
        shift_one_grad,
        qkv_matrix_grad,
        proj_matrix_grad,
        proj_offset_grad,
        gain_two_grad,
        shift_two_grad,
        up_matrix_grad,
        up_offset_grad,
        down_matrix_grad,
        down_offset_grad,
    )
    return (residual_part, skip_part, grads)


def sum_stacked(stacked):
    return (
        lax.psum_scatter(stacked[0], "dp", scatter_dimension=1, tiled=True),
        lax.psum_scatter(stacked[1], "dp", scatter_dimension=1, tiled=True),
        lax.psum_scatter(stacked[2], "dp", scatter_dimension=1, tiled=True),
        lax.psum_scatter(stacked[3], "dp", scatter_dimension=1, tiled=True),
        lax.psum_scatter(stacked[4], "dp", scatter_dimension=1, tiled=True),
        lax.psum_scatter(stacked[5], "dp", scatter_dimension=1, tiled=True),
        lax.psum_scatter(stacked[6], "dp", scatter_dimension=1, tiled=True),
        lax.psum_scatter(stacked[7], "dp", scatter_dimension=1, tiled=True),
        lax.psum_scatter(stacked[8], "dp", scatter_dimension=1, tiled=True),
        lax.psum_scatter(stacked[9], "dp", scatter_dimension=1, tiled=True),
        lax.psum_scatter(stacked[10], "dp", scatter_dimension=1, tiled=True),
        lax.psum_scatter(stacked[11], "dp", scatter_dimension=1, tiled=True),
        lax.psum_scatter(stacked[12], "dp", scatter_dimension=1, tiled=True),
    )


def body(
    inputs,
    skips,
    cotangent,
    skip_weight,
    skip_bias,
    attn_norm_gain,
    attn_norm_bias,
    qkv_weight,
    proj_weight,
    proj_bias,
    ffn_norm_gain,
    ffn_norm_bias,
    up_weight,
    up_bias,
    down_weight,
    down_bias,
):
    all_params = (
        skip_weight,
        skip_bias,
        attn_norm_gain,
        attn_norm_bias,
        qkv_weight,
        proj_weight,
        proj_bias,
        ffn_norm_gain,
        ffn_norm_bias,
        up_weight,
        up_bias,
        down_weight,
        down_bias,
    )
    layer_total = skip_weight.shape[0]
    residual = inputs.astype(jnp.float32)
    saved = []
    for layer_index in range(layer_total):
        params = tuple((item[layer_index] for item in all_params))
        residual, kept = layer_forward(residual, skips[layer_index], params)
        saved.append(kept)
    output = residual.astype(jnp.bfloat16)
    gradient = cotangent.astype(jnp.float32)
    skip_grads = []
    collected = []
    for layer_index in reversed(range(layer_total)):
        params = tuple((item[layer_index] for item in all_params))
        gradient, skip_part, grads = layer_backward(
            gradient, saved[layer_index], params, layer_index == 0
        )
        skip_grads.insert(0, skip_part)
        collected.insert(0, grads)
    stacked = tuple(
        (jnp.stack([entry[member] for entry in collected], axis=0) for member in range(13))
    )
    summed = sum_stacked(stacked)
    skip_grad = jnp.stack(skip_grads, axis=0)
    return (
        output,
        gradient,
        skip_grad,
        summed[0][:, None],
        summed[1],
        summed[2],
        summed[3],
        summed[4],
        summed[5],
        summed[6],
        summed[7],
        summed[8],
        summed[9],
        summed[10],
        summed[11],
        summed[12],
    )


def solution(mesh):
    return jax.shard_map(
        body,
        mesh=mesh,
        in_specs=(
            P("dp", None),
            P(None, "dp", None),
            P("dp", None),
            P(None, "tensor", None, None),
            P(),
            P(),
            P(),
            P(None, None, None, "tensor"),
            P(None, None, "tensor"),
            P(),
            P(),
            P(),
            P(None, None, "tensor"),
            P(None, "tensor"),
            P(None, None, "tensor"),
            P(),
        ),
        out_specs=(
            P("dp", None),
            P("dp", None),
            P(None, "dp", None),
            P(None, "tensor", "dp", None),
            P(None, "dp"),
            P(None, "dp"),
            P(None, "dp"),
            P(None, "dp", None, "tensor"),
            P(None, "dp", "tensor"),
            P(None, "dp"),
            P(None, "dp"),
            P(None, "dp"),
            P(None, "dp", "tensor"),
            P(None, ("tensor", "dp")),
            P(None, "dp", "tensor"),
            P(None, "dp"),
        ),
        check_vma=False,
    )
```

profile of v0, /device:TPU:0, one launch (start us, length us, event | category | flops | bytes accessed | tf_op | source)
XLA Modules:
  0.0 2646.9 jit_solution(7227146696561155734)
XLA Ops:
  7.2 9.8 fusion.191
  34.6 21.0 all-reduce.12.cloned.1.call-done
  88.2 10.1 fusion.1
  98.2 9.5 fusion.145
  107.7 10.0 fusion
  134.6 26.7 %all-reduce.14.cloned.1.call-done = f32[1026,1024]{1,0:T(8,128)} async-done(((f32[1026,1024]{1,0:T(8,128)}), f32[1026,1024]{1,0:T(8,128)}) %all-reduce.14.cloned.1.call-update) | async-done | bytes 4202512 | tf_op jit(solution)/shard_map/psum | solution.py:155
  168.7 25.3 multiply_convert_fusion.5
  202.7 21.9 all-reduce.16.cloned.1.call-done
  241.3 24.9 all-reduce.18.cloned.1.call-done
  298.9 10.1 fusion.3
  318.4 10.1 fusion.2
  342.2 29.7 %all-reduce.20.cloned.1.call-done = f32[1026,1024]{1,0:T(8,128)} async-done(((f32[1026,1024]{1,0:T(8,128)}), f32[1026,1024]{1,0:T(8,128)}) %all-reduce.20.cloned.1.call-update) | async-done | bytes 4202512 | tf_op jit(solution)/shard_map/psum | solution.py:155
  379.4 25.9 multiply_convert_fusion.4
  405.4 12.6 fusion.198
  429.3 19.8 all-reduce.22.cloned.1.call-done
  469.0 11.7 fusion.12
  480.7 13.0 multiply_reduce_fusion.2
  495.8 15.0 multiply_reduce_fusion.3
  510.8 13.2 multiply_convert_fusion.3
  538.9 13.0 multiply_convert_fusion.2
  565.4 22.3 all-reduce.24.cloned.1.call-done
  607.6 22.5 all-reduce.26.cloned.1.call-done
  630.1 13.7 fusion.199
  665.2 11.4 all-reduce.28.cloned.1.call-done
  693.5 11.8 fusion.8
  705.4 13.0 multiply_reduce_fusion
  720.5 15.2 multiply_reduce_fusion.1
  735.7 13.2 multiply_convert_fusion.1
  763.8 13.0 multiply_convert_fusion
  795.9 26.9 %all-reduce.30.cloned.1.call-done = (bf16[1026,1024]{1,0:T(8,128)(2,1)}, bf16[1026,1024]{1,0:T(8,128)(2,1)}, bf16[1,1026,1024]{2,1,0:T(8,128)(2,1)}) async-done(((bf16[1026,1024]{1,0:T(8,128)(2,1)}, bf16[1026,1024]{1,0:T(8,128)(2,1)}, bf16[1,1026,1024]{2,1,0:T(8,128)(2,1)}), (bf16[1026,1024]{1,0:T(8,128)(2,1)}, bf16[1026,1024]{1,0:T(8,128)(2,1)}, ...) | async-done | bytes 6303760 | tf_op jit(solution)/shard_map/psum | solution.py:166
  870.1 11.1 convolution_bitcast_fusion.4
  889.3 12.2 pad_maximum_fusion.2
  902.2 9.8 convolution_bitcast_fusion.2
  912.1 9.8 convolution_bitcast_fusion.3
  952.8 26.4 reduce-scatter.46.cloned.1.call-done
  980.6 73.9 %reduce-scatter.48.cloned.1.call-done = f32[64,2]{1,0:T(8,128)} async-done(((f32[1024,2]{1,0:T(8,128)}), f32[64,2]{1,0:T(8,128)}) %reduce-scatter.48.cloned.1.call-update) | async-done | bytes 528
  1055.8 73.6 %reduce-scatter.50.cloned.1.call-done = f32[64,2]{1,0:T(8,128)} async-done(((f32[1024,2]{1,0:T(8,128)}), f32[64,2]{1,0:T(8,128)}) %reduce-scatter.50.cloned.1.call-update) | async-done | bytes 528
  1130.9 73.7 %reduce-scatter.54.cloned.1.call-done = f32[64,2]{1,0:T(8,128)} async-done(((f32[1024,2]{1,0:T(8,128)}), f32[64,2]{1,0:T(8,128)}) %reduce-scatter.54.cloned.1.call-update) | async-done | bytes 528
  1210.3 69.3 %reduce-scatter.40.cloned.1.call-done = f32[64,2]{1,0:T(8,128)} async-done(((f32[1024,2]{1,0:T(8,128)}), f32[64,2]{1,0:T(8,128)}) %reduce-scatter.40.cloned.1.call-update) | async-done | bytes 528
  1281.0 73.7 %reduce-scatter.42.cloned.1.call-done = f32[64,2]{1,0:T(8,128)} async-done(((f32[1024,2]{1,0:T(8,128)}), f32[64,2]{1,0:T(8,128)}) %reduce-scatter.42.cloned.1.call-update) | async-done | bytes 528
  1356.1 73.6 %reduce-scatter.44.cloned.1.call-done = f32[64,2]{1,0:T(8,128)} async-done(((f32[1024,2]{1,0:T(8,128)}), f32[64,2]{1,0:T(8,128)}) %reduce-scatter.44.cloned.1.call-update) | async-done | bytes 528
  1431.1 10.9 all-gather.2.cloned.1.call-done
  1446.4 30.1 %copy.81 = bf16[2,1026,1024]{2,0,1:T(2,128)(2,1)} copy(bf16[2,1026,1024]{2,1,0:T(8,128)(2,1)S(1)} %pad_maximum_fusion.4) | data formatting | bytes 8404992
  1476.5 64.7 %reduce-scatter.34.cloned.1.call-done = f32[2,64,512]{2,1,0:T(8,128)} async-done(((f32[2,1024,512]{2,1,0:T(8,128)}), f32[2,64,512]{2,1,0:T(8,128)}) %reduce-scatter.34.cloned.1.call-update) | async-done | bytes 262160 | tf_op jit(solution)/shard_map/reduce_scatter | solution.py:317
  1541.2 180.4 %reduce-scatter.30.cloned.1.call-done = f32[2,64,1024]{2,1,0:T(8,128)} async-done(((f32[2,1024,1024]{2,1,0:T(8,128)}), f32[2,64,1024]{2,1,0:T(8,128)}) %reduce-scatter.30.cloned.1.call-update) | async-done | bytes 524304 | tf_op jit(solution)/shard_map/reduce_scatter | solution.py:312
  1721.6 214.3 %reduce-scatter.32.cloned.1.call-done = f32[2,64,3,512]{3,1,2,0:T(8,128)} async-done(((f32[2,1024,3,512]{3,1,2,0:T(8,128)}), f32[2,64,3,512]{3,1,2,0:T(8,128)}) %reduce-scatter.32.cloned.1.call-update) | async-done | bytes 786448 | tf_op jit(solution)/shard_map/reduce_scatter | solution.py:316
  1935.9 348.9 %reduce-scatter.36.cloned.1.call-done = f32[2,64,2048]{2,1,0:T(8,128)} async-done(((f32[2,1024,2048]{2,1,0:T(8,128)}), f32[2,64,2048]{2,1,0:T(8,128)}) %reduce-scatter.36.cloned.1.call-update) | async-done | bytes 1048592 | tf_op jit(solution)/shard_map/reduce_scatter | solution.py:321
  2284.7 354.8 %reduce-scatter.38.cloned.1.call-done = f32[2,64,2048]{2,1,0:T(8,128)} async-done(((f32[2,1024,2048]{2,1,0:T(8,128)}), f32[2,64,2048]{2,1,0:T(8,128)}) %reduce-scatter.38.cloned.1.call-update) | async-done | bytes 1048592 | tf_op jit(solution)/shard_map/reduce_scatter | solution.py:323
  (496 shorter events, 422.7 us)
Async XLA Ops:
  7.2 48.4 %all-reduce.12.cloned.1.call-start = ((), (), s32[]{:S(2)}) async-start(), calls=%async_computation.13 | async-start | bytes 8454144 | tf_op jit(solution)/shard_map/psum | solution.py:139
  24.3 137.0 %all-reduce.14.cloned.1.call-start = ((), (), s32[]{:S(2)}) async-start(), calls=%async_computation.14 | async-start | bytes 8454144 | tf_op jit(solution)/shard_map/psum | solution.py:155
  34.6 126.7 %copy-start.62 = (f32[1,1024]{1,0:T(1,128)}, f32[1,1024]{1,0:T(1,128)S(1)}, u32[]{:S(2)}) copy-start(f32[1,1024]{1,0:T(1,128)S(1)} %get-tuple-element.176) | copy-start | bytes 12292
  70.7 47.1 %copy-start.4 = (bf16[1026,1536]{0,1:T(8,128)(2,1)}, bf16[1026,1536]{0,1:T(8,128)(2,1)S(1)}, u32[]{:S(2)}) copy-start(bf16[1026,1536]{0,1:T(8,128)(2,1)S(1)} %copy.70) | copy-start | bytes 9455620
  131.5 93.1 %all-reduce.16.cloned.1.call-start = ((), (), s32[]{:S(2)}) async-start(), calls=%async_computation.15 | async-start | bytes 4227072 | tf_op jit(solution)/shard_map/psum | solution.py:166
  133.3 33.5 %copy-start.126 = (f32[1,1024]{1,0:T(1,128)}, f32[1,1024]{1,0:T(1,128)S(1)}, u32[]{:S(2)}) copy-start(f32[1,1024]{1,0:T(1,128)S(1)} %get-tuple-element.174) | copy-start | bytes 12292
  134.0 32.9 %copy-start.91 = (f32[1,1024]{1,0:T(1,128)}, f32[1,1024]{1,0:T(1,128)S(1)}, u32[]{:S(2)}) copy-start(f32[1,1024]{1,0:T(1,128)S(1)} %get-tuple-element.172) | copy-start | bytes 12292
  161.3 34.9 %slice-start.8 = ((s8[8388608]{0:T(1024)(128)(4,1)}), s8[4194304]{0:T(1024)(128)(4,1)S(1)}, s32[]{:S(2)}) async-start(s8[8388608]{0:T(1024)(128)(4,1)} %bitcast.451), calls=%async_computation.45 | async-start | bytes 8388608
  165.6 28.5 %copy-start.3 = (f32[1026,1024]{1,0:T(8,128)}, f32[1026,1024]{1,0:T(8,128)S(1)}, u32[]{:S(2)}) copy-start(f32[1026,1024]{1,0:T(8,128)S(1)} %get-tuple-element.152) | copy-start | bytes 12607492
  165.6 28.4 %copy-start.54 = (f32[1026]{0:T(1024)}, f32[1026]{0:T(1024)S(1)}, u32[]{:S(2)}) copy-start(f32[1026]{0:T(1024)S(1)} %broadcast_multiply_fusion.2) | copy-start | bytes 12316
  168.7 27.4 %slice-start.9 = ((s8[8388608]{0:T(1024)(128)(4,1)}), s8[4194304]{0:T(1024)(128)(4,1)S(1)}, s32[]{:S(2)}) async-start(s8[8388608]{0:T(1024)(128)(4,1)} %bitcast.451), calls=%async_computation.46 | async-start | bytes 8388608
  202.0 64.3 %all-reduce.18.cloned.1.call-start = ((), (), s32[]{:S(2)}) async-start(), calls=%async_computation.16 | async-start | bytes 8454144 | tf_op jit(solution)/shard_map/psum | solution.py:139
  236.4 29.9 %copy-start.64 = (f32[1,1024]{1,0:T(1,128)S(1)}, f32[1,1024]{1,0:T(1,128)}, u32[]{:S(2)}) copy-start(f32[1,1024]{1,0:T(1,128)} %get-tuple-element.175) | copy-start | bytes 12292
  236.4 135.6 %all-reduce.20.cloned.1.call-start = ((), (), s32[]{:S(2)}) async-start(), calls=%async_computation.17 | async-start | bytes 8454144 | tf_op jit(solution)/shard_map/psum | solution.py:155
  342.2 29.8 %copy-start.109 = (f32[1,1024]{1,0:T(1,128)S(1)}, f32[1,1024]{1,0:T(1,128)}, u32[]{:S(2)}) copy-start(f32[1,1024]{1,0:T(1,128)} %get-tuple-element.182) | copy-start | bytes 12292
  342.2 106.9 %all-reduce.22.cloned.1.call-start = ((), (), s32[]{:S(2)}) async-start(), calls=%async_computation.18 | async-start | bytes 4227072 | tf_op jit(solution)/shard_map/psum | solution.py:238
  372.0 33.3 %slice-start.10 = ((s8[8388608]{0:T(1024)(128)(4,1)}), s8[4194304]{0:T(1024)(128)(4,1)S(1)}, s32[]{:S(2)}) async-start(s8[8388608]{0:T(1024)(128)(4,1)} %bitcast.453), calls=%async_computation.47 | async-start | bytes 8388608
  376.3 29.0 %copy-start.1 = (f32[1026,1024]{1,0:T(8,128)}, f32[1026,1024]{1,0:T(8,128)S(1)}, u32[]{:S(2)}) copy-start(f32[1026,1024]{1,0:T(8,128)S(1)} %get-tuple-element.148) | copy-start | bytes 12607492
  376.4 82.7 %copy-start.60 = (f32[1026]{0:T(1024)}, f32[1026]{0:T(1024)S(1)}, u32[]{:S(2)}) copy-start(f32[1026]{0:T(1024)S(1)} %broadcast_multiply_fusion) | copy-start | bytes 12316
  377.0 82.1 %copy-start.81 = (f32[1026]{0:T(1024)}, f32[1026]{0:T(1024)S(1)}, u32[]{:S(2)}) copy-start(f32[1026]{0:T(1024)S(1)} %fusion.175) | copy-start | bytes 12316
  426.5 161.2 %all-reduce.24.cloned.1.call-start = ((), (), s32[]{:S(2)}) async-start(), calls=%async_computation.19 | async-start | bytes 4227072 | tf_op jit(solution)/shard_map/psum | solution.py:272
  565.1 27.7 %copy-start.88 = (f32[1026]{0:T(1024)S(1)}, f32[1026]{0:T(1024)}, u32[]{:S(2)}) copy-start(f32[1026]{0:T(1024)} %copy-done.87) | copy-start | bytes 12316
  565.1 27.7 %copy-start.79 = (f32[1026]{0:T(1024)S(1)}, f32[1026]{0:T(1024)}, u32[]{:S(2)}) copy-start(f32[1026]{0:T(1024)} %copy-done.78) | copy-start | bytes 12316
  565.1 65.0 %all-reduce.26.cloned.1.call-start = ((), (), s32[]{:S(2)}) async-start(), calls=%async_computation.20 | async-start | bytes 4227072 | tf_op jit(solution)/shard_map/psum | solution.py:15
  607.5 69.1 %all-reduce.28.cloned.1.call-start = ((), (), s32[]{:S(2)}) async-start(), calls=%async_computation.21 | async-start | bytes 4227072 | tf_op jit(solution)/shard_map/psum | solution.py:238
  654.0 168.8 %all-reduce.30.cloned.1.call-start = ((), (), s32[]{:S(2)}) async-start(), calls=%async_computation.36 | async-start | bytes 12681216 | tf_op jit(solution)/shard_map/psum | solution.py:166
  789.2 33.6 %copy-start.53 = (f32[1026]{0:T(1024)S(1)}, f32[1026]{0:T(1024)}, u32[]{:S(2)}) copy-start(f32[1026]{0:T(1024)} %copy-done.52) | copy-start | bytes 12316
  789.2 33.6 %copy-start.63 = (f32[1,1024]{1,0:T(1,128)S(1)}, f32[1,1024]{1,0:T(1,128)}, u32[]{:S(2)}) copy-start(f32[1,1024]{1,0:T(1,128)} %copy-done.62) | copy-start | bytes 12292
  789.2 33.6 %copy-start.98 = (f32[1,1024]{1,0:T(1,128)S(1)}, f32[1,1024]{1,0:T(1,128)}, u32[]{:S(2)}) copy-start(f32[1,1024]{1,0:T(1,128)} %copy-done.97) | copy-start | bytes 12292
  789.2 161.9 %reduce-scatter.52.cloned.1.call-start = ((), (), s32[]{:S(2)}) async-start(), calls=%async_computation.34 | async-start | bytes 1114112
  791.2 40.6 %slice-start = ((s8[4227072]{0:T(1024)(128)(4,1)}), s8[32768]{0:T(1024)(128)(4,1)S(1)}, s32[]{:S(2)}) async-start(s8[4227072]{0:T(1024)(128)(4,1)} %bitcast.321), calls=%async_computation.37 | async-start | bytes 65536
  791.3 187.9 %reduce-scatter.46.cloned.1.call-start = ((), (), s32[]{:S(2)}) async-start(), calls=%async_computation.31 | async-start | bytes 557056
  792.4 262.1 %reduce-scatter.48.cloned.1.call-start = ((), (), s32[]{:S(2)}) async-start(), calls=%async_computation.32 | async-start | bytes 557056
  793.5 335.9 %reduce-scatter.50.cloned.1.call-start = ((), (), s32[]{:S(2)}) async-start(), calls=%async_computation.33 | async-start | bytes 557056
  793.6 33.7 %copy-start.84 = (f32[1026]{0:T(1024)S(1)}, f32[1026]{0:T(1024)}, u32[]{:S(2)}) copy-start(f32[1026]{0:T(1024)} %copy-done.83) | copy-start | bytes 12316
  793.6 33.7 %copy-start.74 = (f32[1026]{0:T(1024)S(1)}, f32[1026]{0:T(1024)}, u32[]{:S(2)}) copy-start(f32[1026]{0:T(1024)} %copy-done.73) | copy-start | bytes 12316
  794.7 409.9 %reduce-scatter.54.cloned.1.call-start = ((), (), s32[]{:S(2)}) async-start(), calls=%async_computation.35 | async-start | bytes 557056
  795.9 483.7 %reduce-scatter.40.cloned.1.call-start = ((), (), s32[]{:S(2)}) async-start(), calls=%async_computation.28 | async-start | bytes 557056
  836.8 517.9 %reduce-scatter.42.cloned.1.call-start = ((), (), s32[]{:S(2)}) async-start(), calls=%async_computation.29 | async-start | bytes 557056
  838.0 591.8 %reduce-scatter.44.cloned.1.call-start = ((), (), s32[]{:S(2)}) async-start(), calls=%async_computation.30 | async-start | bytes 557056
  839.1 602.9 %all-gather.2.cloned.1.call-start = ((), (), s32[]{:S(2)}) async-start(), calls=%async_computation.22 | async-start | bytes 6340608 | tf_op jit(solution)/shard_map/all_gather | solution.py:191
  844.6 696.6 %reduce-scatter.34.cloned.1.call-start = ((), (), s32[]{:S(2)}) async-start(), calls=%async_computation.25 | async-start | bytes 4456448 | tf_op jit(solution)/shard_map/reduce_scatter | solution.py:317
  854.9 866.7 %reduce-scatter.30.cloned.1.call-start = ((), (), s32[]{:S(2)}) async-start(), calls=%async_computation.23 | async-start | bytes 8912896 | tf_op jit(solution)/shard_map/reduce_scatter | solution.py:312
  869.5 1066.4 %reduce-scatter.32.cloned.1.call-start = ((), (), s32[]{:S(2)}) async-start(), calls=%async_computation.24 | async-start | bytes 13369344 | tf_op jit(solution)/shard_map/reduce_scatter | solution.py:316
  901.5 1383.2 %reduce-scatter.36.cloned.1.call-start = ((), (), s32[]{:S(2)}) async-start(), calls=%async_computation.26 | async-start | bytes 17825792 | tf_op jit(solution)/shard_map/reduce_scatter | solution.py:321
  928.0 1711.6 %reduce-scatter.38.cloned.1.call-start = ((), (), s32[]{:S(2)}) async-start(), calls=%async_computation.27 | async-start | bytes 17825792 | tf_op jit(solution)/shard_map/reduce_scatter | solution.py:323
  951.1 254.9 %copy-start.39 = (bf16[1026,1024]{1,0:T(8,128)(2,1)S(1)}, bf16[1026,1024]{1,0:T(8,128)(2,1)}, u32[]{:S(2)}) copy-start(bf16[1026,1024]{1,0:T(8,128)(2,1)} %get-tuple-element.134) | copy-start | bytes 6303748
  951.1 254.9 %copy-start.106 = (f32[1,1024]{1,0:T(1,128)S(1)}, f32[1,1024]{1,0:T(1,128)}, u32[]{:S(2)}) copy-start(f32[1,1024]{1,0:T(1,128)} %get-tuple-element.169) | copy-start | bytes 12292
  (128 other events, 887.1 us)
Sparse Core Ops, SparseCore 0:
  24.4 31.1 all-reduce.11
  131.6 29.6 all-reduce.13
  202.1 22.4 all-reduce.15
  236.6 29.6 all-reduce.17
  342.3 29.6 all-reduce.19
  426.7 22.4 all-reduce.21
  565.2 22.4 all-reduce.23
  607.7 22.4 all-reduce.25
  654.1 22.4 all-reduce.27
  789.3 33.4 all-reduce.29
  825.2 78.8 reduce-scatter.51
  906.1 72.9 reduce-scatter.45
  981.5 72.9 reduce-scatter.47
  1056.5 72.8 reduce-scatter.49
  1131.6 72.8 reduce-scatter.53
  1206.7 72.8 reduce-scatter.39
  1281.8 72.8 reduce-scatter.41
  1356.8 72.8 reduce-scatter.43
  1431.9 10.0 all-gather.1
  1444.8 96.2 reduce-scatter.33
  1544.1 177.3 reduce-scatter.29
  1728.7 207.0 reduce-scatter.31
  1938.7 345.9 reduce-scatter.35
  2287.5 352.0 reduce-scatter.37
where the time goes:
time: 2660 us; the launch traced here: 2650 us
  waiting for transfers between devices  1870 us (70%)
  matrix products  424 us (16%)
  other arithmetic  218 us (8%)
  local copies, waits for them, and re-layouts  118 us (4%)
    unnamed x32, waiting for transfers between devices  465 us
    reduce_scatter x1, waiting for transfers between devices, sum_stacked(): lax.psum_scatter(stacked[11], 'dp', scatter_dimension=1, tiled=True)  355 us
    reduce_scatter x1, waiting for transfers between devices, sum_stacked(): lax.psum_scatter(stacked[9], 'dp', scatter_dimension=1, tiled=True)  349 us
    reduce_scatter x1, waiting for transfers between devices, sum_stacked(): lax.psum_scatter(stacked[4], 'dp', scatter_dimension=1, tiled=True)  214 us
    reduce_scatter x1, waiting for transfers between devices, sum_stacked(): lax.psum_scatter(stacked[0], 'dp', scatter_dimension=1, tiled=True)  180 us
    unnamed x323, local copies, waits for them, and re-layouts  81.9 us
    reduce_scatter x1, waiting for transfers between devices, sum_stacked(): lax.psum_scatter(stacked[5], 'dp', scatter_dimension=1, tiled=True)  64.7 us
    psum x2, waiting for transfers between devices, layer_forward(): lax.psum(jnp.einsum('rc,dc->rd', attended, proj_matrix, preferred_element...  56.5 us
  transfers between devices with their start and end apart: 24, of which 23 were waited for; matrix products, arithmetic and copies ran while one was open for 8% of the time, Pallas kernels for 0%

commit v1 on v0

v1 whole, which is shorter than its diff:
```python
import functools
import jax
import jax.numpy as jnp
from jax import lax
from jax.experimental import pallas as pl
from jax.experimental.pallas import tpu as pltpu
from jax.sharding import PartitionSpec as P

F32 = jnp.float32
BF16 = jnp.bfloat16
HD = 64
MAIN = 512
PAD = 528
GROUP = 256
HEADS_IN_GROUP = GROUP // HD
VMEM_LIMIT = 60 * 1024 * 1024


def _dot(a, b, dims):
    return lax.dot_general(a, b, (dims, ((), ())), preferred_element_type=F32)


def _extra_rows(mine_ref, other_ref):
    row = lax.broadcasted_iota(jnp.int32, (16, GROUP), 0)
    lane = lax.broadcasted_iota(jnp.int32, (16, GROUP), 1)
    mine = jnp.broadcast_to(mine_ref[MAIN : MAIN + 16, :][0:1].astype(F32), (16, GROUP))
    other = jnp.broadcast_to(other_ref[MAIN : MAIN + 16, :][0:1].astype(F32), (16, GROUP))
    value = jnp.where(row % 2 == 0, mine, other)
    return jnp.where(row // 2 == lane // HD, value, 0.0).astype(BF16)


def _attn_fwd_kernel(q_ref, km_ref, vm_ref, ko_ref, vo_ref, o_ref, e_ref, ex_ref, il_ref, k_s, v_s):
    k_s[:MAIN] = km_ref[:MAIN]
    k_s[MAIN:] = ko_ref[:MAIN]
    v_s[:MAIN] = vm_ref[:MAIN]
    v_s[MAIN:] = vo_ref[:MAIN]
    lane = lax.broadcasted_iota(jnp.int32, (PAD, GROUP), 1) // HD
    slot = lax.broadcasted_iota(jnp.int32, (PAD, 16), 1) // 2
    q = q_ref[...] * jnp.asarray(HD**-0.5, BF16)
    kx = _extra_rows(km_ref, ko_ref)
    vx = _extra_rows(vm_ref, vo_ref)
    sx = _dot(q, kx, ((1,), (1,)))
    out = jnp.zeros((PAD, GROUP), F32)
    ex_all = jnp.zeros((PAD, 16), F32)
    il_all = jnp.zeros((PAD, 16), F32)
    for h in range(HEADS_IN_GROUP):
        qh = jnp.where(lane == h, q, jnp.zeros_like(q))
        s = _dot(qh, k_s[...], ((1,), (1,)))
        sxh = jnp.where(slot == h, sx, -jnp.inf)
        top = jnp.maximum(jnp.max(s, axis=1, keepdims=True), jnp.max(sxh, axis=1, keepdims=True))
        e = jnp.exp(s - top)
        exh = jnp.exp(sxh - top)
        total = jnp.sum(e, axis=1, keepdims=True) + jnp.sum(exh, axis=1, keepdims=True)
        inverse = 1.0 / total
        low = e.astype(BF16)
        e_ref[h] = low
        out = out + jnp.where(lane == h, _dot(low, v_s[...], ((1,), (0,))) * inverse, 0.0)
        ex_all = ex_all + exh
        il_all = il_all + jnp.where(slot == h, inverse, 0.0)
    out = out + _dot((ex_all * il_all).astype(BF16), vx, ((1,), (0,)))
    o_ref[...] = out.astype(BF16)
    ex_ref[0] = ex_all
    il_ref[0] = il_all


def attn_forward(q, kv, kv_other):
    width = q.shape[1]
    groups = width // GROUP

    def near(offset):
        return pl.BlockSpec((PAD, GROUP), lambda g: (0, g + offset))

    def far(offset):
        return pl.BlockSpec((PAD, GROUP), lambda g: (0, (g + groups // 2) % groups + offset))

    heads = width // HD
    elements = heads * PAD * (2 * MAIN)
    return pl.pallas_call(
        _attn_fwd_kernel,
        grid=(groups,),
        in_specs=[near(0), near(0), near(groups), far(0), far(groups)],
        out_specs=[
            near(0),
            pl.BlockSpec((HEADS_IN_GROUP, PAD, 2 * MAIN), lambda g: (g, 0, 0)),
            pl.BlockSpec((1, PAD, 16), lambda g: (g, 0, 0)),
            pl.BlockSpec((1, PAD, 16), lambda g: (g, 0, 0)),
        ],
        out_shape=[
            jax.ShapeDtypeStruct((PAD, width), BF16),
            jax.ShapeDtypeStruct((heads, PAD, 2 * MAIN), BF16),
            jax.ShapeDtypeStruct((groups, PAD, 16), F32),
            jax.ShapeDtypeStruct((groups, PAD, 16), F32),
        ],
        scratch_shapes=[pltpu.VMEM((2 * MAIN, GROUP), BF16), pltpu.VMEM((2 * MAIN, GROUP), BF16)],
        compiler_params=pltpu.CompilerParams(vmem_limit_bytes=VMEM_LIMIT),
        cost_estimate=pl.CostEstimate(
            flops=4 * elements * GROUP, bytes_accessed=3 * elements, transcendentals=elements
        ),
        name="attn_forward",
    )(q, kv, kv, kv_other, kv_other)


def _attn_bwd_kernel(
    q_ref, km_ref, vm_ref, ko_ref, vo_ref, do_ref, o_ref, e_ref, ex_ref, il_ref,
    dq_ref, dkm_ref, dko_ref, dvm_ref, dvo_ref, k_s, v_s, dk_s, dv_s,
):
    k_s[:MAIN] = km_ref[:MAIN]
    k_s[MAIN:] = ko_ref[:MAIN]
    v_s[:MAIN] = vm_ref[:MAIN]
    v_s[MAIN:] = vo_ref[:MAIN]
    scale = HD**-0.5
    lane = lax.broadcasted_iota(jnp.int32, (PAD, GROUP), 1) // HD
    slot = lax.broadcasted_iota(jnp.int32, (PAD, 16), 1) // 2
    q = q_ref[...] * jnp.asarray(scale, BF16)
    kx = _extra_rows(km_ref, ko_ref)
    vx = _extra_rows(vm_ref, vo_ref)
    il = il_ref[0]
    do = do_ref[...].astype(F32)
    product = do * o_ref[...].astype(F32)
    spread = jnp.zeros((PAD, GROUP), F32)
    inner = jnp.zeros((PAD, 16), F32)
    inners = []
    for h in range(HEADS_IN_GROUP):
        inverse = il[:, 2 * h : 2 * h + 1]
        spread = jnp.where(lane == h, inverse, spread)
        one = jnp.sum(jnp.where(lane == h, product, 0.0), axis=1, keepdims=True) * inverse
        inners.append(one)
        inner = jnp.where(slot == h, one, inner)
    dos = (do * spread).astype(BF16)
    dos_t = dos.T
    q_t = q.T
    dq = jnp.zeros((PAD, GROUP), F32)
    for h in range(HEADS_IN_GROUP):
        rows = slice(h * HD, (h + 1) * HD)
        dosh = jnp.where(lane == h, dos, jnp.zeros_like(dos))
        e = e_ref[h]
        dp = _dot(dosh, v_s[...], ((1,), (1,)))
        ds = (e.astype(F32) * (dp - inners[h])).astype(BF16)
        dq = dq + jnp.where(lane == h, _dot(ds, k_s[...], ((1,), (0,))), 0.0)
        dk_s[rows, :] = (
            _dot(q_t[rows, :MAIN], ds[:MAIN], ((1,), (0,)))
            + q_t[rows, MAIN : MAIN + 1].astype(F32) * ds[MAIN : MAIN + 16].astype(F32)[0:1]
        )
        dv_s[rows, :] = (
            _dot(dos_t[rows, :MAIN], e[:MAIN], ((1,), (0,)))
            + dos_t[rows, MAIN : MAIN + 1].astype(F32) * e[MAIN : MAIN + 16].astype(F32)[0:1]
        )
    ex = ex_ref[0]
    dsx = (ex * (_dot(dos, vx, ((1,), (1,))) - inner)).astype(BF16)
    dq = dq + _dot(dsx, kx, ((1,), (0,)))
    dq_ref[...] = (dq * scale).astype(BF16)
    dkx = _dot(dsx, q, ((0,), (0,)))
    dvx = _dot(ex.astype(BF16), dos, ((0,), (0,)))
    row = lax.broadcasted_iota(jnp.int32, (16, GROUP), 0)
    own = row // 2 == lax.broadcasted_iota(jnp.int32, (16, GROUP), 1) // HD
    for half, (dk_ref, dv_ref) in enumerate(((dkm_ref, dvm_ref), (dko_ref, dvo_ref))):
        keep = jnp.logical_and(own, row % 2 == half)
        for ref, grad_s, tail in ((dk_ref, dk_s, dkx), (dv_ref, dv_s, dvx)):
            ref[:MAIN] = grad_s[:, half * MAIN : (half + 1) * MAIN].T.astype(BF16)
            last = jnp.sum(jnp.where(keep, tail, 0.0), axis=0, keepdims=True)
            ref[MAIN:] = jnp.where(row == 0, jnp.broadcast_to(last, (16, GROUP)), 0.0).astype(BF16)


def attn_backward(q, kv, kv_other, dout, out, e, ex, il):
    width = q.shape[1]
    groups = width // GROUP

    def near(offset):
        return pl.BlockSpec((PAD, GROUP), lambda g: (0, g + offset))

    def far(offset):
        return pl.BlockSpec((PAD, GROUP), lambda g: (0, (g + groups // 2) % groups + offset))

    small = pl.BlockSpec((1, PAD, 16), lambda g: (g, 0, 0))
    heads = width // HD
    elements = heads * PAD * (2 * MAIN)
    block = jax.ShapeDtypeStruct((PAD, width), BF16)
    far_out = pl.BlockSpec((PAD, GROUP), lambda g: (0, (g + groups // 2) % groups))
    return pl.pallas_call(
        _attn_bwd_kernel,
        grid=(groups,),
        in_specs=[
            near(0), near(0), near(groups), far(0), far(groups), near(0), near(0),
            pl.BlockSpec((HEADS_IN_GROUP, PAD, 2 * MAIN), lambda g: (g, 0, 0)), small, small,
        ],
        out_specs=[near(0), near(0), far_out, near(0), far_out],
        out_shape=[block] * 5,
        scratch_shapes=[
            pltpu.VMEM((2 * MAIN, GROUP), BF16),
            pltpu.VMEM((2 * MAIN, GROUP), BF16),
            pltpu.VMEM((GROUP, 2 * MAIN), F32),
            pltpu.VMEM((GROUP, 2 * MAIN), F32),
        ],
        compiler_params=pltpu.CompilerParams(vmem_limit_bytes=VMEM_LIMIT),
        cost_estimate=pl.CostEstimate(
            flops=8 * elements * GROUP, bytes_accessed=3 * elements, transcendentals=0
        ),
        name="attn_backward",
    )(q, kv, kv, kv_other, kv_other, dout, out, e, ex, il)


def _grad_kernel(has_received, pieces, coords_ref, x_ref, dy_ref, *refs):
    if has_received:
        received_ref, send_ref, keep_ref, xt_s, column_s = refs
    else:
        all_ref, xt_s, column_s = refs
    rows = xt_s.shape[0] // pieces
    span = max(rows, 128)

    @pl.when(pl.program_id(0) == 0)
    def _():
        for start in range(0, xt_s.shape[0], span):
            turned = x_ref[:MAIN, start : start + span].T
            last = x_ref[MAIN:, start : start + span].T.astype(F32)[:, 0:1]
            for part in range(span // rows):
                piece = start // rows + part
                first = jnp.bitwise_xor((piece >> coords_ref[2]) & 1, coords_ref[0])
                second = jnp.bitwise_xor((piece >> coords_ref[3]) & 1, coords_ref[1])
                place = first * (pieces // 2) + second * (pieces // 4) + (piece >> 2)
                at = pl.ds(pl.multiple_of(place * rows, rows), rows)
                xt_s[at, :] = turned[part * rows : (part + 1) * rows]
                column_s[at, :] = jnp.broadcast_to(
                    last[part * rows : (part + 1) * rows], (rows, 128)
                )

    width = dy_ref.shape[1]
    half = xt_s.shape[0] // 2
    last_row = dy_ref[MAIN:, :].astype(F32)[0:1]
    for part in range(2):
        at = slice(part * half, (part + 1) * half)
        total = _dot(xt_s[at, :], dy_ref[:MAIN, :], ((1,), (0,)))
        column = jnp.concatenate([column_s[at, :]] * (width // 128), axis=1)
        total = total + column * last_row
        if has_received:
            total = total + received_ref[at, :].astype(F32)
            (keep_ref if part == 0 else send_ref)[...] = total.astype(BF16)
        else:
            all_ref[at, :] = total.astype(BF16)


def weight_grad(coords, pieces, x, dy, offset, width, received=None):
    features = x.shape[1]
    tile = 512
    start = offset // tile
    in_specs = [
        pl.BlockSpec((PAD, features), lambda j, c: (0, 0)),
        pl.BlockSpec((PAD, tile), lambda j, c: (0, start + j)),
    ]
    whole = pl.BlockSpec((features, tile), lambda j, c: (0, j))
    half = pl.BlockSpec((features // 2, tile), lambda j, c: (0, j))
    operands = [x, dy]
    if received is None:
        out_specs = [whole]
        out_shape = [jax.ShapeDtypeStruct((features, width), BF16)]
    else:
        in_specs.append(whole)
        operands.append(received)
        out_specs = [half, half]
        out_shape = [jax.ShapeDtypeStruct((features // 2, width), BF16)] * 2
    result = pl.pallas_call(
        functools.partial(_grad_kernel, received is not None, pieces),
        grid_spec=pltpu.PrefetchScalarGridSpec(
            num_scalar_prefetch=1,
            grid=(width // tile,),
            in_specs=in_specs,
            out_specs=out_specs,
            scratch_shapes=[
                pltpu.VMEM((features, MAIN), BF16),
                pltpu.VMEM((features, 128), F32),
            ],
        ),
        out_shape=out_shape,
        compiler_params=pltpu.CompilerParams(vmem_limit_bytes=VMEM_LIMIT),
        cost_estimate=pl.CostEstimate(
            flops=2 * PAD * features * width,
            bytes_accessed=2 * features * width * (1 if received is None else 2),
            transcendentals=0,
        ),
        name="weight_grad",
    )(coords, *operands)
    return result[0] if received is None else result


epsilon = 1e-05


def swap_cores(value):
    return lax.ppermute(value, "tensor", [(0, 1), (1, 0)])


def swap_bit(value, bit, size):
    return lax.ppermute(value, "dp", [(i, i ^ (1 << bit)) for i in range(size)])


def add_low(a, b):
    return (a.astype(F32) + b.astype(F32)).astype(BF16)


class Reducer:
    def __init__(self, size):
        self.size = size
        self.bits = size.bit_length() - 1
        assert size == 1 << self.bits and self.bits >= 2
        self.index = lax.axis_index("dp")

    def bit(self, which):
        return (self.index >> which) & 1

    def order(self, flip):
        return (1, 0) if flip else (0, 1)

    def coords(self, flip):
        first, second = self.order(flip)
        values = [self.bit(first), self.bit(second), first, second]
        return jnp.stack([jnp.asarray(v, jnp.int32) for v in values])

    def arrange(self, value, flip):
        first, second = self.order(flip)
        rows = value.shape[0] // self.size
        view = value.reshape(self.size // 4, 2, 2, rows, value.shape[1])
        if not flip:
            view = view.transpose(2, 1, 0, 3, 4)
        else:
            view = view.transpose(1, 2, 0, 3, 4)
        view = jnp.where(self.bit(first) == 1, view[::-1], view)
        view = jnp.where(self.bit(second) == 1, view[:, ::-1], view)
        return view.reshape(value.shape)

    def finish(self, keep, send, flip):
        first, second = self.order(flip)
        got = swap_bit(send, first, self.size)
        half = keep.shape[0] // 2
        send = add_low(keep[half:], got[half:])
        keep = add_low(keep[:half], got[:half])
        got = swap_bit(send, second, self.size)
        total = add_low(keep, got)
        width = total.shape[1]
        rows = total.shape[0] // (self.size // 4)
        blocks = self.size // 4
        for which in range(2, self.bits):
            view = total.reshape(blocks // 2, 2, rows, width)
            mine = self.bit(which)
            keep = lax.dynamic_index_in_dim(view, mine, 1, keepdims=False)
            send = lax.dynamic_index_in_dim(view, 1 - mine, 1, keepdims=False)
            got = swap_bit(send, which, self.size)
            if which == self.bits - 1:
                total = keep.astype(F32) + got.astype(F32)
            else:
                total = add_low(keep, got)
            blocks = blocks // 2
        return total.reshape(rows, width)


def localize(value, core):
    main = lax.dynamic_slice_in_dim(value, core * MAIN, MAIN, 0)
    extra = lax.dynamic_slice_in_dim(value, 2 * MAIN + core, 1, 0)
    blank = jnp.zeros((PAD - MAIN - 1, value.shape[1]), value.dtype)
    return jnp.concatenate([main, extra, blank], axis=0)


def globalize(mine, core):
    theirs = swap_cores(mine)
    low = jnp.where(core == 0, mine, theirs)
    high = jnp.where(core == 0, theirs, mine)
    return jnp.concatenate(
        [low[:MAIN], high[:MAIN], low[MAIN : MAIN + 1], high[MAIN : MAIN + 1]], axis=0
    )


def layer_norm(values_in, gain_row, shift_row):
    average = jnp.mean(values_in, axis=-1, keepdims=True)
    centred = values_in - average
    variance = jnp.mean(centred * centred, axis=-1, keepdims=True)
    return centred * lax.rsqrt(variance + epsilon) * gain_row + shift_row


def norm_backward(values_in, gain_row, grad):
    average = jnp.mean(values_in, axis=-1, keepdims=True)
    centred = values_in - average
    variance = jnp.mean(centred * centred, axis=-1, keepdims=True)
    inverse = lax.rsqrt(variance + epsilon)
    normed = centred * inverse
    scaled = grad * gain_row
    back = (
        scaled
        - jnp.mean(scaled, axis=-1, keepdims=True)
        - normed * jnp.mean(scaled * normed, axis=-1, keepdims=True)
    ) * inverse
    return back, jnp.sum(grad * normed, axis=0), jnp.sum(grad, axis=0)


def matmul(a, b):
    return _dot(a, b, ((1,), (0,)))


def matmul_t(a, b):
    return _dot(a, b, ((1,), (1,)))


def gelu_parts(up):
    cumulative = 0.5 * lax.erfc(-up * (0.5**0.5))
    density = jnp.exp(-0.5 * up * up) * 0.3989422804014327
    return up * cumulative, cumulative + up * density


def both(own, axis):
    return jnp.concatenate([own, swap_cores(own)], axis=axis)


def layer_forward(residual, skip_rows, params, core):
    (
        skip_own, skip_peer, skip_offset, gain_one, shift_one, qkv_matrix, proj_matrix, proj_offset,
        gain_two, shift_two, up_matrix, up_offset, down_matrix, down_offset,
    ) = params
    first = residual.astype(BF16)
    x_own = jnp.where(core == 0, first, skip_rows)
    x_peer = jnp.where(core == 0, skip_rows, first)
    hidden = matmul(x_own, skip_own) + matmul(x_peer, skip_peer) + skip_offset
    normed_one = layer_norm(hidden, gain_one, shift_one).astype(BF16)
    width = qkv_matrix.shape[1] // 3
    kv = matmul(normed_one, qkv_matrix[:, width:]).astype(BF16)
    kv_other = swap_cores(kv)
    q = matmul(normed_one, qkv_matrix[:, :width]).astype(BF16)
    attended, e, ex, il = attn_forward(q, kv, kv_other)
    middle = hidden + matmul_t(attended, proj_matrix) + proj_offset
    normed_two = layer_norm(middle, gain_two, shift_two).astype(BF16)
    up = matmul(normed_two, up_matrix) + up_offset
    activation, slope = gelu_parts(up)
    activation = activation.astype(BF16)
    slope = slope.astype(BF16)
    result = middle + matmul_t(activation, down_matrix) + down_offset
    kept = (x_own, x_peer, hidden, normed_one, q, kv, kv_other, attended, e, ex, il, middle, normed_two,
            activation, slope)
    return result, kept


def layer_backward(gradient, kept, params, core, reducer):
    (
        skip_own, skip_peer, skip_offset, gain_one, shift_one, qkv_matrix, proj_matrix, proj_offset,
        gain_two, shift_two, up_matrix, up_offset, down_matrix, down_offset,
    ) = params
    (x_own, x_peer, hidden, normed_one, q, kv, kv_other, attended, e, ex, il, middle, normed_two,
     activation, slope) = kept
    size = reducer.size

    def reduced(pairs, flip):
        coords = reducer.coords(flip)
        keeps, sends = [], []
        for x, x_other, dy, own_at, peer_at, width in pairs:
            theirs = weight_grad(coords, size, x_other, dy, peer_at, width)
            got = swap_cores(theirs)
            send, keep = weight_grad(coords, size, x, dy, own_at, width, got)
            keeps.append(keep)
            sends.append(send)
        return reducer.finish(jnp.concatenate(keeps, axis=1), jnp.concatenate(sends, axis=1), flip)

    model = gradient.shape[1]
    half_units = activation.shape[1] // 2
    grad_low = gradient.astype(BF16)
    down_offset_grad = jnp.sum(gradient, axis=0)
    down_grad = reduced([(grad_low, grad_low, activation, 0, half_units, half_units)], False)
    act_grad = matmul(grad_low, down_matrix)
    up_grad = act_grad * slope.astype(F32)
    up_offset_grad = jnp.sum(up_grad, axis=0)
    up_low = up_grad.astype(BF16)
    up_matrix_grad = reduced([(normed_two, normed_two, up_low, 0, half_units, half_units)], True)
    normed_two_grad = matmul_t(up_low, up_matrix)
    middle_part, gain_two_grad, shift_two_grad = norm_backward(middle, gain_two, normed_two_grad)
    middle_grad = gradient + middle_part
    proj_offset_grad = jnp.sum(middle_grad, axis=0)
    middle_low = middle_grad.astype(BF16)
    attended_grad = matmul(middle_low, proj_matrix).astype(BF16)
    half_heads = model // 2
    proj_grad = reduced([(middle_low, middle_low, attended, 0, half_heads, half_heads)], False)
    dq, dk_mine, dk_other, dv_mine, dv_other = attn_backward(
        q, kv, kv_other, attended_grad, attended, e, ex, il
    )
    dk_got = swap_cores(dk_other)
    dv_got = swap_cores(dv_other)
    dk = add_low(dk_mine, dk_got)
    dv = add_low(dv_mine, dv_got)
    dqkv = jnp.concatenate([dq, dk, dv], axis=1)
    normed_one_grad = matmul_t(dqkv, qkv_matrix)
    qkv_grad = reduced(
        [
            (normed_one, normed_one, dqkv, part * model, part * model + half_heads, half_heads)
            for part in range(3)
        ],
        True,
    )
    hidden_part, gain_one_grad, shift_one_grad = norm_backward(hidden, gain_one, normed_one_grad)
    hidden_grad = middle_grad + hidden_part
    skip_offset_grad = jnp.sum(hidden_grad, axis=0)
    hidden_low = hidden_grad.astype(BF16)
    skip_grad = reduced([(x_own, x_peer, hidden_low, 0, 0, model)], False)
    back_own = matmul_t(hidden_low, skip_own)
    back_peer = matmul_t(hidden_low, skip_peer)
    residual_part = jnp.where(core == 0, back_own, back_peer)
    skip_part = jnp.where(core == 0, back_peer, back_own).astype(BF16)
    weights = (skip_grad, qkv_grad, proj_grad, up_matrix_grad, down_grad)
    shared = jnp.stack(
        [skip_offset_grad, gain_one_grad, shift_one_grad, proj_offset_grad, gain_two_grad,
         shift_two_grad, down_offset_grad]
    )
    return residual_part, skip_part, weights, shared, up_offset_grad


def sum_vectors(shared, up_offsets, reducer):
    layers, count, width = shared.shape
    half = up_offsets.shape[1] // 2
    shared = shared.reshape(layers * count, width)

    def columns(value):
        parts = value.reshape(layers, reducer.size, half // width, width // reducer.size)
        return parts.transpose(0, 2, 1, 3).reshape(-1, width)

    mine = jnp.concatenate([shared, columns(up_offsets[:, :half])], axis=0).T
    theirs = jnp.concatenate([shared, columns(up_offsets[:, half:])], axis=0).T
    total = add_low(mine, swap_cores(theirs.astype(BF16)))
    total = reducer.arrange(total, False)
    middle = total.shape[0] // 2
    result = reducer.finish(total[:middle], total[middle:], False).T
    vectors = result[: layers * count].reshape(layers, count, -1)
    return vectors, result[layers * count :].reshape(layers, -1)


def body(
    inputs, skips, cotangent, skip_weight, skip_bias, attn_norm_gain, attn_norm_bias, qkv_weight,
    proj_weight, proj_bias, ffn_norm_gain, ffn_norm_bias, up_weight, up_bias, down_weight, down_bias,
):
    core = lax.axis_index("tensor")
    reducer = Reducer(lax.axis_size("dp"))
    layer_total, model = skip_bias.shape
    skip_own = skip_weight[:, 0]
    skip_peer = swap_cores(skip_own)
    qkv_full = jnp.stack([qkv_weight, swap_cores(qkv_weight)], axis=3)
    qkv_full = qkv_full.reshape(layer_total, model, -1)
    proj_full = both(proj_weight, 2)
    up_full = both(up_weight, 2)
    down_full = both(down_weight, 2)
    units = up_weight.shape[2]
    up_own = up_bias
    up_bias_full = jnp.concatenate([up_own, swap_cores(up_own)], axis=1)
    rows = tuple(
        item.astype(F32)
        for item in (skip_bias, attn_norm_gain, attn_norm_bias, proj_bias, ffn_norm_gain,
                     ffn_norm_bias, up_bias_full, down_bias)
    )
    every = (
        skip_own, skip_peer, rows[0], rows[1], rows[2], qkv_full, proj_full, rows[3], rows[4], rows[5],
        up_full, rows[6], down_full, rows[7],
    )
    residual = localize(inputs, core).astype(F32)
    saved = []
    for layer_index in range(layer_total):
        params = tuple(item[layer_index] for item in every)
        skip_rows = localize(skips[layer_index], core)
        residual, kept = layer_forward(residual, skip_rows, params, core)
        saved.append(kept)
    output = globalize(residual.astype(BF16), core)
    gradient = localize(cotangent, core).astype(F32)
    skip_grads, collected, shared, offsets = [], [], [], []
    for layer_index in reversed(range(layer_total)):
        params = tuple(item[layer_index] for item in every)
        gradient, skip_part, weights, vector, offset = layer_backward(
            gradient, saved[layer_index], params, core, reducer
        )
        skip_grads.insert(0, globalize(skip_part, core))
        collected.insert(0, weights)
        shared.insert(0, vector)
        offsets.insert(0, offset)
    vectors, up_bias_grad = sum_vectors(jnp.stack(shared), jnp.stack(offsets), reducer)
    skip_w, qkv_w, proj_w, up_w, down_w = (
        jnp.stack([entry[member] for entry in collected]) for member in range(5)
    )
    return (
        output, globalize(gradient.astype(BF16), core), jnp.stack(skip_grads), skip_w[:, None],
        vectors[:, 0], vectors[:, 1], vectors[:, 2],
        qkv_w.reshape(layer_total, -1, 3, qkv_weight.shape[3]), proj_w, vectors[:, 3], vectors[:, 4],
        vectors[:, 5], up_w, up_bias_grad, down_w, vectors[:, 6],
    )


def solution(mesh):
    return jax.shard_map(
        body,
        mesh=mesh,
        in_specs=(
            P("dp", None), P(None, "dp", None), P("dp", None), P(None, "tensor", None, None), P(), P(),
            P(), P(None, None, None, "tensor"), P(None, None, "tensor"), P(), P(), P(),
            P(None, None, "tensor"), P(None, "tensor"), P(None, None, "tensor"), P(),
        ),
        out_specs=(
            P("dp", None), P("dp", None), P(None, "dp", None), P(None, "tensor", "dp", None),
            P(None, "dp"), P(None, "dp"), P(None, "dp"), P(None, "dp", None, "tensor"),
            P(None, "dp", "tensor"), P(None, "dp"), P(None, "dp"), P(None, "dp"),
            P(None, "dp", "tensor"), P(None, ("tensor", "dp")), P(None, "dp", "tensor"), P(None, "dp"),
        ),
        check_vma=False,
    )
```

time: 2660 us -> 972 us (0.37)
  waiting for transfers between devices: 1870 us -> 235 us
  Pallas kernels: 0 us -> 236 us
  matrix products: 424 us -> 192 us
  other arithmetic: 218 us -> 79.2 us
  starting transfers between devices: 3.37 us -> 58.2 us
  local copies, waits for them, and re-layouts: 118 us -> 154 us
    reduce_scatter x5 -> x0, waiting for transfers between devices: 1160 us -> none  [the longest x1 355 us: sum_stacked(): lax.psum_scatter(stacked[11], 'dp', scatter_dimension=1, tiled=True)]
    unnamed x32 -> x0, waiting for transfers between devices: 465 us -> none
    pallas_call x0 -> x32, Pallas kernels: none -> 236 us  [the longest x28 150 us: weight_grad(): pl.pallas_call(functools.partial(_grad_kernel, received is not None, piec...]
    ppermute x0 -> x75, waiting for transfers between devices: none -> 235 us  [the longest x44 235 us: swap_bit(): return lax.ppermute(value, 'dp', [(i, i ^ 1 << bit) for i in range(size)])]
    dot_general x54 -> x26, matrix products: 424 us -> 192 us  [_dot(): return lax.dot_general(a, b, (dims, ((), ())), preferred_element_type=F32)]
    psum x10 -> x0, waiting for transfers between devices: 227 us -> none  [the longest x2 56.5 us: layer_forward(): lax.psum(jnp.einsum('rc,dc->rd', attended, proj_matrix, preferred_element...]
    reduce_sum x16 -> x1, other arithmetic: 91.9 us -> 3.08 us  [layer_backward(): down_offset_grad = jnp.sum(gradient, axis=0)]
    ppermute x0 -> x75, starting transfers between devices: none -> 58.2 us  [the longest x44 50.7 us: swap_bit(): return lax.ppermute(value, 'dp', [(i, i ^ 1 << bit) for i in range(size)])]
  transfers between devices with their start and end apart: 24 -> 75, of which waited for: 23 -> 26; matrix products, arithmetic and copies ran while one was open for 8% -> 31% of each run, Pallas kernels for 0% -> 18%
where the time goes in v1:
time: 972 us; the launch traced here: 959 us
  Pallas kernels  236 us (24%)
  waiting for transfers between devices  235 us (24%)
  matrix products  192 us (20%)
  local copies, waits for them, and re-layouts  154 us (16%)
  other arithmetic  79.2 us (8%)
  starting transfers between devices  58.2 us (6%)
    ppermute x44, waiting for transfers between devices, swap_bit(): return lax.ppermute(value, 'dp', [(i, i ^ 1 << bit) for i in range(size)])  235 us
    dot_general x26, matrix products, _dot(): return lax.dot_general(a, b, (dims, ((), ())), preferred_element_type=F32)  192 us
    pallas_call x28, Pallas kernels, weight_grad(): pl.pallas_call(functools.partial(_grad_kernel, received is not None, piec...  150 us
    unnamed x265, local copies, waits for them, and re-layouts  71.8 us
    ppermute x44, starting transfers between devices, swap_bit(): return lax.ppermute(value, 'dp', [(i, i ^ 1 << bit) for i in range(size)])  50.7 us
    pallas_call x2, Pallas kernels, attn_backward(): pl.pallas_call(_attn_bwd_kernel, grid=(groups,), in_specs=[near(0), near(...  49 us
    pallas_call x2, Pallas kernels, attn_forward(): pl.pallas_call(_attn_fwd_kernel, grid=(groups,), in_specs=[near(0), near(...  37.9 us
    convert_element_type x39, other arithmetic, add_low(): return (a.astype(F32) + b.astype(F32)).astype(BF16)  34.5 us
  transfers between devices with their start and end apart: 75, of which 26 were waited for; matrix products, arithmetic and copies ran while one was open for 31% of the time, Pallas kernels for 18%

profile of v1, /device:TPU:0, one launch (start us, length us, event | category | flops | bytes accessed | tf_op | source)
XLA Modules:
  0.0 958.6 jit_solution(5205354176807394374)
XLA Ops:
  1.2 8.7 copy.61
  10.9 9.7 %fusion.108 = (bf16[1,1026,1024]{2,0,1:T(2,128)(2,1)}, bf16[1,1026,1024]{2,0,1:T(2,128)(2,1)}) fusion(bf16[2,1026,1024]{2,0,1:T(2,128)(2,1)} %param.17), kind=kLoop, calls=%fused_computation.334 | loop fusion | bytes 8404992 | tf_op jit(solution)/shard_map/slice | solution.py:557
  41.4 8.3 constant_dynamic-update-slice_fusion.3
  49.7 8.3 constant_dynamic-update-slice_fusion.5
  65.5 7.3 pad_maximum_fusion
  80.7 8.3 constant_dynamic-update-slice_fusion.2
  89.1 8.3 constant_dynamic-update-slice_fusion.4
  97.4 18.8 %attn_forward.2 = (bf16[528,1024]{1,0:T(8,128)(2,1)}, bf16[16,528,1024]{2,1,0:T(8,128)(2,1)}, f32[4,528,16]{2,1,0:T(8,128)}, f32[4,528,16]{2,1,0:T(8,128)}) custom-call(bf16[528,1024]{1,0:T(8,128)(2,1)} %fusion.71.q_ref, bf16[528,2048]{1,0:T(8,128)(2,1)} %copy-done.119, bf16[528,2048]{1,0:T(8,128)(2,1)} %copy-done.119, ...), custom_call_target="tpu_custom_call" | custom-call | flops 8858370048 | bytes 25952256 | tf_op jit(solution)/shard_map/attn_forward/pallas_call | solution.py:78
  120.9 37.6 %multiply_convert_fusion.1 = (bf16[528,4096]{1,0:T(8,128)(2,1)S(1)}, f32[528,4096]{1,0:T(8,128)}, f32[528,4096]{1,0:T(8,128)}) fusion(f32[4096]{0:T(1024)S(1)} %bitcast.373, bf16[528,1024]{1,0:T(8,128)(2,1)S(1)} %add_convert_fusion.8.x_ref, bf16[2,1024,4096]{2,1,0:T(8,128)(2,1)} %constant_dynamic-update-slice_fusion.2), kind=kOutput, calls=%fused_computation.36 | convolution fusion | flops 4571922432 | bytes 31113216 | tf_op jit(solution)/shard_map/dot_general | solution.py:20
  158.5 10.1 %broadcast_select_fusion.9 = (bf16[528,1024]{1,0:T(8,128)(2,1)S(1)}, bf16[528,1024]{1,0:T(8,128)(2,1)S(1)}) fusion(pred[]{:T(512)S(6)} %eq.6, bf16[1,1024]{1,0:T(2,128)(2,1)S(1)} %fusion.96, bf16[512,1024]{1,0:T(8,128)(2,1)S(1)} %bitcast.333, bf16[528]{0:T(1024)(128)(2,1)S(1)} %pad.55.clone, f32[1024]{0:T(1024)S(1)} %bitcast.381, ...), kind=kOutput, calls=%fused_computation.182 | convolution fusion | flops 4435132416 | bytes 18095136 | tf_op jit(solution)/shard_map/dot_general | solution.py:20
  187.7 19.1 %attn_forward.3 = (bf16[528,1024]{1,0:T(8,128)(2,1)}, bf16[16,528,1024]{2,1,0:T(8,128)(2,1)}, f32[4,528,16]{2,1,0:T(8,128)}, f32[4,528,16]{2,1,0:T(8,128)}) custom-call(bf16[528,1024]{1,0:T(8,128)(2,1)} %fusion.74.q_ref, bf16[528,2048]{1,0:T(8,128)(2,1)} %fusion.42.km_ref.vm_ref, bf16[528,2048]{1,0:T(8,128)(2,1)} %fusion.42.km_ref.vm_ref, ...), custom_call_target="tpu_custom_call" | custom-call | flops 8858370048 | bytes 25952256 | tf_op jit(solution)/shard_map/attn_forward/pallas_call | solution.py:78
  211.3 27.1 %multiply_convert_fusion = (bf16[528,4096]{1,0:T(8,128)(2,1)}, f32[528,4096]{1,0:T(8,128)}, f32[528,4096]{1,0:T(8,128)}) fusion(f32[4096]{0:T(1024)S(1)} %bitcast.375, bf16[528,1024]{1,0:T(8,128)(2,1)S(1)} %add_convert_fusion.5.x_ref, bf16[2,1024,4096]{2,1,0:T(8,128)(2,1)} %constant_dynamic-update-slice_fusion.2), kind=kOutput, calls=%fused_computation.22 | convolution fusion | flops 4571922432 | bytes 31113216 | tf_op jit(solution)/shard_map/dot_general | solution.py:20
  238.5 12.1 %fusion.106 = (f32[4096]{0:T(1024)S(1)}, bf16[528,4096]{1,0:T(8,128)(2,1)S(1)}) fusion(f32[528,4096]{1,0:T(8,128)} %get-tuple-element.187, f32[528,4096]{1,0:T(8,128)} %get-tuple-element.246, f32[4096]{0:T(1024)S(1)} %bitcast.376, bf16[528,1024]{1,0:T(8,128)(2,1)S(1)} %copy-done.11, bf16[2,1024,4096]{2,1,0:T(8,128)(2,1)} %constant_dynamic-update-slice_fusion.4), kind=kOutput, calls=%fused_computation.332 | convolution fusion | flops 4452970496 | bytes 31129600 | tf_op jit(solution)/shard_map/dot_general | solution.py:20
  250.6 9.9 %multiply_reduce_fusion = (f32[1024]{0:T(1024)}, f32[528]{0:T(1024)S(1)}, f32[528]{0:T(1024)S(1)}, f32[1024]{0:T(1024)}, f32[528,1024]{1,0:T(8,128)S(1)}) fusion(f32[528,1024]{1,0:T(8,128)S(1)} %get-tuple-element.245, f32[528]{0:T(1024)S(1)} %add_rsqrt_fusion, f32[528]{0:T(1024)S(1)} %broadcast_multiply_fusion.8, f32[1024]{0:T(1024)S(1)} %bitcast.361, ...), kind=kOutput, calls=%fused_computation.77 | convolution fusion | flops 4434048000 | bytes 17060096 | tf_op jit(solution)/shard_map/dot_general | solution.py:20
  265.1 24.5 %attn_backward.2 = (bf16[528,1024]{1,0:T(8,128)(2,1)}, bf16[528,1024]{1,0:T(8,128)(2,1)}, bf16[528,1024]{1,0:T(8,128)(2,1)}, bf16[528,1024]{1,0:T(8,128)(2,1)}, bf16[528,1024]{1,0:T(8,128)(2,1)}) custom-call(bf16[528,1024]{1,0:T(8,128)(2,1)} %fusion.74.q_ref, bf16[528,2048]{1,0:T(8,128)(2,1)} %fusion.42.km_ref.vm_ref, ...), custom_call_target="tpu_custom_call" | custom-call | flops 17716740096 | bytes 25952256 | tf_op jit(solution)/shard_map/attn_backward/pallas_call | solution.py:179
  294.3 11.1 %add_convert_fusion.4 = bf16[528,1024]{1,0:T(8,128)(2,1)} fusion(f32[528,1024]{1,0:T(8,128)} %copy-done.9, bf16[528,4096]{1,0:T(8,128)(2,1)} %get-tuple-element.186.dy_ref, bf16[2,1024,4096]{2,1,0:T(8,128)(2,1)} %constant_dynamic-update-slice_fusion.4, f32[1024]{0:T(1024)S(1)} %bitcast.378), kind=kOutput, calls=%fused_computation.95 | convolution fusion | flops 4430807040 | bytes 15962112 | tf_op jit(solution)/shard_map/dot_general | solution.py:20
  305.9 7.2 weight_grad.54
  313.1 7.6 weight_grad.50
  332.0 7.5 multiply_reduce_fusion.1
  347.9 12.1 %fusion.107 = (f32[4096]{0:T(1024)S(1)}, bf16[528,4096]{1,0:T(8,128)(2,1)S(1)}) fusion(f32[528,4096]{1,0:T(8,128)} %get-tuple-element.189, f32[528,4096]{1,0:T(8,128)} %get-tuple-element.241, f32[4096]{0:T(1024)S(1)} %bitcast.374, bf16[528,1024]{1,0:T(8,128)(2,1)S(1)} %convert_element_type.716.x_ref, ...), kind=kOutput, calls=%fused_computation.333 | convolution fusion | flops 4452970496 | bytes 31129600 | tf_op jit(solution)/shard_map/dot_general | solution.py:20
  360.1 9.8 %multiply_reduce_fusion.2 = (f32[1024]{0:T(1024)}, f32[528]{0:T(1024)S(1)}, f32[528]{0:T(1024)S(1)}, f32[1024]{0:T(1024)}, f32[528,1024]{1,0:T(8,128)S(1)}) fusion(f32[528,1024]{1,0:T(8,128)S(1)} %copy-done.6, f32[528]{0:T(1024)S(1)} %copy-done.81, f32[528]{0:T(1024)S(1)} %copy-done.74, f32[1024]{0:T(1024)S(1)} %bitcast.352, ...), kind=kOutput, calls=%fused_computation.79 | convolution fusion | flops 4434048000 | bytes 17060096 | tf_op jit(solution)/shard_map/dot_general | solution.py:20
  391.3 24.5 %attn_backward.3 = (bf16[528,1024]{1,0:T(8,128)(2,1)}, bf16[528,1024]{1,0:T(8,128)(2,1)}, bf16[528,1024]{1,0:T(8,128)(2,1)}, bf16[528,1024]{1,0:T(8,128)(2,1)}, bf16[528,1024]{1,0:T(8,128)(2,1)}) custom-call(bf16[528,1024]{1,0:T(8,128)(2,1)} %fusion.71.q_ref, bf16[528,2048]{1,0:T(8,128)(2,1)} %copy-done.119, bf16[528,2048]{1,0:T(8,128)(2,1)} %copy-done.119, ...), custom_call_target="tpu_custom_call" | custom-call | flops 17716740096 | bytes 25952256 | tf_op jit(solution)/shard_map/attn_backward/pallas_call | solution.py:179
  430.7 9.3 concatenate.68
  440.0 7.4 weight_grad.52
  450.2 7.2 weight_grad.48
  520.9 6.9 collective-permute-done.47
  591.9 8.6 concatenate.73
  602.5 6.4 collective-permute-done.41
  615.2 30.1 %copy.77 = bf16[2,1026,1024]{2,0,1:T(2,128)(2,1)} copy(bf16[2,1026,1024]{2,1,0:T(8,128)(2,1)S(1)} %pad_maximum_fusion.1) | data formatting | bytes 8404992
  645.3 6.1 concatenate.72
  651.4 8.3 weight_grad.55
  660.8 8.0 weight_grad.51
  680.7 27.2 %collective-permute-done.23 = bf16[256,1024]{1,0:T(8,128)(2,1)S(1)} collective-permute-done((bf16[256,1024]{1,0:T(8,128)(2,1)}, bf16[256,1024]{1,0:T(8,128)(2,1)S(1)}, u32[]{:S(2)}, u32[]{:S(2)}) %collective-permute-start.23) | collective-permute-done | bytes 524320 | tf_op jit(solution)/shard_map/ppermute | solution.py:292
  714.6 6.0 collective-permute-done.43
  729.6 6.7 collective-permute-done.44
  736.3 7.2 collective-permute-done.25
  745.0 8.0 weight_grad.53
  754.1 8.2 weight_grad.49
  767.7 74.4 %collective-permute-done.18 = bf16[256,1024]{1,0:T(8,128)(2,1)S(1)} collective-permute-done((bf16[256,1024]{1,0:T(8,128)(2,1)S(1)}, bf16[256,1024]{1,0:T(8,128)(2,1)S(1)}, u32[]{:S(2)}, u32[]{:S(2)}) %collective-permute-start.18) | collective-permute-done | bytes 524320 | tf_op jit(solution)/shard_map/ppermute | solution.py:292
  846.8 6.7 collective-permute-done.36
  855.9 6.3 collective-permute-done.19
  864.8 7.5 collective-permute-done.37
  880.5 9.3 collective-permute-done.72
  905.1 11.1 %collective-permute-done.63 = bf16[2,64,2048]{2,1,0:T(8,128)(2,1)S(1)} collective-permute-done((bf16[2,64,2048]{2,1,0:T(8,128)(2,1)S(1)}, bf16[2,64,2048]{2,1,0:T(8,128)(2,1)S(1)}, u32[]{:S(2)}, u32[]{:S(2)}) %collective-permute-start.63) | collective-permute-done | bytes 524320 | tf_op jit(solution)/shard_map/ppermute | solution.py:292
  916.5 10.8 %collective-permute-done.64 = bf16[1,64,2048]{2,1,0:T(8,128)(2,1)S(1)} collective-permute-done((bf16[1,64,2048]{2,1,0:T(8,128)(2,1)S(1)}, bf16[1,64,2048]{2,1,0:T(8,128)(2,1)S(1)}, u32[]{:S(2)}, u32[]{:S(2)}) %collective-permute-start.64) | collective-permute-done | bytes 262176 | tf_op jit(solution)/shard_map/ppermute | solution.py:292
  932.1 9.3 collective-permute-done.68
  941.6 5.5 collective-permute-done.58
  947.3 7.0 collective-permute-done.69
  (624 shorter events, 347.7 us)
Async XLA Ops:
  0.7 59.6 %collective-permute-start = (bf16[2,1024,1024]{2,1,0:T(8,128)(2,1)}, bf16[2,1024,1024]{2,1,0:T(8,128)(2,1)}, u32[]{:S(2)}, u32[]{:S(2)}) collective-permute-start(bf16[2,1024,1024]{2,1,0:T(8,128)(2,1)} %bitcast.332), channel_id=1, source_target_pairs={{0,1},{1,0},{2,3},{3,2},{4,5},{5,4},{6,7},{7,6},{8,9},{9,8},{10,11... | collective-permute-start | bytes 12582920 | tf_op jit(solution)/shard_map/ppermute | solution.py:288
  9.8 55.6 %collective-permute-start.1 = (bf16[2,1024,3,512]{1,3,2,0:T(8,128)(2,1)}, bf16[2,1024,3,512]{1,3,2,0:T(8,128)(2,1)}, u32[]{:S(2)}, u32[]{:S(2)}) collective-permute-start(bf16[2,1024,3,512]{1,3,2,0:T(8,128)(2,1)} %copy.61), channel_id=1, source_target_pairs={{0,1},{1,0},{2,3},{3,2},{4,5},{5,4},{6,7},{7,6},{8,9},{9,8},{10,11... | collective-permute-start | bytes 18874376 | tf_op jit(solution)/shard_map/ppermute | solution.py:288
  9.9 70.8 %collective-permute-start.4 = (bf16[2,1024,2048]{2,1,0:T(8,128)(2,1)}, bf16[2,1024,2048]{2,1,0:T(8,128)(2,1)}, u32[]{:S(2)}, u32[]{:S(2)}) collective-permute-start(bf16[2,1024,2048]{2,1,0:T(8,128)(2,1)} %param.28), channel_id=1, source_target_pairs={{0,1},{1,0},{2,3},{3,2},{4,5},{5,4},{6,7},{7,6},{8,9},{9,8},{10,11... | collective-permute-start | bytes 25165832 | tf_op jit(solution)/shard_map/ppermute | solution.py:288
  10.3 49.9 %collective-permute-start.5 = (bf16[2,2048]{1,0:T(2,128)(2,1)S(1)}, bf16[2,2048]{1,0:T(2,128)(2,1)S(1)}, u32[]{:S(2)}, u32[]{:S(2)}) collective-permute-start(bf16[2,2048]{1,0:T(2,128)(2,1)S(1)} %copy-done.110), channel_id=1, source_target_pairs={{0,1},{1,0},{2,3},{3,2},{4,5},{5,4},{6,7},{7,6},{8,9},{9,8},{10,11... | collective-permute-start | bytes 24584 | tf_op jit(solution)/shard_map/ppermute | solution.py:288
  10.4 78.7 %collective-permute-start.6 = (bf16[2,1024,2048]{2,1,0:T(8,128)(2,1)}, bf16[2,1024,2048]{2,1,0:T(8,128)(2,1)}, u32[]{:S(2)}, u32[]{:S(2)}) collective-permute-start(bf16[2,1024,2048]{2,1,0:T(8,128)(2,1)} %param.30), channel_id=1, source_target_pairs={{0,1},{1,0},{2,3},{3,2},{4,5},{5,4},{6,7},{7,6},{8,9},{9,8},{10,11... | collective-permute-start | bytes 25165832 | tf_op jit(solution)/shard_map/ppermute | solution.py:288
  75.3 22.1 %collective-permute-start.2 = (bf16[528,2048]{1,0:T(8,128)(2,1)S(1)}, bf16[528,2048]{1,0:T(8,128)(2,1)}, u32[]{:S(2)}, u32[]{:S(2)}) collective-permute-start(bf16[528,2048]{1,0:T(8,128)(2,1)S(1)} %fusion.39.km_ref.vm_ref), channel_id=1, source_target_pairs={{0,1},{1,0},{2,3},{3,2},{4,5},{5,4},{6,7},{7,6},{8,9},{9,8},{10,11... | collective-permute-start | bytes 6488072 | tf_op jit(solution)/shard_map/ppermute | solution.py:288
  289.6 38.1 %collective-permute-start.9 = (bf16[528,1024]{1,0:T(8,128)(2,1)}, bf16[528,1024]{1,0:T(8,128)(2,1)}, u32[]{:S(2)}, u32[]{:S(2)}) collective-permute-start(bf16[528,1024]{1,0:T(8,128)(2,1)} %get-tuple-element.69), channel_id=1, source_target_pairs={{0,1},{1,0},{2,3},{3,2},{4,5},{5,4},{6,7},{7,6},{8,9},{9,8},{10,11... | collective-permute-start | bytes 3244040 | tf_op jit(solution)/shard_map/ppermute | solution.py:288
  289.7 39.7 %collective-permute-start.10 = (bf16[528,1024]{1,0:T(8,128)(2,1)}, bf16[528,1024]{1,0:T(8,128)(2,1)}, u32[]{:S(2)}, u32[]{:S(2)}) collective-permute-start(bf16[528,1024]{1,0:T(8,128)(2,1)} %get-tuple-element.71), channel_id=1, source_target_pairs={{0,1},{1,0},{2,3},{3,2},{4,5},{5,4},{6,7},{7,6},{8,9},{9,8},{10,11... | collective-permute-start | bytes 3244040 | tf_op jit(solution)/shard_map/ppermute | solution.py:288
  294.2 26.6 %collective-permute-start.50 = (bf16[1024,512]{1,0:T(8,128)(2,1)}, bf16[1024,512]{1,0:T(8,128)(2,1)}, u32[]{:S(2)}, u32[]{:S(2)}) collective-permute-start(bf16[1024,512]{1,0:T(8,128)(2,1)} %weight_grad.46), channel_id=1, source_target_pairs={{0,1},{1,0},{2,3},{3,2},{4,5},{5,4},{6,7},{7,6},{8,9},{9,8},{10,11... | collective-permute-start | bytes 3145736 | tf_op jit(solution)/shard_map/ppermute | solution.py:288
  305.4 113.4 %collective-permute-start.8 = (bf16[528,1024]{1,0:T(8,128)(2,1)}, bf16[528,1024]{1,0:T(8,128)(2,1)}, u32[]{:S(2)}, u32[]{:S(2)}) collective-permute-start(bf16[528,1024]{1,0:T(8,128)(2,1)} %add_convert_fusion.4), channel_id=1, source_target_pairs={{0,1},{1,0},{2,3},{3,2},{4,5},{5,4},{6,7},{7,6},{8,9},{9,8},{10,11... | collective-permute-start | bytes 3244040 | tf_op jit(solution)/shard_map/ppermute | solution.py:288
  325.1 95.4 %collective-permute-start.51 = (bf16[512,512]{1,0:T(8,128)(2,1)}, bf16[512,512]{1,0:T(8,128)(2,1)}, u32[]{:S(2)}, u32[]{:S(2)}) collective-permute-start(bf16[512,512]{1,0:T(8,128)(2,1)} %get-tuple-element.99), channel_id=1, source_target_pairs={{0,2},{2,0},{4,6},{6,4},{8,10},{10,8},{12,14},{14,12},{16,18},{18,... | collective-permute-start | bytes 1572872 | tf_op jit(solution)/shard_map/ppermute | solution.py:292
  390.6 74.6 %collective-permute-start.45 = (bf16[1024,512]{1,0:T(8,128)(2,1)}, bf16[1024,512]{1,0:T(8,128)(2,1)}, u32[]{:S(2)}, u32[]{:S(2)}) collective-permute-start(bf16[1024,512]{1,0:T(8,128)(2,1)} %weight_grad.44), channel_id=1, source_target_pairs={{0,1},{1,0},{2,3},{3,2},{4,5},{5,4},{6,7},{7,6},{8,9},{9,8},{10,11... | collective-permute-start | bytes 3145736 | tf_op jit(solution)/shard_map/ppermute | solution.py:288
  390.8 79.2 %collective-permute-start.38 = (bf16[1024,512]{1,0:T(8,128)(2,1)}, bf16[1024,512]{1,0:T(8,128)(2,1)}, u32[]{:S(2)}, u32[]{:S(2)}) collective-permute-start(bf16[1024,512]{1,0:T(8,128)(2,1)} %weight_grad.38), channel_id=1, source_target_pairs={{0,1},{1,0},{2,3},{3,2},{4,5},{5,4},{6,7},{7,6},{8,9},{9,8},{10,11... | collective-permute-start | bytes 3145736 | tf_op jit(solution)/shard_map/ppermute | solution.py:288
  391.1 87.9 %collective-permute-start.40 = (bf16[1024,512]{1,0:T(8,128)(2,1)}, bf16[1024,512]{1,0:T(8,128)(2,1)}, u32[]{:S(2)}, u32[]{:S(2)}) collective-permute-start(bf16[1024,512]{1,0:T(8,128)(2,1)} %weight_grad.42), channel_id=1, source_target_pairs={{0,1},{1,0},{2,3},{3,2},{4,5},{5,4},{6,7},{7,6},{8,9},{9,8},{10,11... | collective-permute-start | bytes 3145736 | tf_op jit(solution)/shard_map/ppermute | solution.py:288
  421.6 25.8 %collective-permute-start.52 = (bf16[256,512]{1,0:T(8,128)(2,1)S(1)}, bf16[256,512]{1,0:T(8,128)(2,1)}, u32[]{:S(2)}, u32[]{:S(2)}) collective-permute-start(bf16[256,512]{1,0:T(8,128)(2,1)S(1)} %add_convert_fusion.35), channel_id=1, source_target_pairs={{0,4},{2,6},{4,0},{6,2},{8,12},{10,14},{12,8},{14,10},{16,20},{18,... | collective-permute-start | bytes 786440 | tf_op jit(solution)/shard_map/ppermute | solution.py:292
  429.6 44.7 %collective-permute-start.39 = (bf16[1024,512]{1,0:T(8,128)(2,1)}, bf16[1024,512]{1,0:T(8,128)(2,1)}, u32[]{:S(2)}, u32[]{:S(2)}) collective-permute-start(bf16[1024,512]{1,0:T(8,128)(2,1)} %weight_grad.40), channel_id=1, source_target_pairs={{0,1},{1,0},{2,3},{3,2},{4,5},{5,4},{6,7},{7,6},{8,9},{9,8},{10,11... | collective-permute-start | bytes 3145736 | tf_op jit(solution)/shard_map/ppermute | solution.py:288
  465.1 23.5 %collective-permute-start.11 = (bf16[528,1024]{1,0:T(8,128)(2,1)}, bf16[528,1024]{1,0:T(8,128)(2,1)S(1)}, u32[]{:S(2)}, u32[]{:S(2)}) collective-permute-start(bf16[528,1024]{1,0:T(8,128)(2,1)} %get-tuple-element.77), channel_id=1, source_target_pairs={{0,1},{1,0},{2,3},{3,2},{4,5},{5,4},{6,7},{7,6},{8,9},{9,8},{10,11... | collective-permute-start | bytes 3244040 | tf_op jit(solution)/shard_map/ppermute | solution.py:288
  465.2 186.3 %collective-permute-start.70 = (bf16[1024,2048]{1,0:T(8,128)(2,1)}, bf16[1024,2048]{1,0:T(8,128)(2,1)}, u32[]{:S(2)}, u32[]{:S(2)}) collective-permute-start(bf16[1024,2048]{1,0:T(8,128)(2,1)} %weight_grad.54), channel_id=1, source_target_pairs={{0,1},{1,0},{2,3},{3,2},{4,5},{5,4},{6,7},{7,6},{8,9},{9,8},{10,11... | collective-permute-start | bytes 12582920 | tf_op jit(solution)/shard_map/ppermute | solution.py:288
  470.0 19.7 %collective-permute-start.12 = (bf16[528,1024]{1,0:T(8,128)(2,1)}, bf16[528,1024]{1,0:T(8,128)(2,1)}, u32[]{:S(2)}, u32[]{:S(2)}) collective-permute-start(bf16[528,1024]{1,0:T(8,128)(2,1)} %get-tuple-element.79), channel_id=1, source_target_pairs={{0,1},{1,0},{2,3},{3,2},{4,5},{5,4},{6,7},{7,6},{8,9},{9,8},{10,11... | collective-permute-start | bytes 3244040 | tf_op jit(solution)/shard_map/ppermute | solution.py:288
  474.3 185.5 %collective-permute-start.60 = (bf16[1024,2048]{1,0:T(8,128)(2,1)}, bf16[1024,2048]{1,0:T(8,128)(2,1)}, u32[]{:S(2)}, u32[]{:S(2)}) collective-permute-start(bf16[1024,2048]{1,0:T(8,128)(2,1)} %weight_grad.50), channel_id=1, source_target_pairs={{0,1},{1,0},{2,3},{3,2},{4,5},{5,4},{6,7},{7,6},{8,9},{9,8},{10,11... | collective-permute-start | bytes 12582920 | tf_op jit(solution)/shard_map/ppermute | solution.py:288
  479.0 72.0 %collective-permute-start.21 = (bf16[1024,1024]{1,0:T(8,128)(2,1)}, bf16[1024,1024]{1,0:T(8,128)(2,1)}, u32[]{:S(2)}, u32[]{:S(2)}) collective-permute-start(bf16[1024,1024]{1,0:T(8,128)(2,1)} %weight_grad.30), channel_id=1, source_target_pairs={{0,1},{1,0},{2,3},{3,2},{4,5},{5,4},{6,7},{7,6},{8,9},{9,8},{10,11... | collective-permute-start | bytes 6291464 | tf_op jit(solution)/shard_map/ppermute | solution.py:288
  488.7 27.8 %collective-permute-start.46 = (bf16[512,512]{1,0:T(8,128)(2,1)}, bf16[512,512]{1,0:T(8,128)(2,1)}, u32[]{:S(2)}, u32[]{:S(2)}) collective-permute-start(bf16[512,512]{1,0:T(8,128)(2,1)} %get-tuple-element.97), channel_id=1, source_target_pairs={{0,2},{2,0},{4,6},{6,4},{8,10},{10,8},{12,14},{14,12},{16,18},{18,... | collective-permute-start | bytes 1572872 | tf_op jit(solution)/shard_map/ppermute | solution.py:292
  516.4 20.1 %collective-permute-start.15 = (bf16[528,1024]{1,0:T(8,128)(2,1)S(1)}, bf16[528,1024]{1,0:T(8,128)(2,1)S(1)}, u32[]{:S(2)}, u32[]{:S(2)}) collective-permute-start(bf16[528,1024]{1,0:T(8,128)(2,1)S(1)} %copy-done.30), channel_id=1, source_target_pairs={{0,1},{1,0},{2,3},{3,2},{4,5},{5,4},{6,7},{7,6},{8,9},{9,8},{10,11... | collective-permute-start | bytes 3244040 | tf_op jit(solution)/shard_map/ppermute | solution.py:288
  536.5 28.3 %collective-permute-start.31 = (bf16[1024,512]{1,0:T(8,128)(2,1)}, bf16[1024,512]{1,0:T(8,128)(2,1)}, u32[]{:S(2)}, u32[]{:S(2)}) collective-permute-start(bf16[1024,512]{1,0:T(8,128)(2,1)} %weight_grad.32), channel_id=1, source_target_pairs={{0,1},{1,0},{2,3},{3,2},{4,5},{5,4},{6,7},{7,6},{8,9},{9,8},{10,11... | collective-permute-start | bytes 3145736 | tf_op jit(solution)/shard_map/ppermute | solution.py:288
  546.9 24.8 %collective-permute-start.32 = (bf16[1024,512]{1,0:T(8,128)(2,1)}, bf16[1024,512]{1,0:T(8,128)(2,1)}, u32[]{:S(2)}, u32[]{:S(2)}) collective-permute-start(bf16[1024,512]{1,0:T(8,128)(2,1)} %weight_grad.34), channel_id=1, source_target_pairs={{0,1},{1,0},{2,3},{3,2},{4,5},{5,4},{6,7},{7,6},{8,9},{9,8},{10,11... | collective-permute-start | bytes 3145736 | tf_op jit(solution)/shard_map/ppermute | solution.py:288
  551.1 29.7 %collective-permute-start.33 = (bf16[1024,512]{1,0:T(8,128)(2,1)}, bf16[1024,512]{1,0:T(8,128)(2,1)}, u32[]{:S(2)}, u32[]{:S(2)}) collective-permute-start(bf16[1024,512]{1,0:T(8,128)(2,1)} %weight_grad.36), channel_id=1, source_target_pairs={{0,1},{1,0},{2,3},{3,2},{4,5},{5,4},{6,7},{7,6},{8,9},{9,8},{10,11... | collective-permute-start | bytes 3145736 | tf_op jit(solution)/shard_map/ppermute | solution.py:288
  564.8 25.5 %collective-permute-start.14 = (bf16[528,1024]{1,0:T(8,128)(2,1)}, bf16[528,1024]{1,0:T(8,128)(2,1)S(1)}, u32[]{:S(2)}, u32[]{:S(2)}) collective-permute-start(bf16[528,1024]{1,0:T(8,128)(2,1)} %get-tuple-element.200), channel_id=1, source_target_pairs={{0,1},{1,0},{2,3},{3,2},{4,5},{5,4},{6,7},{7,6},{8,9},{9,8},{10,11... | collective-permute-start | bytes 3244040 | tf_op jit(solution)/shard_map/ppermute | solution.py:288
  571.7 37.2 %collective-permute-start.41 = (bf16[512,1536]{1,0:T(8,128)(2,1)}, bf16[512,1536]{1,0:T(8,128)(2,1)}, u32[]{:S(2)}, u32[]{:S(2)}) collective-permute-start(bf16[512,1536]{1,0:T(8,128)(2,1)} %pad_maximum_fusion.5), channel_id=1, source_target_pairs={{0,4},{2,6},{4,0},{6,2},{8,12},{10,14},{12,8},{14,10},{16,20},{18,... | collective-permute-start | bytes 4718600 | tf_op jit(solution)/shard_map/ppermute | solution.py:292
  580.8 90.0 %collective-permute-start.16 = (bf16[1024,1024]{1,0:T(8,128)(2,1)}, bf16[1024,1024]{1,0:T(8,128)(2,1)}, u32[]{:S(2)}, u32[]{:S(2)}) collective-permute-start(bf16[1024,1024]{1,0:T(8,128)(2,1)} %weight_grad.28), channel_id=1, source_target_pairs={{0,1},{1,0},{2,3},{3,2},{4,5},{5,4},{6,7},{7,6},{8,9},{9,8},{10,11... | collective-permute-start | bytes 6291464 | tf_op jit(solution)/shard_map/ppermute | solution.py:288
  590.3 22.2 %collective-permute-start.13 = (bf16[528,1024]{1,0:T(8,128)(2,1)}, bf16[528,1024]{1,0:T(8,128)(2,1)}, u32[]{:S(2)}, u32[]{:S(2)}) collective-permute-start(bf16[528,1024]{1,0:T(8,128)(2,1)} %get-tuple-element.201), channel_id=1, source_target_pairs={{0,1},{1,0},{2,3},{3,2},{4,5},{5,4},{6,7},{7,6},{8,9},{9,8},{10,11... | collective-permute-start | bytes 3244040 | tf_op jit(solution)/shard_map/ppermute | solution.py:288
  608.9 51.4 %collective-permute-start.22 = (bf16[512,1024]{1,0:T(8,128)(2,1)}, bf16[512,1024]{1,0:T(8,128)(2,1)}, u32[]{:S(2)}, u32[]{:S(2)}) collective-permute-start(bf16[512,1024]{1,0:T(8,128)(2,1)} %get-tuple-element.83), channel_id=1, source_target_pairs={{0,2},{2,0},{4,6},{6,4},{8,10},{10,8},{12,14},{14,12},{16,18},{18,... | collective-permute-start | bytes 3145736 | tf_op jit(solution)/shard_map/ppermute | solution.py:292
  612.5 64.5 %collective-permute-start.42 = (bf16[256,1536]{1,0:T(8,128)(2,1)}, bf16[256,1536]{1,0:T(8,128)(2,1)}, u32[]{:S(2)}, u32[]{:S(2)}) collective-permute-start(bf16[256,1536]{1,0:T(8,128)(2,1)} %add_convert_fusion.23), channel_id=1, source_target_pairs={{0,2},{2,0},{4,6},{6,4},{8,10},{10,8},{12,14},{14,12},{16,18},{18,... | collective-permute-start | bytes 2359304 | tf_op jit(solution)/shard_map/ppermute | solution.py:292
  651.4 92.9 %collective-permute-start.65 = (bf16[1024,2048]{1,0:T(8,128)(2,1)}, bf16[1024,2048]{1,0:T(8,128)(2,1)}, u32[]{:S(2)}, u32[]{:S(2)}) collective-permute-start(bf16[1024,2048]{1,0:T(8,128)(2,1)} %weight_grad.52), channel_id=1, source_target_pairs={{0,1},{1,0},{2,3},{3,2},{4,5},{5,4},{6,7},{7,6},{8,9},{9,8},{10,11... | collective-permute-start | bytes 12582920 | tf_op jit(solution)/shard_map/ppermute | solution.py:288
  659.8 93.2 %collective-permute-start.55 = (bf16[1024,2048]{1,0:T(8,128)(2,1)}, bf16[1024,2048]{1,0:T(8,128)(2,1)}, u32[]{:S(2)}, u32[]{:S(2)}) collective-permute-start(bf16[1024,2048]{1,0:T(8,128)(2,1)} %weight_grad.48), channel_id=1, source_target_pairs={{0,1},{1,0},{2,3},{3,2},{4,5},{5,4},{6,7},{7,6},{8,9},{9,8},{10,11... | collective-permute-start | bytes 12582920 | tf_op jit(solution)/shard_map/ppermute | solution.py:288
  660.2 50.2 %collective-permute-start.34 = (bf16[512,1536]{1,0:T(8,128)(2,1)S(1)}, bf16[512,1536]{1,0:T(8,128)(2,1)}, u32[]{:S(2)}, u32[]{:S(2)}) collective-permute-start(bf16[512,1536]{1,0:T(8,128)(2,1)S(1)} %copy-done.38), channel_id=1, source_target_pairs={{0,4},{2,6},{4,0},{6,2},{8,12},{10,14},{12,8},{14,10},{16,20},{18,... | collective-permute-start | bytes 4718600 | tf_op jit(solution)/shard_map/ppermute | solution.py:292
  670.8 201.6 %collective-permute-start.71 = (bf16[512,2048]{1,0:T(8,128)(2,1)}, bf16[512,2048]{1,0:T(8,128)(2,1)S(1)}, u32[]{:S(2)}, u32[]{:S(2)}) collective-permute-start(bf16[512,2048]{1,0:T(8,128)(2,1)} %get-tuple-element.107), channel_id=1, source_target_pairs={{0,2},{2,0},{4,6},{6,4},{8,10},{10,8},{12,14},{14,12},{16,18},{18,... | collective-permute-start | bytes 6291464 | tf_op jit(solution)/shard_map/ppermute | solution.py:292
  677.0 30.9 %collective-permute-start.23 = (bf16[256,1024]{1,0:T(8,128)(2,1)}, bf16[256,1024]{1,0:T(8,128)(2,1)S(1)}, u32[]{:S(2)}, u32[]{:S(2)}) collective-permute-start(bf16[256,1024]{1,0:T(8,128)(2,1)} %add_convert_fusion.29), channel_id=1, source_target_pairs={{0,4},{2,6},{4,0},{6,2},{8,12},{10,14},{12,8},{14,10},{16,20},{18,... | collective-permute-start | bytes 1572872 | tf_op jit(solution)/shard_map/ppermute | solution.py:292
  707.9 54.4 %collective-permute-start.17 = (bf16[512,1024]{1,0:T(8,128)(2,1)}, bf16[512,1024]{1,0:T(8,128)(2,1)}, u32[]{:S(2)}, u32[]{:S(2)}) collective-permute-start(bf16[512,1024]{1,0:T(8,128)(2,1)} %get-tuple-element.81), channel_id=1, source_target_pairs={{0,2},{2,0},{4,6},{6,4},{8,10},{10,8},{12,14},{14,12},{16,18},{18,... | collective-permute-start | bytes 3145736 | tf_op jit(solution)/shard_map/ppermute | solution.py:292
  743.5 21.8 %collective-permute-start.35 = (bf16[256,1536]{1,0:T(8,128)(2,1)}, bf16[256,1536]{1,0:T(8,128)(2,1)}, u32[]{:S(2)}, u32[]{:S(2)}) collective-permute-start(bf16[256,1536]{1,0:T(8,128)(2,1)} %add_convert_fusion.26), channel_id=1, source_target_pairs={{0,2},{2,0},{4,6},{6,4},{8,10},{10,8},{12,14},{14,12},{16,18},{18,... | collective-permute-start | bytes 2359304 | tf_op jit(solution)/shard_map/ppermute | solution.py:292
  744.4 130.0 %collective-permute-start.61 = (bf16[512,2048]{1,0:T(8,128)(2,1)}, bf16[512,2048]{1,0:T(8,128)(2,1)}, u32[]{:S(2)}, u32[]{:S(2)}) collective-permute-start(bf16[512,2048]{1,0:T(8,128)(2,1)} %get-tuple-element.103), channel_id=1, source_target_pairs={{0,4},{2,6},{4,0},{6,2},{8,12},{10,14},{12,8},{14,10},{16,20},{18,... | collective-permute-start | bytes 6291464 | tf_op jit(solution)/shard_map/ppermute | solution.py:292
  753.0 146.1 %collective-permute-start.66 = (bf16[512,2048]{1,0:T(8,128)(2,1)}, bf16[512,2048]{1,0:T(8,128)(2,1)}, u32[]{:S(2)}, u32[]{:S(2)}) collective-permute-start(bf16[512,2048]{1,0:T(8,128)(2,1)} %get-tuple-element.105), channel_id=1, source_target_pairs={{0,2},{2,0},{4,6},{6,4},{8,10},{10,8},{12,14},{14,12},{16,18},{18,... | collective-permute-start | bytes 6291464 | tf_op jit(solution)/shard_map/ppermute | solution.py:292
  762.3 139.5 %collective-permute-start.56 = (bf16[512,2048]{1,0:T(8,128)(2,1)}, bf16[512,2048]{1,0:T(8,128)(2,1)S(1)}, u32[]{:S(2)}, u32[]{:S(2)}) collective-permute-start(bf16[512,2048]{1,0:T(8,128)(2,1)} %get-tuple-element.101), channel_id=1, source_target_pairs={{0,4},{2,6},{4,0},{6,2},{8,12},{10,14},{12,8},{14,10},{16,20},{18,... | collective-permute-start | bytes 6291464 | tf_op jit(solution)/shard_map/ppermute | solution.py:292
  765.3 76.8 %collective-permute-start.18 = (bf16[256,1024]{1,0:T(8,128)(2,1)S(1)}, bf16[256,1024]{1,0:T(8,128)(2,1)S(1)}, u32[]{:S(2)}, u32[]{:S(2)}) collective-permute-start(bf16[256,1024]{1,0:T(8,128)(2,1)S(1)} %add_convert_fusion.32), channel_id=1, source_target_pairs={{0,4},{2,6},{4,0},{6,2},{8,12},{10,14},{12,8},{14,10},{16,20},{18,... | collective-permute-start | bytes 1572872 | tf_op jit(solution)/shard_map/ppermute | solution.py:292
  876.0 19.1 %collective-permute-start.62 = (bf16[256,2048]{1,0:T(8,128)(2,1)S(1)}, bf16[256,2048]{1,0:T(8,128)(2,1)S(1)}, u32[]{:S(2)}, u32[]{:S(2)}) collective-permute-start(bf16[256,2048]{1,0:T(8,128)(2,1)S(1)} %add_convert_fusion.17), channel_id=1, source_target_pairs={{0,2},{2,0},{4,6},{6,4},{8,10},{10,8},{12,14},{14,12},{16,18},{18,... | collective-permute-start | bytes 3145736 | tf_op jit(solution)/shard_map/ppermute | solution.py:292
  896.9 19.3 %collective-permute-start.63 = (bf16[2,64,2048]{2,1,0:T(8,128)(2,1)S(1)}, bf16[2,64,2048]{2,1,0:T(8,128)(2,1)S(1)}, u32[]{:S(2)}, u32[]{:S(2)}) collective-permute-start(bf16[2,64,2048]{2,1,0:T(8,128)(2,1)S(1)} %dynamic-slice_bitcast_fusion.2), channel_id=1, source_target_pairs={{0,8},{2,10},{4,12},{6,14},{8,0},{10,2},{12,4},{14,6},{16,24},{18,... | collective-permute-start | bytes 1572872 | tf_op jit(solution)/shard_map/ppermute | solution.py:292
  900.7 26.7 %collective-permute-start.67 = (bf16[256,2048]{1,0:T(8,128)(2,1)S(1)}, bf16[256,2048]{1,0:T(8,128)(2,1)S(1)}, u32[]{:S(2)}, u32[]{:S(2)}) collective-permute-start(bf16[256,2048]{1,0:T(8,128)(2,1)S(1)} %add_convert_fusion.14), channel_id=1, source_target_pairs={{0,4},{2,6},{4,0},{6,2},{8,12},{10,14},{12,8},{14,10},{16,20},{18,... | collective-permute-start | bytes 3145736 | tf_op jit(solution)/shard_map/ppermute | solution.py:292
  902.3 27.1 %collective-permute-start.57 = (bf16[256,2048]{1,0:T(8,128)(2,1)S(1)}, bf16[256,2048]{1,0:T(8,128)(2,1)S(1)}, u32[]{:S(2)}, u32[]{:S(2)}) collective-permute-start(bf16[256,2048]{1,0:T(8,128)(2,1)S(1)} %add_convert_fusion.20), channel_id=1, source_target_pairs={{0,2},{2,0},{4,6},{6,4},{8,10},{10,8},{12,14},{14,12},{16,18},{18,... | collective-permute-start | bytes 3145736 | tf_op jit(solution)/shard_map/ppermute | solution.py:292
  930.0 17.0 %collective-permute-start.58 = (bf16[2,64,2048]{2,1,0:T(8,128)(2,1)S(1)}, bf16[2,64,2048]{2,1,0:T(8,128)(2,1)S(1)}, u32[]{:S(2)}, u32[]{:S(2)}) collective-permute-start(bf16[2,64,2048]{2,1,0:T(8,128)(2,1)S(1)} %dynamic-slice_bitcast_fusion.3), channel_id=1, source_target_pairs={{0,8},{2,10},{4,12},{6,14},{8,0},{10,2},{12,4},{14,6},{16,24},{18,... | collective-permute-start | bytes 1572872 | tf_op jit(solution)/shard_map/ppermute | solution.py:292
  (153 other events, 1538.1 us)

commit v2 on v1

v2 whole, which is shorter than its diff:
```python
import functools
import jax
import jax.numpy as jnp
from jax import lax
from jax.experimental import pallas as pl
from jax.experimental.pallas import tpu as pltpu
from jax.sharding import PartitionSpec as P

F32 = jnp.float32
BF16 = jnp.bfloat16
HD = 64
MAIN = 512
PAD = 528
GROUP = 256
HEADS_IN_GROUP = GROUP // HD
VMEM_LIMIT = 60 * 1024 * 1024
LIGHT = pl.CostEstimate(flops=1, bytes_accessed=1, transcendentals=0)


def _dot(a, b, dims):
    return lax.dot_general(a, b, (dims, ((), ())), preferred_element_type=F32)


def _extra_rows(mine_ref, other_ref):
    row = lax.broadcasted_iota(jnp.int32, (16, GROUP), 0)
    lane = lax.broadcasted_iota(jnp.int32, (16, GROUP), 1)
    mine = jnp.broadcast_to(mine_ref[MAIN : MAIN + 16, :][0:1].astype(F32), (16, GROUP))
    other = jnp.broadcast_to(other_ref[MAIN : MAIN + 16, :][0:1].astype(F32), (16, GROUP))
    value = jnp.where(row % 2 == 0, mine, other)
    return jnp.where(row // 2 == lane // HD, value, 0.0).astype(BF16)


def _attn_fwd_kernel(q_ref, km_ref, vm_ref, ko_ref, vo_ref, o_ref, of_ref, e_ref, ex_ref, il_ref, k_s, v_s):
    k_s[:MAIN] = km_ref[:MAIN]
    k_s[MAIN:] = ko_ref[:MAIN]
    v_s[:MAIN] = vm_ref[:MAIN]
    v_s[MAIN:] = vo_ref[:MAIN]
    lane = lax.broadcasted_iota(jnp.int32, (PAD, GROUP), 1) // HD
    slot = lax.broadcasted_iota(jnp.int32, (PAD, 16), 1) // 2
    q = q_ref[...] * jnp.asarray(HD**-0.5, BF16)
    kx = _extra_rows(km_ref, ko_ref)
    vx = _extra_rows(vm_ref, vo_ref)
    sx = _dot(q, kx, ((1,), (1,)))
    out = jnp.zeros((PAD, GROUP), F32)
    ex_all = jnp.zeros((PAD, 16), F32)
    il_all = jnp.zeros((PAD, 16), F32)
    for h in range(HEADS_IN_GROUP):
        qh = jnp.where(lane == h, q, jnp.zeros_like(q))
        s = _dot(qh, k_s[...], ((1,), (1,)))
        sxh = jnp.where(slot == h, sx, -jnp.inf)
        top = jnp.maximum(jnp.max(s, axis=1, keepdims=True), jnp.max(sxh, axis=1, keepdims=True))
        e = jnp.exp(s - top)
        exh = jnp.exp(sxh - top)
        total = jnp.sum(e, axis=1, keepdims=True) + jnp.sum(exh, axis=1, keepdims=True)
        inverse = 1.0 / total
        low = e.astype(BF16)
        e_ref[h] = low
        out = out + jnp.where(lane == h, _dot(low, v_s[...], ((1,), (0,))) * inverse, 0.0)
        ex_all = ex_all + exh
        il_all = il_all + jnp.where(slot == h, inverse, 0.0)
    out = out + _dot((ex_all * il_all).astype(BF16), vx, ((1,), (0,)))
    o_ref[...] = out.astype(BF16)
    of_ref[...] = out
    ex_ref[0] = ex_all
    il_ref[0] = il_all


def attn_forward(q, kv, kv_other):
    width = q.shape[1]
    groups = width // GROUP

    def near(offset):
        return pl.BlockSpec((PAD, GROUP), lambda g: (0, g + offset))

    def far(offset):
        return pl.BlockSpec((PAD, GROUP), lambda g: (0, (g + groups // 2) % groups + offset))

    heads = width // HD
    return pl.pallas_call(
        _attn_fwd_kernel,
        grid=(groups,),
        in_specs=[near(0), near(0), near(groups), far(0), far(groups)],
        out_specs=[
            near(0),
            near(0),
            pl.BlockSpec((HEADS_IN_GROUP, PAD, 2 * MAIN), lambda g: (g, 0, 0)),
            pl.BlockSpec((1, PAD, 16), lambda g: (g, 0, 0)),
            pl.BlockSpec((1, PAD, 16), lambda g: (g, 0, 0)),
        ],
        out_shape=[
            jax.ShapeDtypeStruct((PAD, width), BF16),
            jax.ShapeDtypeStruct((PAD, width), F32),
            jax.ShapeDtypeStruct((heads, PAD, 2 * MAIN), BF16),
            jax.ShapeDtypeStruct((groups, PAD, 16), F32),
            jax.ShapeDtypeStruct((groups, PAD, 16), F32),
        ],
        scratch_shapes=[pltpu.VMEM((2 * MAIN, GROUP), BF16), pltpu.VMEM((2 * MAIN, GROUP), BF16)],
        compiler_params=pltpu.CompilerParams(vmem_limit_bytes=VMEM_LIMIT),
        cost_estimate=LIGHT,
        name="attn_forward",
    )(q, kv, kv, kv_other, kv_other)


def _attn_bwd_kernel(
    q_ref, km_ref, vm_ref, ko_ref, vo_ref, do_ref, o_ref, e_ref, ex_ref, il_ref,
    dq_ref, dkm_ref, dko_ref, dvm_ref, dvo_ref, k_s, v_s, dk_s, dv_s,
):
    k_s[:MAIN] = km_ref[:MAIN]
    k_s[MAIN:] = ko_ref[:MAIN]
    v_s[:MAIN] = vm_ref[:MAIN]
    v_s[MAIN:] = vo_ref[:MAIN]
    scale = HD**-0.5
    lane = lax.broadcasted_iota(jnp.int32, (PAD, GROUP), 1) // HD
    slot = lax.broadcasted_iota(jnp.int32, (PAD, 16), 1) // 2
    q = q_ref[...] * jnp.asarray(scale, BF16)
    kx = _extra_rows(km_ref, ko_ref)
    vx = _extra_rows(vm_ref, vo_ref)
    il = il_ref[0]
    do = do_ref[...].astype(F32)
    spread = jnp.zeros((PAD, GROUP), F32)
    for h in range(HEADS_IN_GROUP):
        spread = jnp.where(lane == h, il[:, 2 * h : 2 * h + 1], spread)
    dos = (do * spread).astype(BF16)
    product = dos.astype(F32) * o_ref[...]
    inner = jnp.zeros((PAD, 16), F32)
    inners = []
    for h in range(HEADS_IN_GROUP):
        one = jnp.sum(jnp.where(lane == h, product, 0.0), axis=1, keepdims=True)
        inners.append(one)
        inner = jnp.where(slot == h, one, inner)
    dos_t = dos.T
    q_t = q.T
    dq = jnp.zeros((PAD, GROUP), F32)
    for h in range(HEADS_IN_GROUP):
        rows = slice(h * HD, (h + 1) * HD)
        dosh = jnp.where(lane == h, dos, jnp.zeros_like(dos))
        e = e_ref[h]
        dp = _dot(dosh, v_s[...], ((1,), (1,)))
        ds = (e.astype(F32) * (dp - inners[h])).astype(BF16)
        dq = dq + jnp.where(lane == h, _dot(ds, k_s[...], ((1,), (0,))), 0.0)
        dk_s[rows, :] = (
            _dot(q_t[rows, :MAIN], ds[:MAIN], ((1,), (0,)))
            + q_t[rows, MAIN : MAIN + 1].astype(F32) * ds[MAIN : MAIN + 16].astype(F32)[0:1]
        )
        dv_s[rows, :] = (
            _dot(dos_t[rows, :MAIN], e[:MAIN], ((1,), (0,)))
            + dos_t[rows, MAIN : MAIN + 1].astype(F32) * e[MAIN : MAIN + 16].astype(F32)[0:1]
        )
    ex = ex_ref[0]
    dsx = (ex * (_dot(dos, vx, ((1,), (1,))) - inner)).astype(BF16)
    dq = dq + _dot(dsx, kx, ((1,), (0,)))
    dq_ref[...] = (dq * scale).astype(BF16)
    dkx = _dot(dsx, q, ((0,), (0,)))
    dvx = _dot(ex.astype(BF16), dos, ((0,), (0,)))
    row = lax.broadcasted_iota(jnp.int32, (16, GROUP), 0)
    own = row // 2 == lax.broadcasted_iota(jnp.int32, (16, GROUP), 1) // HD
    for half, (dk_ref, dv_ref) in enumerate(((dkm_ref, dvm_ref), (dko_ref, dvo_ref))):
        keep = jnp.logical_and(own, row % 2 == half)
        for ref, grad_s, tail in ((dk_ref, dk_s, dkx), (dv_ref, dv_s, dvx)):
            ref[:MAIN] = grad_s[:, half * MAIN : (half + 1) * MAIN].T.astype(BF16)
            last = jnp.sum(jnp.where(keep, tail, 0.0), axis=0, keepdims=True)
            ref[MAIN:] = jnp.where(row == 0, jnp.broadcast_to(last, (16, GROUP)), 0.0).astype(BF16)


def attn_backward(q, kv, kv_other, dout, out, e, ex, il):
    width = q.shape[1]
    groups = width // GROUP

    def near(offset):
        return pl.BlockSpec((PAD, GROUP), lambda g: (0, g + offset))

    def far(offset):
        return pl.BlockSpec((PAD, GROUP), lambda g: (0, (g + groups // 2) % groups + offset))

    small = pl.BlockSpec((1, PAD, 16), lambda g: (g, 0, 0))
    heads = width // HD
    block = jax.ShapeDtypeStruct((PAD, width), BF16)
    far_out = pl.BlockSpec((PAD, GROUP), lambda g: (0, (g + groups // 2) % groups))
    return pl.pallas_call(
        _attn_bwd_kernel,
        grid=(groups,),
        in_specs=[
            near(0), near(0), near(groups), far(0), far(groups), near(0), near(0),
            pl.BlockSpec((HEADS_IN_GROUP, PAD, 2 * MAIN), lambda g: (g, 0, 0)), small, small,
        ],
        out_specs=[near(0), near(0), far_out, near(0), far_out],
        out_shape=[block] * 5,
        scratch_shapes=[
            pltpu.VMEM((2 * MAIN, GROUP), BF16),
            pltpu.VMEM((2 * MAIN, GROUP), BF16),
            pltpu.VMEM((GROUP, 2 * MAIN), F32),
            pltpu.VMEM((GROUP, 2 * MAIN), F32),
        ],
        compiler_params=pltpu.CompilerParams(vmem_limit_bytes=VMEM_LIMIT),
        cost_estimate=LIGHT,
        name="attn_backward",
    )(q, kv, kv, kv_other, kv_other, dout, out, e, ex, il)


EPSILON = 1e-05
TILE = 512


def _row(ref, layer):
    return ref[layer : layer + 1, :].astype(F32)


def _fill_turned(coords_ref, order, pieces, x_ref, xt_s, column_s, theirs=False):
    features = xt_s.shape[0]
    rows = features // pieces
    span = max(rows, 128)
    me = coords_ref[0]
    for start in range(0, features, span):
        turned = x_ref[:MAIN, start : start + span].T
        last = x_ref[MAIN:, start : start + span].T.astype(F32)[:, 0:1]
        for part in range(span // rows):
            relative = jnp.bitwise_xor(me, start // rows + part)
            place = jnp.int32(0)
            for bit in order:
                shift = jnp.bitwise_xor(coords_ref[1], bit ^ int(theirs)) if bit < 2 else bit
                place = place * 2 + (jnp.right_shift(relative, shift) & 1)
            at = pl.ds(pl.multiple_of(place * rows, rows), rows)
            xt_s[at, :] = turned[part * rows : (part + 1) * rows]
            column_s[at, :] = jnp.broadcast_to(last[part * rows : (part + 1) * rows], (rows, 128))


def _outer(xt_s, column_s, dy, out_ref):
    width = dy.shape[1]
    last_row = dy[MAIN:].astype(F32)[0:1]
    step = xt_s.shape[0] // 2
    for start in range(0, xt_s.shape[0], step):
        at = slice(start, start + step)
        column = jnp.concatenate([column_s[at, :]] * (width // 128), axis=1)
        total = _dot(xt_s[at, :], dy[:MAIN], ((1,), (0,))) + column * last_row
        out_ref[at, :] = total.astype(BF16)


def _moments(values):
    average = jnp.mean(values, axis=-1, keepdims=True)
    centred = values - average
    inverse = lax.rsqrt(jnp.mean(centred * centred, axis=-1, keepdims=True) + EPSILON)
    return centred * inverse, inverse


def _norm_back(normed, inverse, gain, grad):
    scaled = grad * gain
    first = jnp.mean(scaled, axis=-1, keepdims=True)
    second = jnp.mean(scaled * normed, axis=-1, keepdims=True)
    return (scaled - first - normed * second) * inverse


def _gelu_parts(up):
    square = up * up
    bell = jnp.exp(-0.5 * square)
    size = jnp.abs(up)
    t = 1.0 / (1.0 + (0.375 * 0.5**0.5) * size)
    terms = (
        0.21133947372436523, 0.21568892896175385, 0.16666550934314728, 0.2830598056316376,
        -0.1295955926179886, 0.3879369795322418, -0.1350957304239273,
    )
    value = jnp.full_like(t, 0.5 * terms[-1])
    for term in terms[-2::-1]:
        value = value * t + 0.5 * term
    tail = value * t * bell
    cumulative = jnp.where(up < 0.0, tail, 1.0 - tail)
    return up * cumulative, cumulative + up * (bell * 0.3989422804014327)


def _entry_kernel(
    layer, xa_ref, xb_ref, wa_ref, wb_ref, bias_ref, gain_ref, shift_ref, qa_ref, qb_ref,
    hidden_ref, normed_ref, q_ref, kv_ref, normed_s,
):
    step = pl.program_id(0)

    @pl.when(step == 0)
    def _():
        hidden = (
            _dot(xa_ref[...], wa_ref[...], ((1,), (0,)))
            + _dot(xb_ref[...], wb_ref[...], ((1,), (0,)))
            + _row(bias_ref, layer)
        )
        hidden_ref[...] = hidden
        normed, _unused = _moments(hidden)
        low = (normed * _row(gain_ref, layer) + _row(shift_ref, layer)).astype(BF16)
        normed_s[...] = low
        normed_ref[...] = low

    @pl.when(jnp.logical_and(step >= 1, step <= 2))
    def _():
        half = qa_ref.shape[1]
        kv_ref[:, :half] = _dot(normed_s[...], qa_ref[...], ((1,), (0,))).astype(BF16)
        kv_ref[:, half:] = _dot(normed_s[...], qb_ref[...], ((1,), (0,))).astype(BF16)

    @pl.when(step == 3)
    def _():
        half = qa_ref.shape[1]
        q_ref[:, :half] = _dot(normed_s[...], qa_ref[...], ((1,), (0,))).astype(BF16)
        q_ref[:, half:] = _dot(normed_s[...], qb_ref[...], ((1,), (0,))).astype(BF16)


def entry_forward(layer, xa, xb, wa, wb, bias, gain, shift, qa, qb):
    model = xa.shape[1]
    half = qa.shape[3]

    def part(step):
        return jnp.where(step == 3, 0, jnp.maximum(step, 1))

    rows = pl.BlockSpec((PAD, model), lambda j: (0, 0))
    square = pl.BlockSpec((None, None, model, model), lambda j: (layer, 0, 0, 0))
    single = pl.BlockSpec((None, None, model, model), lambda j: (0, 0, 0, 0))
    vector = pl.BlockSpec(bias.shape, lambda j: (0, 0))
    third = pl.BlockSpec((None, None, model, half), lambda j: (layer, part(j), 0, 0))
    single_third = pl.BlockSpec((None, None, model, half), lambda j: (0, part(j), 0, 0))
    return pl.pallas_call(
        functools.partial(_entry_kernel, layer),
        grid=(4,),
        in_specs=[rows, rows, square, single, vector, vector, vector, third, single_third],
        out_specs=[
            rows,
            rows,
            rows,
            pl.BlockSpec((PAD, 2 * half), lambda j: (0, jnp.clip(j - 1, 0, 1))),
        ],
        out_shape=[
            jax.ShapeDtypeStruct((PAD, model), F32),
            jax.ShapeDtypeStruct((PAD, model), BF16),
            jax.ShapeDtypeStruct((PAD, 2 * half), BF16),
            jax.ShapeDtypeStruct((PAD, 4 * half), BF16),
        ],
        scratch_shapes=[pltpu.VMEM((PAD, model), BF16)],
        compiler_params=pltpu.CompilerParams(vmem_limit_bytes=VMEM_LIMIT),
        cost_estimate=LIGHT,
        name="entry_forward",
    )(xa, xb, wa, wb, bias, gain, shift, qa, qb)


class _Refs:
    def __init__(self):
        self.names, self.values = [], []

    def add(self, name, *value):
        self.names.append(name)
        self.values.append(value[0] if len(value) == 1 else value)


def _mlp_kernel(names, plan, coords_ref, *refs):
    layer, first, last, forward, backward, sets, pieces, order = plan
    ref = dict(zip(names, refs, strict=True))
    step = pl.program_id(0)
    steps_per_set = pl.num_programs(0) // len(sets)

    @pl.when(step == 0)
    def _():
        if first and forward:
            half = ref["proj_own"].shape[1]
            middle = (
                ref["hidden"][...]
                + _dot(ref["attended"][:, :half], ref["proj_own"][...], ((1,), (1,)))
                + _dot(ref["attended"][:, half:], ref["proj_peer"][...], ((1,), (1,)))
                + _row(ref["proj_bias"], layer)
            )
            ref["middle_out"][...] = middle
            normed, _unused = _moments(middle)
            low = (normed * _row(ref["gain"], layer) + _row(ref["shift"], layer)).astype(BF16)
            ref["normed_out"][...] = low
            ref["normed_s"][...] = low
            ref["acc_s"][...] = middle + _row(ref["down_bias"], layer)
        else:
            ref["normed_s"][...] = ref["normed"][...]
            if forward:
                ref["acc_s"][...] = ref["acc"][...]
        if backward:
            assert len(sets) == 1
            ref["grad_s"][...] = ref["grad"][...].astype(BF16)
            if first:
                ref["dn_s"][...] = jnp.zeros_like(ref["dn_s"])
            else:
                ref["dn_s"][...] = ref["dn"][...]
            _fill_turned(coords_ref, order, pieces, ref["grad_s"], ref["grad_t"], ref["grad_c"], sets[0] == "peer")
            _fill_turned(coords_ref, order, pieces, ref["normed_s"], ref["normed_t"], ref["normed_c"], sets[0] == "peer")

    for number, name in enumerate(sets):

        def tile(name=name):
            up_w = ref["up_" + name]
            down_w = ref["down_" + name]
            if forward:
                up = _dot(ref["normed_s"][...], up_w[...], ((1,), (0,))) + _row(ref["up_bias_" + name], layer)
                active, slope = _gelu_parts(up)
                active = active.astype(BF16)
                ref["acc_s"][...] += _dot(active, down_w[...], ((1,), (1,)))
                if not backward:
                    ref["active_" + name][...] = active
                    ref["slope_" + name][...] = slope.astype(BF16)
            else:
                active = ref["active_" + name][...]
                slope = ref["slope_" + name][...].astype(F32)
            if backward:
                du = _dot(ref["grad_s"][...], down_w[...], ((1,), (0,))) * slope
                ref["up_bias_grad_" + name][...] = jnp.sum(du, axis=0, keepdims=True)
                du = du.astype(BF16)
                ref["dn_s"][...] += _dot(du, up_w[...], ((1,), (1,)))
                _outer(ref["grad_t"], ref["grad_c"], active, ref["grads_own"].at[0] if name == "own" else ref["down_grad"])
                _outer(ref["normed_t"], ref["normed_c"], du, ref["grads_own"].at[1] if name == "own" else ref["up_grad"])

        if len(sets) == 1:
            tile()
        else:
            pl.when(step // steps_per_set == number)(tile)

    @pl.when(step == pl.num_programs(0) - 1)
    def _():
        if not last:
            if forward:
                ref["acc_out"][...] = ref["acc_s"][...]
            if backward:
                ref["dn_out"][...] = ref["dn_s"][...]
            return
        if forward:
            ref["result"][...] = ref["acc_s"][...].astype(BF16)
        if backward:
            gradient = ref["grad"][...].astype(F32)
            dn = ref["dn_s"][...]
            normed, inverse = _moments(ref["middle"][...])
            sums = ref["sums"]
            sums[0:1, :] = jnp.sum(gradient, axis=0, keepdims=True)
            sums[1:2, :] = jnp.sum(dn * normed, axis=0, keepdims=True)
            sums[2:3, :] = jnp.sum(dn, axis=0, keepdims=True)
            dmid = gradient + _norm_back(normed, inverse, _row(ref["gain"], layer), dn)
            sums[3:4, :] = jnp.sum(dmid, axis=0, keepdims=True)
            sums[4:8, :] = jnp.zeros_like(sums[4:8, :])
            ref["dmid"][...] = dmid
            low = dmid.astype(BF16)
            half = ref["proj_own"].shape[1]
            for at, name in ((0, "own"), (half, "peer")):
                ref["dattn"][:, at : at + half] = _dot(low, ref["proj_" + name][...], ((1,), (0,))).astype(BF16)


def mlp(layer, first, last, forward, backward, sets, pieces, order, values):
    _unused, model, units = values["up_" + sets[0]].shape
    steps = units // TILE
    plan = (layer, first, last, forward, backward, sets, pieces, order)
    names, in_specs, operands = [], [], []
    rows = pl.BlockSpec((PAD, model), lambda j, c: (0, 0))
    vector = pl.BlockSpec(values["gain"].shape, lambda j, c: (0, 0))

    def take(name, spec):
        names.append(name)
        in_specs.append(spec)
        operands.append(values[name])

    def moving(number, shape):
        def index(j, c):
            tile = (0, jnp.clip(j - number * steps, 0, steps - 1))
            return tile if len(shape) == 2 else (layer, *tile)

        return pl.BlockSpec(shape, index)

    half = values["proj_own"].shape[2]
    whole_proj = pl.BlockSpec((None, model, half), lambda j, c: (layer, 0, 0))

    if first and forward:
        for name, spec in (("hidden", rows), ("attended", rows), ("proj_own", whole_proj), ("proj_peer", whole_proj),
                           ("proj_bias", vector), ("gain", vector), ("shift", vector), ("down_bias", vector)):
            take(name, spec)
    else:
        take("normed", rows)
        if forward:
            take("acc", rows)
    if backward:
        take("grad", rows)
        if not first:
            take("dn", rows)
        if last:
            take("middle", rows)
            for name, spec in (("proj_own", whole_proj), ("proj_peer", whole_proj), ("gain", vector)):
                if name not in names:
                    take(name, spec)
    for number, name in enumerate(sets):
        take("up_" + name, moving(number, (None, model, TILE)))
        take("down_" + name, moving(number, (None, model, TILE)))
        if forward:
            take("up_bias_" + name, moving(number, (2, TILE)))
        else:
            take("active_" + name, moving(number, (PAD, TILE)))
            take("slope_" + name, moving(number, (PAD, TILE)))
    out_names, out_specs, out_shape = [], [], []

    def give(name, spec, shape, kind):
        out_names.append(name)
        out_specs.append(spec)
        out_shape.append(jax.ShapeDtypeStruct(shape, kind))

    full = (PAD, model)
    if first and forward:
        give("middle_out", rows, full, F32)
        give("normed_out", rows, full, BF16)
    if not last:
        if forward:
            give("acc_out", rows, full, F32)
        if backward:
            give("dn_out", rows, full, F32)
    else:
        if forward:
            give("result", rows, full, BF16)
        if backward:
            give("sums", pl.BlockSpec((8, model), lambda j, c: (0, 0)), (8, model), F32)
            give("dmid", rows, full, F32)
            give("dattn", rows, full, BF16)
    for number, name in enumerate(sets):
        if forward and not backward:
            for kind in ("active_", "slope_"):
                give(kind + name, moving(number, (PAD, TILE)), (PAD, units), BF16)
        if backward:
            stacked = pl.BlockSpec(
                (2, model, TILE),
                lambda j, c, number=number: (0, 0, jnp.clip(j - number * steps, 0, steps - 1)),
            )
            if name == "own":
                give("grads_own", stacked, (2, model, units), BF16)
            else:
                for kind in ("down_grad", "up_grad"):
                    give(kind, moving(number, (model, TILE)), (model, units), BF16)
            give("up_bias_grad_" + name, moving(number, (1, TILE)), (1, units), F32)
    scratch_names = ["normed_s"]
    scratch = [pltpu.VMEM(full, BF16)]
    if forward:
        scratch_names.append("acc_s")
        scratch.append(pltpu.VMEM(full, F32))
    if backward:
        for name, shape, kind in (("grad_s", full, BF16), ("dn_s", full, F32), ("grad_t", (model, MAIN), BF16),
                                  ("grad_c", (model, 128), F32), ("normed_t", (model, MAIN), BF16),
                                  ("normed_c", (model, 128), F32)):
            scratch_names.append(name)
            scratch.append(pltpu.VMEM(shape, kind))
    results = pl.pallas_call(
        functools.partial(_mlp_kernel, tuple(names + out_names + scratch_names), plan),
        grid_spec=pltpu.PrefetchScalarGridSpec(
            num_scalar_prefetch=1,
            grid=(steps * len(sets),),
            in_specs=in_specs,
            out_specs=out_specs,
            scratch_shapes=scratch,
        ),
        out_shape=out_shape,
        compiler_params=pltpu.CompilerParams(vmem_limit_bytes=VMEM_LIMIT),
        cost_estimate=LIGHT,
        name="mlp_" + ("f" if forward else "") + ("b" if backward else "") + "_" + "_".join(sets),
    )(values["coords"], *operands)
    return dict(zip(out_names, results, strict=True))


def _entry_back_kernel(
    layer, pieces, order, coords_ref, dq_ref, dk_ref, dk_got_ref, dv_ref, dv_got_ref, dmid_ref, hidden_ref,
    normed_ref, xa_ref, xb_ref, attended_ref, gain_ref, qa_ref, qb_ref, wa_ref, wb_ref,
    own_ref, peer_ref, peer_rest_ref, back_ref, skip_back_ref, sums_ref,
    da_s, low_s, xt_s, column_s, yt_s, column_y,
):
    step = pl.program_id(0)
    half = qa_ref.shape[1]

    def turn(x_ref, to_s, to_c, theirs):
        _fill_turned(coords_ref, order, pieces, x_ref, to_s, to_c, theirs)

    @pl.when(step == 0)
    def _():
        da_s[...] = jnp.zeros_like(da_s)
        turn(normed_ref, xt_s, column_s, False)
        turn(normed_ref, yt_s, column_y, True)

    def columns(refs):
        def run():
            total = refs[0][...]
            if len(refs) == 2:
                total = (total.astype(F32) + refs[1][...].astype(F32)).astype(BF16)
            own, peer = total[:, :half], total[:, half:]
            da_s[...] += _dot(own, qa_ref[...], ((1,), (1,))) + _dot(peer, qb_ref[...], ((1,), (1,)))
            _outer(xt_s, column_s, own, own_ref)
            _outer(yt_s, column_y, peer, peer_ref)

        return run

    pl.when(step == 0)(columns((dq_ref,)))
    pl.when(step == 1)(columns((dk_ref, dk_got_ref)))
    pl.when(step == 2)(columns((dv_ref, dv_got_ref)))

    @pl.when(step == 3)
    def _():
        da = da_s[...]
        normed, inverse = _moments(hidden_ref[...])
        sums_ref[0:1, :] = jnp.sum(da * normed, axis=0, keepdims=True)
        sums_ref[1:2, :] = jnp.sum(da, axis=0, keepdims=True)
        dhid = dmid_ref[...] + _norm_back(normed, inverse, _row(gain_ref, layer), da)
        sums_ref[2:3, :] = jnp.sum(dhid, axis=0, keepdims=True)
        sums_ref[3:8, :] = jnp.zeros_like(sums_ref[3:8, :])
        low_s[...] = dhid.astype(BF16)
        turn(xa_ref, xt_s, column_s, False)
        turn(xb_ref, yt_s, column_y, True)

    for number in range(2):

        @pl.when(step == 3 + number)
        def _(number=number):
            dy = low_s[:, number * half : (number + 1) * half]
            _outer(xt_s, column_s, dy, own_ref)
            _outer(yt_s, column_y, dy, peer_rest_ref)

    @pl.when(step == 4)
    def _():
        first = coords_ref[1] == 0
        one = _dot(low_s[...], wa_ref[...], ((1,), (1,)))
        two = _dot(low_s[...], wb_ref[...], ((1,), (1,)))
        back_ref[...] = jnp.where(first, one, two)
        skip_back_ref[...] = jnp.where(first, two, one).astype(BF16)

    @pl.when(step == 5)
    def _():
        low_s[...] = dmid_ref[...].astype(BF16)
        turn(low_s, xt_s, column_s, False)
        turn(low_s, yt_s, column_y, True)
        _outer(xt_s, column_s, attended_ref[:, :half], own_ref)
        _outer(yt_s, column_y, attended_ref[:, half:], peer_rest_ref)


def entry_backward(layer, pieces, order, coords, dq, dk, dk_got, dv, dv_got, dmid, hidden, normed, xa, xb, attended, gain, qa, qb, wa, wb):
    model = xa.shape[1]
    half = qa.shape[3]
    rows = pl.BlockSpec((PAD, model), lambda j, c: (0, 0))
    linear = pl.BlockSpec((None, None, model, model), lambda j, c: (layer, 0, 0, 0))
    single = pl.BlockSpec((None, None, model, model), lambda j, c: (0, 0, 0, 0))
    single_third = pl.BlockSpec((None, None, model, half), lambda j, c: (0, jnp.minimum(j, 2), 0, 0))
    vector = pl.BlockSpec(gain.shape, lambda j, c: (0, 0))
    third = pl.BlockSpec((None, None, model, half), lambda j, c: (layer, jnp.minimum(j, 2), 0, 0))
    grads = pl.BlockSpec((model, half), lambda j, c: (0, j))
    early = pl.BlockSpec((model, half), lambda j, c: (0, jnp.minimum(j, 2)))
    late = pl.BlockSpec((model, half), lambda j, c: (0, jnp.maximum(j, 3) - 3))
    weight = jax.ShapeDtypeStruct((model, 6 * half), BF16)
    part = jax.ShapeDtypeStruct((model, 3 * half), BF16)
    return pl.pallas_call(
        functools.partial(_entry_back_kernel, layer, pieces, order),
        grid_spec=pltpu.PrefetchScalarGridSpec(
            num_scalar_prefetch=1,
            grid=(6,),
            in_specs=[rows] * 11 + [vector, third, single_third, linear, single],
            out_specs=[grads, early, late, rows, rows, pl.BlockSpec((8, model), lambda j, c: (0, 0))],
            scratch_shapes=[
                pltpu.VMEM((PAD, model), F32),
                pltpu.VMEM((PAD, model), BF16),
                pltpu.VMEM((model, MAIN), BF16),
                pltpu.VMEM((model, 128), F32),
                pltpu.VMEM((model, MAIN), BF16),
                pltpu.VMEM((model, 128), F32),
            ],
        ),
        out_shape=[
            weight,
            part,
            part,
            jax.ShapeDtypeStruct((PAD, model), F32),
            jax.ShapeDtypeStruct((PAD, model), BF16),
            jax.ShapeDtypeStruct((8, model), F32),
        ],
        compiler_params=pltpu.CompilerParams(vmem_limit_bytes=VMEM_LIMIT),
        cost_estimate=LIGHT,
        name="entry_backward",
    )(coords, dq, dk, dk_got, dv, dv_got, dmid, hidden, normed, xa, xb, attended, gain, qa, qb, wa, wb)


def _gather_kernel(count, core_ref, *refs):
    first = core_ref[0] == 0
    out_ref = refs[-1]
    for layer in range(count):
        mine, theirs = refs[2 * layer][...], refs[2 * layer + 1][...]
        low = jnp.where(first, mine, theirs)
        high = jnp.where(first, theirs, mine)
        for start, part in ((0, low[:MAIN]), (MAIN, high[:MAIN]), (2 * MAIN, low[MAIN : MAIN + 1]), (2 * MAIN + 1, high[MAIN : MAIN + 1])):
            at = slice(start, start + part.shape[0])
            if count == 1:
                out_ref[at, :] = part
            else:
                out_ref[at, layer, :] = part


def gather_rows(core, *pairs):
    width = pairs[0][0].shape[1]
    count = len(pairs)
    shape = (2 * MAIN + 2, width) if count == 1 else (2 * MAIN + 2, count, width)
    flat = [value for pair in pairs for value in pair]
    return pl.pallas_call(
        functools.partial(_gather_kernel, count),
        in_specs=[pl.BlockSpec(memory_space=pltpu.SMEM)] + [pl.BlockSpec(memory_space=pltpu.VMEM)] * len(flat),
        out_specs=pl.BlockSpec(memory_space=pltpu.VMEM),
        out_shape=jax.ShapeDtypeStruct(shape, BF16),
        compiler_params=pltpu.CompilerParams(vmem_limit_bytes=VMEM_LIMIT),
        cost_estimate=LIGHT,
        name="gather_rows",
    )(jnp.reshape(core, (1,)).astype(jnp.int32), *flat)


def swap_cores(value):
    return lax.ppermute(value, "tensor", [(0, 1), (1, 0)])


def swap_bit(value, bit, size, crossed):
    cores = 2
    pairs = []
    for index in range(size):
        for core in range(cores):
            other = index ^ (1 << ((bit ^ core) if crossed and bit < 2 else bit))
            pairs.append((index * cores + core, other * cores + core))
    return lax.ppermute(value, ("dp", "tensor"), pairs)


def after(value, *others):
    return lax.optimization_barrier((value, others))[0]


def total(parts):
    result = parts[0].astype(F32)
    for part in parts[1:]:
        result = result + part.astype(F32)
    return result


class Reduction:
    def __init__(self, parts, order, size, axis=0, crossed=True):
        self.parts = [(part if isinstance(part, tuple) else (part,), 0) for part in parts]
        self.length, self.order, self.size = parts[0].shape[axis], list(order), size
        self.axis, self.crossed = axis, crossed

    def span(self, start, stop):
        values = []
        for arrays, at in self.parts:
            if len(arrays) == 1:
                values.append(lax.slice_in_dim(arrays[0], at + start, at + stop, axis=self.axis))
            elif self.axis == 1:
                values.append(jnp.stack([array[at + start : at + stop] for array in arrays]))
            else:
                values.append(jnp.concatenate([array[at + start : at + stop] for array in arrays], axis=1))
        return total(values)

    def send(self, gate):
        bit = self.order.pop(0)
        half = self.length // 2
        held = lax.optimization_barrier(([arrays for arrays, _ in self.parts], gate))[0]
        self.parts = [(arrays, at) for arrays, (_, at) in zip(held, self.parts)]
        payload = self.span(half, self.length).astype(held[0][0].dtype)
        self.parts.append(((swap_bit(payload, bit, self.size, self.crossed),), 0))
        self.length = half
        return payload

    def result(self):
        return self.span(0, self.length)


def arrange(value, order, size):
    bits = size.bit_length() - 1
    index = lax.axis_index("dp")
    view = value.reshape((2,) * bits + value.shape[1:])
    for bit in range(bits):
        axis = bits - 1 - bit
        view = jnp.where((index >> bit) & 1 == 1, jnp.flip(view, axis), view)
    axes = [bits - 1 - bit for bit in order] + list(range(bits, view.ndim))
    return view.transpose(axes).reshape(value.shape)


def localize(value, core):
    main = lax.dynamic_slice_in_dim(value, core * MAIN, MAIN, 0)
    extra = lax.dynamic_slice_in_dim(value, 2 * MAIN + core, 1, 0)
    blank = jnp.zeros((PAD - MAIN - 1,) + value.shape[1:], value.dtype)
    return jnp.concatenate([main, extra, blank], axis=0)


def globalize(core, *mine):
    return gather_rows(core, *((value, swap_cores(value)) for value in mine))


def sum_vectors(shared, up_own, up_peer, size):
    count, model = shared.shape
    layers, units = up_own.shape
    order = tuple(range(size.bit_length() - 1))

    def blocks(offsets):
        first = shared.reshape(count, size, model // size).transpose(1, 0, 2)
        second = offsets.reshape(layers, size, units // model, model // size)
        second = second.transpose(1, 0, 2, 3).reshape(size, -1, model // size)
        return arrange(jnp.concatenate([first, second], axis=1), order, size)

    return Reduction([blocks(up_own), swap_cores(blocks(up_peer))], order, size, crossed=False)


def body(
    inputs, skips, cotangent, skip_weight, skip_bias, attn_norm_gain, attn_norm_bias, qkv_weight,
    proj_weight, proj_bias, ffn_norm_gain, ffn_norm_bias, up_weight, up_bias, down_weight, down_bias,
):
    core = lax.axis_index("tensor")
    size = lax.axis_size("dp")
    bits = size.bit_length() - 1
    assert size == 1 << bits and bits >= 2
    order = tuple(range(bits))
    layers, model = skip_bias.shape
    assert layers == 2
    coords = jnp.stack([lax.axis_index("dp"), core]).astype(jnp.int32)

    qkv_turned = qkv_weight.transpose(0, 2, 1, 3)
    skip_own = [skip_weight[layer : layer + 1] for layer in range(layers)]
    qkv_own = [qkv_turned[layer : layer + 1] for layer in range(layers)]
    skip_peer = [swap_cores(skip_own[0]), None]
    qkv_peer = [swap_cores(qkv_own[0]), None]
    up_bias_peer = swap_cores(up_bias)
    weights = {
        "coords": coords, "proj_own": proj_weight, "up_own": up_weight, "down_own": down_weight,
        "up_bias_own": up_bias, "up_bias_peer": up_bias_peer, "proj_bias": proj_bias,
        "down_bias": down_bias, "gain": ffn_norm_gain, "shift": ffn_norm_bias,
    }
    skip_parts = localize(skips.transpose(1, 0, 2), core)

    def enter(layer, residual):
        skip_rows = skip_parts[:, layer]
        xa = jnp.where(core == 0, residual, skip_rows)
        xb = jnp.where(core == 0, skip_rows, residual)
        hidden, normed, q, kv = entry_forward(
            layer, xa, xb, skip_weight, skip_peer[layer], skip_bias, attn_norm_gain, attn_norm_bias,
            qkv_turned, qkv_peer[layer],
        )
        kv_other = swap_cores(kv)
        attended, exact, e, ex, il = attn_forward(q, kv, kv_other)
        return dict(xa=xa, xb=xb, hidden=hidden, normed=normed, q=q, kv=kv, kv_other=kv_other,
                    attended=attended, exact=exact, e=e, ex=ex, il=il)

    items = {}

    def add(layer, name, own, peer, axis):
        theirs = tuple(swap_cores(value) for value in peer)
        items[name, layer] = Reduction([own, theirs], order, size, axis)

    def sends(gate, *keys):
        made = []
        for key in keys:
            if items[key].order:
                made.append(items[key].send(gate))
        return after(gate, *made)

    def back(layer, kept, mid, dattn, *keys):
        dq, dk, dk_other, dv, dv_other = attn_backward(
            kept["q"], kept["kv"], kept["kv_other"], dattn, kept["exact"], kept["e"], kept["ex"], kept["il"]
        )
        dk_got, dv_got = swap_cores(dk_other), swap_cores(dv_other)
        dq = sends(dq, *keys)
        own, peer, peer_rest, gradient, skip_grad, sums = entry_backward(
            layer, size, order, coords, dq, dk, dk_got, dv, dv_got, mid["dmid"], kept["hidden"], kept["normed"],
            kept["xa"], kept["xb"], kept["attended"], attn_norm_gain, qkv_turned, qkv_peer[layer],
            skip_weight, skip_peer[layer],
        )
        add(layer, "attn", own, (peer, peer_rest), 0)
        return gradient, skip_grad, sums

    kept = [None] * layers
    kept[0] = enter(0, localize(inputs, core))
    weights["up_peer"] = swap_cores(after(up_weight, skip_peer[0], qkv_peer[0]))
    late = after((proj_weight, down_weight, skip_own[1], qkv_own[1]), kept[0]["kv_other"])
    weights["proj_peer"], weights["down_peer"], skip_peer[1], qkv_peer[1] = (swap_cores(item) for item in late)
    mid0 = mlp(0, True, True, True, False, ("peer", "own"), size, order, {**weights, **kept[0]})
    kept[1] = enter(1, mid0["result"])
    values = {**weights, **kept[1], "grad": localize(cotangent, core)}
    one = mlp(1, True, False, True, True, ("peer",), size, order, values)
    values.update(normed=one["normed_out"], middle=one["middle_out"], acc=one["acc_out"], dn=one["dn_out"])
    two = mlp(1, False, True, True, True, ("own",), size, order, values)
    add(1, "mlp", two["grads_own"], (one["down_grad"], one["up_grad"]), 1)
    output = globalize(core, two["result"])
    dattn = sends(two["dattn"], ("mlp", 1))
    gradient, skip_grad1, sums1 = back(1, kept[1], two, dattn)
    gradient = sends(gradient, ("mlp", 1))

    values = {**weights, **kept[0], **mid0, "normed": mid0["normed_out"], "middle": mid0["middle_out"], "grad": gradient}
    one0 = mlp(0, True, False, False, True, ("peer",), size, order, values)
    values.update(dn=sends(one0["dn_out"], ("attn", 1), ("mlp", 1)))
    low = mlp(0, False, True, False, True, ("own",), size, order, values)
    add(0, "mlp", low["grads_own"], (one0["down_grad"], one0["up_grad"]), 1)
    dattn = sends(low["dattn"], ("mlp", 0), ("mlp", 1))
    gradient, skip_grad0, sums0 = back(0, kept[0], low, dattn, ("attn", 1))
    shared = jnp.concatenate([low["sums"][:4], two["sums"][:4], sums0[:3], sums1[:3]], axis=0)
    items["vectors", 0] = sum_vectors(
        shared,
        jnp.concatenate([low["up_bias_grad_own"], two["up_bias_grad_own"]], axis=0),
        jnp.concatenate([one0["up_bias_grad_peer"], one["up_bias_grad_peer"]], axis=0),
        size,
    )
    finish = gradient
    for keys in (
        (("mlp", 0), ("attn", 1)),
        (("attn", 0),),
        (("vectors", 0),),
        (("mlp", 0), ("attn", 1), ("vectors", 0)),
        (("attn", 0), ("vectors", 0)),
        (("mlp", 0), ("vectors", 0)),
        (("attn", 0),),
        (("attn", 0),),
    ):
        finish = sends(finish, *keys)
    while any(item.order for item in items.values()):
        finish = sends(finish, *items)
    result = {key: item.result() for key, item in items.items()}
    count = shared.shape[0]
    vectors = result["vectors", 0][0, :count]
    up_bias_grad = result["vectors", 0][0, count:].reshape(layers, -1)
    input_grad = globalize(core, gradient.astype(BF16))
    skip_grad = globalize(core, skip_grad0, skip_grad1).transpose(1, 0, 2)
    outer = vectors[:8].reshape(2, 4, -1)
    inner = vectors[8:].reshape(2, 3, -1)

    half = model // 2

    def columns(start, stop):
        return jnp.stack([result["attn", layer][:, start:stop] for layer in range(layers)])

    def matrix(which):
        return jnp.stack([result["mlp", layer][which] for layer in range(layers)])

    return (
        output, input_grad, skip_grad, columns(3 * half, 5 * half)[:, None],
        inner[:, 2], inner[:, 0], inner[:, 1],
        columns(0, 3 * half).reshape(layers, -1, 3, qkv_weight.shape[3]), columns(5 * half, 6 * half),
        outer[:, 3], outer[:, 1], outer[:, 2],
        matrix(1), up_bias_grad, matrix(0), outer[:, 0],
    )


def solution(mesh):
    return jax.shard_map(
        body,
        mesh=mesh,
        in_specs=(
            P("dp", None), P(None, "dp", None), P("dp", None), P(None, "tensor", None, None), P(), P(),
            P(), P(None, None, None, "tensor"), P(None, None, "tensor"), P(), P(), P(),
            P(None, None, "tensor"), P(None, "tensor"), P(None, None, "tensor"), P(),
        ),
        out_specs=(
            P("dp", None), P("dp", None), P(None, "dp", None), P(None, "tensor", "dp", None),
            P(None, "dp"), P(None, "dp"), P(None, "dp"), P(None, "dp", None, "tensor"),
            P(None, "dp", "tensor"), P(None, "dp"), P(None, "dp"), P(None, "dp"),
            P(None, "dp", "tensor"), P(None, ("tensor", "dp")), P(None, "dp", "tensor"), P(None, "dp"),
        ),
        check_vma=False,
    )
```

time: 972 us -> 593 us (0.61)
  matrix products: 192 us -> 0 us
  waiting for transfers between devices: 235 us -> 113 us
  local copies, waits for them, and re-layouts: 154 us -> 60.2 us
  Pallas kernels: 236 us -> 308 us
  starting transfers between devices: 58.2 us -> 31.6 us
    dot_general x26 -> x0, matrix products: 192 us -> none  [_dot(): return lax.dot_general(a, b, (dims, ((), ())), preferred_element_type=F32)]
    ppermute x44 -> x20, waiting for transfers between devices: 235 us -> 87.2 us  [swap_bit(): return lax.ppermute(value, ('dp', 'tensor'), pairs)]
    pallas_call x28 -> x12, Pallas kernels: 150 us -> 223 us  [the longest x5 126 us: mlp(): pl.pallas_call(functools.partial(_mlp_kernel, tuple(names + out_names + s...]
    unnamed x265 -> x72, local copies, waits for them, and re-layouts: 71.8 us -> 10.8 us
    concatenate x9 -> x3, local copies, waits for them, and re-layouts: 46.8 us -> 0.07 us  [blocks(): return arrange(jnp.concatenate([first, second], axis=1), order, size)]
    ppermute x44 -> x20, starting transfers between devices: 50.7 us -> 23.5 us  [swap_bit(): return lax.ppermute(value, ('dp', 'tensor'), pairs)]
    another operation x3 -> x25, local copies, waits for them, and re-layouts: 0.12 us -> 26.6 us  [the longest x16 20.9 us: span(): values.append(jnp.stack([array[at + start:at + stop] for array in arrays]))]
    ppermute x31 -> x27, waiting for transfers between devices: 0.08 us -> 26.1 us  [swap_cores(): return lax.ppermute(value, 'tensor', [(0, 1), (1, 0)])]
  transfers between devices with their start and end apart: 75 -> 47, of which waited for: 26 -> 14; matrix products, arithmetic and copies ran while one was open for 31% -> 18% of each run, Pallas kernels for 18% -> 40%
where the time goes in v2:
time: 593 us; the launch traced here: 587 us
  Pallas kernels  308 us (52%)
  waiting for transfers between devices  113 us (19%)
  other arithmetic  72.8 us (12%)
  local copies, waits for them, and re-layouts  60.2 us (10%)
  starting transfers between devices  31.6 us (5%)
    pallas_call x5, Pallas kernels, mlp(): pl.pallas_call(functools.partial(_mlp_kernel, tuple(names + out_names + s...  126 us
    ppermute x20, waiting for transfers between devices, swap_bit(): return lax.ppermute(value, ('dp', 'tensor'), pairs)  87.2 us
    pallas_call x2, Pallas kernels, entry_backward(): pl.pallas_call(functools.partial(_entry_back_kernel, layer, pieces, order...  56 us
    convert_element_type x16, other arithmetic, send(): payload = self.span(half, self.length).astype(held[0][0].dtype)  49 us
    pallas_call x2, Pallas kernels, attn_backward(): pl.pallas_call(_attn_bwd_kernel, grid=(groups,), in_specs=[near(0), near(...  46.6 us
    pallas_call x2, Pallas kernels, attn_forward(): pl.pallas_call(_attn_fwd_kernel, grid=(groups,), in_specs=[near(0), near(...  38.4 us
    pallas_call x2, Pallas kernels, entry_forward(): pl.pallas_call(functools.partial(_entry_kernel, layer), grid=(4,), in_spe...  27.3 us
    ppermute x27, waiting for transfers between devices, swap_cores(): return lax.ppermute(value, 'tensor', [(0, 1), (1, 0)])  26.1 us
  transfers between devices with their start and end apart: 47, of which 14 were waited for; matrix products, arithmetic and copies ran while one was open for 18% of the time, Pallas kernels for 40%

profile of v2, /device:TPU:0, one launch (start us, length us, event | category | flops | bytes accessed | tf_op | source)
XLA Modules:
  0.0 587.3 jit_solution(12028776280707708088)
XLA Ops:
  0.7 6.5 %fusion = (bf16[1,3,1024,512]{3,2,1,0:T(8,128)(2,1)}, bf16[1,3,1024,512]{3,2,1,0:T(8,128)(2,1)}) fusion(bf16[2,3,1024,512]{3,2,1,0:T(8,128)(2,1)} %bitcast.96), kind=kLoop, calls=%fused_computation.84 | loop fusion | bytes 12582912 | tf_op jit(solution)/shard_map/slice | solution.py:807
  7.6 2.4 fusion.1
  10.1 3.0 constant_dynamic-slice_fusion.2
  19.3 2.4 broadcast_select_fusion.2
  23.4 13.7 %entry_forward.2 = (f32[528,1024]{1,0:T(8,128)}, bf16[528,1024]{1,0:T(8,128)(2,1)}, bf16[528,1024]{1,0:T(8,128)(2,1)}, bf16[528,2048]{1,0:T(8,128)(2,1)}) custom-call(bf16[528,1024]{1,0:T(8,128)(2,1)} %get-tuple-element.403.xa_ref, bf16[528,1024]{1,0:T(8,128)(2,1)} %get-tuple-element.402.xb_ref, bf16[2,1,1024,1024]{3,2,1,0:T(8,128)(2,1)} %wa_ref.7, ...), custom_call_target="tpu_custom_call" | custom-call | flops 1 | bytes 1 | tf_op jit(solution)/shard_map/entry_forward/pallas_call | solution.py:314
  37.6 6.4 %collective-permute-done.2.ko_ref.vo_ref = bf16[528,2048]{1,0:T(8,128)(2,1)S(1)} collective-permute-done((bf16[528,2048]{1,0:T(8,128)(2,1)}, bf16[528,2048]{1,0:T(8,128)(2,1)S(1)}, u32[]{:S(2)}, u32[]{:S(2)}) %collective-permute-start.2) | collective-permute-done | bytes 2162720 | tf_op jit(solution)/shard_map/ppermute | solution.py:701
  45.0 8.4 %collective-permute-done.6.refs_10_.refs_11_ = bf16[2,2048]{1,0:T(2,128)(2,1)S(1)} collective-permute-done((bf16[2,2048]{1,0:T(2,128)(2,1)S(1)}, bf16[2,2048]{1,0:T(2,128)(2,1)S(1)}, u32[]{:S(2)}, u32[]{:S(2)}) %collective-permute-start.6) | collective-permute-done | bytes 8224 | tf_op jit(solution)/shard_map/ppermute | solution.py:701
  54.4 19.0 %attn_forward.2 = (bf16[528,1024]{1,0:T(8,128)(2,1)}, f32[528,1024]{1,0:T(8,128)}, bf16[16,528,1024]{2,1,0:T(8,128)(2,1)}, f32[4,528,16]{2,1,0:T(8,128)}, f32[4,528,16]{2,1,0:T(8,128)}) custom-call(bf16[528,1024]{1,0:T(8,128)(2,1)} %get-tuple-element.187.q_ref, bf16[528,2048]{1,0:T(8,128)(2,1)} %get-tuple-element.188.km_ref.vm_ref, ...), custom_call_target="tpu_custom_call" | custom-call | flops 1 | bytes 1 | tf_op jit(solution)/shard_map/attn_forward/pallas_call | solution.py:79
  73.5 28.4 %mlp_f_peer_own.1 = (f32[528,1024]{1,0:T(8,128)}, bf16[528,1024]{1,0:T(8,128)(2,1)}, bf16[528,1024]{1,0:T(8,128)(2,1)}, bf16[528,2048]{1,0:T(8,128)(2,1)}, bf16[...) custom-call(s32[2]{0:T(128)} %pad_add_fusion.coords_ref, ...), custom_call_target="tpu_custom_call" | custom-call | flops 1 | bytes 1 | tf_op jit(solution)/shard_map/mlp_f_peer_own/pallas_call | solution.py:536
  101.8 2.7 broadcast_select_fusion
  104.6 13.6 %entry_forward.3 = (f32[528,1024]{1,0:T(8,128)}, bf16[528,1024]{1,0:T(8,128)(2,1)}, bf16[528,1024]{1,0:T(8,128)(2,1)}, bf16[528,2048]{1,0:T(8,128)(2,1)}) custom-call(bf16[528,1024]{1,0:T(8,128)(2,1)} %get-tuple-element.401.xa_ref, bf16[528,1024]{1,0:T(8,128)(2,1)} %get-tuple-element.400.xb_ref, bf16[2,1,1024,1024]{3,2,1,0:T(8,128)(2,1)} %wa_ref.7, ...), custom_call_target="tpu_custom_call" | custom-call | flops 1 | bytes 1 | tf_op jit(solution)/shard_map/entry_forward/pallas_call | solution.py:314
  118.4 4.3 collective-permute-done.9.ko_ref.vo_ref
  124.0 19.4 %attn_forward.3 = (bf16[528,1024]{1,0:T(8,128)(2,1)}, f32[528,1024]{1,0:T(8,128)}, bf16[16,528,1024]{2,1,0:T(8,128)(2,1)}, f32[4,528,16]{2,1,0:T(8,128)}, f32[4,528,16]{2,1,0:T(8,128)}) custom-call(bf16[528,1024]{1,0:T(8,128)(2,1)} %get-tuple-element.197.q_ref, bf16[528,2048]{1,0:T(8,128)(2,1)} %get-tuple-element.198.km_ref.vm_ref, ...), custom_call_target="tpu_custom_call" | custom-call | flops 1 | bytes 1 | tf_op jit(solution)/shard_map/attn_forward/pallas_call | solution.py:79
  143.4 28.5 %mlp_fb_peer.1 = (f32[528,1024]{1,0:T(8,128)}, bf16[528,1024]{1,0:T(8,128)(2,1)}, f32[528,1024]{1,0:T(8,128)}, f32[528,1024]{1,0:T(8,128)}, bf16[1024,2048]{1,0:...) custom-call(s32[2]{0:T(128)} %pad_add_fusion.coords_ref, ...), custom_call_target="tpu_custom_call" | custom-call | flops 1 | bytes 1 | tf_op jit(solution)/shard_map/mlp_fb_peer/pallas_call | solution.py:536
  172.5 30.3 %mlp_fb_own.1 = (bf16[528,1024]{1,0:T(8,128)(2,1)}, f32[8,1024]{1,0:T(8,128)}, f32[528,1024]{1,0:T(8,128)}, bf16[528,1024]{1,0:T(8,128)(2,1)}, bf16[2,1024,2048]{2,1,0:T(8,128)(2,1)}, /*index=5*/f32[1,2048]{1,0:T(1,128)}) custom-call(s32[2]{0:T(128)} %pad_add_fusion.coords_ref, bf16[528,1024]{1,0:T(8,128)(2,1)} %get-tuple-element.200.refs_0_, ...), custom_call_target="tpu_custom_call" | custom-call | flops 1 | bytes 1 | tf_op jit(solution)/shard_map/mlp_fb_own/pallas_call | solution.py:536
  206.3 4.5 add_convert_fusion.1
  210.8 2.7 collective-permute-start.15
  213.4 23.3 %attn_backward.2 = (bf16[528,1024]{1,0:T(8,128)(2,1)}, bf16[528,1024]{1,0:T(8,128)(2,1)}, bf16[528,1024]{1,0:T(8,128)(2,1)}, bf16[528,1024]{1,0:T(8,128)(2,1)}, bf16[528,1024]{1,0:T(8,128)(2,1)}) custom-call(bf16[528,1024]{1,0:T(8,128)(2,1)} %get-tuple-element.197.q_ref, bf16[528,2048]{1,0:T(8,128)(2,1)} %get-tuple-element.198.km_ref.vm_ref, ...), custom_call_target="tpu_custom_call" | custom-call | flops 1 | bytes 1 | tf_op jit(solution)/shard_map/attn_backward/pallas_call | solution.py:179
  237.3 2.4 collective-permute-done.13.dk_got_ref
  242.2 28.0 %entry_backward.2 = (bf16[1024,3072]{1,0:T(8,128)(2,1)}, bf16[1024,1536]{1,0:T(8,128)(2,1)}, bf16[1024,1536]{1,0:T(8,128)(2,1)}, f32[528,1024]{1,0:T(8,128)}, bf...) custom-call(s32[2]{0:T(128)} %pad_add_fusion.coords_ref, bf16[528,1024]{1,0:T(8,128)(2,1)} %get-tuple-element.218.dq_ref, ...), custom_call_target="tpu_custom_call" | custom-call | flops 1 | bytes 1 | tf_op jit(solution)/shard_map/entry_backward/pallas_call | solution.py:639
  273.6 4.8 add_convert_fusion.5
  279.9 3.0 collective-permute-done.10.refs_1_
  282.9 3.1 gather_rows.3
  286.0 17.1 %mlp_b_peer.1 = (f32[528,1024]{1,0:T(8,128)}, bf16[1024,2048]{1,0:T(8,128)(2,1)}, bf16[1024,2048]{1,0:T(8,128)(2,1)}, f32[1,2048]{1,0:T(1,128)}) custom-call(s32[2]{0:T(128)} %pad_add_fusion.coords_ref, bf16[528,1024]{1,0:T(8,128)(2,1)} %get-tuple-element.205.refs_0_, f32[528,1024]{1,0:T(8,128)} %get-tuple-element.230.refs_1_, ...), custom_call_target="tpu_custom_call" | custom-call | flops 1 | bytes 1 | tf_op jit(solution)/shard_map/mlp_b_peer/pallas_call | solution.py:536
  304.8 2.4 slice.455
  309.5 2.7 add_convert_fusion.9
  313.8 3.5 add_convert_fusion.3
  317.9 21.9 %mlp_b_own.1 = (f32[8,1024]{1,0:T(8,128)}, f32[528,1024]{1,0:T(8,128)}, bf16[528,1024]{1,0:T(8,128)(2,1)}, bf16[2,1024,2048]{2,1,0:T(8,128)(2,1)}, f32[1,2048]{1,0:T(1,128)}) custom-call(s32[2]{0:T(128)} %pad_add_fusion.coords_ref, bf16[528,1024]{1,0:T(8,128)(2,1)} %get-tuple-element.205.refs_0_, f32[528,1024]{1,0:T(8,128)} %get-tuple-element.230.refs_1_, ...), custom_call_target="tpu_custom_call" | custom-call | flops 1 | bytes 1 | tf_op jit(solution)/shard_map/mlp_b_own/pallas_call | solution.py:536
  345.8 2.7 collective-permute-start.46
  351.9 2.9 add_convert_fusion
  356.2 23.3 %attn_backward.3 = (bf16[528,1024]{1,0:T(8,128)(2,1)}, bf16[528,1024]{1,0:T(8,128)(2,1)}, bf16[528,1024]{1,0:T(8,128)(2,1)}, bf16[528,1024]{1,0:T(8,128)(2,1)}, bf16[528,1024]{1,0:T(8,128)(2,1)}) custom-call(bf16[528,1024]{1,0:T(8,128)(2,1)} %get-tuple-element.187.q_ref, bf16[528,2048]{1,0:T(8,128)(2,1)} %get-tuple-element.188.km_ref.vm_ref, ...), custom_call_target="tpu_custom_call" | custom-call | flops 1 | bytes 1 | tf_op jit(solution)/shard_map/attn_backward/pallas_call | solution.py:179
  383.5 3.7 add_convert_fusion.7
  388.2 27.9 %entry_backward.3 = (bf16[1024,3072]{1,0:T(8,128)(2,1)}, bf16[1024,1536]{1,0:T(8,128)(2,1)}, bf16[1024,1536]{1,0:T(8,128)(2,1)}, f32[528,1024]{1,0:T(8,128)}, bf...) custom-call(s32[2]{0:T(128)} %pad_add_fusion.coords_ref, bf16[528,1024]{1,0:T(8,128)(2,1)} %get-tuple-element.272.dq_ref, ...), custom_call_target="tpu_custom_call" | custom-call | flops 1 | bytes 1 | tf_op jit(solution)/shard_map/entry_backward/pallas_call | solution.py:639
  426.3 5.0 add_convert_fusion.4
  434.0 2.3 add_convert_fusion.2
  438.0 13.3 %collective-permute-done.35 = bf16[128,3072]{1,0:T(8,128)(2,1)S(1)} collective-permute-done((bf16[128,3072]{1,0:T(8,128)(2,1)S(1)}, bf16[128,3072]{1,0:T(8,128)(2,1)S(1)}, u32[]{:S(2)}, u32[]{:S(2)}) %collective-permute-start.35) | collective-permute-done | bytes 786464 | tf_op jit(solution)/shard_map/ppermute | solution.py:711
  458.4 3.1 gather_rows.4
  461.6 7.0 %gather_rows.5 = bf16[1026,2,1024]{2,1,0:T(2,128)(2,1)} custom-call(s32[1]{0:T(128)} %bitcast.core_ref, bf16[528,1024]{1,0:T(8,128)(2,1)} %get-tuple-element.280.refs_0_, bf16[528,1024]{1,0:T(8,128)(2,1)} %collective-permute-done.26.refs_1_, bf16[528,1024]{1,0:T(8,128)(2,1)} %get-tuple-element.281.refs_2_, bf16[528,1024]{1,0:T(8,128)(2,1)} %collective-permute-done.27.refs_3_), custom_call_target="tpu_custom_call" | custom-call | flops 1 | bytes 1 | tf_op jit(solution)/shard_map/gather_rows/pallas_call | solution.py:689
  471.7 5.5 collective-permute-done.40
  481.6 3.6 add_convert_fusion.8
  489.2 16.9 %collective-permute-done.32 = bf16[512,3072]{1,0:T(8,128)(2,1)} collective-permute-done((bf16[512,3072]{1,0:T(8,128)(2,1)}, bf16[512,3072]{1,0:T(8,128)(2,1)}, u32[]{:S(2)}, u32[]{:S(2)}) %collective-permute-start.32) | collective-permute-done | bytes 3145760 | tf_op jit(solution)/shard_map/ppermute | solution.py:711
  506.1 3.7 add_convert_fusion.6
  515.9 2.8 add_convert_fusion.12
  522.2 8.4 %collective-permute-done.37 = bf16[256,3072]{1,0:T(8,128)(2,1)} collective-permute-done((bf16[256,3072]{1,0:T(8,128)(2,1)}, bf16[256,3072]{1,0:T(8,128)(2,1)}, u32[]{:S(2)}, u32[]{:S(2)}) %collective-permute-start.37) | collective-permute-done | bytes 1572896 | tf_op jit(solution)/shard_map/ppermute | solution.py:711
  533.2 11.3 %collective-permute-done.45 = bf16[2,64,2048]{2,1,0:T(8,128)(2,1)} collective-permute-done((bf16[2,64,2048]{2,1,0:T(8,128)(2,1)}, bf16[2,64,2048]{2,1,0:T(8,128)(2,1)}, u32[]{:S(2)}, u32[]{:S(2)}) %collective-permute-start.45) | collective-permute-done | bytes 524320 | tf_op jit(solution)/shard_map/ppermute | solution.py:711
  544.5 2.3 convert_add_fusion.1
  546.9 14.2 %collective-permute-done.38 = bf16[128,3072]{1,0:T(8,128)(2,1)S(1)} collective-permute-done((bf16[128,3072]{1,0:T(8,128)(2,1)S(1)}, bf16[128,3072]{1,0:T(8,128)(2,1)S(1)}, u32[]{:S(2)}, u32[]{:S(2)}) %collective-permute-start.38) | collective-permute-done | bytes 786464 | tf_op jit(solution)/shard_map/ppermute | solution.py:711
  564.8 17.4 %collective-permute-done.39 = bf16[64,3072]{1,0:T(8,128)(2,1)S(1)} collective-permute-done((bf16[64,3072]{1,0:T(8,128)(2,1)S(1)}, bf16[64,3072]{1,0:T(8,128)(2,1)S(1)}, u32[]{:S(2)}, u32[]{:S(2)}) %collective-permute-start.39) | collective-permute-done | bytes 393248 | tf_op jit(solution)/shard_map/ppermute | solution.py:711
  (259 shorter events, 99.7 us)
Async XLA Ops:
  7.2 14.5 %collective-permute-start.1 = (bf16[1,3,1024,512]{3,2,1,0:T(8,128)(2,1)}, bf16[1,3,1024,512]{3,2,1,0:T(8,128)(2,1)S(1)}, u32[]{:S(2)}, u32[]{:S(2)}) collective-permute-start(bf16[1,3,1024,512]{3,2,1,0:T(8,128)(2,1)} %get-tuple-element.389), channel_id=1, source_target_pairs={{0,1},{1,0},{2,3},{3,2},{4,5},{5,4},{6,7},{7,6},{8,9},{9,8},{10,11... | collective-permute-start | bytes 9437192 | tf_op jit(solution)/shard_map/ppermute | solution.py:701
  10.0 11.7 %collective-permute-start = (bf16[1,1,1024,1024]{3,2,1,0:T(8,128)(2,1)}, bf16[1,1,1024,1024]{3,2,1,0:T(8,128)(2,1)}, u32[]{:S(2)}, u32[]{:S(2)}) collective-permute-start(bf16[1,1,1024,1024]{3,2,1,0:T(8,128)(2,1)} %get-tuple-element.399), channel_id=1, source_target_pairs={{0,1},{1,0},{2,3},{3,2},{4,5},{5,4},{6,7},{7,6},{8,9},{9,8},{10,11... | collective-permute-start | bytes 6291464 | tf_op jit(solution)/shard_map/ppermute | solution.py:701
  37.1 6.9 %collective-permute-start.2 = (bf16[528,2048]{1,0:T(8,128)(2,1)}, bf16[528,2048]{1,0:T(8,128)(2,1)S(1)}, u32[]{:S(2)}, u32[]{:S(2)}) collective-permute-start(bf16[528,2048]{1,0:T(8,128)(2,1)} %get-tuple-element.188.km_ref.vm_ref), channel_id=1, source_target_pairs={{0,1},{1,0},{2,3},{3,2},{4,5},{5,4},{6,7},{7,6},{8,9},{9,8},{10,11... | collective-permute-start | bytes 6488072 | tf_op jit(solution)/shard_map/ppermute | solution.py:701
  37.5 35.9 %collective-permute-start.4 = (bf16[2,1024,2048]{2,1,0:T(8,128)(2,1)}, bf16[2,1024,2048]{2,1,0:T(8,128)(2,1)}, u32[]{:S(2)}, u32[]{:S(2)}) collective-permute-start(bf16[2,1024,2048]{2,1,0:T(8,128)(2,1)} %refs_7_.7), channel_id=1, source_target_pairs={{0,1},{1,0},{2,3},{3,2},{4,5},{5,4},{6,7},{7,6},{8,9},{9,8},{10,11... | collective-permute-start | bytes 25165832 | tf_op jit(solution)/shard_map/ppermute | solution.py:701
  44.0 29.4 %collective-permute-start.5 = (bf16[2,1024,2048]{2,1,0:T(8,128)(2,1)}, bf16[2,1024,2048]{2,1,0:T(8,128)(2,1)}, u32[]{:S(2)}, u32[]{:S(2)}) collective-permute-start(bf16[2,1024,2048]{2,1,0:T(8,128)(2,1)} %refs_8_.3), channel_id=1, source_target_pairs={{0,1},{1,0},{2,3},{3,2},{4,5},{5,4},{6,7},{7,6},{8,9},{9,8},{10,11... | collective-permute-start | bytes 25165832 | tf_op jit(solution)/shard_map/ppermute | solution.py:701
  44.4 60.2 %collective-permute-start.8 = (bf16[1,3,1024,512]{3,2,1,0:T(8,128)(2,1)}, bf16[1,3,1024,512]{3,2,1,0:T(8,128)(2,1)}, u32[]{:S(2)}, u32[]{:S(2)}) collective-permute-start(bf16[1,3,1024,512]{3,2,1,0:T(8,128)(2,1)} %get-tuple-element.195), channel_id=1, source_target_pairs={{0,1},{1,0},{2,3},{3,2},{4,5},{5,4},{6,7},{7,6},{8,9},{9,8},{10,11... | collective-permute-start | bytes 9437192 | tf_op jit(solution)/shard_map/ppermute | solution.py:701
  44.5 28.9 %collective-permute-start.3 = (bf16[2,1024,512]{2,1,0:T(8,128)(2,1)}, bf16[2,1024,512]{2,1,0:T(8,128)(2,1)}, u32[]{:S(2)}, u32[]{:S(2)}) collective-permute-start(bf16[2,1024,512]{2,1,0:T(8,128)(2,1)} %refs_4_.5), channel_id=1, source_target_pairs={{0,1},{1,0},{2,3},{3,2},{4,5},{5,4},{6,7},{7,6},{8,9},{9,8},{10,11... | collective-permute-start | bytes 6291464 | tf_op jit(solution)/shard_map/ppermute | solution.py:701
  44.9 8.5 %collective-permute-start.6 = (bf16[2,2048]{1,0:T(2,128)(2,1)S(1)}, bf16[2,2048]{1,0:T(2,128)(2,1)S(1)}, u32[]{:S(2)}, u32[]{:S(2)}) collective-permute-start(bf16[2,2048]{1,0:T(2,128)(2,1)S(1)} %copy-done.27), channel_id=1, source_target_pairs={{0,1},{1,0},{2,3},{3,2},{4,5},{5,4},{6,7},{7,6},{8,9},{9,8},{10,11... | collective-permute-start | bytes 24584 | tf_op jit(solution)/shard_map/ppermute | solution.py:701
  53.4 51.1 %collective-permute-start.7 = (bf16[1,1,1024,1024]{3,2,1,0:T(8,128)(2,1)}, bf16[1,1,1024,1024]{3,2,1,0:T(8,128)(2,1)}, u32[]{:S(2)}, u32[]{:S(2)}) collective-permute-start(bf16[1,1,1024,1024]{3,2,1,0:T(8,128)(2,1)} %get-tuple-element.194), channel_id=1, source_target_pairs={{0,1},{1,0},{2,3},{3,2},{4,5},{5,4},{6,7},{7,6},{8,9},{9,8},{10,11... | collective-permute-start | bytes 6291464 | tf_op jit(solution)/shard_map/ppermute | solution.py:701
  118.2 4.5 collective-permute-start.9
  171.9 30.9 %collective-permute-start.11 = (bf16[1024,2048]{1,0:T(8,128)(2,1)}, bf16[1024,2048]{1,0:T(8,128)(2,1)}, u32[]{:S(2)}, u32[]{:S(2)}) collective-permute-start(bf16[1024,2048]{1,0:T(8,128)(2,1)} %get-tuple-element.208), channel_id=1, source_target_pairs={{0,1},{1,0},{2,3},{3,2},{4,5},{5,4},{6,7},{7,6},{8,9},{9,8},{10,11... | collective-permute-start | bytes 12582920 | tf_op jit(solution)/shard_map/ppermute | solution.py:701
  172.1 30.7 %collective-permute-start.12 = (bf16[1024,2048]{1,0:T(8,128)(2,1)}, bf16[1024,2048]{1,0:T(8,128)(2,1)}, u32[]{:S(2)}, u32[]{:S(2)}) collective-permute-start(bf16[1024,2048]{1,0:T(8,128)(2,1)} %get-tuple-element.209), channel_id=1, source_target_pairs={{0,1},{1,0},{2,3},{3,2},{4,5},{5,4},{6,7},{7,6},{8,9},{9,8},{10,11... | collective-permute-start | bytes 12582920 | tf_op jit(solution)/shard_map/ppermute | solution.py:701
  210.8 60.1 %collective-permute-start.15 = (bf16[2,512,2048]{2,1,0:T(8,128)(2,1)}, bf16[2,512,2048]{2,1,0:T(8,128)(2,1)}, u32[]{:S(2)}, u32[]{:S(2)}) collective-permute-start(bf16[2,512,2048]{2,1,0:T(8,128)(2,1)} %add_convert_fusion.1), channel_id=1, source_target_pairs={{0,2},{1,5},{2,0},{3,7},{4,6},{5,1},{6,4},{7,3},{8,10},{9,13},{10,... | collective-permute-start | bytes 12582920 | tf_op jit(solution)/shard_map/ppermute | solution.py:711
  236.7 3.0 collective-permute-start.13
  236.9 4.4 collective-permute-start.14
  270.3 34.3 %collective-permute-start.16 = (bf16[1024,1536]{1,0:T(8,128)(2,1)}, bf16[1024,1536]{1,0:T(8,128)(2,1)S(1)}, u32[]{:S(2)}, u32[]{:S(2)}) collective-permute-start(bf16[1024,1536]{1,0:T(8,128)(2,1)} %get-tuple-element.235), channel_id=1, source_target_pairs={{0,1},{1,0},{2,3},{3,2},{4,5},{5,4},{6,7},{7,6},{8,9},{9,8},{10,11... | collective-permute-start | bytes 9437192 | tf_op jit(solution)/shard_map/ppermute | solution.py:701
  270.5 34.3 %collective-permute-start.17 = (bf16[1024,1536]{1,0:T(8,128)(2,1)}, bf16[1024,1536]{1,0:T(8,128)(2,1)}, u32[]{:S(2)}, u32[]{:S(2)}) collective-permute-start(bf16[1024,1536]{1,0:T(8,128)(2,1)} %get-tuple-element.236), channel_id=1, source_target_pairs={{0,1},{1,0},{2,3},{3,2},{4,5},{5,4},{6,7},{7,6},{8,9},{9,8},{10,11... | collective-permute-start | bytes 9437192 | tf_op jit(solution)/shard_map/ppermute | solution.py:701
  278.4 28.9 %collective-permute-start.18 = (bf16[2,256,2048]{2,1,0:T(8,128)(2,1)}, bf16[2,256,2048]{2,1,0:T(8,128)(2,1)}, u32[]{:S(2)}, u32[]{:S(2)}) collective-permute-start(bf16[2,256,2048]{2,1,0:T(8,128)(2,1)} %add_convert_fusion.5), channel_id=1, source_target_pairs={{0,4},{1,3},{2,6},{3,1},{4,0},{5,7},{6,2},{7,5},{8,12},{9,11},{10,... | collective-permute-start | bytes 6291464 | tf_op jit(solution)/shard_map/ppermute | solution.py:711
  279.9 3.0 collective-permute-start.10
  303.2 45.3 %collective-permute-start.19 = (bf16[1024,2048]{1,0:T(8,128)(2,1)}, bf16[1024,2048]{1,0:T(8,128)(2,1)}, u32[]{:S(2)}, u32[]{:S(2)}) collective-permute-start(bf16[1024,2048]{1,0:T(8,128)(2,1)} %get-tuple-element.251), channel_id=1, source_target_pairs={{0,1},{1,0},{2,3},{3,2},{4,5},{5,4},{6,7},{7,6},{8,9},{9,8},{10,11... | collective-permute-start | bytes 12582920 | tf_op jit(solution)/shard_map/ppermute | solution.py:701
  303.4 45.1 %collective-permute-start.20 = (bf16[1024,2048]{1,0:T(8,128)(2,1)}, bf16[1024,2048]{1,0:T(8,128)(2,1)}, u32[]{:S(2)}, u32[]{:S(2)}) collective-permute-start(bf16[1024,2048]{1,0:T(8,128)(2,1)} %get-tuple-element.252), channel_id=1, source_target_pairs={{0,1},{1,0},{2,3},{3,2},{4,5},{5,4},{6,7},{7,6},{8,9},{9,8},{10,11... | collective-permute-start | bytes 12582920 | tf_op jit(solution)/shard_map/ppermute | solution.py:701
  304.6 156.9 %collective-permute-start.27 = (bf16[528,1024]{1,0:T(8,128)(2,1)}, bf16[528,1024]{1,0:T(8,128)(2,1)}, u32[]{:S(2)}, u32[]{:S(2)}) collective-permute-start(bf16[528,1024]{1,0:T(8,128)(2,1)} %get-tuple-element.281.refs_2_), channel_id=1, source_target_pairs={{0,1},{1,0},{2,3},{3,2},{4,5},{5,4},{6,7},{7,6},{8,9},{9,8},{10,11... | collective-permute-start | bytes 3244040 | tf_op jit(solution)/shard_map/ppermute | solution.py:701
  312.1 29.4 %collective-permute-start.21 = (bf16[2,128,2048]{2,1,0:T(8,128)(2,1)S(1)}, bf16[2,128,2048]{2,1,0:T(8,128)(2,1)}, u32[]{:S(2)}, u32[]{:S(2)}) collective-permute-start(bf16[2,128,2048]{2,1,0:T(8,128)(2,1)S(1)} %add_convert_fusion.9), channel_id=1, source_target_pairs={{0,8},{1,9},{2,10},{3,11},{4,12},{5,13},{6,14},{7,15},{8,0},{9,1},... | collective-permute-start | bytes 3145736 | tf_op jit(solution)/shard_map/ppermute | solution.py:711
  317.3 64.9 %collective-permute-start.22 = (bf16[512,3072]{1,0:T(8,128)(2,1)}, bf16[512,3072]{1,0:T(8,128)(2,1)}, u32[]{:S(2)}, u32[]{:S(2)}) collective-permute-start(bf16[512,3072]{1,0:T(8,128)(2,1)} %add_convert_fusion.3), channel_id=1, source_target_pairs={{0,2},{1,5},{2,0},{3,7},{4,6},{5,1},{6,4},{7,3},{8,10},{9,13},{10,... | collective-permute-start | bytes 9437192 | tf_op jit(solution)/shard_map/ppermute | solution.py:711
  345.8 33.9 %collective-permute-start.46 = (bf16[2,64,2048]{2,1,0:T(8,128)(2,1)S(1)}, bf16[2,64,2048]{2,1,0:T(8,128)(2,1)S(1)}, u32[]{:S(2)}, u32[]{:S(2)}) collective-permute-start(bf16[2,64,2048]{2,1,0:T(8,128)(2,1)S(1)} %add_convert_fusion.13), channel_id=1, source_target_pairs={{0,16},{1,17},{2,18},{3,19},{4,20},{5,21},{6,22},{7,23},{8,24},{9,... | collective-permute-start | bytes 1572872 | tf_op jit(solution)/shard_map/ppermute | solution.py:711
  354.9 68.2 %collective-permute-start.30 = (bf16[2,512,2048]{2,1,0:T(8,128)(2,1)}, bf16[2,512,2048]{2,1,0:T(8,128)(2,1)}, u32[]{:S(2)}, u32[]{:S(2)}) collective-permute-start(bf16[2,512,2048]{2,1,0:T(8,128)(2,1)} %add_convert_fusion), channel_id=1, source_target_pairs={{0,2},{1,5},{2,0},{3,7},{4,6},{5,1},{6,4},{7,3},{8,10},{9,13},{10,... | collective-permute-start | bytes 12582920 | tf_op jit(solution)/shard_map/ppermute | solution.py:711
  379.6 8.7 %collective-permute-start.23 = (bf16[528,1024]{1,0:T(8,128)(2,1)}, bf16[528,1024]{1,0:T(8,128)(2,1)}, u32[]{:S(2)}, u32[]{:S(2)}) collective-permute-start(bf16[528,1024]{1,0:T(8,128)(2,1)} %get-tuple-element.274), channel_id=1, source_target_pairs={{0,1},{1,0},{2,3},{3,2},{4,5},{5,4},{6,7},{7,6},{8,9},{9,8},{10,11... | collective-permute-start | bytes 3244040 | tf_op jit(solution)/shard_map/ppermute | solution.py:701
  379.6 8.6 %collective-permute-start.24 = (bf16[528,1024]{1,0:T(8,128)(2,1)}, bf16[528,1024]{1,0:T(8,128)(2,1)}, u32[]{:S(2)}, u32[]{:S(2)}) collective-permute-start(bf16[528,1024]{1,0:T(8,128)(2,1)} %get-tuple-element.276), channel_id=1, source_target_pairs={{0,1},{1,0},{2,3},{3,2},{4,5},{5,4},{6,7},{7,6},{8,9},{9,8},{10,11... | collective-permute-start | bytes 3244040 | tf_op jit(solution)/shard_map/ppermute | solution.py:701
  387.2 31.8 %collective-permute-start.31 = (bf16[256,3072]{1,0:T(8,128)(2,1)}, bf16[256,3072]{1,0:T(8,128)(2,1)S(1)}, u32[]{:S(2)}, u32[]{:S(2)}) collective-permute-start(bf16[256,3072]{1,0:T(8,128)(2,1)} %add_convert_fusion.7), channel_id=1, source_target_pairs={{0,4},{1,3},{2,6},{3,1},{4,0},{5,7},{6,2},{7,5},{8,12},{9,11},{10,... | collective-permute-start | bytes 4718600 | tf_op jit(solution)/shard_map/ppermute | solution.py:711
  417.1 14.1 %collective-permute-start.28 = (bf16[1024,1536]{1,0:T(8,128)(2,1)}, bf16[1024,1536]{1,0:T(8,128)(2,1)S(1)}, u32[]{:S(2)}, u32[]{:S(2)}) collective-permute-start(bf16[1024,1536]{1,0:T(8,128)(2,1)} %get-tuple-element.283), channel_id=1, source_target_pairs={{0,1},{1,0},{2,3},{3,2},{4,5},{5,4},{6,7},{7,6},{8,9},{9,8},{10,11... | collective-permute-start | bytes 9437192 | tf_op jit(solution)/shard_map/ppermute | solution.py:701
  417.2 14.4 %collective-permute-start.29 = (bf16[1024,1536]{1,0:T(8,128)(2,1)}, bf16[1024,1536]{1,0:T(8,128)(2,1)S(1)}, u32[]{:S(2)}, u32[]{:S(2)}) collective-permute-start(bf16[1024,1536]{1,0:T(8,128)(2,1)} %get-tuple-element.284), channel_id=1, source_target_pairs={{0,1},{1,0},{2,3},{3,2},{4,5},{5,4},{6,7},{7,6},{8,9},{9,8},{10,11... | collective-permute-start | bytes 9437192 | tf_op jit(solution)/shard_map/ppermute | solution.py:701
  419.1 35.3 %copy-start.16 = (bf16[256,3072]{1,0:T(8,128)(2,1)}, bf16[256,3072]{1,0:T(8,128)(2,1)S(1)}, u32[]{:S(2)}) copy-start(bf16[256,3072]{1,0:T(8,128)(2,1)S(1)} %collective-permute-done.31) | copy-start | bytes 4718596
  419.1 17.2 %collective-permute-start.33 = (f32[16,18,64]{2,1,0:T(8,128)S(1)}, f32[16,18,64]{2,1,0:T(8,128)S(1)}, u32[]{:S(2)}, u32[]{:S(2)}) collective-permute-start(f32[16,18,64]{2,1,0:T(8,128)S(1)} %bitcast.111), channel_id=1, source_target_pairs={{0,1},{1,0},{2,3},{3,2},{4,5},{5,4},{6,7},{7,6},{8,9},{9,8},{10,11... | collective-permute-start | bytes 221192 | tf_op jit(solution)/shard_map/ppermute | solution.py:701
  423.1 38.4 %collective-permute-start.26 = (bf16[528,1024]{1,0:T(8,128)(2,1)}, bf16[528,1024]{1,0:T(8,128)(2,1)}, u32[]{:S(2)}, u32[]{:S(2)}) collective-permute-start(bf16[528,1024]{1,0:T(8,128)(2,1)} %get-tuple-element.280.refs_0_), channel_id=1, source_target_pairs={{0,1},{1,0},{2,3},{3,2},{4,5},{5,4},{6,7},{7,6},{8,9},{9,8},{10,11... | collective-permute-start | bytes 3244040 | tf_op jit(solution)/shard_map/ppermute | solution.py:701
  431.3 25.3 %collective-permute-start.25 = (bf16[528,1024]{1,0:T(8,128)(2,1)S(1)}, bf16[528,1024]{1,0:T(8,128)(2,1)S(1)}, u32[]{:S(2)}, u32[]{:S(2)}) collective-permute-start(bf16[528,1024]{1,0:T(8,128)(2,1)S(1)} %convert_element_type.319.refs_0_), channel_id=1, source_target_pairs={{0,1},{1,0},{2,3},{3,2},{4,5},{5,4},{6,7},{7,6},{8,9},{9,8},{10,11... | collective-permute-start | bytes 3244040 | tf_op jit(solution)/shard_map/ppermute | solution.py:701
  431.6 19.7 %collective-permute-start.35 = (bf16[128,3072]{1,0:T(8,128)(2,1)S(1)}, bf16[128,3072]{1,0:T(8,128)(2,1)S(1)}, u32[]{:S(2)}, u32[]{:S(2)}) collective-permute-start(bf16[128,3072]{1,0:T(8,128)(2,1)S(1)} %add_convert_fusion.11), channel_id=1, source_target_pairs={{0,8},{1,9},{2,10},{3,11},{4,12},{5,13},{6,14},{7,15},{8,0},{9,1},... | collective-permute-start | bytes 2359304 | tf_op jit(solution)/shard_map/ppermute | solution.py:711
  436.3 43.2 %collective-permute-start.34 = (bf16[2,256,2048]{2,1,0:T(8,128)(2,1)}, bf16[2,256,2048]{2,1,0:T(8,128)(2,1)}, u32[]{:S(2)}, u32[]{:S(2)}) collective-permute-start(bf16[2,256,2048]{2,1,0:T(8,128)(2,1)} %add_convert_fusion.4), channel_id=1, source_target_pairs={{0,4},{1,3},{2,6},{3,1},{4,0},{5,7},{6,2},{7,5},{8,12},{9,11},{10,... | collective-permute-start | bytes 6291464 | tf_op jit(solution)/shard_map/ppermute | solution.py:711
  451.3 17.9 %collective-permute-start.36 = (f32[8,18,64]{2,1,0:T(8,128)}, f32[8,18,64]{2,1,0:T(8,128)}, u32[]{:S(2)}, u32[]{:S(2)}) collective-permute-start(f32[8,18,64]{2,1,0:T(8,128)} %slice_add_fusion), channel_id=1, source_target_pairs={{0,2},{1,3},{2,0},{3,1},{4,6},{5,7},{6,4},{7,5},{8,10},{9,11},{10,... | collective-permute-start | bytes 110600 | tf_op jit(solution)/shard_map/ppermute | solution.py:711
  457.5 19.7 %collective-permute-start.40 = (bf16[64,3072]{1,0:T(8,128)(2,1)}, bf16[64,3072]{1,0:T(8,128)(2,1)S(1)}, u32[]{:S(2)}, u32[]{:S(2)}) collective-permute-start(bf16[64,3072]{1,0:T(8,128)(2,1)} %add_convert_fusion.15), channel_id=1, source_target_pairs={{0,16},{1,17},{2,18},{3,19},{4,20},{5,21},{6,22},{7,23},{8,24},{9,... | collective-permute-start | bytes 1179656 | tf_op jit(solution)/shard_map/ppermute | solution.py:711
  468.5 37.6 %collective-permute-start.32 = (bf16[512,3072]{1,0:T(8,128)(2,1)}, bf16[512,3072]{1,0:T(8,128)(2,1)}, u32[]{:S(2)}, u32[]{:S(2)}) collective-permute-start(bf16[512,3072]{1,0:T(8,128)(2,1)} %add_convert_fusion.2), channel_id=1, source_target_pairs={{0,2},{1,5},{2,0},{3,7},{4,6},{5,1},{6,4},{7,3},{8,10},{9,13},{10,... | collective-permute-start | bytes 9437192 | tf_op jit(solution)/shard_map/ppermute | solution.py:711
  470.7 15.5 %collective-permute-start.41 = (f32[4,18,64]{2,1,0:T(8,128)}, f32[4,18,64]{2,1,0:T(8,128)}, u32[]{:S(2)}, u32[]{:S(2)}) collective-permute-start(f32[4,18,64]{2,1,0:T(8,128)} %slice_add_fusion.1), channel_id=1, source_target_pairs={{0,4},{1,5},{2,6},{3,7},{4,0},{5,1},{6,2},{7,3},{8,12},{9,13},{10,... | collective-permute-start | bytes 55304 | tf_op jit(solution)/shard_map/ppermute | solution.py:711
  485.2 25.7 %collective-permute-start.44 = (bf16[2,128,2048]{2,1,0:T(8,128)(2,1)}, bf16[2,128,2048]{2,1,0:T(8,128)(2,1)}, u32[]{:S(2)}, u32[]{:S(2)}) collective-permute-start(bf16[2,128,2048]{2,1,0:T(8,128)(2,1)} %add_convert_fusion.8), channel_id=1, source_target_pairs={{0,8},{1,9},{2,10},{3,11},{4,12},{5,13},{6,14},{7,15},{8,0},{9,1},... | collective-permute-start | bytes 3145736 | tf_op jit(solution)/shard_map/ppermute | solution.py:711
  487.2 24.8 %collective-permute-start.42 = (f32[2,18,64]{2,1,0:T(8,128)S(1)}, f32[2,18,64]{2,1,0:T(8,128)S(1)}, u32[]{:S(2)}, u32[]{:S(2)}) collective-permute-start(f32[2,18,64]{2,1,0:T(8,128)S(1)} %slice_add_fusion.2), channel_id=1, source_target_pairs={{0,8},{1,9},{2,10},{3,11},{4,12},{5,13},{6,14},{7,15},{8,0},{9,1},... | collective-permute-start | bytes 27656 | tf_op jit(solution)/shard_map/ppermute | solution.py:711
  509.9 20.7 %collective-permute-start.37 = (bf16[256,3072]{1,0:T(8,128)(2,1)}, bf16[256,3072]{1,0:T(8,128)(2,1)}, u32[]{:S(2)}, u32[]{:S(2)}) collective-permute-start(bf16[256,3072]{1,0:T(8,128)(2,1)} %add_convert_fusion.6), channel_id=1, source_target_pairs={{0,4},{1,3},{2,6},{3,1},{4,0},{5,7},{6,2},{7,5},{8,12},{9,11},{10,... | collective-permute-start | bytes 4718600 | tf_op jit(solution)/shard_map/ppermute | solution.py:711
  512.7 6.9 %collective-permute-start.43 = (f32[1,18,64]{2,1,0:T(8,128)S(1)}, f32[1,18,64]{2,1,0:T(8,128)S(1)}, u32[]{:S(2)}, u32[]{:S(2)}) collective-permute-start(f32[1,18,64]{2,1,0:T(8,128)S(1)} %slice_add_fusion.3), channel_id=1, source_target_pairs={{0,16},{1,17},{2,18},{3,19},{4,20},{5,21},{6,22},{7,23},{8,24},{9,... | collective-permute-start | bytes 13832 | tf_op jit(solution)/shard_map/ppermute | solution.py:711
  518.8 25.7 %collective-permute-start.45 = (bf16[2,64,2048]{2,1,0:T(8,128)(2,1)}, bf16[2,64,2048]{2,1,0:T(8,128)(2,1)}, u32[]{:S(2)}, u32[]{:S(2)}) collective-permute-start(bf16[2,64,2048]{2,1,0:T(8,128)(2,1)} %add_convert_fusion.12), channel_id=1, source_target_pairs={{0,16},{1,17},{2,18},{3,19},{4,20},{5,21},{6,22},{7,23},{8,24},{9,... | collective-permute-start | bytes 1572872 | tf_op jit(solution)/shard_map/ppermute | solution.py:711
  532.6 28.5 %collective-permute-start.38 = (bf16[128,3072]{1,0:T(8,128)(2,1)S(1)}, bf16[128,3072]{1,0:T(8,128)(2,1)S(1)}, u32[]{:S(2)}, u32[]{:S(2)}) collective-permute-start(bf16[128,3072]{1,0:T(8,128)(2,1)S(1)} %add_convert_fusion.10), channel_id=1, source_target_pairs={{0,8},{1,9},{2,10},{3,11},{4,12},{5,13},{6,14},{7,15},{8,0},{9,1},... | collective-permute-start | bytes 2359304 | tf_op jit(solution)/shard_map/ppermute | solution.py:711
  562.7 19.6 %collective-permute-start.39 = (bf16[64,3072]{1,0:T(8,128)(2,1)S(1)}, bf16[64,3072]{1,0:T(8,128)(2,1)S(1)}, u32[]{:S(2)}, u32[]{:S(2)}) collective-permute-start(bf16[64,3072]{1,0:T(8,128)(2,1)S(1)} %add_convert_fusion.14), channel_id=1, source_target_pairs={{0,16},{1,17},{2,18},{3,19},{4,20},{5,21},{6,22},{7,23},{8,24},{9,... | collective-permute-start | bytes 1179656 | tf_op jit(solution)/shard_map/ppermute | solution.py:711
  (41 other events, 410.4 us)

commit v3 on v2

v3 whole, which is shorter than its diff:
```python
import functools
import math
import types

import jax
import jax.numpy as jnp
from jax import lax
from jax.experimental import pallas as pl
from jax.experimental.pallas import tpu as pltpu
from jax.sharding import PartitionSpec as P

F32 = jnp.float32
BF16 = jnp.bfloat16
HD = 64
MAIN = 512
PAD = 528
GROUP = 256
HEADS_IN_GROUP = GROUP // HD
MIB = 1024 * 1024
SCALE = 0.5


def cost(microseconds):
    return pl.CostEstimate(flops=1, bytes_accessed=int(microseconds * SCALE * 3.5e6), transcendentals=0)


def _dot(a, b, dims):
    return lax.dot_general(a, b, (dims, ((), ())), preferred_element_type=F32)


def _extra_rows(mine_ref, other_ref):
    row = lax.broadcasted_iota(jnp.int32, (16, GROUP), 0)
    lane = lax.broadcasted_iota(jnp.int32, (16, GROUP), 1)
    mine = jnp.broadcast_to(mine_ref[MAIN : MAIN + 16, :][0:1].astype(F32), (16, GROUP))
    other = jnp.broadcast_to(other_ref[MAIN : MAIN + 16, :][0:1].astype(F32), (16, GROUP))
    value = jnp.where(row % 2 == 0, mine, other)
    return jnp.where(row // 2 == lane // HD, value, 0.0).astype(BF16)


def _attn_fwd_kernel(q_ref, km_ref, vm_ref, ko_ref, vo_ref, o_ref, of_ref, e_ref, ex_ref, il_ref, k_s, v_s):
    k_s[:MAIN] = km_ref[:MAIN]
    k_s[MAIN:] = ko_ref[:MAIN]
    v_s[:MAIN] = vm_ref[:MAIN]
    v_s[MAIN:] = vo_ref[:MAIN]
    lane = lax.broadcasted_iota(jnp.int32, (PAD, GROUP), 1) // HD
    slot = lax.broadcasted_iota(jnp.int32, (PAD, 16), 1) // 2
    q = q_ref[...] * jnp.asarray(HD**-0.5, BF16)
    kx = _extra_rows(km_ref, ko_ref)
    vx = _extra_rows(vm_ref, vo_ref)
    sx = _dot(q, kx, ((1,), (1,)))
    out = jnp.zeros((PAD, GROUP), F32)
    ex_all = jnp.zeros((PAD, 16), F32)
    il_all = jnp.zeros((PAD, 16), F32)
    for h in range(HEADS_IN_GROUP):
        qh = jnp.where(lane == h, q, jnp.zeros_like(q))
        s = _dot(qh, k_s[...], ((1,), (1,)))
        sxh = jnp.where(slot == h, sx, -jnp.inf)
        top = jnp.maximum(jnp.max(s, axis=1, keepdims=True), jnp.max(sxh, axis=1, keepdims=True))
        e = jnp.exp(s - top)
        exh = jnp.exp(sxh - top)
        total = jnp.sum(e, axis=1, keepdims=True) + jnp.sum(exh, axis=1, keepdims=True)
        inverse = 1.0 / total
        low = e.astype(BF16)
        e_ref[h] = low
        out = out + jnp.where(lane == h, _dot(low, v_s[...], ((1,), (0,))) * inverse, 0.0)
        ex_all = ex_all + exh
        il_all = il_all + jnp.where(slot == h, inverse, 0.0)
    out = out + _dot((ex_all * il_all).astype(BF16), vx, ((1,), (0,)))
    o_ref[...] = out.astype(BF16)
    of_ref[...] = out
    ex_ref[0] = ex_all
    il_ref[0] = il_all


def _far(value):
    return pltpu.with_memory_space_constraint(value, pltpu.HBM)


def attn_forward(q, kv, kv_other):
    width = q.shape[1]
    groups = width // GROUP

    def near(offset):
        return pl.BlockSpec((PAD, GROUP), lambda g: (0, g + offset))

    def far(offset):
        return pl.BlockSpec((PAD, GROUP), lambda g: (0, (g + groups // 2) % groups + offset))

    heads = width // HD
    kv, kv_other = _far(kv), _far(kv_other)
    return pl.pallas_call(
        _attn_fwd_kernel,
        grid=(groups,),
        in_specs=[near(0), near(0), near(groups), far(0), far(groups)],
        out_specs=[
            near(0),
            near(0),
            pl.BlockSpec((HEADS_IN_GROUP, PAD, 2 * MAIN), lambda g: (g, 0, 0)),
            pl.BlockSpec((1, PAD, 16), lambda g: (g, 0, 0)),
            pl.BlockSpec((1, PAD, 16), lambda g: (g, 0, 0)),
        ],
        out_shape=[
            pltpu.HBM((PAD, width), BF16),
            pltpu.HBM((PAD, width), F32),
            pltpu.HBM((heads, PAD, 2 * MAIN), BF16),
            pltpu.HBM((groups, PAD, 16), F32),
            pltpu.HBM((groups, PAD, 16), F32),
        ],
        scratch_shapes=[pltpu.VMEM((2 * MAIN, GROUP), BF16), pltpu.VMEM((2 * MAIN, GROUP), BF16)],
        compiler_params=pltpu.CompilerParams(vmem_limit_bytes=24 * MIB),
        cost_estimate=cost(19),
        name="attn_forward",
    )(q, kv, kv, kv_other, kv_other)


def _attn_bwd_kernel(
    q_ref, km_ref, vm_ref, ko_ref, vo_ref, do_ref, o_ref, e_ref, ex_ref, il_ref,
    dq_ref, dkm_ref, dko_ref, dvm_ref, dvo_ref, k_s, v_s, dk_s, dv_s,
):
    k_s[:MAIN] = km_ref[:MAIN]
    k_s[MAIN:] = ko_ref[:MAIN]
    v_s[:MAIN] = vm_ref[:MAIN]
    v_s[MAIN:] = vo_ref[:MAIN]
    scale = HD**-0.5
    lane = lax.broadcasted_iota(jnp.int32, (PAD, GROUP), 1) // HD
    slot = lax.broadcasted_iota(jnp.int32, (PAD, 16), 1) // 2
    q = q_ref[...] * jnp.asarray(scale, BF16)
    kx = _extra_rows(km_ref, ko_ref)
    vx = _extra_rows(vm_ref, vo_ref)
    il = il_ref[0]
    do = do_ref[...].astype(F32)
    spread = jnp.zeros((PAD, GROUP), F32)
    for h in range(HEADS_IN_GROUP):
        spread = jnp.where(lane == h, il[:, 2 * h : 2 * h + 1], spread)
    dos = (do * spread).astype(BF16)
    product = dos.astype(F32) * o_ref[...]
    inner = jnp.zeros((PAD, 16), F32)
    inners = []
    for h in range(HEADS_IN_GROUP):
        one = jnp.sum(jnp.where(lane == h, product, 0.0), axis=1, keepdims=True)
        inners.append(one)
        inner = jnp.where(slot == h, one, inner)
    dos_t = dos.T
    q_t = q.T
    dq = jnp.zeros((PAD, GROUP), F32)
    for h in range(HEADS_IN_GROUP):
        rows = slice(h * HD, (h + 1) * HD)
        dosh = jnp.where(lane == h, dos, jnp.zeros_like(dos))
        e = e_ref[h]
        dp = _dot(dosh, v_s[...], ((1,), (1,)))
        ds = (e.astype(F32) * (dp - inners[h])).astype(BF16)
        dq = dq + jnp.where(lane == h, _dot(ds, k_s[...], ((1,), (0,))), 0.0)
        dk_s[rows, :] = (
            _dot(q_t[rows, :MAIN], ds[:MAIN], ((1,), (0,)))
            + q_t[rows, MAIN : MAIN + 1].astype(F32) * ds[MAIN : MAIN + 16].astype(F32)[0:1]
        )
        dv_s[rows, :] = (
            _dot(dos_t[rows, :MAIN], e[:MAIN], ((1,), (0,)))
            + dos_t[rows, MAIN : MAIN + 1].astype(F32) * e[MAIN : MAIN + 16].astype(F32)[0:1]
        )
    ex = ex_ref[0]
    dsx = (ex * (_dot(dos, vx, ((1,), (1,))) - inner)).astype(BF16)
    dq = dq + _dot(dsx, kx, ((1,), (0,)))
    dq_ref[...] = (dq * scale).astype(BF16)
    dkx = _dot(dsx, q, ((0,), (0,)))
    dvx = _dot(ex.astype(BF16), dos, ((0,), (0,)))
    row = lax.broadcasted_iota(jnp.int32, (16, GROUP), 0)
    own = row // 2 == lax.broadcasted_iota(jnp.int32, (16, GROUP), 1) // HD
    for half, (dk_ref, dv_ref) in enumerate(((dkm_ref, dvm_ref), (dko_ref, dvo_ref))):
        keep = jnp.logical_and(own, row % 2 == half)
        for ref, grad_s, tail in ((dk_ref, dk_s, dkx), (dv_ref, dv_s, dvx)):
            ref[:MAIN] = grad_s[:, half * MAIN : (half + 1) * MAIN].T.astype(BF16)
            last = jnp.sum(jnp.where(keep, tail, 0.0), axis=0, keepdims=True)
            ref[MAIN:] = jnp.where(row == 0, jnp.broadcast_to(last, (16, GROUP)), 0.0).astype(BF16)


def attn_backward(q, kv, kv_other, dout, out, e, ex, il):
    width = q.shape[1]
    groups = width // GROUP

    def near(offset):
        return pl.BlockSpec((PAD, GROUP), lambda g: (0, g + offset))

    def far(offset):
        return pl.BlockSpec((PAD, GROUP), lambda g: (0, (g + groups // 2) % groups + offset))

    small = pl.BlockSpec((1, PAD, 16), lambda g: (g, 0, 0))
    heads = width // HD
    block = jax.ShapeDtypeStruct((PAD, width), BF16)
    far_out = pl.BlockSpec((PAD, GROUP), lambda g: (0, (g + groups // 2) % groups))
    q, kv, kv_other, out, e, ex, il = (_far(value) for value in (q, kv, kv_other, out, e, ex, il))
    return pl.pallas_call(
        _attn_bwd_kernel,
        grid=(groups,),
        in_specs=[
            near(0), near(0), near(groups), far(0), far(groups), near(0), near(0),
            pl.BlockSpec((HEADS_IN_GROUP, PAD, 2 * MAIN), lambda g: (g, 0, 0)), small, small,
        ],
        out_specs=[near(0), near(0), far_out, near(0), far_out],
        out_shape=[block] * 5,
        scratch_shapes=[
            pltpu.VMEM((2 * MAIN, GROUP), BF16),
            pltpu.VMEM((2 * MAIN, GROUP), BF16),
            pltpu.VMEM((GROUP, 2 * MAIN), F32),
            pltpu.VMEM((GROUP, 2 * MAIN), F32),
        ],
        compiler_params=pltpu.CompilerParams(vmem_limit_bytes=23 * MIB),
        cost_estimate=cost(23),
        name="attn_backward",
    )(q, kv, kv, kv_other, kv_other, dout, out, e, ex, il)


EPSILON = 1e-05
TILE = 512
SUB = 256


def _row(ref, layer):
    return ref[layer : layer + 1, :].astype(F32)


def _fill_turned(coords_ref, order, pieces, x_ref, xt_s, column_s, theirs=False):
    features = xt_s.shape[0]
    rows = features // pieces
    span = max(rows, 128)
    me = coords_ref[0]
    for start in range(0, features, span):
        turned = x_ref[:MAIN, start : start + span].T
        last = x_ref[MAIN:, start : start + span].T.astype(F32)[:, 0:1]
        for part in range(span // rows):
            relative = jnp.bitwise_xor(me, start // rows + part)
            place = jnp.int32(0)
            for bit in order:
                shift = jnp.bitwise_xor(coords_ref[1], bit ^ int(theirs)) if bit < 2 else bit
                place = place * 2 + (jnp.right_shift(relative, shift) & 1)
            at = pl.ds(pl.multiple_of(place * rows, rows), rows)
            xt_s[at, :] = turned[part * rows : (part + 1) * rows]
            column_s[at, :] = jnp.broadcast_to(last[part * rows : (part + 1) * rows], (rows, 128))


def _outer(xt_s, column_s, dy, out_ref):
    width = dy.shape[1]
    last_row = dy[MAIN:].astype(F32)[0:1]
    step = xt_s.shape[0] // 2
    for start in range(0, xt_s.shape[0], step):
        at = slice(start, start + step)
        column = jnp.concatenate([column_s[at, :]] * (width // 128), axis=1)
        total = _dot(xt_s[at, :], dy[:MAIN], ((1,), (0,))) + column * last_row
        out_ref[at, :] = total.astype(BF16)


def _moments(values):
    average = jnp.mean(values, axis=-1, keepdims=True)
    centred = values - average
    inverse = lax.rsqrt(jnp.mean(centred * centred, axis=-1, keepdims=True) + EPSILON)
    return centred * inverse, inverse


def _norm_back(normed, inverse, gain, grad):
    scaled = grad * gain
    first = jnp.mean(scaled, axis=-1, keepdims=True)
    second = jnp.mean(scaled * normed, axis=-1, keepdims=True)
    return (scaled - first - normed * second) * inverse


def _gelu_parts(up):
    square = up * up
    bell = jnp.exp(-0.5 * square)
    size = jnp.abs(up)
    t = 1.0 / (1.0 + (0.375 * 0.5**0.5) * size)
    terms = (
        0.21133947372436523, 0.21568892896175385, 0.16666550934314728, 0.2830598056316376,
        -0.1295955926179886, 0.3879369795322418, -0.1350957304239273,
    )
    value = jnp.full_like(t, 0.5 * terms[-1])
    for term in terms[-2::-1]:
        value = value * t + 0.5 * term
    tail = value * t * bell
    cumulative = jnp.where(up < 0.0, tail, 1.0 - tail)
    return up * cumulative, cumulative + up * (bell * 0.3989422804014327)


def _entry_kernel(
    layer, coords_ref, xa_ref, xb_ref, wa_ref, wb_ref, bias_ref, gain_ref, shift_ref, qa_ref, qb_ref,
    hidden_ref, normed_ref, q_ref, kv_ref, normed_s,
):
    step = pl.program_id(0)

    @pl.when(step == 0)
    def _():
        first = coords_ref[1] == 0
        xa, xb = xa_ref[...], xb_ref[...]
        hidden = (
            _dot(jnp.where(first, xa, xb), wa_ref[...], ((1,), (0,)))
            + _dot(jnp.where(first, xb, xa), wb_ref[...], ((1,), (0,)))
            + _row(bias_ref, layer)
        )
        hidden_ref[...] = hidden
        normed, _unused = _moments(hidden)
        low = (normed * _row(gain_ref, layer) + _row(shift_ref, layer)).astype(BF16)
        normed_s[...] = low
        normed_ref[...] = low

    @pl.when(jnp.logical_and(step >= 1, step <= 2))
    def _():
        half = qa_ref.shape[1]
        kv_ref[:, :half] = _dot(normed_s[...], qa_ref[...], ((1,), (0,))).astype(BF16)
        kv_ref[:, half:] = _dot(normed_s[...], qb_ref[...], ((1,), (0,))).astype(BF16)

    @pl.when(step == 3)
    def _():
        half = qa_ref.shape[1]
        q_ref[:, :half] = _dot(normed_s[...], qa_ref[...], ((1,), (0,))).astype(BF16)
        q_ref[:, half:] = _dot(normed_s[...], qb_ref[...], ((1,), (0,))).astype(BF16)


def entry_forward(layer, coords, residual, skip_rows, wa, wb, bias, gain, shift, qa, qb):
    model = residual.shape[1]
    half = qa.shape[3]

    def part(step):
        return jnp.where(step == 3, 0, jnp.maximum(step, 1))

    once = pl.Buffered(1)
    rows = pl.BlockSpec((PAD, model), lambda j, c: (0, 0), pipeline_mode=once)
    square = pl.BlockSpec((None, None, model, model), lambda j, c: (layer, 0, 0, 0), pipeline_mode=once)
    vector = pl.BlockSpec(bias.shape, lambda j, c: (0, 0))
    third = pl.BlockSpec((None, None, model, half), lambda j, c: (layer, part(j), 0, 0))
    return pl.pallas_call(
        functools.partial(_entry_kernel, layer),
        grid_spec=pltpu.PrefetchScalarGridSpec(
            num_scalar_prefetch=1,
            grid=(4,),
            in_specs=[rows, rows, square, square, vector, vector, vector, third, third],
            out_specs=[
                rows,
                rows,
                rows,
                pl.BlockSpec((PAD, 2 * half), lambda j, c: (0, jnp.clip(j - 1, 0, 1))),
            ],
            scratch_shapes=[pltpu.VMEM((PAD, model), BF16)],
        ),
        out_shape=[
            pltpu.HBM((PAD, model), F32),
            pltpu.HBM((PAD, model), BF16),
            pltpu.HBM((PAD, 2 * half), BF16),
            pltpu.HBM((PAD, 4 * half), BF16),
        ],
        compiler_params=pltpu.CompilerParams(vmem_limit_bytes=22 * MIB),
        cost_estimate=cost(14),
        name="entry_forward",
    )(coords, residual, skip_rows, wa, wb, bias, gain, shift, qa, qb)


def _mlp_kernel(names, plan, coords_ref, *refs):
    layer, first, last, forward, backward, sets, pieces, order = plan
    ref = types.SimpleNamespace(**dict(zip(names, refs, strict=True)))
    step = pl.program_id(0)
    steps_per_set = pl.num_programs(0) // len(sets)

    @pl.when(step == 0)
    def _():
        if first and forward:
            half = ref.proj_own.shape[1]
            middle = (
                ref.hidden[...]
                + _dot(ref.attended[:, :half], ref.proj_own[...], ((1,), (1,)))
                + _dot(ref.attended[:, half:], ref.proj_peer[...], ((1,), (1,)))
                + _row(ref.proj_bias, layer)
            )
            ref.middle_out[...] = middle
            normed, _unused = _moments(middle)
            low = (normed * _row(ref.gain, layer) + _row(ref.shift, layer)).astype(BF16)
            ref.normed_out[...] = low
            ref.normed_s[...] = low
            ref.acc_s[...] = middle + _row(ref.down_bias, layer)
        else:
            ref.normed_s[...] = ref.normed[...]
            if forward:
                ref.acc_s[...] = ref.acc[...]
        if backward:
            assert len(sets) == 1
            theirs = sets[0] == "peer"
            ref.grad_s[...] = ref.grad[...].astype(BF16)
            if first:
                ref.dn_s[...] = jnp.zeros_like(ref.dn_s)
            else:
                ref.dn_s[...] = ref.dn[...]
            _fill_turned(coords_ref, order, pieces, ref.grad_s, ref.grad_t, ref.grad_c, theirs)
            _fill_turned(coords_ref, order, pieces, ref.normed_s, ref.normed_t, ref.normed_c, theirs)

    for number, name in enumerate(sets):

        def tile(name=name):
            up_w, down_w = getattr(ref, "up_" + name), getattr(ref, "down_" + name)
            spans = [slice(at, at + SUB) for at in range(0, TILE, SUB)]
            active, slopes = [], []
            if forward:
                bias = _row(getattr(ref, "up_bias_" + name), layer)
                for span in spans:
                    up = _dot(ref.normed_s[...], up_w[:, span], ((1,), (0,))) + bias[:, span]
                    value, slope = _gelu_parts(up)
                    active.append(value.astype(BF16))
                    slopes.append(slope if backward else slope.astype(BF16))
                ref.acc_s[...] += sum(
                    _dot(value, down_w[:, span], ((1,), (1,))) for value, span in zip(active, spans)
                )
                if not backward:
                    for value, slope, span in zip(active, slopes, spans):
                        getattr(ref, "active_" + name)[:, span] = value
                        getattr(ref, "slope_" + name)[:, span] = slope
            else:
                for span in spans:
                    active.append(getattr(ref, "active_" + name)[:, span])
                    slopes.append(getattr(ref, "slope_" + name)[:, span].astype(F32))
            if backward:
                if name == "own":
                    down_out, up_out = ref.grads_own.at[0], ref.grads_own.at[1]
                else:
                    down_out, up_out = ref.down_grad, ref.up_grad
                units = []
                for slope, span in zip(slopes, spans):
                    du = _dot(ref.grad_s[...], down_w[:, span], ((1,), (0,))) * slope
                    getattr(ref, "bias_grad_" + name)[:, span] = jnp.sum(du, axis=0, keepdims=True)
                    units.append(du.astype(BF16))
                ref.dn_s[...] += sum(_dot(du, up_w[:, span], ((1,), (1,))) for du, span in zip(units, spans))
                for value, du, span in zip(active, units, spans):
                    _outer(ref.grad_t, ref.grad_c, value, down_out.at[:, span])
                    _outer(ref.normed_t, ref.normed_c, du, up_out.at[:, span])

        if len(sets) == 1:
            tile()
        else:
            pl.when(step // steps_per_set == number)(tile)

    @pl.when(step == pl.num_programs(0) - 1)
    def _():
        if not last:
            if forward:
                ref.acc_out[...] = ref.acc_s[...]
            if backward:
                ref.dn_out[...] = ref.dn_s[...]
            return
        if forward:
            ref.result[...] = ref.acc_s[...].astype(BF16)
        if backward:
            gradient = ref.grad[...].astype(F32)
            dn = ref.dn_s[...]
            normed, inverse = _moments(ref.middle[...])
            sums = ref.sums
            sums[0:1, :] = jnp.sum(gradient, axis=0, keepdims=True)
            sums[1:2, :] = jnp.sum(dn * normed, axis=0, keepdims=True)
            sums[2:3, :] = jnp.sum(dn, axis=0, keepdims=True)
            dmid = gradient + _norm_back(normed, inverse, _row(ref.gain, layer), dn)
            sums[3:4, :] = jnp.sum(dmid, axis=0, keepdims=True)
            sums[4:8, :] = jnp.zeros_like(sums[4:8, :])
            ref.dmid[...] = dmid
            low = dmid.astype(BF16)
            half = ref.proj_own.shape[1]
            ref.dattn[:, :half] = _dot(low, ref.proj_own[...], ((1,), (0,))).astype(BF16)
            ref.dattn[:, half:] = _dot(low, ref.proj_peer[...], ((1,), (0,))).astype(BF16)


def mlp(layer, first, last, forward, backward, sets, pieces, order, values):
    _unused, model, units = values["up_" + sets[0]].shape
    steps = units // TILE
    plan = (layer, first, last, forward, backward, sets, pieces, order)
    names, in_specs, operands = [], [], []
    once = pl.Buffered(1)
    rows = pl.BlockSpec((PAD, model), lambda j, c: (0, 0), pipeline_mode=once)
    vector = pl.BlockSpec(values["gain"].shape, lambda j, c: (0, 0), pipeline_mode=once)

    def take(**specs):
        for name, spec in specs.items():
            names.append(name)
            in_specs.append(spec)
            operands.append(values[name])

    def moving(number, shape):
        def index(j, c):
            tile = (0, jnp.clip(j - number * steps, 0, steps - 1))
            return tile if len(shape) == 2 else (layer, *tile)

        return pl.BlockSpec(shape, index)

    half = values["proj_own"].shape[2]
    proj = pl.BlockSpec((None, model, half), lambda j, c: (layer, 0, 0), pipeline_mode=once)
    if first and forward:
        take(hidden=rows, attended=rows, proj_own=proj, proj_peer=proj, proj_bias=vector, gain=vector, shift=vector,
             down_bias=vector)
    else:
        take(normed=rows)
        if forward:
            take(acc=rows)
    if backward:
        take(grad=rows)
        if not first:
            take(dn=rows)
        if last:
            take(middle=rows, proj_own=proj, proj_peer=proj, gain=vector)
    for number, name in enumerate(sets):
        take(**{"up_" + name: moving(number, (None, model, TILE)), "down_" + name: moving(number, (None, model, TILE))})
        if forward:
            take(**{"up_bias_" + name: moving(number, (2, TILE))})
        else:
            take(**{"active_" + name: moving(number, (PAD, TILE)), "slope_" + name: moving(number, (PAD, TILE))})
    out_names, out_specs, out_shape = [], [], []

    def give(spec, shape, kind, *given, make=jax.ShapeDtypeStruct):
        for name in given:
            out_names.append(name)
            out_specs.append(spec)
            out_shape.append(make(shape, kind))

    full = (PAD, model)
    if first and forward:
        give(rows, full, F32, "middle_out", make=pltpu.HBM)
        give(rows, full, BF16, "normed_out", make=pltpu.HBM)
    if not last:
        if forward:
            give(rows, full, F32, "acc_out")
        if backward:
            give(rows, full, F32, "dn_out")
    else:
        if forward:
            give(rows, full, BF16, "result")
        if backward:
            give(pl.BlockSpec((8, model), lambda j, c: (0, 0)), (8, model), F32, "sums")
            give(rows, full, F32, "dmid")
            give(rows, full, BF16, "dattn")
    for number, name in enumerate(sets):
        if forward and not backward:
            give(moving(number, (PAD, TILE)), (PAD, units), BF16, "active_" + name, "slope_" + name, make=pltpu.HBM)
        if backward:
            if name == "own":
                stacked = pl.BlockSpec((2, model, TILE), lambda j, c: (0, 0, j))
                give(stacked, (2, model, units), BF16, "grads_own", make=pltpu.HBM)
            else:
                give(moving(number, (model, TILE)), (model, units), BF16, "down_grad", "up_grad")
            give(moving(number, (1, TILE)), (1, units), F32, "bias_grad_" + name)
    scratch = dict(normed_s=pltpu.VMEM(full, BF16))
    if forward:
        scratch.update(acc_s=pltpu.VMEM(full, F32))
    if backward:
        scratch.update(
            grad_s=pltpu.VMEM(full, BF16),
            dn_s=pltpu.VMEM(full, F32),
            grad_t=pltpu.VMEM((model, MAIN), BF16),
            grad_c=pltpu.VMEM((model, 128), F32),
            normed_t=pltpu.VMEM((model, MAIN), BF16),
            normed_c=pltpu.VMEM((model, 128), F32),
        )
    results = pl.pallas_call(
        functools.partial(_mlp_kernel, (*names, *out_names, *scratch), plan),
        grid_spec=pltpu.PrefetchScalarGridSpec(
            num_scalar_prefetch=1,
            grid=(steps * len(sets),),
            in_specs=in_specs,
            out_specs=out_specs,
            scratch_shapes=list(scratch.values()),
        ),
        out_shape=out_shape,
        compiler_params=pltpu.CompilerParams(vmem_limit_bytes=(30 if not backward else 44 if forward else 38 if last else 27) * MIB),
        cost_estimate=cost(5 * steps * len(sets) * ((0.7 if forward else 0) + (0.9 if backward else 0))),
        name="mlp_" + ("f" if forward else "") + ("b" if backward else "") + "_" + "_".join(sets),
    )(values["coords"], *operands)
    return dict(zip(out_names, results, strict=True))


def _head_grad_kernel(
    pieces, order, coords_ref, dq_ref, dk_ref, dk_got_ref, dv_ref, dv_got_ref, dmid_ref, normed_ref, attended_ref,
    own_ref, peer_ref, dkv_ref, low_s, xt_s, column_s, yt_s, column_y,
):
    step = pl.program_id(0)
    half = own_ref.shape[1]

    def turn(x_ref):
        _fill_turned(coords_ref, order, pieces, x_ref, xt_s, column_s, False)
        _fill_turned(coords_ref, order, pieces, x_ref, yt_s, column_y, True)

    def outer(total):
        _outer(xt_s, column_s, total[:, :half], own_ref)
        _outer(yt_s, column_y, total[:, half:], peer_ref)

    @pl.when(step == 0)
    def _():
        turn(normed_ref)
        outer(dq_ref[...])

    for number, (mine, got) in enumerate(((dk_ref, dk_got_ref), (dv_ref, dv_got_ref))):

        @pl.when(step == 1 + number)
        def _(number=number, mine=mine, got=got):
            total = (mine[...].astype(F32) + got[...].astype(F32)).astype(BF16)
            dkv_ref[:, number * 2 * half : (number + 1) * 2 * half] = total
            outer(total)

    @pl.when(step == 3)
    def _():
        low_s[...] = dmid_ref[...].astype(BF16)
        turn(low_s)
        outer(attended_ref[...])


def head_gradients(pieces, order, coords, dq, dk, dk_got, dv, dv_got, dmid, normed, attended):
    model = dq.shape[1]
    half = model // 2
    rows = pl.BlockSpec((PAD, model), lambda j, c: (0, 0), pipeline_mode=pl.Buffered(1))
    grads = pl.BlockSpec((model, half), lambda j, c: (0, j))
    weight = pltpu.HBM((model, 4 * half), BF16)
    return pl.pallas_call(
        functools.partial(_head_grad_kernel, pieces, order),
        grid_spec=pltpu.PrefetchScalarGridSpec(
            num_scalar_prefetch=1,
            grid=(4,),
            in_specs=[rows] * 8,
            out_specs=[grads, grads, pl.BlockSpec((PAD, 2 * model), lambda j, c: (0, 0))],
            scratch_shapes=[
                pltpu.VMEM((PAD, model), BF16),
                pltpu.VMEM((model, MAIN), BF16),
                pltpu.VMEM((model, 128), F32),
                pltpu.VMEM((model, MAIN), BF16),
                pltpu.VMEM((model, 128), F32),
            ],
        ),
        out_shape=[weight, weight, jax.ShapeDtypeStruct((PAD, 2 * model), BF16)],
        compiler_params=pltpu.CompilerParams(vmem_limit_bytes=25 * MIB),
        cost_estimate=cost(13),
        name="head_gradients",
    )(coords, dq, dk, dk_got, dv, dv_got, dmid, normed, attended)


def _entry_back_kernel(
    layer, pieces, order, coords_ref, dq_ref, dkv_ref, dmid_ref, hidden_ref, xa_ref, xb_ref, gain_ref,
    qa_ref, qb_ref, wa_ref, wb_ref, own_ref, peer_ref, back_ref, skip_back_ref, sums_ref,
    da_s, low_s, xt_s, column_s, yt_s, column_y,
):
    step = pl.program_id(0)
    half = qa_ref.shape[1]

    def columns(ref, at):
        def run():
            total = _dot(ref[:, at : at + half], qa_ref[...], ((1,), (1,)))
            total = total + _dot(ref[:, at + half : at + 2 * half], qb_ref[...], ((1,), (1,)))
            da_s[...] = total if ref is dq_ref else da_s[...] + total

        return run

    pl.when(step == 0)(columns(dq_ref, 0))
    pl.when(step == 1)(columns(dkv_ref, 0))
    pl.when(step == 2)(columns(dkv_ref, 2 * half))

    @pl.when(step == 3)
    def _():
        da = da_s[...]
        normed, inverse = _moments(hidden_ref[...])
        sums_ref[0:1, :] = jnp.sum(da * normed, axis=0, keepdims=True)
        sums_ref[1:2, :] = jnp.sum(da, axis=0, keepdims=True)
        dhid = dmid_ref[...] + _norm_back(normed, inverse, _row(gain_ref, layer), da)
        sums_ref[2:3, :] = jnp.sum(dhid, axis=0, keepdims=True)
        sums_ref[3:8, :] = jnp.zeros_like(sums_ref[3:8, :])
        first = coords_ref[1] == 0
        low_s[...] = jnp.where(first, xa_ref[...], xb_ref[...])
        _fill_turned(coords_ref, order, pieces, low_s, xt_s, column_s, False)
        low_s[...] = jnp.where(first, xb_ref[...], xa_ref[...])
        _fill_turned(coords_ref, order, pieces, low_s, yt_s, column_y, True)
        low_s[...] = dhid.astype(BF16)

    for number in range(2):

        @pl.when(step == 3 + number)
        def _(number=number):
            dy = low_s[:, number * half : (number + 1) * half]
            _outer(xt_s, column_s, dy, own_ref)
            _outer(yt_s, column_y, dy, peer_ref)

    @pl.when(step == 4)
    def _():
        first = coords_ref[1] == 0
        one = _dot(low_s[...], wa_ref[...], ((1,), (1,)))
        two = _dot(low_s[...], wb_ref[...], ((1,), (1,)))
        back_ref[...] = jnp.where(first, one, two).astype(back_ref.dtype)
        skip_back_ref[...] = jnp.where(first, two, one).astype(BF16)


def entry_backward(layer, pieces, order, coords, dq, dkv, dmid, hidden, xa, xb, gain, qa, qb, wa, wb):
    model = xa.shape[1]
    half = qa.shape[3]
    once = pl.Buffered(1)
    rows = pl.BlockSpec((PAD, model), lambda j, c: (0, 0), pipeline_mode=once)
    pair = pl.BlockSpec((PAD, 2 * model), lambda j, c: (0, 0), pipeline_mode=once)
    linear = pl.BlockSpec((None, None, model, model), lambda j, c: (layer, 0, 0, 0), pipeline_mode=once)
    vector = pl.BlockSpec(gain.shape, lambda j, c: (0, 0))
    third = pl.BlockSpec((None, None, model, half), lambda j, c: (layer, jnp.minimum(j, 2), 0, 0))
    grads = pl.BlockSpec((model, half), lambda j, c: (0, jnp.maximum(j, 3) - 3))
    weight = pltpu.HBM((model, 2 * half), BF16)
    return pl.pallas_call(
        functools.partial(_entry_back_kernel, layer, pieces, order),
        grid_spec=pltpu.PrefetchScalarGridSpec(
            num_scalar_prefetch=1,
            grid=(5,),
            in_specs=[rows, pair, rows, rows, rows, rows, vector, third, third, linear, linear],
            out_specs=[grads, grads, rows, rows, pl.BlockSpec((8, model), lambda j, c: (0, 0))],
            scratch_shapes=[
                pltpu.VMEM((PAD, model), F32),
                pltpu.VMEM((PAD, model), BF16),
                pltpu.VMEM((model, MAIN), BF16),
                pltpu.VMEM((model, 128), F32),
                pltpu.VMEM((model, MAIN), BF16),
                pltpu.VMEM((model, 128), F32),
            ],
        ),
        out_shape=[
            weight,
            weight,
            jax.ShapeDtypeStruct((PAD, model), BF16 if layer == 0 else F32),
            jax.ShapeDtypeStruct((PAD, model), BF16),
            jax.ShapeDtypeStruct((8, model), F32),
        ],
        compiler_params=pltpu.CompilerParams(vmem_limit_bytes=40 * MIB),
        cost_estimate=cost(20),
        name="entry_backward",
    )(coords, dq, dkv, dmid, hidden, xa, xb, gain, qa, qb, wa, wb)


def _gather_kernel(count, core_ref, *refs):
    first = core_ref[0] == 0
    out_ref = refs[-1]
    for layer in range(count):
        mine, theirs = refs[2 * layer][...], refs[2 * layer + 1][...]
        low = jnp.where(first, mine, theirs)
        high = jnp.where(first, theirs, mine)
        for start, part in ((0, low[:MAIN]), (MAIN, high[:MAIN]), (2 * MAIN, low[MAIN : MAIN + 1]), (2 * MAIN + 1, high[MAIN : MAIN + 1])):
            at = slice(start, start + part.shape[0])
            if count == 1:
                out_ref[at, :] = part
            else:
                out_ref[at, layer, :] = part


def gather_rows(core, *pairs):
    width = pairs[0][0].shape[1]
    count = len(pairs)
    shape = (2 * MAIN + 2, width) if count == 1 else (2 * MAIN + 2, count, width)
    flat = [value for pair in pairs for value in pair]
    return pl.pallas_call(
        functools.partial(_gather_kernel, count),
        in_specs=[pl.BlockSpec(memory_space=pltpu.SMEM)] + [pl.BlockSpec(memory_space=pltpu.VMEM)] * len(flat),
        out_specs=pl.BlockSpec(memory_space=pltpu.VMEM),
        out_shape=jax.ShapeDtypeStruct(shape, BF16),
        compiler_params=pltpu.CompilerParams(vmem_limit_bytes=16 * MIB),
        cost_estimate=cost(3),
        name="gather_rows",
    )(jnp.reshape(core, (1,)).astype(jnp.int32), *flat)


def _pack_kernel(counts, lead, *refs):
    out_ref = refs[-1]
    for which in range(lead):
        value, at = None, 0
        for count in counts:
            term = (refs[at][which] if lead == 2 else refs[at][...]) if count == 1 else refs[at + which][...]
            value = term.astype(F32) if value is None else value + term.astype(F32)
            at += count
        if lead == 2:
            out_ref[which] = value.astype(BF16)
        else:
            out_ref[...] = value.astype(BF16)


def pack(parts, start, stop):
    block = math.gcd(math.gcd(start, stop), 128)
    columns = parts[0][0][0].shape[-1]
    lead = 2 if parts[0][0][0].ndim == 3 else 1
    in_specs, operands = [], []
    for arrays, at in parts:
        first = (at + start) // block
        for array in arrays:
            if array.ndim == 3:
                in_specs.append(pl.BlockSpec((2, block, columns), lambda j, first=first: (0, first + j, 0)))
            else:
                in_specs.append(pl.BlockSpec((block, columns), lambda j, first=first: (first + j, 0)))
            operands.append(_far(array))
    if lead == 2:
        out_spec = pl.BlockSpec((2, block, columns), lambda j: (0, j, 0))
        out_shape = jax.ShapeDtypeStruct((2, stop - start, columns), BF16)
    else:
        out_spec = pl.BlockSpec((block, columns), lambda j: (j, 0))
        out_shape = jax.ShapeDtypeStruct((stop - start, columns), BF16)
    return pl.pallas_call(
        functools.partial(_pack_kernel, tuple(len(arrays) for arrays, _ in parts), lead),
        grid=((stop - start) // block,),
        in_specs=in_specs,
        out_specs=out_spec,
        out_shape=out_shape,
        compiler_params=pltpu.CompilerParams(vmem_limit_bytes=12 * MIB),
        cost_estimate=cost(3 * (stop - start) * columns * lead / 2**20),
        name="pack",
    )(*operands)


def swap_cores(value):
    return lax.ppermute(value, "tensor", [(0, 1), (1, 0)])


def swap_bits(value, bits, size, crossed):
    cores = 2
    pairs = []
    for index in range(size):
        for core in range(cores):
            other = index
            for bit in bits:
                other = other ^ (1 << ((bit ^ core) if crossed and bit < 2 else bit))
            pairs.append((index * cores + core, other * cores + core))
    return lax.ppermute(value, ("dp", "tensor"), pairs)


def after(value, *others):
    return lax.optimization_barrier((value, others))[0]


def total(parts):
    result = parts[0].astype(F32)
    for part in parts[1:]:
        result = result + part.astype(F32)
    return result


class Reduction:
    def __init__(self, parts, order, size, axis=0, crossed=True):
        self.parts = [(part if isinstance(part, tuple) else (part,), 0) for part in parts]
        self.length, self.order, self.size = parts[0].shape[axis], list(order), size
        self.axis, self.crossed = axis, crossed

    def span(self, start, stop):
        values = []
        for arrays, at in self.parts:
            if len(arrays) == 1:
                values.append(lax.slice_in_dim(arrays[0], at + start, at + stop, axis=self.axis))
            else:
                values.append(jnp.stack([array[at + start : at + stop] for array in arrays]))
        return total(values)

    def piece(self, start, stop):
        if self.parts[0][0][0].dtype == BF16:
            return pack(self.parts, start, stop)
        return self.span(start, stop)

    def send(self, gate, count=1):
        bits, self.order = self.order[:count], self.order[count:]
        held = lax.optimization_barrier(([arrays for arrays, _ in self.parts], gate))[0]
        self.parts = [(arrays, at) for arrays, (_, at) in zip(held, self.parts)]
        self.length >>= len(bits)
        sent, got = [], []
        for block in range(1, 1 << len(bits)):
            start = block * self.length
            sent.append(self.piece(start, start + self.length))
            across = [bit for place, bit in enumerate(reversed(bits)) if (block >> place) & 1]
            got.append(swap_bits(sent[-1], across, self.size, self.crossed))
        self.parts += [((value,), 0) for value in got]
        return sent, got

    def result(self, gate):
        held = lax.optimization_barrier(([arrays for arrays, _ in self.parts], gate))[0]
        self.parts = [(arrays, at) for arrays, (_, at) in zip(held, self.parts)]
        return self.span(0, self.length)


def arrange(value, order, size):
    bits = size.bit_length() - 1
    index = lax.axis_index("dp")
    view = value.reshape((2,) * bits + value.shape[1:])
    for bit in range(bits):
        axis = bits - 1 - bit
        view = jnp.where((index >> bit) & 1 == 1, jnp.flip(view, axis), view)
    axes = [bits - 1 - bit for bit in order] + list(range(bits, view.ndim))
    return view.transpose(axes).reshape(value.shape)


def localize(value, core):
    main = lax.dynamic_slice_in_dim(value, core * MAIN, MAIN, 0)
    extra = lax.dynamic_slice_in_dim(value, 2 * MAIN + core, 1, 0)
    blank = jnp.zeros((PAD - MAIN - 1,) + value.shape[1:], value.dtype)
    return jnp.concatenate([main, extra, blank], axis=0)


def globalize(core, *mine):
    return gather_rows(core, *((value, swap_cores(value)) for value in mine))


def sum_vectors(shared, up_own, up_peer, size):
    count, model = shared.shape
    layers, units = up_own.shape
    order = tuple(range(size.bit_length() - 1))

    def blocks(offsets):
        first = shared.reshape(count, size, model // size).transpose(1, 0, 2)
        second = offsets.reshape(layers, size, units // model, model // size)
        second = second.transpose(1, 0, 2, 3).reshape(size, -1, model // size)
        return arrange(jnp.concatenate([first, second], axis=1), order, size)

    return Reduction([blocks(up_own), swap_cores(blocks(up_peer))], order, size, crossed=False)


def body(
    inputs, skips, cotangent, skip_weight, skip_bias, attn_norm_gain, attn_norm_bias, qkv_weight,
    proj_weight, proj_bias, ffn_norm_gain, ffn_norm_bias, up_weight, up_bias, down_weight, down_bias,
):
    core = lax.axis_index("tensor")
    size = lax.axis_size("dp")
    bits = size.bit_length() - 1
    assert size == 1 << bits and bits >= 2
    order = tuple(range(bits))
    order_mlp = order
    layers, model = skip_bias.shape
    assert layers == 2
    coords = jnp.stack([lax.axis_index("dp"), core]).astype(jnp.int32)

    qkv_turned = qkv_weight.transpose(0, 2, 1, 3)
    skip_peer, qkv_peer, up_bias_peer = swap_cores(skip_weight), swap_cores(qkv_turned), swap_cores(up_bias)
    weights = dict(
        coords=coords, proj_own=proj_weight, up_own=up_weight, down_own=down_weight, up_bias_own=up_bias,
        up_bias_peer=up_bias_peer, proj_bias=proj_bias, down_bias=down_bias, gain=ffn_norm_gain, shift=ffn_norm_bias,
    )
    skip_parts = localize(skips.transpose(1, 0, 2), core)

    rows0 = localize(inputs, core)
    weights["up_peer"] = swap_cores(after(up_weight, skip_peer, qkv_peer, skip_parts, rows0))

    def enter(layer, residual):
        skip_rows = skip_parts[:, layer]
        hidden, normed, q, kv = entry_forward(
            layer, coords, residual, skip_rows, skip_weight, skip_peer, skip_bias, attn_norm_gain, attn_norm_bias,
            qkv_turned, qkv_peer,
        )
        kv_other = swap_cores(kv)
        if layer == 0:
            kv_other = after(kv_other, weights["up_peer"], up_bias_peer)
        attended, exact, e, ex, il = attn_forward(q, kv, kv_other)
        return dict(xa=residual, xb=skip_rows, hidden=hidden, normed=normed, q=q, kv=kv, kv_other=kv_other,
                    attended=attended, exact=exact, e=e, ex=ex, il=il)

    items, result, flying = {}, {}, []

    def add(name, layer, own, *peer):
        theirs = tuple(swap_cores(value) for value in peer)
        flying.extend(theirs)
        items[name, layer] = Reduction([own, theirs], order, size, own.ndim - 2)

    def settle(gate):
        gate = after(gate, *flying)
        flying.clear()
        return gate

    def sends(gate, *keys, count=1):
        made = []
        for key in keys:
            item = items[key]
            if item.order:
                sent, got = item.send(gate, count)
                made.extend(sent)
                flying.extend(got)
            elif key not in result:
                result[key] = item.result(gate)
                made.append(result[key])
        return after(gate, *made) if made else gate

    def back(layer, kept, mid, dattn, *keys):
        dq, dk, dk_other, dv, dv_other = attn_backward(
            kept["q"], kept["kv"], kept["kv_other"], dattn, kept["exact"], kept["e"], kept["ex"], kept["il"]
        )
        own, peer, dkv = head_gradients(
            size, order, coords, dq, dk, swap_cores(dk_other), dv, swap_cores(dv_other), mid["dmid"], kept["normed"],
            kept["attended"],
        )
        dkv = settle(dkv)
        add("head", layer, own, after(peer, dkv))
        dkv = sends(dkv, *keys)
        own, peer, gradient, skip_grad, sums = entry_backward(
            layer, size, order, coords, dq, dkv, mid["dmid"], kept["hidden"], kept["xa"], kept["xb"], attn_norm_gain,
            qkv_turned, qkv_peer, skip_weight, skip_peer,
        )
        gradient = settle(gradient)
        add("skip", layer, own, after(peer, gradient))
        return gradient, skip_grad, sums

    kept = [None] * layers
    kept[0] = enter(0, rows0)
    late = after((proj_weight, down_weight), kept[0]["kv_other"])
    weights["proj_peer"], weights["down_peer"] = (swap_cores(item) for item in late)
    mid0 = mlp(0, True, True, True, False, ("peer", "own"), size, order_mlp, {**weights, **kept[0]})
    kept[1] = enter(1, mid0["result"])
    values = {**weights, **kept[1], "grad": localize(cotangent, core)}
    one = mlp(1, True, False, True, True, ("peer",), size, order_mlp, values)
    values.update(normed=one["normed_out"], middle=one["middle_out"], acc=one["acc_out"], dn=one["dn_out"])
    theirs = tuple(swap_cores(one[name]) for name in ("down_grad", "up_grad"))
    flying.extend(theirs)
    two = mlp(1, False, True, True, True, ("own",), size, order, values)
    items["mlp", 1] = Reduction([two["grads_own"], theirs], order, size, 1)
    dattn = sends(settle(two["dattn"]), ("mlp", 1))
    gradient, skip_grad1, sums1 = back(1, kept[1], two, dattn, ("mlp", 1))
    gradient = sends(gradient, ("head", 1), ("mlp", 1))

    values = {**weights, **kept[0], **mid0, "normed": mid0["normed_out"], "middle": mid0["middle_out"], "grad": gradient}
    one0 = mlp(0, True, False, False, True, ("peer",), size, order, values)
    gate = settle(one0["dn_out"])
    peers = [after(one0[name], gate) for name in ("down_grad", "up_grad")]
    theirs = tuple(swap_cores(value) for value in peers)
    flying.extend(theirs)
    values.update(dn=sends(gate, ("skip", 1), ("head", 1), ("mlp", 1)))
    low = mlp(0, False, True, False, True, ("own",), size, order, values)
    items["mlp", 0] = Reduction([low["grads_own"], theirs], order, size, 1)
    dattn = sends(settle(low["dattn"]), ("mlp", 0), ("head", 1), ("mlp", 1), ("skip", 1))
    gradient, skip_grad0, sums0 = back(0, kept[0], low, dattn, ("mlp", 0), ("head", 1), ("skip", 1))
    shared = jnp.concatenate([low["sums"][:4], two["sums"][:4], sums0[:3], sums1[:3]], axis=0)
    items["vectors", 0] = sum_vectors(
        shared,
        jnp.concatenate([low["bias_grad_own"], two["bias_grad_own"]], axis=0),
        jnp.concatenate([one0["bias_grad_peer"], one["bias_grad_peer"]], axis=0),
        size,
    )
    rest = bits - 2
    finish = sends(gradient, ("head", 0), ("mlp", 0), ("skip", 1), ("head", 1))
    others = [swap_cores(after(value, finish)) for value in (gradient, skip_grad0, skip_grad1, two["result"])]
    input_grad = gather_rows(core, (after(gradient, finish), others[0]))
    skip_grad = gather_rows(core, (after(skip_grad0, input_grad), others[1]), (skip_grad1, others[2]))
    output = gather_rows(core, (after(two["result"], skip_grad), others[3]))
    finish = settle(after(finish, output))
    finish = sends(finish, ("head", 0), ("skip", 0), ("mlp", 0), ("skip", 1))
    finish = settle(sends(finish, ("vectors", 0), count=2))
    finish = sends(finish, ("head", 0), count=rest)
    finish = settle(sends(finish, ("skip", 0), ("vectors", 0), ("mlp", 0)))
    finish = sends(finish, ("skip", 0), count=rest)
    finish = settle(sends(finish, ("vectors", 0), ("head", 0)))
    while len(result) < len(items):
        finish = settle(sends(finish, *items))
    count = shared.shape[0]
    vectors = result["vectors", 0][0, :count]
    up_bias_grad = result["vectors", 0][0, count:].reshape(layers, -1)
    skip_grad = skip_grad.transpose(1, 0, 2)
    outer = vectors[:8].reshape(2, 4, -1)
    inner = vectors[8:].reshape(2, 3, -1)

    half = model // 2

    def columns(start, stop):
        return jnp.stack([result["head", layer][:, start:stop] for layer in range(layers)])

    def matrix(which):
        return jnp.stack([result["mlp", layer][which] for layer in range(layers)])

    return (
        output, input_grad, skip_grad, jnp.stack([result["skip", layer] for layer in range(layers)])[:, None],
        inner[:, 2], inner[:, 0], inner[:, 1],
        columns(0, 3 * half).reshape(layers, -1, 3, qkv_weight.shape[3]), columns(3 * half, 4 * half),
        outer[:, 3], outer[:, 1], outer[:, 2],
        matrix(1), up_bias_grad, matrix(0), outer[:, 0],
    )


def solution(mesh):
    return jax.shard_map(
        body,
        mesh=mesh,
        in_specs=(
            P("dp", None), P(None, "dp", None), P("dp", None), P(None, "tensor", None, None), P(), P(),
            P(), P(None, None, None, "tensor"), P(None, None, "tensor"), P(), P(), P(),
            P(None, None, "tensor"), P(None, "tensor"), P(None, None, "tensor"), P(),
        ),
        out_specs=(
            P("dp", None), P("dp", None), P(None, "dp", None), P(None, "tensor", "dp", None),
            P(None, "dp"), P(None, "dp"), P(None, "dp"), P(None, "dp", None, "tensor"),
            P(None, "dp", "tensor"), P(None, "dp"), P(None, "dp"), P(None, "dp"),
            P(None, "dp", "tensor"), P(None, ("tensor", "dp")), P(None, "dp", "tensor"), P(None, "dp"),
        ),
        check_vma=False,
    )
```

time: 593 us -> 582 us (0.981)
  other arithmetic: 72.8 us -> 23 us
  Pallas kernels: 308 us -> 343 us
  starting transfers between devices: 31.6 us -> 48.7 us
  waiting for transfers between devices: 113 us -> 106 us
    pallas_call x7 -> x35, Pallas kernels: 154 us -> 212 us  [the longest x5 110 us: mlp(): pl.pallas_call(functools.partial(_mlp_kernel, (*names, *out_names, *scrat...]
    convert_element_type x17 -> x0, other arithmetic: 49.2 us -> none  [the longest x16 49 us: send(): payload = self.span(half, self.length).astype(held[0][0].dtype)]
    unnamed x72 -> x170, local copies, waits for them, and re-layouts: 10.8 us -> 35.7 us
    pallas_call x2, Pallas kernels: 56 us -> 34.2 us  [entry_backward(): pl.pallas_call(functools.partial(_entry_back_kernel, layer, pieces, order...]
    ppermute x20 -> x31, starting transfers between devices: 23.5 us -> 43.1 us  [swap_bits(): return lax.ppermute(value, ('dp', 'tensor'), pairs)]
    another operation x16 -> x4, local copies, waits for them, and re-layouts: 20.9 us -> 3.87 us  [span(): values.append(jnp.stack([array[at + start:at + stop] for array in arrays]))]
    slice x27 -> x3, local copies, waits for them, and re-layouts: 15.8 us -> 0.03 us  [columns(): result['head', layer][:, start:stop]]
    ppermute x20 -> x31, waiting for transfers between devices: 87.2 us -> 78.7 us  [swap_bits(): return lax.ppermute(value, ('dp', 'tensor'), pairs)]
  transfers between devices with their start and end apart: 47 -> 56, of which waited for: 14 -> 22; matrix products, arithmetic and copies ran while one was open for 18% -> 6% of each run, Pallas kernels for 40% -> 40%
where the time goes in v3:
time: 582 us; the launch traced here: 577 us
  Pallas kernels  343 us (59%)
  waiting for transfers between devices  106 us (18%)
  local copies, waits for them, and re-layouts  54.9 us (9%)
  starting transfers between devices  48.7 us (8%)
  other arithmetic  23 us (4%)
    pallas_call x5, Pallas kernels, mlp(): pl.pallas_call(functools.partial(_mlp_kernel, (*names, *out_names, *scrat...  110 us
    ppermute x31, waiting for transfers between devices, swap_bits(): return lax.ppermute(value, ('dp', 'tensor'), pairs)  78.7 us
    pallas_call x26, Pallas kernels, pack(): pl.pallas_call(functools.partial(_pack_kernel, tuple((len(arrays) for arr...  59.9 us
    pallas_call x2, Pallas kernels, attn_backward(): pl.pallas_call(_attn_bwd_kernel, grid=(groups,), in_specs=[near(0), near(...  46.7 us
    ppermute x31, starting transfers between devices, swap_bits(): return lax.ppermute(value, ('dp', 'tensor'), pairs)  43.1 us
    pallas_call x2, Pallas kernels, attn_forward(): pl.pallas_call(_attn_fwd_kernel, grid=(groups,), in_specs=[near(0), near(...  38.6 us
    unnamed x170, local copies, waits for them, and re-layouts  35.7 us
    pallas_call x2, Pallas kernels, entry_backward(): pl.pallas_call(functools.partial(_entry_back_kernel, layer, pieces, order...  34.2 us
  transfers between devices with their start and end apart: 56, of which 22 were waited for; matrix products, arithmetic and copies ran while one was open for 6% of the time, Pallas kernels for 40%

profile of v3, /device:TPU:0, one launch (start us, length us, event | category | flops | bytes accessed | tf_op | source)
XLA Modules:
  0.0 576.9 jit_solution(15628510505529062508)
XLA Ops:
  1.9 3.0 constant_dynamic-slice_fusion.2
  10.4 6.9 %collective-permute-done.wb_ref = bf16[2,1,1024,1024]{3,2,1,0:T(8,128)(2,1)} collective-permute-done((bf16[2,1,1024,1024]{3,2,1,0:T(8,128)(2,1)}, bf16[2,1,1024,1024]{3,2,1,0:T(8,128)(2,1)}, u32[]{:S(2)}, u32[]{:S(2)}) %collective-permute-start) | collective-permute-done | bytes 4194336 | tf_op jit(solution)/shard_map/ppermute | solution.py:803
  18.0 2.7 copy-done.1
  20.7 2.8 copy-done
  24.7 12.7 %entry_forward.2 = (f32[528,1024]{1,0:T(8,128)}, bf16[528,1024]{1,0:T(8,128)(2,1)}, bf16[528,1024]{1,0:T(8,128)(2,1)}, bf16[528,2048]{1,0:T(8,128)(2,1)}) custom-call(s32[2]{0:T(128)S(1)} %pad_add_fusion.coords_ref, bf16[528,1024]{1,0:T(8,128)(2,1)S(1)} %copy-done.6, bf16[528,1024]{1,0:T(8,128)(2,1)S(1)} %get-tuple-element.561.xb_ref, ...), custom_call_target="tpu_custom_call" | custom-call | flops 1 | bytes 24500000 | tf_op jit(solution)/shard_map/entry_forward/pallas_call | solution.py:329
  37.9 3.5 collective-permute-done.4.refs_10_.refs_11_
  44.5 19.2 %attn_forward.2 = (bf16[528,1024]{1,0:T(8,128)(2,1)}, f32[528,1024]{1,0:T(8,128)}, bf16[16,528,1024]{2,1,0:T(8,128)(2,1)}, f32[4,528,16]{2,1,0:T(8,128)}, f32[4,528,16]{2,1,0:T(8,128)}) custom-call(bf16[528,1024]{1,0:T(8,128)(2,1)S(1)} %copy-done.22, bf16[528,2048]{1,0:T(8,128)(2,1)} %get-tuple-element.274.km_ref.vm_ref, ...), custom_call_target="tpu_custom_call" | custom-call | flops 1 | bytes 33250000 | tf_op jit(solution)/shard_map/attn_forward/pallas_call | solution.py:91
  63.7 3.2 copy-done.53
  68.5 24.7 %mlp_f_peer_own.1 = (f32[528,1024]{1,0:T(8,128)}, bf16[528,1024]{1,0:T(8,128)(2,1)}, bf16[528,1024]{1,0:T(8,128)(2,1)S(1)}, bf16[528,2048]{1,0:T(8,128)(2,1)}, b...) custom-call(s32[2]{0:T(128)S(1)} %pad_add_fusion.coords_ref, ...), custom_call_target="tpu_custom_call" | custom-call | flops 1 | bytes 49000000 | tf_op jit(solution)/shard_map/mlp_f_peer_own/pallas_call | solution.py:553
  93.2 12.2 %entry_forward.3 = (f32[528,1024]{1,0:T(8,128)}, bf16[528,1024]{1,0:T(8,128)(2,1)}, bf16[528,1024]{1,0:T(8,128)(2,1)}, bf16[528,2048]{1,0:T(8,128)(2,1)}) custom-call(s32[2]{0:T(128)S(1)} %pad_add_fusion.coords_ref, bf16[528,1024]{1,0:T(8,128)(2,1)S(1)} %get-tuple-element.280.xa_ref, bf16[528,1024]{1,0:T(8,128)(2,1)S(1)} %get-tuple-element.560.xb_ref, ...), custom_call_target="tpu_custom_call" | custom-call | flops 1 | bytes 24500000 | tf_op jit(solution)/shard_map/entry_forward/pallas_call | solution.py:329
  105.6 4.3 collective-permute-done.7.ko_ref.vo_ref
  112.5 19.4 %attn_forward.3 = (bf16[528,1024]{1,0:T(8,128)(2,1)}, f32[528,1024]{1,0:T(8,128)}, bf16[16,528,1024]{2,1,0:T(8,128)(2,1)}, f32[4,528,16]{2,1,0:T(8,128)}, f32[4,528,16]{2,1,0:T(8,128)}) custom-call(bf16[528,1024]{1,0:T(8,128)(2,1)S(1)} %copy-done.23, bf16[528,2048]{1,0:T(8,128)(2,1)} %get-tuple-element.283.km_ref.vm_ref, ...), custom_call_target="tpu_custom_call" | custom-call | flops 1 | bytes 33250000 | tf_op jit(solution)/shard_map/attn_forward/pallas_call | solution.py:91
  133.2 25.8 %mlp_fb_peer.1 = (f32[528,1024]{1,0:T(8,128)}, bf16[528,1024]{1,0:T(8,128)(2,1)}, f32[528,1024]{1,0:T(8,128)S(1)}, f32[528,1024]{1,0:T(8,128)}, bf16[1024,2048]{...) custom-call(s32[2]{0:T(128)S(1)} %pad_add_fusion.coords_ref, ...), custom_call_target="tpu_custom_call" | custom-call | flops 1 | bytes 56000000 | tf_op jit(solution)/shard_map/mlp_fb_peer/pallas_call | solution.py:553
  162.1 27.3 %mlp_fb_own.1 = (bf16[528,1024]{1,0:T(8,128)(2,1)S(1)}, f32[8,1024]{1,0:T(8,128)S(1)}, f32[528,1024]{1,0:T(8,128)}, bf16[528,1024]{1,0:T(8,128)(2,1)S(1)}, bf16[...) custom-call(s32[2]{0:T(128)S(1)} %pad_add_fusion.coords_ref, bf16[528,1024]{1,0:T(8,128)(2,1)S(1)} %copy-done.30, ...), custom_call_target="tpu_custom_call" | custom-call | flops 1 | bytes 56000000 | tf_op jit(solution)/shard_map/mlp_fb_own/pallas_call | solution.py:553
  191.4 4.4 pack.26
  195.9 2.7 collective-permute-start.12
  198.6 23.4 %attn_backward.2 = (bf16[528,1024]{1,0:T(8,128)(2,1)S(1)}, bf16[528,1024]{1,0:T(8,128)(2,1)S(1)}, bf16[528,1024]{1,0:T(8,128)(2,1)S(1)}, bf16[528,1024]{1,0:T(8,128)(2,1)S(1)}, bf16[528,1024]{1,0:T(8,128)(2,1)S(1)}) custom-call(bf16[528,1024]{1,0:T(8,128)(2,1)} %get-tuple-element.282.q_ref, bf16[528,2048]{1,0:T(8,128)(2,1)} %get-tuple-element.283.km_ref.vm_ref, ...), custom_call_target="tpu_custom_call" | custom-call | flops 1 | bytes 40250000 | tf_op jit(solution)/shard_map/attn_backward/pallas_call | solution.py:192
  226.3 8.6 %head_gradients.2 = (bf16[1024,2048]{1,0:T(8,128)(2,1)}, bf16[1024,2048]{1,0:T(8,128)(2,1)}, bf16[528,2048]{1,0:T(8,128)(2,1)S(1)}) custom-call(s32[2]{0:T(128)S(1)} %pad_add_fusion.coords_ref, bf16[528,1024]{1,0:T(8,128)(2,1)S(1)} %get-tuple-element.304.dq_ref, bf16[528,1024]{1,0:T(8,128)(2,1)S(1)} %get-tuple-element.305.dk_ref, ...), custom_call_target="tpu_custom_call" | custom-call | flops 1 | bytes 22750000 | tf_op jit(solution)/shard_map/head_gradients/pallas_call | solution.py:611
  234.9 10.2 %collective-permute-done.12.refs_3_ = bf16[2,512,2048]{2,1,0:T(8,128)(2,1)S(1)} collective-permute-done((bf16[2,512,2048]{2,1,0:T(8,128)(2,1)S(1)}, bf16[2,512,2048]{2,1,0:T(8,128)(2,1)S(1)}, u32[]{:S(2)}, u32[]{:S(2)}) %collective-permute-start.12) | collective-permute-done | bytes 4194336 | tf_op jit(solution)/shard_map/ppermute | solution.py:815
  247.2 3.6 pack.27
  252.9 16.8 %entry_backward.2 = (bf16[1024,1024]{1,0:T(8,128)(2,1)}, bf16[1024,1024]{1,0:T(8,128)(2,1)}, f32[528,1024]{1,0:T(8,128)S(1)}, bf16[528,1024]{1,0:T(8,128)(2,1)S(1)}, f32[8,1024]{1,0:T(8,128)S(1)}) custom-call(s32[2]{0:T(128)S(1)} %pad_add_fusion.coords_ref, bf16[528,1024]{1,0:T(8,128)(2,1)S(1)} %get-tuple-element.304.dq_ref, ...), custom_call_target="tpu_custom_call" | custom-call | flops 1 | bytes 35000000 | tf_op jit(solution)/shard_map/entry_backward/pallas_call | solution.py:697
  269.7 7.2 %collective-permute-done.14.refs_4_ = bf16[2,256,2048]{2,1,0:T(8,128)(2,1)S(1)} collective-permute-done((bf16[2,256,2048]{2,1,0:T(8,128)(2,1)S(1)}, bf16[2,256,2048]{2,1,0:T(8,128)(2,1)S(1)}, u32[]{:S(2)}, u32[]{:S(2)}) %collective-permute-start.14) | collective-permute-done | bytes 2097184 | tf_op jit(solution)/shard_map/ppermute | solution.py:815
  276.9 3.8 pack.28
  282.9 2.7 pack.29
  287.2 14.8 %mlp_b_peer.1 = (f32[528,1024]{1,0:T(8,128)S(1)}, bf16[1024,2048]{1,0:T(8,128)(2,1)}, bf16[1024,2048]{1,0:T(8,128)(2,1)S(1)}, f32[1,2048]{1,0:T(1,128)S(1)}) custom-call(s32[2]{0:T(128)S(1)} %pad_add_fusion.coords_ref, bf16[528,1024]{1,0:T(8,128)(2,1)S(1)} %copy-done.21, f32[528,1024]{1,0:T(8,128)S(1)} %get-tuple-element.330.refs_1_, ...), custom_call_target="tpu_custom_call" | custom-call | flops 1 | bytes 31500000 | tf_op jit(solution)/shard_map/mlp_b_peer/pallas_call | solution.py:553
  302.1 9.1 %collective-permute-done.17.refs_5_ = bf16[2,128,2048]{2,1,0:T(8,128)(2,1)S(1)} collective-permute-done((bf16[2,128,2048]{2,1,0:T(8,128)(2,1)S(1)}, bf16[2,128,2048]{2,1,0:T(8,128)(2,1)S(1)}, u32[]{:S(2)}, u32[]{:S(2)}) %collective-permute-start.17) | collective-permute-done | bytes 1048608 | tf_op jit(solution)/shard_map/ppermute | solution.py:815
  323.2 17.4 %mlp_b_own.1 = (f32[8,1024]{1,0:T(8,128)S(1)}, f32[528,1024]{1,0:T(8,128)S(1)}, bf16[528,1024]{1,0:T(8,128)(2,1)S(1)}, bf16[2,1024,2048]{2,1,0:T(8,128)(2,1)}, f32[1,2048]{1,0:T(1,128)S(1)}) custom-call(s32[2]{0:T(128)S(1)} %pad_add_fusion.coords_ref, bf16[528,1024]{1,0:T(8,128)(2,1)S(1)} %copy-done.21, f32[528,1024]{1,0:T(8,128)S(1)} %get-tuple-element.330.refs_1_, ...), custom_call_target="tpu_custom_call" | custom-call | flops 1 | bytes 31500000 | tf_op jit(solution)/shard_map/mlp_b_own/pallas_call | solution.py:553
  340.5 5.5 collective-permute-done.22
  346.1 5.2 pack.33
  358.1 2.8 convert_add_fusion.1
  361.0 23.3 %attn_backward.3 = (bf16[528,1024]{1,0:T(8,128)(2,1)S(1)}, bf16[528,1024]{1,0:T(8,128)(2,1)S(1)}, bf16[528,1024]{1,0:T(8,128)(2,1)S(1)}, bf16[528,1024]{1,0:T(8,128)(2,1)S(1)}, bf16[528,1024]{1,0:T(8,128)(2,1)S(1)}) custom-call(bf16[528,1024]{1,0:T(8,128)(2,1)} %get-tuple-element.273.q_ref, bf16[528,2048]{1,0:T(8,128)(2,1)} %get-tuple-element.274.km_ref.vm_ref, ...), custom_call_target="tpu_custom_call" | custom-call | flops 1 | bytes 40250000 | tf_op jit(solution)/shard_map/attn_backward/pallas_call | solution.py:192
  388.6 8.6 %head_gradients.3 = (bf16[1024,2048]{1,0:T(8,128)(2,1)}, bf16[1024,2048]{1,0:T(8,128)(2,1)}, bf16[528,2048]{1,0:T(8,128)(2,1)S(1)}) custom-call(s32[2]{0:T(128)S(1)} %pad_add_fusion.coords_ref, bf16[528,1024]{1,0:T(8,128)(2,1)S(1)} %get-tuple-element.382.dq_ref, bf16[528,1024]{1,0:T(8,128)(2,1)S(1)} %get-tuple-element.383.dk_ref, ...), custom_call_target="tpu_custom_call" | custom-call | flops 1 | bytes 22750000 | tf_op jit(solution)/shard_map/head_gradients/pallas_call | solution.py:611
  399.8 5.7 collective-permute-done.25.refs_3_
  407.5 4.2 pack.36
  416.6 3.4 collective-permute-start.30
  429.6 17.5 %entry_backward.3 = (bf16[1024,1024]{1,0:T(8,128)(2,1)}, bf16[1024,1024]{1,0:T(8,128)(2,1)}, bf16[528,1024]{1,0:T(8,128)(2,1)}, bf16[528,1024]{1,0:T(8,128)(2,1)}, f32[8,1024]{1,0:T(8,128)S(1)}) custom-call(s32[2]{0:T(128)S(1)} %pad_add_fusion.coords_ref, bf16[528,1024]{1,0:T(8,128)(2,1)S(1)} %get-tuple-element.382.dq_ref, bf16[528,2048]{1,0:T(8,128)(2,1)S(1)} %copy-done.25, ...), custom_call_target="tpu_custom_call" | custom-call | flops 1 | bytes 35000000 | tf_op jit(solution)/shard_map/entry_backward/pallas_call | solution.py:697
  447.1 3.3 pack.39
  451.7 2.7 pack.40
  462.7 5.5 collective-permute-done.34.refs_3_
  468.2 3.1 gather_rows.3
  471.3 6.3 %gather_rows.4 = bf16[1026,2,1024]{2,1,0:T(2,128)(2,1)} custom-call(s32[1]{0:T(128)} %bitcast.core_ref, bf16[528,1024]{1,0:T(8,128)(2,1)} %get-tuple-element.432.refs_0_, bf16[528,1024]{1,0:T(8,128)(2,1)} %collective-permute-done.33.refs_1_, bf16[528,1024]{1,0:T(8,128)(2,1)S(1)} %copy-done.32, bf16[528,1024]{1,0:T(8,128)(2,1)S(1)} %collective-permute-done.34.refs_3_), custom_call_target="tpu_custom_call" | custom-call | flops 1 | bytes 5250000 | tf_op jit(solution)/shard_map/gather_rows/pallas_call | solution.py:746
  479.3 9.0 %collective-permute-done.39 = bf16[64,1024]{1,0:T(8,128)(2,1)S(1)} collective-permute-done((bf16[64,1024]{1,0:T(8,128)(2,1)S(1)}, bf16[64,1024]{1,0:T(8,128)(2,1)S(1)}, u32[]{:S(2)}, u32[]{:S(2)}) %collective-permute-start.39) | collective-permute-done | bytes 131104 | tf_op jit(solution)/shard_map/ppermute | solution.py:815
  507.7 15.8 %collective-permute-done.46 = f32[4,18,64]{2,1,0:T(8,128)S(1)} collective-permute-done((f32[4,18,64]{2,1,0:T(8,128)S(1)}, f32[4,18,64]{2,1,0:T(8,128)S(1)}, u32[]{:S(2)}, u32[]{:S(2)}) %collective-permute-start.46) | collective-permute-done | bytes 18464 | tf_op jit(solution)/shard_map/ppermute | solution.py:815
  525.1 2.8 collective-permute-done.44
  533.5 2.8 collective-permute-start.50
  545.7 4.0 collective-permute-done.51
  555.9 4.8 collective-permute-start.52
  567.3 4.4 collective-permute-done.55
  (349 shorter events, 141.5 us)
Async XLA Ops:
  0.6 16.6 %collective-permute-start.1 = (bf16[2,3,1024,512]{3,2,1,0:T(8,128)(2,1)}, bf16[2,3,1024,512]{3,2,1,0:T(8,128)(2,1)}, u32[]{:S(2)}, u32[]{:S(2)}) collective-permute-start(bf16[2,3,1024,512]{3,2,1,0:T(8,128)(2,1)} %bitcast.55), channel_id=1, source_target_pairs={{0,1},{1,0},{2,3},{3,2},{4,5},{5,4},{6,7},{7,6},{8,9},{9,8},{10,11... | collective-permute-start | bytes 18874376 | tf_op jit(solution)/shard_map/ppermute | solution.py:803
  1.2 16.1 %collective-permute-start = (bf16[2,1,1024,1024]{3,2,1,0:T(8,128)(2,1)}, bf16[2,1,1024,1024]{3,2,1,0:T(8,128)(2,1)}, u32[]{:S(2)}, u32[]{:S(2)}) collective-permute-start(bf16[2,1,1024,1024]{3,2,1,0:T(8,128)(2,1)} %wa_ref.7), channel_id=1, source_target_pairs={{0,1},{1,0},{2,3},{3,2},{4,5},{5,4},{6,7},{7,6},{8,9},{9,8},{10,11... | collective-permute-start | bytes 12582920 | tf_op jit(solution)/shard_map/ppermute | solution.py:803
  17.3 24.6 %collective-permute-start.3 = (bf16[2,1024,2048]{2,1,0:T(8,128)(2,1)}, bf16[2,1024,2048]{2,1,0:T(8,128)(2,1)}, u32[]{:S(2)}, u32[]{:S(2)}) collective-permute-start(bf16[2,1024,2048]{2,1,0:T(8,128)(2,1)} %refs_7_.7), channel_id=1, source_target_pairs={{0,1},{1,0},{2,3},{3,2},{4,5},{5,4},{6,7},{7,6},{8,9},{9,8},{10,11... | collective-permute-start | bytes 25165832 | tf_op jit(solution)/shard_map/ppermute | solution.py:803
  41.9 21.8 %collective-permute-start.6 = (bf16[2,1024,2048]{2,1,0:T(8,128)(2,1)}, bf16[2,1024,2048]{2,1,0:T(8,128)(2,1)S(1)}, u32[]{:S(2)}, u32[]{:S(2)}) collective-permute-start(bf16[2,1024,2048]{2,1,0:T(8,128)(2,1)} %refs_8_.3), channel_id=1, source_target_pairs={{0,1},{1,0},{2,3},{3,2},{4,5},{5,4},{6,7},{7,6},{8,9},{9,8},{10,11... | collective-permute-start | bytes 25165832 | tf_op jit(solution)/shard_map/ppermute | solution.py:803
  42.0 21.6 %collective-permute-start.5 = (bf16[2,1024,512]{2,1,0:T(8,128)(2,1)S(1)}, bf16[2,1024,512]{2,1,0:T(8,128)(2,1)S(1)}, u32[]{:S(2)}, u32[]{:S(2)}) collective-permute-start(bf16[2,1024,512]{2,1,0:T(8,128)(2,1)S(1)} %copy-done.2), channel_id=1, source_target_pairs={{0,1},{1,0},{2,3},{3,2},{4,5},{5,4},{6,7},{7,6},{8,9},{9,8},{10,11... | collective-permute-start | bytes 6291464 | tf_op jit(solution)/shard_map/ppermute | solution.py:803
  160.3 29.1 %collective-permute-start.8 = (bf16[1024,2048]{1,0:T(8,128)(2,1)}, bf16[1024,2048]{1,0:T(8,128)(2,1)S(1)}, u32[]{:S(2)}, u32[]{:S(2)}) collective-permute-start(bf16[1024,2048]{1,0:T(8,128)(2,1)} %get-tuple-element.292), channel_id=1, source_target_pairs={{0,1},{1,0},{2,3},{3,2},{4,5},{5,4},{6,7},{7,6},{8,9},{9,8},{10,11... | collective-permute-start | bytes 12582920 | tf_op jit(solution)/shard_map/ppermute | solution.py:803
  160.5 29.0 %collective-permute-start.9 = (bf16[1024,2048]{1,0:T(8,128)(2,1)}, bf16[1024,2048]{1,0:T(8,128)(2,1)}, u32[]{:S(2)}, u32[]{:S(2)}) collective-permute-start(bf16[1024,2048]{1,0:T(8,128)(2,1)} %get-tuple-element.293), channel_id=1, source_target_pairs={{0,1},{1,0},{2,3},{3,2},{4,5},{5,4},{6,7},{7,6},{8,9},{9,8},{10,11... | collective-permute-start | bytes 12582920 | tf_op jit(solution)/shard_map/ppermute | solution.py:803
  195.9 49.2 %collective-permute-start.12 = (bf16[2,512,2048]{2,1,0:T(8,128)(2,1)S(1)}, bf16[2,512,2048]{2,1,0:T(8,128)(2,1)S(1)}, u32[]{:S(2)}, u32[]{:S(2)}) collective-permute-start(bf16[2,512,2048]{2,1,0:T(8,128)(2,1)S(1)} %pack.26), channel_id=1, source_target_pairs={{0,2},{1,5},{2,0},{3,7},{4,6},{5,1},{6,4},{7,3},{8,10},{9,13},{10,... | collective-permute-start | bytes 12582920 | tf_op jit(solution)/shard_map/ppermute | solution.py:815
  245.1 31.9 %collective-permute-start.13 = (bf16[1024,2048]{1,0:T(8,128)(2,1)}, bf16[1024,2048]{1,0:T(8,128)(2,1)}, u32[]{:S(2)}, u32[]{:S(2)}) collective-permute-start(bf16[1024,2048]{1,0:T(8,128)(2,1)} %get-tuple-element.320), channel_id=1, source_target_pairs={{0,1},{1,0},{2,3},{3,2},{4,5},{5,4},{6,7},{7,6},{8,9},{9,8},{10,11... | collective-permute-start | bytes 12582920 | tf_op jit(solution)/shard_map/ppermute | solution.py:803
  250.8 26.1 %collective-permute-start.14 = (bf16[2,256,2048]{2,1,0:T(8,128)(2,1)S(1)}, bf16[2,256,2048]{2,1,0:T(8,128)(2,1)S(1)}, u32[]{:S(2)}, u32[]{:S(2)}) collective-permute-start(bf16[2,256,2048]{2,1,0:T(8,128)(2,1)S(1)} %pack.27), channel_id=1, source_target_pairs={{0,4},{1,3},{2,6},{3,1},{4,0},{5,7},{6,2},{7,5},{8,12},{9,11},{10,... | collective-permute-start | bytes 6291464 | tf_op jit(solution)/shard_map/ppermute | solution.py:815
  280.8 30.4 %collective-permute-start.16 = (bf16[512,2048]{1,0:T(8,128)(2,1)S(1)}, bf16[512,2048]{1,0:T(8,128)(2,1)}, u32[]{:S(2)}, u32[]{:S(2)}) collective-permute-start(bf16[512,2048]{1,0:T(8,128)(2,1)S(1)} %pack.28), channel_id=1, source_target_pairs={{0,2},{1,5},{2,0},{3,7},{4,6},{5,1},{6,4},{7,3},{8,10},{9,13},{10,... | collective-permute-start | bytes 6291464 | tf_op jit(solution)/shard_map/ppermute | solution.py:815
  282.9 28.3 %collective-permute-start.15 = (bf16[1024,1024]{1,0:T(8,128)(2,1)}, bf16[1024,1024]{1,0:T(8,128)(2,1)}, u32[]{:S(2)}, u32[]{:S(2)}) collective-permute-start(bf16[1024,1024]{1,0:T(8,128)(2,1)} %get-tuple-element.335), channel_id=1, source_target_pairs={{0,1},{1,0},{2,3},{3,2},{4,5},{5,4},{6,7},{7,6},{8,9},{9,8},{10,11... | collective-permute-start | bytes 6291464 | tf_op jit(solution)/shard_map/ppermute | solution.py:803
  285.6 25.6 %collective-permute-start.17 = (bf16[2,128,2048]{2,1,0:T(8,128)(2,1)S(1)}, bf16[2,128,2048]{2,1,0:T(8,128)(2,1)S(1)}, u32[]{:S(2)}, u32[]{:S(2)}) collective-permute-start(bf16[2,128,2048]{2,1,0:T(8,128)(2,1)S(1)} %pack.29), channel_id=1, source_target_pairs={{0,8},{1,9},{2,10},{3,11},{4,12},{5,13},{6,14},{7,15},{8,0},{9,1},... | collective-permute-start | bytes 3145736 | tf_op jit(solution)/shard_map/ppermute | solution.py:815
  311.2 34.8 %collective-permute-start.18 = (bf16[1024,2048]{1,0:T(8,128)(2,1)}, bf16[1024,2048]{1,0:T(8,128)(2,1)}, u32[]{:S(2)}, u32[]{:S(2)}) collective-permute-start(bf16[1024,2048]{1,0:T(8,128)(2,1)} %get-tuple-element.355), channel_id=1, source_target_pairs={{0,1},{1,0},{2,3},{3,2},{4,5},{5,4},{6,7},{7,6},{8,9},{9,8},{10,11... | collective-permute-start | bytes 12582920 | tf_op jit(solution)/shard_map/ppermute | solution.py:803
  311.3 34.7 %collective-permute-start.19 = (bf16[1024,2048]{1,0:T(8,128)(2,1)S(1)}, bf16[1024,2048]{1,0:T(8,128)(2,1)}, u32[]{:S(2)}, u32[]{:S(2)}) collective-permute-start(bf16[1024,2048]{1,0:T(8,128)(2,1)S(1)} %get-tuple-element.357), channel_id=1, source_target_pairs={{0,1},{1,0},{2,3},{3,2},{4,5},{5,4},{6,7},{7,6},{8,9},{9,8},{10,11... | collective-permute-start | bytes 12582920 | tf_op jit(solution)/shard_map/ppermute | solution.py:803
  313.9 32.1 %collective-permute-start.21 = (bf16[256,2048]{1,0:T(8,128)(2,1)S(1)}, bf16[256,2048]{1,0:T(8,128)(2,1)S(1)}, u32[]{:S(2)}, u32[]{:S(2)}) collective-permute-start(bf16[256,2048]{1,0:T(8,128)(2,1)S(1)} %pack.31), channel_id=1, source_target_pairs={{0,4},{1,3},{2,6},{3,1},{4,0},{5,7},{6,2},{7,5},{8,12},{9,11},{10,... | collective-permute-start | bytes 3145736 | tf_op jit(solution)/shard_map/ppermute | solution.py:815
  317.9 28.2 %collective-permute-start.20 = (bf16[512,1024]{1,0:T(8,128)(2,1)S(1)}, bf16[512,1024]{1,0:T(8,128)(2,1)S(1)}, u32[]{:S(2)}, u32[]{:S(2)}) collective-permute-start(bf16[512,1024]{1,0:T(8,128)(2,1)S(1)} %pack.30), channel_id=1, source_target_pairs={{0,2},{1,5},{2,0},{3,7},{4,6},{5,1},{6,4},{7,3},{8,10},{9,13},{10,... | collective-permute-start | bytes 3145736 | tf_op jit(solution)/shard_map/ppermute | solution.py:815
  320.5 25.5 %collective-permute-start.22 = (bf16[2,64,2048]{2,1,0:T(8,128)(2,1)S(1)}, bf16[2,64,2048]{2,1,0:T(8,128)(2,1)S(1)}, u32[]{:S(2)}, u32[]{:S(2)}) collective-permute-start(bf16[2,64,2048]{2,1,0:T(8,128)(2,1)S(1)} %pack.32), channel_id=1, source_target_pairs={{0,16},{1,17},{2,18},{3,19},{4,20},{5,21},{6,22},{7,23},{8,24},{9,... | collective-permute-start | bytes 1572872 | tf_op jit(solution)/shard_map/ppermute | solution.py:815
  351.3 54.2 %collective-permute-start.25 = (bf16[2,512,2048]{2,1,0:T(8,128)(2,1)S(1)}, bf16[2,512,2048]{2,1,0:T(8,128)(2,1)S(1)}, u32[]{:S(2)}, u32[]{:S(2)}) collective-permute-start(bf16[2,512,2048]{2,1,0:T(8,128)(2,1)S(1)} %pack.33), channel_id=1, source_target_pairs={{0,2},{1,5},{2,0},{3,7},{4,6},{5,1},{6,4},{7,3},{8,10},{9,13},{10,... | collective-permute-start | bytes 12582920 | tf_op jit(solution)/shard_map/ppermute | solution.py:815
  384.9 14.9 %collective-permute-start.27 = (bf16[256,1024]{1,0:T(8,128)(2,1)S(1)}, bf16[256,1024]{1,0:T(8,128)(2,1)S(1)}, u32[]{:S(2)}, u32[]{:S(2)}) collective-permute-start(bf16[256,1024]{1,0:T(8,128)(2,1)S(1)} %pack.35), channel_id=1, source_target_pairs={{0,4},{1,3},{2,6},{3,1},{4,0},{5,7},{6,2},{7,5},{8,12},{9,11},{10,... | collective-permute-start | bytes 1572872 | tf_op jit(solution)/shard_map/ppermute | solution.py:815
  385.5 14.2 %collective-permute-start.26 = (bf16[128,2048]{1,0:T(8,128)(2,1)S(1)}, bf16[128,2048]{1,0:T(8,128)(2,1)S(1)}, u32[]{:S(2)}, u32[]{:S(2)}) collective-permute-start(bf16[128,2048]{1,0:T(8,128)(2,1)S(1)} %pack.34), channel_id=1, source_target_pairs={{0,8},{1,9},{2,10},{3,11},{4,12},{5,13},{6,14},{7,15},{8,0},{9,1},... | collective-permute-start | bytes 1572872 | tf_op jit(solution)/shard_map/ppermute | solution.py:815
  405.5 41.7 %collective-permute-start.28 = (bf16[1024,2048]{1,0:T(8,128)(2,1)}, bf16[1024,2048]{1,0:T(8,128)(2,1)}, u32[]{:S(2)}, u32[]{:S(2)}) collective-permute-start(bf16[1024,2048]{1,0:T(8,128)(2,1)} %get-tuple-element.408), channel_id=1, source_target_pairs={{0,1},{1,0},{2,3},{3,2},{4,5},{5,4},{6,7},{7,6},{8,9},{9,8},{10,11... | collective-permute-start | bytes 12582920 | tf_op jit(solution)/shard_map/ppermute | solution.py:803
  411.7 35.4 %collective-permute-start.29 = (bf16[2,256,2048]{2,1,0:T(8,128)(2,1)}, bf16[2,256,2048]{2,1,0:T(8,128)(2,1)}, u32[]{:S(2)}, u32[]{:S(2)}) collective-permute-start(bf16[2,256,2048]{2,1,0:T(8,128)(2,1)} %pack.36), channel_id=1, source_target_pairs={{0,4},{1,3},{2,6},{3,1},{4,0},{5,7},{6,2},{7,5},{8,12},{9,11},{10,... | collective-permute-start | bytes 6291464 | tf_op jit(solution)/shard_map/ppermute | solution.py:815
  413.7 33.4 %collective-permute-start.31 = (bf16[128,1024]{1,0:T(8,128)(2,1)S(1)}, bf16[128,1024]{1,0:T(8,128)(2,1)}, u32[]{:S(2)}, u32[]{:S(2)}) collective-permute-start(bf16[128,1024]{1,0:T(8,128)(2,1)S(1)} %pack.38), channel_id=1, source_target_pairs={{0,8},{1,9},{2,10},{3,11},{4,12},{5,13},{6,14},{7,15},{8,0},{9,1},... | collective-permute-start | bytes 786440 | tf_op jit(solution)/shard_map/ppermute | solution.py:815
  416.6 30.5 %collective-permute-start.30 = (bf16[64,2048]{1,0:T(8,128)(2,1)}, bf16[64,2048]{1,0:T(8,128)(2,1)}, u32[]{:S(2)}, u32[]{:S(2)}) collective-permute-start(bf16[64,2048]{1,0:T(8,128)(2,1)} %pack.37), channel_id=1, source_target_pairs={{0,16},{1,17},{2,18},{3,19},{4,20},{5,21},{6,22},{7,23},{8,24},{9,... | collective-permute-start | bytes 786440 | tf_op jit(solution)/shard_map/ppermute | solution.py:815
  457.9 4.5 collective-permute-start.32
  457.9 4.7 collective-permute-start.33
  459.1 31.4 %collective-permute-start.37 = (bf16[512,2048]{1,0:T(8,128)(2,1)S(1)}, bf16[512,2048]{1,0:T(8,128)(2,1)}, u32[]{:S(2)}, u32[]{:S(2)}) collective-permute-start(bf16[512,2048]{1,0:T(8,128)(2,1)S(1)} %pack.39), channel_id=1, source_target_pairs={{0,2},{1,5},{2,0},{3,7},{4,6},{5,1},{6,4},{7,3},{8,10},{9,13},{10,... | collective-permute-start | bytes 6291464 | tf_op jit(solution)/shard_map/ppermute | solution.py:815
  460.7 29.8 %collective-permute-start.36 = (bf16[1024,1024]{1,0:T(8,128)(2,1)}, bf16[1024,1024]{1,0:T(8,128)(2,1)}, u32[]{:S(2)}, u32[]{:S(2)}) collective-permute-start(bf16[1024,1024]{1,0:T(8,128)(2,1)} %get-tuple-element.439), channel_id=1, source_target_pairs={{0,1},{1,0},{2,3},{3,2},{4,5},{5,4},{6,7},{7,6},{8,9},{9,8},{10,11... | collective-permute-start | bytes 6291464 | tf_op jit(solution)/shard_map/ppermute | solution.py:803
  461.8 6.4 %collective-permute-start.34 = (bf16[528,1024]{1,0:T(8,128)(2,1)S(1)}, bf16[528,1024]{1,0:T(8,128)(2,1)S(1)}, u32[]{:S(2)}, u32[]{:S(2)}) collective-permute-start(bf16[528,1024]{1,0:T(8,128)(2,1)S(1)} %copy-done.32), channel_id=1, source_target_pairs={{0,1},{1,0},{2,3},{3,2},{4,5},{5,4},{6,7},{7,6},{8,9},{9,8},{10,11... | collective-permute-start | bytes 3244040 | tf_op jit(solution)/shard_map/ppermute | solution.py:803
  462.4 28.2 %collective-permute-start.38 = (bf16[2,128,2048]{2,1,0:T(8,128)(2,1)}, bf16[2,128,2048]{2,1,0:T(8,128)(2,1)S(1)}, u32[]{:S(2)}, u32[]{:S(2)}) collective-permute-start(bf16[2,128,2048]{2,1,0:T(8,128)(2,1)} %copy-done.37), channel_id=1, source_target_pairs={{0,8},{1,9},{2,10},{3,11},{4,12},{5,13},{6,14},{7,15},{8,0},{9,1},... | collective-permute-start | bytes 3145736 | tf_op jit(solution)/shard_map/ppermute | solution.py:815
  462.6 15.1 %collective-permute-start.35 = (bf16[528,1024]{1,0:T(8,128)(2,1)}, bf16[528,1024]{1,0:T(8,128)(2,1)S(1)}, u32[]{:S(2)}, u32[]{:S(2)}) collective-permute-start(bf16[528,1024]{1,0:T(8,128)(2,1)} %copy-done.35), channel_id=1, source_target_pairs={{0,1},{1,0},{2,3},{3,2},{4,5},{5,4},{6,7},{7,6},{8,9},{9,8},{10,11... | collective-permute-start | bytes 3244040 | tf_op jit(solution)/shard_map/ppermute | solution.py:803
  468.2 20.1 %collective-permute-start.39 = (bf16[64,1024]{1,0:T(8,128)(2,1)S(1)}, bf16[64,1024]{1,0:T(8,128)(2,1)S(1)}, u32[]{:S(2)}, u32[]{:S(2)}) collective-permute-start(bf16[64,1024]{1,0:T(8,128)(2,1)S(1)} %pack.41), channel_id=1, source_target_pairs={{0,16},{1,17},{2,18},{3,19},{4,20},{5,21},{6,22},{7,23},{8,24},{9,... | collective-permute-start | bytes 393224 | tf_op jit(solution)/shard_map/ppermute | solution.py:815
  477.7 25.6 %collective-permute-start.41 = (f32[16,18,64]{2,1,0:T(8,128)S(1)}, f32[16,18,64]{2,1,0:T(8,128)S(1)}, u32[]{:S(2)}, u32[]{:S(2)}) collective-permute-start(f32[16,18,64]{2,1,0:T(8,128)S(1)} %bitcast.70), channel_id=1, source_target_pairs={{0,1},{1,0},{2,3},{3,2},{4,5},{5,4},{6,7},{7,6},{8,9},{9,8},{10,11... | collective-permute-start | bytes 221192 | tf_op jit(solution)/shard_map/ppermute | solution.py:803
  493.5 34.4 %collective-permute-start.43 = (bf16[2,64,2048]{2,1,0:T(8,128)(2,1)S(1)}, bf16[2,64,2048]{2,1,0:T(8,128)(2,1)}, u32[]{:S(2)}, u32[]{:S(2)}) collective-permute-start(bf16[2,64,2048]{2,1,0:T(8,128)(2,1)S(1)} %pack.44), channel_id=1, source_target_pairs={{0,16},{1,17},{2,18},{3,19},{4,20},{5,21},{6,22},{7,23},{8,24},{9,... | collective-permute-start | bytes 1572872 | tf_op jit(solution)/shard_map/ppermute | solution.py:815
  496.8 31.1 %collective-permute-start.42 = (bf16[256,2048]{1,0:T(8,128)(2,1)S(1)}, bf16[256,2048]{1,0:T(8,128)(2,1)}, u32[]{:S(2)}, u32[]{:S(2)}) collective-permute-start(bf16[256,2048]{1,0:T(8,128)(2,1)S(1)} %pack.43), channel_id=1, source_target_pairs={{0,4},{1,3},{2,6},{3,1},{4,0},{5,7},{6,2},{7,5},{8,12},{9,11},{10,... | collective-permute-start | bytes 3145736 | tf_op jit(solution)/shard_map/ppermute | solution.py:815
  500.7 27.2 %collective-permute-start.40 = (bf16[512,1024]{1,0:T(8,128)(2,1)S(1)}, bf16[512,1024]{1,0:T(8,128)(2,1)}, u32[]{:S(2)}, u32[]{:S(2)}) collective-permute-start(bf16[512,1024]{1,0:T(8,128)(2,1)S(1)} %pack.42), channel_id=1, source_target_pairs={{0,2},{1,5},{2,0},{3,7},{4,6},{5,1},{6,4},{7,3},{8,10},{9,13},{10,... | collective-permute-start | bytes 3145736 | tf_op jit(solution)/shard_map/ppermute | solution.py:815
  504.0 19.5 %collective-permute-start.46 = (f32[4,18,64]{2,1,0:T(8,128)S(1)}, f32[4,18,64]{2,1,0:T(8,128)S(1)}, u32[]{:S(2)}, u32[]{:S(2)}) collective-permute-start(f32[4,18,64]{2,1,0:T(8,128)S(1)} %get-tuple-element.566), channel_id=1, source_target_pairs={{0,6},{1,7},{2,4},{3,5},{4,2},{5,3},{6,0},{7,1},{8,14},{9,15},{10,... | collective-permute-start | bytes 55304 | tf_op jit(solution)/shard_map/ppermute | solution.py:815
  506.6 18.5 %collective-permute-start.45 = (f32[4,18,64]{2,1,0:T(8,128)}, f32[4,18,64]{2,1,0:T(8,128)}, u32[]{:S(2)}, u32[]{:S(2)}) collective-permute-start(f32[4,18,64]{2,1,0:T(8,128)} %get-tuple-element.567), channel_id=1, source_target_pairs={{0,2},{1,3},{2,0},{3,1},{4,6},{5,7},{6,4},{7,5},{8,10},{9,11},{10,... | collective-permute-start | bytes 55304 | tf_op jit(solution)/shard_map/ppermute | solution.py:815
  531.9 18.2 %collective-permute-start.48 = (bf16[64,2048]{1,0:T(8,128)(2,1)S(1)}, bf16[64,2048]{1,0:T(8,128)(2,1)S(1)}, u32[]{:S(2)}, u32[]{:S(2)}) collective-permute-start(bf16[64,2048]{1,0:T(8,128)(2,1)S(1)} %pack.45), channel_id=1, source_target_pairs={{0,16},{1,17},{2,18},{3,19},{4,20},{5,21},{6,22},{7,23},{8,24},{9,... | collective-permute-start | bytes 786440 | tf_op jit(solution)/shard_map/ppermute | solution.py:815
  533.5 16.5 %collective-permute-start.49 = (bf16[64,2048]{1,0:T(8,128)(2,1)S(1)}, bf16[64,2048]{1,0:T(8,128)(2,1)S(1)}, u32[]{:S(2)}, u32[]{:S(2)}) collective-permute-start(bf16[64,2048]{1,0:T(8,128)(2,1)S(1)} %pack.46), channel_id=1, source_target_pairs={{0,8},{1,9},{2,10},{3,11},{4,12},{5,13},{6,14},{7,15},{8,0},{9,1},... | collective-permute-start | bytes 786440 | tf_op jit(solution)/shard_map/ppermute | solution.py:815
  533.5 16.5 %collective-permute-start.50 = (bf16[64,2048]{1,0:T(8,128)(2,1)S(1)}, bf16[64,2048]{1,0:T(8,128)(2,1)S(1)}, u32[]{:S(2)}, u32[]{:S(2)}) collective-permute-start(bf16[64,2048]{1,0:T(8,128)(2,1)S(1)} %pack.47), channel_id=1, source_target_pairs={{0,24},{1,25},{2,26},{3,27},{4,28},{5,29},{6,30},{7,31},{8,16},{9,... | collective-permute-start | bytes 786440 | tf_op jit(solution)/shard_map/ppermute | solution.py:815
  537.1 12.5 %collective-permute-start.51 = (f32[2,18,64]{2,1,0:T(8,128)S(1)}, f32[2,18,64]{2,1,0:T(8,128)S(1)}, u32[]{:S(2)}, u32[]{:S(2)}) collective-permute-start(f32[2,18,64]{2,1,0:T(8,128)S(1)} %slice_add_fusion.3), channel_id=1, source_target_pairs={{0,8},{1,9},{2,10},{3,11},{4,12},{5,13},{6,14},{7,15},{8,0},{9,1},... | collective-permute-start | bytes 27656 | tf_op jit(solution)/shard_map/ppermute | solution.py:815
  540.8 9.3 %collective-permute-start.47 = (bf16[256,1024]{1,0:T(8,128)(2,1)S(1)}, bf16[256,1024]{1,0:T(8,128)(2,1)S(1)}, u32[]{:S(2)}, u32[]{:S(2)}) collective-permute-start(bf16[256,1024]{1,0:T(8,128)(2,1)S(1)} %pack.48), channel_id=1, source_target_pairs={{0,4},{1,3},{2,6},{3,1},{4,0},{5,7},{6,2},{7,5},{8,12},{9,11},{10,... | collective-permute-start | bytes 1572872 | tf_op jit(solution)/shard_map/ppermute | solution.py:815
  555.9 15.9 %collective-permute-start.52 = (bf16[64,1024]{1,0:T(8,128)(2,1)S(1)}, bf16[64,1024]{1,0:T(8,128)(2,1)S(1)}, u32[]{:S(2)}, u32[]{:S(2)}) collective-permute-start(bf16[64,1024]{1,0:T(8,128)(2,1)S(1)} %pack.49), channel_id=1, source_target_pairs={{0,16},{1,17},{2,18},{3,19},{4,20},{5,21},{6,22},{7,23},{8,24},{9,... | collective-permute-start | bytes 393224 | tf_op jit(solution)/shard_map/ppermute | solution.py:815
  560.7 11.1 %collective-permute-start.53 = (bf16[64,1024]{1,0:T(8,128)(2,1)S(1)}, bf16[64,1024]{1,0:T(8,128)(2,1)S(1)}, u32[]{:S(2)}, u32[]{:S(2)}) collective-permute-start(bf16[64,1024]{1,0:T(8,128)(2,1)S(1)} %pack.50), channel_id=1, source_target_pairs={{0,8},{1,9},{2,10},{3,11},{4,12},{5,13},{6,14},{7,15},{8,0},{9,1},... | collective-permute-start | bytes 393224 | tf_op jit(solution)/shard_map/ppermute | solution.py:815
  560.7 11.1 %collective-permute-start.54 = (bf16[64,1024]{1,0:T(8,128)(2,1)S(1)}, bf16[64,1024]{1,0:T(8,128)(2,1)S(1)}, u32[]{:S(2)}, u32[]{:S(2)}) collective-permute-start(bf16[64,1024]{1,0:T(8,128)(2,1)S(1)} %pack.51), channel_id=1, source_target_pairs={{0,24},{1,25},{2,26},{3,27},{4,28},{5,29},{6,30},{7,31},{8,16},{9,... | collective-permute-start | bytes 393224 | tf_op jit(solution)/shard_map/ppermute | solution.py:815
  563.2 8.6 %collective-permute-start.55 = (f32[1,18,64]{2,1,0:T(8,128)S(1)}, f32[1,18,64]{2,1,0:T(8,128)S(1)}, u32[]{:S(2)}, u32[]{:S(2)}) collective-permute-start(f32[1,18,64]{2,1,0:T(8,128)S(1)} %slice_add_fusion.4), channel_id=1, source_target_pairs={{0,16},{1,17},{2,18},{3,19},{4,20},{5,21},{6,22},{7,23},{8,24},{9,... | collective-permute-start | bytes 13832 | tf_op jit(solution)/shard_map/ppermute | solution.py:815
  (93 other events, 996.7 us)

commit v4 on v3

--- a/solution.py
+++ b/solution.py
@@ -17,7 +17,7 @@
 GROUP = 256
 HEADS_IN_GROUP = GROUP // HD
 MIB = 1024 * 1024
-SCALE = 0.5
+SCALE = 0.1
 
 
 def cost(microseconds):
@@ -349,7 +349,7 @@
         compiler_params=pltpu.CompilerParams(vmem_limit_bytes=22 * MIB),
         cost_estimate=cost(14),
         name="entry_forward",
-    )(coords, residual, skip_rows, wa, wb, bias, gain, shift, qa, qb)
+    )(coords, residual, skip_rows, _far(wa), _far(wb), bias, gain, shift, _far(qa), _far(qb))
 
 
 def _mlp_kernel(names, plan, coords_ref, *refs):
@@ -794,7 +794,7 @@
         out_specs=out_spec,
         out_shape=out_shape,
         compiler_params=pltpu.CompilerParams(vmem_limit_bytes=12 * MIB),
-        cost_estimate=cost(3 * (stop - start) * columns * lead / 2**20),
+        cost_estimate=cost(80),
         name="pack",
     )(*operands)
 
@@ -846,7 +846,7 @@
             return pack(self.parts, start, stop)
         return self.span(start, stop)
 
-    def send(self, gate, count=1):
+    def send(self, gate, count=1, hold=()):
         bits, self.order = self.order[:count], self.order[count:]
         held = lax.optimization_barrier(([arrays for arrays, _ in self.parts], gate))[0]
         self.parts = [(arrays, at) for arrays, (_, at) in zip(held, self.parts)]
@@ -856,7 +856,8 @@
             start = block * self.length
             sent.append(self.piece(start, start + self.length))
             across = [bit for place, bit in enumerate(reversed(bits)) if (block >> place) & 1]
-            got.append(swap_bits(sent[-1], across, self.size, self.crossed))
+            ready = after(sent[-1], *hold) if hold else sent[-1]
+            got.append(swap_bits(ready, across, self.size, self.crossed))
         self.parts += [((value,), 0) for value in got]
         return sent, got
 
@@ -940,24 +941,19 @@
         return dict(xa=residual, xb=skip_rows, hidden=hidden, normed=normed, q=q, kv=kv, kv_other=kv_other,
                     attended=attended, exact=exact, e=e, ex=ex, il=il)
 
-    items, result, flying = {}, {}, []
+    items, result, flying, crossing = {}, {}, [], []
 
     def add(name, layer, own, *peer):
         theirs = tuple(swap_cores(value) for value in peer)
-        flying.extend(theirs)
+        crossing.extend(theirs)
         items[name, layer] = Reduction([own, theirs], order, size, own.ndim - 2)
 
-    def settle(gate):
-        gate = after(gate, *flying)
-        flying.clear()
-        return gate
-
-    def sends(gate, *keys, count=1):
+    def sends(gate, *keys, count=1, hold=()):
         made = []
         for key in keys:
             item = items[key]
             if item.order:
-                sent, got = item.send(gate, count)
+                sent, got = item.send(gate, count, hold)
                 made.extend(sent)
                 flying.extend(got)
             elif key not in result:
@@ -965,7 +961,15 @@
                 made.append(result[key])
         return after(gate, *made) if made else gate
 
-    def back(layer, kept, mid, dattn, *keys):
+    def turn(gate, early=(), late=(), made=()):
+        gate = after(gate, *crossing)
+        crossing.clear()
+        waiting = list(flying)
+        flying.clear()
+        gate = sends(sends(gate, *early), *made, hold=waiting)
+        return sends(after(gate, *waiting), *late)
+
+    def back(layer, kept, mid, dattn, keys, then):
         dq, dk, dk_other, dv, dv_other = attn_backward(
             kept["q"], kept["kv"], kept["kv_other"], dattn, kept["exact"], kept["e"], kept["ex"], kept["il"]
         )
@@ -973,14 +977,13 @@
             size, order, coords, dq, dk, swap_cores(dk_other), dv, swap_cores(dv_other), mid["dmid"], kept["normed"],
             kept["attended"],
         )
-        dkv = settle(dkv)
+        dkv = turn(dkv, (), keys)
         add("head", layer, own, after(peer, dkv))
-        dkv = sends(dkv, *keys)
         own, peer, gradient, skip_grad, sums = entry_backward(
             layer, size, order, coords, dq, dkv, mid["dmid"], kept["hidden"], kept["xa"], kept["xb"], attn_norm_gain,
             qkv_turned, qkv_peer, skip_weight, skip_peer,
         )
-        gradient = settle(gradient)
+        gradient = turn(gradient, *then)
         add("skip", layer, own, after(peer, gradient))
         return gradient, skip_grad, sums
 
@@ -994,24 +997,25 @@
     one = mlp(1, True, False, True, True, ("peer",), size, order_mlp, values)
     values.update(normed=one["normed_out"], middle=one["middle_out"], acc=one["acc_out"], dn=one["dn_out"])
     theirs = tuple(swap_cores(one[name]) for name in ("down_grad", "up_grad"))
-    flying.extend(theirs)
+    crossing.extend(theirs)
     two = mlp(1, False, True, True, True, ("own",), size, order, values)
     items["mlp", 1] = Reduction([two["grads_own"], theirs], order, size, 1)
-    dattn = sends(settle(two["dattn"]), ("mlp", 1))
-    gradient, skip_grad1, sums1 = back(1, kept[1], two, dattn, ("mlp", 1))
-    gradient = sends(gradient, ("head", 1), ("mlp", 1))
+    dattn = turn(two["dattn"], (("mlp", 1),))
+    gradient, skip_grad1, sums1 = back(1, kept[1], two, dattn, (("mlp", 1),), ((("head", 1),), (("mlp", 1),)))
 
     values = {**weights, **kept[0], **mid0, "normed": mid0["normed_out"], "middle": mid0["middle_out"], "grad": gradient}
     one0 = mlp(0, True, False, False, True, ("peer",), size, order, values)
-    gate = settle(one0["dn_out"])
+    gate = turn(one0["dn_out"], (("skip", 1),), (("head", 1), ("mlp", 1)))
     peers = [after(one0[name], gate) for name in ("down_grad", "up_grad")]
     theirs = tuple(swap_cores(value) for value in peers)
-    flying.extend(theirs)
-    values.update(dn=sends(gate, ("skip", 1), ("head", 1), ("mlp", 1)))
+    crossing.extend(theirs)
+    values.update(dn=gate)
     low = mlp(0, False, True, False, True, ("own",), size, order, values)
     items["mlp", 0] = Reduction([low["grads_own"], theirs], order, size, 1)
-    dattn = sends(settle(low["dattn"]), ("mlp", 0), ("head", 1), ("mlp", 1), ("skip", 1))
-    gradient, skip_grad0, sums0 = back(0, kept[0], low, dattn, ("mlp", 0), ("head", 1), ("skip", 1))
+    dattn = turn(low["dattn"], (), (("head", 1), ("mlp", 1), ("skip", 1)), (("mlp", 0),))
+    gradient, skip_grad0, sums0 = back(
+        0, kept[0], low, dattn, (("mlp", 0), ("head", 1), ("skip", 1)), ((("head", 0),), (("mlp", 0), ("skip", 1)))
+    )
     shared = jnp.concatenate([low["sums"][:4], two["sums"][:4], sums0[:3], sums1[:3]], axis=0)
     items["vectors", 0] = sum_vectors(
         shared,
@@ -1020,20 +1024,19 @@
         size,
     )
     rest = bits - 2
-    finish = sends(gradient, ("head", 0), ("mlp", 0), ("skip", 1), ("head", 1))
-    others = [swap_cores(after(value, finish)) for value in (gradient, skip_grad0, skip_grad1, two["result"])]
-    input_grad = gather_rows(core, (after(gradient, finish), others[0]))
+    others = [swap_cores(after(value, gradient)) for value in (gradient, skip_grad0, skip_grad1, two["result"])]
+    input_grad = gather_rows(core, (gradient, others[0]))
     skip_grad = gather_rows(core, (after(skip_grad0, input_grad), others[1]), (skip_grad1, others[2]))
     output = gather_rows(core, (after(two["result"], skip_grad), others[3]))
-    finish = settle(after(finish, output))
-    finish = sends(finish, ("head", 0), ("skip", 0), ("mlp", 0), ("skip", 1))
-    finish = settle(sends(finish, ("vectors", 0), count=2))
+    finish = turn(after(gradient, output), (("skip", 0),), (("mlp", 0), ("head", 0), ("skip", 1)))
+    finish = sends(finish, ("vectors", 0), count=2)
+    finish = turn(finish)
     finish = sends(finish, ("head", 0), count=rest)
-    finish = settle(sends(finish, ("skip", 0), ("vectors", 0), ("mlp", 0)))
+    finish = turn(sends(finish, ("skip", 0), ("vectors", 0), ("mlp", 0), ("head", 1)))
     finish = sends(finish, ("skip", 0), count=rest)
-    finish = settle(sends(finish, ("vectors", 0), ("head", 0)))
+    finish = turn(sends(finish, ("vectors", 0), ("head", 0)))
     while len(result) < len(items):
-        finish = settle(sends(finish, *items))
+        finish = turn(sends(finish, *items))
     count = shared.shape[0]
     vectors = result["vectors", 0][0, :count]
     up_bias_grad = result["vectors", 0][0, count:].reshape(layers, -1)

time: 582 us -> 560 us (0.962)
  waiting for transfers between devices: 106 us -> 87.9 us
  local copies, waits for them, and re-layouts: 54.9 us -> 48.2 us
    ppermute x31, waiting for transfers between devices: 78.7 us -> 63.6 us  [swap_bits(): return lax.ppermute(value, ('dp', 'tensor'), pairs)]
    unnamed x170 -> x142, local copies, waits for them, and re-layouts: 35.7 us -> 29.6 us
  transfers between devices with their start and end apart: 56 -> 56, of which waited for: 22 -> 20; matrix products, arithmetic and copies ran while one was open for 6% -> 6% of each run, Pallas kernels for 40% -> 41%
where the time goes in v4:
time: 560 us; the launch traced here: 555 us
  Pallas kernels  347 us (62%)
  waiting for transfers between devices  87.9 us (16%)
  starting transfers between devices  49.7 us (9%)
  local copies, waits for them, and re-layouts  48.2 us (9%)
  other arithmetic  20.2 us (4%)
    pallas_call x5, Pallas kernels, mlp(): pl.pallas_call(functools.partial(_mlp_kernel, (*names, *out_names, *scrat...  110 us
    ppermute x31, waiting for transfers between devices, swap_bits(): return lax.ppermute(value, ('dp', 'tensor'), pairs)  63.6 us
    pallas_call x26, Pallas kernels, pack(): pl.pallas_call(functools.partial(_pack_kernel, tuple((len(arrays) for arr...  60.6 us
    pallas_call x2, Pallas kernels, attn_backward(): pl.pallas_call(_attn_bwd_kernel, grid=(groups,), in_specs=[near(0), near(...  46.8 us
    ppermute x31, starting transfers between devices, swap_bits(): return lax.ppermute(value, ('dp', 'tensor'), pairs)  44.3 us
    pallas_call x2, Pallas kernels, attn_forward(): pl.pallas_call(_attn_fwd_kernel, grid=(groups,), in_specs=[near(0), near(...  38.4 us
    pallas_call x2, Pallas kernels, entry_backward(): pl.pallas_call(functools.partial(_entry_back_kernel, layer, pieces, order...  34.5 us
    unnamed x142, local copies, waits for them, and re-layouts  29.6 us
  transfers between devices with their start and end apart: 56, of which 20 were waited for; matrix products, arithmetic and copies ran while one was open for 6% of the time, Pallas kernels for 41%

profile of v4, /device:TPU:0, one launch (start us, length us, event | category | flops | bytes accessed | tf_op | source)
XLA Modules:
  0.0 554.9 jit_solution(16866749038787114242)
XLA Ops:
  1.9 3.0 constant_dynamic-slice_fusion.2
  10.7 6.6 %collective-permute-done.wb_ref = bf16[2,1,1024,1024]{3,2,1,0:T(8,128)(2,1)} collective-permute-done((bf16[2,1,1024,1024]{3,2,1,0:T(8,128)(2,1)}, bf16[2,1,1024,1024]{3,2,1,0:T(8,128)(2,1)}, u32[]{:S(2)}, u32[]{:S(2)}) %collective-permute-start) | collective-permute-done | bytes 4194336 | tf_op jit(solution)/shard_map/ppermute | solution.py:803
  19.7 14.4 %entry_forward.2 = (f32[528,1024]{1,0:T(8,128)}, bf16[528,1024]{1,0:T(8,128)(2,1)}, bf16[528,1024]{1,0:T(8,128)(2,1)}, bf16[528,2048]{1,0:T(8,128)(2,1)}) custom-call(s32[2]{0:T(128)S(1)} %pad_add_fusion.coords_ref, bf16[528,1024]{1,0:T(8,128)(2,1)S(1)} %get-tuple-element.601.xa_ref, bf16[528,1024]{1,0:T(8,128)(2,1)S(1)} %get-tuple-element.583.xb_ref, ...), custom_call_target="tpu_custom_call" | custom-call | flops 1 | bytes 4900000 | tf_op jit(solution)/shard_map/entry_forward/pallas_call | solution.py:329
  34.7 3.5 collective-permute-done.4.refs_10_.refs_11_
  41.2 19.2 %attn_forward.2 = (bf16[528,1024]{1,0:T(8,128)(2,1)}, f32[528,1024]{1,0:T(8,128)}, bf16[16,528,1024]{2,1,0:T(8,128)(2,1)}, f32[4,528,16]{2,1,0:T(8,128)}, f32[4,528,16]{2,1,0:T(8,128)}) custom-call(bf16[528,1024]{1,0:T(8,128)(2,1)S(1)} %copy-done.11, bf16[528,2048]{1,0:T(8,128)(2,1)} %get-tuple-element.285.km_ref.vm_ref, ...), custom_call_target="tpu_custom_call" | custom-call | flops 1 | bytes 6650000 | tf_op jit(solution)/shard_map/attn_forward/pallas_call | solution.py:91
  61.7 24.5 %mlp_f_peer_own.1 = (f32[528,1024]{1,0:T(8,128)}, bf16[528,1024]{1,0:T(8,128)(2,1)}, bf16[528,1024]{1,0:T(8,128)(2,1)S(1)}, bf16[528,2048]{1,0:T(8,128)(2,1)}, b...) custom-call(s32[2]{0:T(128)S(1)} %pad_add_fusion.coords_ref, ...), custom_call_target="tpu_custom_call" | custom-call | flops 1 | bytes 9800000 | tf_op jit(solution)/shard_map/mlp_f_peer_own/pallas_call | solution.py:553
  86.3 13.6 %entry_forward.3 = (f32[528,1024]{1,0:T(8,128)}, bf16[528,1024]{1,0:T(8,128)(2,1)}, bf16[528,1024]{1,0:T(8,128)(2,1)}, bf16[528,2048]{1,0:T(8,128)(2,1)}) custom-call(s32[2]{0:T(128)S(1)} %pad_add_fusion.coords_ref, bf16[528,1024]{1,0:T(8,128)(2,1)S(1)} %get-tuple-element.291.xa_ref, bf16[528,1024]{1,0:T(8,128)(2,1)S(1)} %get-tuple-element.582.xb_ref, ...), custom_call_target="tpu_custom_call" | custom-call | flops 1 | bytes 4900000 | tf_op jit(solution)/shard_map/entry_forward/pallas_call | solution.py:329
  100.0 4.3 collective-permute-done.7.ko_ref.vo_ref
  106.9 19.2 %attn_forward.3 = (bf16[528,1024]{1,0:T(8,128)(2,1)}, f32[528,1024]{1,0:T(8,128)}, bf16[16,528,1024]{2,1,0:T(8,128)(2,1)}, f32[4,528,16]{2,1,0:T(8,128)}, f32[4,528,16]{2,1,0:T(8,128)}) custom-call(bf16[528,1024]{1,0:T(8,128)(2,1)S(1)} %copy-done.12, bf16[528,2048]{1,0:T(8,128)(2,1)} %get-tuple-element.294.km_ref.vm_ref, ...), custom_call_target="tpu_custom_call" | custom-call | flops 1 | bytes 6650000 | tf_op jit(solution)/shard_map/attn_forward/pallas_call | solution.py:91
  127.4 25.8 %mlp_fb_peer.1 = (f32[528,1024]{1,0:T(8,128)}, bf16[528,1024]{1,0:T(8,128)(2,1)}, f32[528,1024]{1,0:T(8,128)S(1)}, f32[528,1024]{1,0:T(8,128)}, bf16[1024,2048]{...) custom-call(s32[2]{0:T(128)S(1)} %pad_add_fusion.coords_ref, ...), custom_call_target="tpu_custom_call" | custom-call | flops 1 | bytes 11200000 | tf_op jit(solution)/shard_map/mlp_fb_peer/pallas_call | solution.py:553
  156.3 27.3 %mlp_fb_own.1 = (bf16[528,1024]{1,0:T(8,128)(2,1)S(1)}, f32[8,1024]{1,0:T(8,128)S(1)}, f32[528,1024]{1,0:T(8,128)}, bf16[528,1024]{1,0:T(8,128)(2,1)S(1)}, bf16[...) custom-call(s32[2]{0:T(128)S(1)} %pad_add_fusion.coords_ref, bf16[528,1024]{1,0:T(8,128)(2,1)S(1)} %copy-done.21, ...), custom_call_target="tpu_custom_call" | custom-call | flops 1 | bytes 11200000 | tf_op jit(solution)/shard_map/mlp_fb_own/pallas_call | solution.py:553
  184.6 4.4 pack.26
  189.0 2.7 collective-permute-start.12
  191.7 23.4 %attn_backward.2 = (bf16[528,1024]{1,0:T(8,128)(2,1)S(1)}, bf16[528,1024]{1,0:T(8,128)(2,1)S(1)}, bf16[528,1024]{1,0:T(8,128)(2,1)S(1)}, bf16[528,1024]{1,0:T(8,128)(2,1)S(1)}, bf16[528,1024]{1,0:T(8,128)(2,1)S(1)}) custom-call(bf16[528,1024]{1,0:T(8,128)(2,1)} %get-tuple-element.293.q_ref, bf16[528,2048]{1,0:T(8,128)(2,1)} %get-tuple-element.294.km_ref.vm_ref, ...), custom_call_target="tpu_custom_call" | custom-call | flops 1 | bytes 8050000 | tf_op jit(solution)/shard_map/attn_backward/pallas_call | solution.py:192
  219.5 8.7 %head_gradients.2 = (bf16[1024,2048]{1,0:T(8,128)(2,1)}, bf16[1024,2048]{1,0:T(8,128)(2,1)}, bf16[528,2048]{1,0:T(8,128)(2,1)S(1)}) custom-call(s32[2]{0:T(128)S(1)} %pad_add_fusion.coords_ref, bf16[528,1024]{1,0:T(8,128)(2,1)S(1)} %get-tuple-element.315.dq_ref, bf16[528,1024]{1,0:T(8,128)(2,1)S(1)} %get-tuple-element.316.dk_ref, ...), custom_call_target="tpu_custom_call" | custom-call | flops 1 | bytes 4550000 | tf_op jit(solution)/shard_map/head_gradients/pallas_call | solution.py:611
  228.1 10.1 %collective-permute-done.12.refs_3_ = bf16[2,512,2048]{2,1,0:T(8,128)(2,1)S(1)} collective-permute-done((bf16[2,512,2048]{2,1,0:T(8,128)(2,1)S(1)}, bf16[2,512,2048]{2,1,0:T(8,128)(2,1)S(1)}, u32[]{:S(2)}, u32[]{:S(2)}) %collective-permute-start.12) | collective-permute-done | bytes 4194336 | tf_op jit(solution)/shard_map/ppermute | solution.py:815
  240.2 3.3 pack.27
  247.3 16.9 %entry_backward.2 = (bf16[1024,1024]{1,0:T(8,128)(2,1)}, bf16[1024,1024]{1,0:T(8,128)(2,1)}, f32[528,1024]{1,0:T(8,128)S(1)}, bf16[528,1024]{1,0:T(8,128)(2,1)S(1)}, f32[8,1024]{1,0:T(8,128)S(1)}) custom-call(s32[2]{0:T(128)S(1)} %pad_add_fusion.coords_ref, bf16[528,1024]{1,0:T(8,128)(2,1)S(1)} %get-tuple-element.315.dq_ref, ...), custom_call_target="tpu_custom_call" | custom-call | flops 1 | bytes 7000000 | tf_op jit(solution)/shard_map/entry_backward/pallas_call | solution.py:697
  264.2 3.5 pack.28
  271.0 2.7 pack.29
  277.4 14.8 %mlp_b_peer.1 = (f32[528,1024]{1,0:T(8,128)S(1)}, bf16[1024,2048]{1,0:T(8,128)(2,1)}, bf16[1024,2048]{1,0:T(8,128)(2,1)S(1)}, f32[1,2048]{1,0:T(1,128)S(1)}) custom-call(s32[2]{0:T(128)S(1)} %pad_add_fusion.coords_ref, bf16[528,1024]{1,0:T(8,128)(2,1)S(1)} %copy-done.10, f32[528,1024]{1,0:T(8,128)S(1)} %get-tuple-element.343.refs_1_, ...), custom_call_target="tpu_custom_call" | custom-call | flops 1 | bytes 6300000 | tf_op jit(solution)/shard_map/mlp_b_peer/pallas_call | solution.py:553
  294.3 2.4 pack.30
  296.7 4.4 collective-permute-done.17.refs_5_
  309.1 2.6 collective-permute-start.22
  311.7 17.5 %mlp_b_own.1 = (f32[8,1024]{1,0:T(8,128)S(1)}, f32[528,1024]{1,0:T(8,128)S(1)}, bf16[528,1024]{1,0:T(8,128)(2,1)S(1)}, bf16[2,1024,2048]{2,1,0:T(8,128)(2,1)}, f32[1,2048]{1,0:T(1,128)S(1)}) custom-call(s32[2]{0:T(128)S(1)} %pad_add_fusion.coords_ref, bf16[528,1024]{1,0:T(8,128)(2,1)S(1)} %copy-done.10, f32[528,1024]{1,0:T(8,128)S(1)} %get-tuple-element.343.refs_1_, ...), custom_call_target="tpu_custom_call" | custom-call | flops 1 | bytes 6300000 | tf_op jit(solution)/shard_map/mlp_b_own/pallas_call | solution.py:553
  329.8 5.2 pack.33
  341.3 2.8 convert_add_fusion.1
  344.2 23.3 %attn_backward.3 = (bf16[528,1024]{1,0:T(8,128)(2,1)S(1)}, bf16[528,1024]{1,0:T(8,128)(2,1)S(1)}, bf16[528,1024]{1,0:T(8,128)(2,1)S(1)}, bf16[528,1024]{1,0:T(8,128)(2,1)S(1)}, bf16[528,1024]{1,0:T(8,128)(2,1)S(1)}) custom-call(bf16[528,1024]{1,0:T(8,128)(2,1)} %get-tuple-element.284.q_ref, bf16[528,2048]{1,0:T(8,128)(2,1)} %get-tuple-element.285.km_ref.vm_ref, ...), custom_call_target="tpu_custom_call" | custom-call | flops 1 | bytes 8050000 | tf_op jit(solution)/shard_map/attn_backward/pallas_call | solution.py:192
  371.8 8.6 %head_gradients.3 = (bf16[1024,2048]{1,0:T(8,128)(2,1)}, bf16[1024,2048]{1,0:T(8,128)(2,1)}, bf16[528,2048]{1,0:T(8,128)(2,1)S(1)}) custom-call(s32[2]{0:T(128)S(1)} %pad_add_fusion.coords_ref, bf16[528,1024]{1,0:T(8,128)(2,1)S(1)} %get-tuple-element.399.dq_ref, bf16[528,1024]{1,0:T(8,128)(2,1)S(1)} %get-tuple-element.400.dk_ref, ...), custom_call_target="tpu_custom_call" | custom-call | flops 1 | bytes 4550000 | tf_op jit(solution)/shard_map/head_gradients/pallas_call | solution.py:611
  380.5 2.5 collective-permute-done.27.refs_3_
  382.9 6.3 %collective-permute-done.25.refs_3_ = bf16[2,512,2048]{2,1,0:T(8,128)(2,1)S(1)} collective-permute-done((bf16[2,512,2048]{2,1,0:T(8,128)(2,1)S(1)}, bf16[2,512,2048]{2,1,0:T(8,128)(2,1)S(1)}, u32[]{:S(2)}, u32[]{:S(2)}) %collective-permute-start.25) | collective-permute-done | bytes 4194336 | tf_op jit(solution)/shard_map/ppermute | solution.py:815
  389.3 2.8 pack.38
  392.1 4.2 pack.36
  409.8 17.6 %entry_backward.3 = (bf16[1024,1024]{1,0:T(8,128)(2,1)}, bf16[1024,1024]{1,0:T(8,128)(2,1)}, bf16[528,1024]{1,0:T(8,128)(2,1)}, bf16[528,1024]{1,0:T(8,128)(2,1)}, f32[8,1024]{1,0:T(8,128)S(1)}) custom-call(s32[2]{0:T(128)S(1)} %pad_add_fusion.coords_ref, bf16[528,1024]{1,0:T(8,128)(2,1)S(1)} %get-tuple-element.399.dq_ref, bf16[528,2048]{1,0:T(8,128)(2,1)S(1)} %copy-done.14, ...), custom_call_target="tpu_custom_call" | custom-call | flops 1 | bytes 7000000 | tf_op jit(solution)/shard_map/entry_backward/pallas_call | solution.py:697
  427.4 3.3 pack.39
  432.1 2.8 pack.40
  441.4 4.8 collective-permute-done.34.refs_3_
  446.9 3.2 gather_rows.3
  450.0 6.3 %gather_rows.4 = bf16[1026,2,1024]{2,1,0:T(2,128)(2,1)} custom-call(s32[1]{0:T(128)} %bitcast.core_ref, bf16[528,1024]{1,0:T(8,128)(2,1)} %get-tuple-element.446.refs_0_, bf16[528,1024]{1,0:T(8,128)(2,1)} %collective-permute-done.33.refs_1_, bf16[528,1024]{1,0:T(8,128)(2,1)S(1)} %copy-done.23, bf16[528,1024]{1,0:T(8,128)(2,1)S(1)} %collective-permute-done.34.refs_3_), custom_call_target="tpu_custom_call" | custom-call | flops 1 | bytes 1050000 | tf_op jit(solution)/shard_map/gather_rows/pallas_call | solution.py:746
  460.6 6.5 %collective-permute-done.40 = bf16[64,1024]{1,0:T(8,128)(2,1)S(1)} collective-permute-done((bf16[64,1024]{1,0:T(8,128)(2,1)S(1)}, bf16[64,1024]{1,0:T(8,128)(2,1)S(1)}, u32[]{:S(2)}, u32[]{:S(2)}) %collective-permute-start.40) | collective-permute-done | bytes 131104 | tf_op jit(solution)/shard_map/ppermute | solution.py:815
  469.3 2.4 pack.44
  480.1 3.0 collective-permute-done.46
  484.3 3.4 collective-permute-done.44
  487.6 13.6 %collective-permute-done.42 = bf16[2,64,2048]{2,1,0:T(8,128)(2,1)S(1)} collective-permute-done((bf16[2,64,2048]{2,1,0:T(8,128)(2,1)S(1)}, bf16[2,64,2048]{2,1,0:T(8,128)(2,1)S(1)}, u32[]{:S(2)}, u32[]{:S(2)}) %collective-permute-start.42) | collective-permute-done | bytes 524320 | tf_op jit(solution)/shard_map/ppermute | solution.py:815
  507.5 3.3 collective-permute-start.50
  522.0 4.5 collective-permute-done.51
  532.4 5.4 collective-permute-start.52
  544.5 5.2 collective-permute-done.55
  (320 shorter events, 132.8 us)
Async XLA Ops:
  0.6 16.6 %collective-permute-start.1 = (bf16[2,3,1024,512]{3,2,1,0:T(8,128)(2,1)}, bf16[2,3,1024,512]{3,2,1,0:T(8,128)(2,1)}, u32[]{:S(2)}, u32[]{:S(2)}) collective-permute-start(bf16[2,3,1024,512]{3,2,1,0:T(8,128)(2,1)} %bitcast.55), channel_id=1, source_target_pairs={{0,1},{1,0},{2,3},{3,2},{4,5},{5,4},{6,7},{7,6},{8,9},{9,8},{10,11... | collective-permute-start | bytes 18874376 | tf_op jit(solution)/shard_map/ppermute | solution.py:803
  1.2 16.1 %collective-permute-start = (bf16[2,1,1024,1024]{3,2,1,0:T(8,128)(2,1)}, bf16[2,1,1024,1024]{3,2,1,0:T(8,128)(2,1)}, u32[]{:S(2)}, u32[]{:S(2)}) collective-permute-start(bf16[2,1,1024,1024]{3,2,1,0:T(8,128)(2,1)} %wa_ref.7), channel_id=1, source_target_pairs={{0,1},{1,0},{2,3},{3,2},{4,5},{5,4},{6,7},{7,6},{8,9},{9,8},{10,11... | collective-permute-start | bytes 12582920 | tf_op jit(solution)/shard_map/ppermute | solution.py:803
  17.3 21.3 %collective-permute-start.3 = (bf16[2,1024,2048]{2,1,0:T(8,128)(2,1)}, bf16[2,1024,2048]{2,1,0:T(8,128)(2,1)}, u32[]{:S(2)}, u32[]{:S(2)}) collective-permute-start(bf16[2,1024,2048]{2,1,0:T(8,128)(2,1)} %refs_7_.7), channel_id=1, source_target_pairs={{0,1},{1,0},{2,3},{3,2},{4,5},{5,4},{6,7},{7,6},{8,9},{9,8},{10,11... | collective-permute-start | bytes 25165832 | tf_op jit(solution)/shard_map/ppermute | solution.py:803
  38.7 21.7 %collective-permute-start.6 = (bf16[2,1024,2048]{2,1,0:T(8,128)(2,1)S(1)}, bf16[2,1024,2048]{2,1,0:T(8,128)(2,1)}, u32[]{:S(2)}, u32[]{:S(2)}) collective-permute-start(bf16[2,1024,2048]{2,1,0:T(8,128)(2,1)S(1)} %bitcast.61), channel_id=1, source_target_pairs={{0,1},{1,0},{2,3},{3,2},{4,5},{5,4},{6,7},{7,6},{8,9},{9,8},{10,11... | collective-permute-start | bytes 25165832 | tf_op jit(solution)/shard_map/ppermute | solution.py:803
  38.9 21.5 %collective-permute-start.5 = (bf16[2,1024,512]{2,1,0:T(8,128)(2,1)S(1)}, bf16[2,1024,512]{2,1,0:T(8,128)(2,1)S(1)}, u32[]{:S(2)}, u32[]{:S(2)}) collective-permute-start(bf16[2,1024,512]{2,1,0:T(8,128)(2,1)S(1)} %copy-done), channel_id=1, source_target_pairs={{0,1},{1,0},{2,3},{3,2},{4,5},{5,4},{6,7},{7,6},{8,9},{9,8},{10,11... | collective-permute-start | bytes 6291464 | tf_op jit(solution)/shard_map/ppermute | solution.py:803
  154.6 29.1 %collective-permute-start.8 = (bf16[1024,2048]{1,0:T(8,128)(2,1)}, bf16[1024,2048]{1,0:T(8,128)(2,1)}, u32[]{:S(2)}, u32[]{:S(2)}) collective-permute-start(bf16[1024,2048]{1,0:T(8,128)(2,1)} %get-tuple-element.303), channel_id=1, source_target_pairs={{0,1},{1,0},{2,3},{3,2},{4,5},{5,4},{6,7},{7,6},{8,9},{9,8},{10,11... | collective-permute-start | bytes 12582920 | tf_op jit(solution)/shard_map/ppermute | solution.py:803
  154.7 28.9 %collective-permute-start.9 = (bf16[1024,2048]{1,0:T(8,128)(2,1)}, bf16[1024,2048]{1,0:T(8,128)(2,1)}, u32[]{:S(2)}, u32[]{:S(2)}) collective-permute-start(bf16[1024,2048]{1,0:T(8,128)(2,1)} %get-tuple-element.304), channel_id=1, source_target_pairs={{0,1},{1,0},{2,3},{3,2},{4,5},{5,4},{6,7},{7,6},{8,9},{9,8},{10,11... | collective-permute-start | bytes 12582920 | tf_op jit(solution)/shard_map/ppermute | solution.py:803
  189.0 49.2 %collective-permute-start.12 = (bf16[2,512,2048]{2,1,0:T(8,128)(2,1)S(1)}, bf16[2,512,2048]{2,1,0:T(8,128)(2,1)S(1)}, u32[]{:S(2)}, u32[]{:S(2)}) collective-permute-start(bf16[2,512,2048]{2,1,0:T(8,128)(2,1)S(1)} %pack.26), channel_id=1, source_target_pairs={{0,2},{1,5},{2,0},{3,7},{4,6},{5,1},{6,4},{7,3},{8,10},{9,13},{10,... | collective-permute-start | bytes 12582920 | tf_op jit(solution)/shard_map/ppermute | solution.py:815
  243.5 20.7 %collective-permute-start.13 = (bf16[1024,2048]{1,0:T(8,128)(2,1)}, bf16[1024,2048]{1,0:T(8,128)(2,1)}, u32[]{:S(2)}, u32[]{:S(2)}) collective-permute-start(bf16[1024,2048]{1,0:T(8,128)(2,1)} %get-tuple-element.331), channel_id=1, source_target_pairs={{0,1},{1,0},{2,3},{3,2},{4,5},{5,4},{6,7},{7,6},{8,9},{9,8},{10,11... | collective-permute-start | bytes 12582920 | tf_op jit(solution)/shard_map/ppermute | solution.py:803
  243.5 26.1 %collective-permute-start.14 = (bf16[2,256,2048]{2,1,0:T(8,128)(2,1)S(1)}, bf16[2,256,2048]{2,1,0:T(8,128)(2,1)S(1)}, u32[]{:S(2)}, u32[]{:S(2)}) collective-permute-start(bf16[2,256,2048]{2,1,0:T(8,128)(2,1)S(1)} %pack.27), channel_id=1, source_target_pairs={{0,4},{1,3},{2,6},{3,1},{4,0},{5,7},{6,2},{7,5},{8,12},{9,11},{10,... | collective-permute-start | bytes 6291464 | tf_op jit(solution)/shard_map/ppermute | solution.py:815
  273.7 20.6 %collective-permute-start.15 = (bf16[1024,1024]{1,0:T(8,128)(2,1)}, bf16[1024,1024]{1,0:T(8,128)(2,1)}, u32[]{:S(2)}, u32[]{:S(2)}) collective-permute-start(bf16[1024,1024]{1,0:T(8,128)(2,1)} %get-tuple-element.348), channel_id=1, source_target_pairs={{0,1},{1,0},{2,3},{3,2},{4,5},{5,4},{6,7},{7,6},{8,9},{9,8},{10,11... | collective-permute-start | bytes 6291464 | tf_op jit(solution)/shard_map/ppermute | solution.py:803
  273.8 28.3 %collective-permute-start.16 = (bf16[512,2048]{1,0:T(8,128)(2,1)S(1)}, bf16[512,2048]{1,0:T(8,128)(2,1)}, u32[]{:S(2)}, u32[]{:S(2)}) collective-permute-start(bf16[512,2048]{1,0:T(8,128)(2,1)S(1)} %pack.28), channel_id=1, source_target_pairs={{0,2},{1,5},{2,0},{3,7},{4,6},{5,1},{6,4},{7,3},{8,10},{9,13},{10,... | collective-permute-start | bytes 6291464 | tf_op jit(solution)/shard_map/ppermute | solution.py:815
  275.8 25.2 %collective-permute-start.17 = (bf16[2,128,2048]{2,1,0:T(8,128)(2,1)S(1)}, bf16[2,128,2048]{2,1,0:T(8,128)(2,1)S(1)}, u32[]{:S(2)}, u32[]{:S(2)}) collective-permute-start(bf16[2,128,2048]{2,1,0:T(8,128)(2,1)S(1)} %pack.29), channel_id=1, source_target_pairs={{0,8},{1,9},{2,10},{3,11},{4,12},{5,13},{6,14},{7,15},{8,0},{9,1},... | collective-permute-start | bytes 3145736 | tf_op jit(solution)/shard_map/ppermute | solution.py:815
  306.3 23.5 %collective-permute-start.18 = (bf16[1024,2048]{1,0:T(8,128)(2,1)}, bf16[1024,2048]{1,0:T(8,128)(2,1)}, u32[]{:S(2)}, u32[]{:S(2)}) collective-permute-start(bf16[1024,2048]{1,0:T(8,128)(2,1)} %get-tuple-element.370), channel_id=1, source_target_pairs={{0,1},{1,0},{2,3},{3,2},{4,5},{5,4},{6,7},{7,6},{8,9},{9,8},{10,11... | collective-permute-start | bytes 12582920 | tf_op jit(solution)/shard_map/ppermute | solution.py:803
  307.1 22.7 %collective-permute-start.19 = (bf16[1024,2048]{1,0:T(8,128)(2,1)S(1)}, bf16[1024,2048]{1,0:T(8,128)(2,1)}, u32[]{:S(2)}, u32[]{:S(2)}) collective-permute-start(bf16[1024,2048]{1,0:T(8,128)(2,1)S(1)} %copy-done.47), channel_id=1, source_target_pairs={{0,1},{1,0},{2,3},{3,2},{4,5},{5,4},{6,7},{7,6},{8,9},{9,8},{10,11... | collective-permute-start | bytes 12582920 | tf_op jit(solution)/shard_map/ppermute | solution.py:803
  307.1 28.0 %collective-permute-start.20 = (bf16[512,1024]{1,0:T(8,128)(2,1)S(1)}, bf16[512,1024]{1,0:T(8,128)(2,1)S(1)}, u32[]{:S(2)}, u32[]{:S(2)}) collective-permute-start(bf16[512,1024]{1,0:T(8,128)(2,1)S(1)} %pack.30), channel_id=1, source_target_pairs={{0,2},{1,5},{2,0},{3,7},{4,6},{5,1},{6,4},{7,3},{8,10},{9,13},{10,... | collective-permute-start | bytes 3145736 | tf_op jit(solution)/shard_map/ppermute | solution.py:815
  308.1 27.0 %collective-permute-start.21 = (bf16[256,2048]{1,0:T(8,128)(2,1)S(1)}, bf16[256,2048]{1,0:T(8,128)(2,1)}, u32[]{:S(2)}, u32[]{:S(2)}) collective-permute-start(bf16[256,2048]{1,0:T(8,128)(2,1)S(1)} %pack.31), channel_id=1, source_target_pairs={{0,4},{1,3},{2,6},{3,1},{4,0},{5,7},{6,2},{7,5},{8,12},{9,11},{10,... | collective-permute-start | bytes 3145736 | tf_op jit(solution)/shard_map/ppermute | solution.py:815
  309.1 26.0 %collective-permute-start.22 = (bf16[2,64,2048]{2,1,0:T(8,128)(2,1)S(1)}, bf16[2,64,2048]{2,1,0:T(8,128)(2,1)S(1)}, u32[]{:S(2)}, u32[]{:S(2)}) collective-permute-start(bf16[2,64,2048]{2,1,0:T(8,128)(2,1)S(1)} %pack.32), channel_id=1, source_target_pairs={{0,16},{1,17},{2,18},{3,19},{4,20},{5,21},{6,22},{7,23},{8,24},{9,... | collective-permute-start | bytes 1572872 | tf_op jit(solution)/shard_map/ppermute | solution.py:815
  335.1 54.2 %collective-permute-start.25 = (bf16[2,512,2048]{2,1,0:T(8,128)(2,1)S(1)}, bf16[2,512,2048]{2,1,0:T(8,128)(2,1)S(1)}, u32[]{:S(2)}, u32[]{:S(2)}) collective-permute-start(bf16[2,512,2048]{2,1,0:T(8,128)(2,1)S(1)} %pack.33), channel_id=1, source_target_pairs={{0,2},{1,5},{2,0},{3,7},{4,6},{5,1},{6,4},{7,3},{8,10},{9,13},{10,... | collective-permute-start | bytes 12582920 | tf_op jit(solution)/shard_map/ppermute | solution.py:815
  368.1 14.9 %collective-permute-start.27 = (bf16[256,1024]{1,0:T(8,128)(2,1)S(1)}, bf16[256,1024]{1,0:T(8,128)(2,1)S(1)}, u32[]{:S(2)}, u32[]{:S(2)}) collective-permute-start(bf16[256,1024]{1,0:T(8,128)(2,1)S(1)} %pack.35), channel_id=1, source_target_pairs={{0,4},{1,3},{2,6},{3,1},{4,0},{5,7},{6,2},{7,5},{8,12},{9,11},{10,... | collective-permute-start | bytes 1572872 | tf_op jit(solution)/shard_map/ppermute | solution.py:815
  369.4 13.6 %collective-permute-start.26 = (bf16[128,2048]{1,0:T(8,128)(2,1)S(1)}, bf16[128,2048]{1,0:T(8,128)(2,1)S(1)}, u32[]{:S(2)}, u32[]{:S(2)}) collective-permute-start(bf16[128,2048]{1,0:T(8,128)(2,1)S(1)} %pack.34), channel_id=1, source_target_pairs={{0,8},{1,9},{2,10},{3,11},{4,12},{5,13},{6,14},{7,15},{8,0},{9,1},... | collective-permute-start | bytes 1572872 | tf_op jit(solution)/shard_map/ppermute | solution.py:815
  397.7 29.7 %collective-permute-start.28 = (bf16[1024,2048]{1,0:T(8,128)(2,1)}, bf16[1024,2048]{1,0:T(8,128)(2,1)}, u32[]{:S(2)}, u32[]{:S(2)}) collective-permute-start(bf16[1024,2048]{1,0:T(8,128)(2,1)} %get-tuple-element.426), channel_id=1, source_target_pairs={{0,1},{1,0},{2,3},{3,2},{4,5},{5,4},{6,7},{7,6},{8,9},{9,8},{10,11... | collective-permute-start | bytes 12582920 | tf_op jit(solution)/shard_map/ppermute | solution.py:803
  397.8 33.0 %collective-permute-start.29 = (bf16[2,256,2048]{2,1,0:T(8,128)(2,1)}, bf16[2,256,2048]{2,1,0:T(8,128)(2,1)}, u32[]{:S(2)}, u32[]{:S(2)}) collective-permute-start(bf16[2,256,2048]{2,1,0:T(8,128)(2,1)} %pack.36), channel_id=1, source_target_pairs={{0,4},{1,3},{2,6},{3,1},{4,0},{5,7},{6,2},{7,5},{8,12},{9,11},{10,... | collective-permute-start | bytes 6291464 | tf_op jit(solution)/shard_map/ppermute | solution.py:815
  399.1 31.6 %collective-permute-start.31 = (bf16[128,1024]{1,0:T(8,128)(2,1)}, bf16[128,1024]{1,0:T(8,128)(2,1)}, u32[]{:S(2)}, u32[]{:S(2)}) collective-permute-start(bf16[128,1024]{1,0:T(8,128)(2,1)} %pack.38), channel_id=1, source_target_pairs={{0,8},{1,9},{2,10},{3,11},{4,12},{5,13},{6,14},{7,15},{8,0},{9,1},... | collective-permute-start | bytes 786440 | tf_op jit(solution)/shard_map/ppermute | solution.py:815
  400.7 30.0 %collective-permute-start.30 = (bf16[64,2048]{1,0:T(8,128)(2,1)S(1)}, bf16[64,2048]{1,0:T(8,128)(2,1)}, u32[]{:S(2)}, u32[]{:S(2)}) collective-permute-start(bf16[64,2048]{1,0:T(8,128)(2,1)S(1)} %pack.37), channel_id=1, source_target_pairs={{0,16},{1,17},{2,18},{3,19},{4,20},{5,21},{6,22},{7,23},{8,24},{9,... | collective-permute-start | bytes 786440 | tf_op jit(solution)/shard_map/ppermute | solution.py:815
  435.8 5.3 collective-permute-start.32
  435.8 5.4 collective-permute-start.33
  437.1 32.2 %collective-permute-start.38 = (bf16[512,2048]{1,0:T(8,128)(2,1)S(1)}, bf16[512,2048]{1,0:T(8,128)(2,1)}, u32[]{:S(2)}, u32[]{:S(2)}) collective-permute-start(bf16[512,2048]{1,0:T(8,128)(2,1)S(1)} %pack.39), channel_id=1, source_target_pairs={{0,2},{1,5},{2,0},{3,7},{4,6},{5,1},{6,4},{7,3},{8,10},{9,13},{10,... | collective-permute-start | bytes 6291464 | tf_op jit(solution)/shard_map/ppermute | solution.py:815
  438.0 19.9 %collective-permute-start.36 = (bf16[1024,1024]{1,0:T(8,128)(2,1)}, bf16[1024,1024]{1,0:T(8,128)(2,1)}, u32[]{:S(2)}, u32[]{:S(2)}) collective-permute-start(bf16[1024,1024]{1,0:T(8,128)(2,1)} %get-tuple-element.453), channel_id=1, source_target_pairs={{0,1},{1,0},{2,3},{3,2},{4,5},{5,4},{6,7},{7,6},{8,9},{9,8},{10,11... | collective-permute-start | bytes 6291464 | tf_op jit(solution)/shard_map/ppermute | solution.py:803
  440.5 5.7 %collective-permute-start.34 = (bf16[528,1024]{1,0:T(8,128)(2,1)S(1)}, bf16[528,1024]{1,0:T(8,128)(2,1)S(1)}, u32[]{:S(2)}, u32[]{:S(2)}) collective-permute-start(bf16[528,1024]{1,0:T(8,128)(2,1)S(1)} %copy-done.23), channel_id=1, source_target_pairs={{0,1},{1,0},{2,3},{3,2},{4,5},{5,4},{6,7},{7,6},{8,9},{9,8},{10,11... | collective-permute-start | bytes 3244040 | tf_op jit(solution)/shard_map/ppermute | solution.py:803
  441.1 28.2 %collective-permute-start.39 = (bf16[2,128,2048]{2,1,0:T(8,128)(2,1)}, bf16[2,128,2048]{2,1,0:T(8,128)(2,1)S(1)}, u32[]{:S(2)}, u32[]{:S(2)}) collective-permute-start(bf16[2,128,2048]{2,1,0:T(8,128)(2,1)} %copy-done.28), channel_id=1, source_target_pairs={{0,8},{1,9},{2,10},{3,11},{4,12},{5,13},{6,14},{7,15},{8,0},{9,1},... | collective-permute-start | bytes 3145736 | tf_op jit(solution)/shard_map/ppermute | solution.py:815
  441.2 15.2 %collective-permute-start.35 = (bf16[528,1024]{1,0:T(8,128)(2,1)}, bf16[528,1024]{1,0:T(8,128)(2,1)S(1)}, u32[]{:S(2)}, u32[]{:S(2)}) collective-permute-start(bf16[528,1024]{1,0:T(8,128)(2,1)} %copy-done.26), channel_id=1, source_target_pairs={{0,1},{1,0},{2,3},{3,2},{4,5},{5,4},{6,7},{7,6},{8,9},{9,8},{10,11... | collective-permute-start | bytes 3244040 | tf_op jit(solution)/shard_map/ppermute | solution.py:803
  446.2 20.9 %collective-permute-start.40 = (bf16[64,1024]{1,0:T(8,128)(2,1)S(1)}, bf16[64,1024]{1,0:T(8,128)(2,1)S(1)}, u32[]{:S(2)}, u32[]{:S(2)}) collective-permute-start(bf16[64,1024]{1,0:T(8,128)(2,1)S(1)} %pack.41), channel_id=1, source_target_pairs={{0,16},{1,17},{2,18},{3,19},{4,20},{5,21},{6,22},{7,23},{8,24},{9,... | collective-permute-start | bytes 393224 | tf_op jit(solution)/shard_map/ppermute | solution.py:815
  460.3 41.0 %collective-permute-start.37 = (bf16[512,1024]{1,0:T(8,128)(2,1)S(1)}, bf16[512,1024]{1,0:T(8,128)(2,1)S(1)}, u32[]{:S(2)}, u32[]{:S(2)}) collective-permute-start(bf16[512,1024]{1,0:T(8,128)(2,1)S(1)} %pack.42), channel_id=1, source_target_pairs={{0,2},{1,5},{2,0},{3,7},{4,6},{5,1},{6,4},{7,3},{8,10},{9,13},{10,... | collective-permute-start | bytes 3145736 | tf_op jit(solution)/shard_map/ppermute | solution.py:815
  471.7 29.6 %collective-permute-start.43 = (bf16[256,2048]{1,0:T(8,128)(2,1)S(1)}, bf16[256,2048]{1,0:T(8,128)(2,1)S(1)}, u32[]{:S(2)}, u32[]{:S(2)}) collective-permute-start(bf16[256,2048]{1,0:T(8,128)(2,1)S(1)} %pack.44), channel_id=1, source_target_pairs={{0,4},{1,3},{2,6},{3,1},{4,0},{5,7},{6,2},{7,5},{8,12},{9,11},{10,... | collective-permute-start | bytes 3145736 | tf_op jit(solution)/shard_map/ppermute | solution.py:815
  472.7 4.6 collective-permute-start.41
  474.8 26.5 %collective-permute-start.42 = (bf16[2,64,2048]{2,1,0:T(8,128)(2,1)S(1)}, bf16[2,64,2048]{2,1,0:T(8,128)(2,1)S(1)}, u32[]{:S(2)}, u32[]{:S(2)}) collective-permute-start(bf16[2,64,2048]{2,1,0:T(8,128)(2,1)S(1)} %pack.43), channel_id=1, source_target_pairs={{0,16},{1,17},{2,18},{3,19},{4,20},{5,21},{6,22},{7,23},{8,24},{9,... | collective-permute-start | bytes 1572872 | tf_op jit(solution)/shard_map/ppermute | solution.py:815
  477.4 5.6 %collective-permute-start.46 = (f32[4,18,64]{2,1,0:T(8,128)S(1)}, f32[4,18,64]{2,1,0:T(8,128)S(1)}, u32[]{:S(2)}, u32[]{:S(2)}) collective-permute-start(f32[4,18,64]{2,1,0:T(8,128)S(1)} %get-tuple-element.588), channel_id=1, source_target_pairs={{0,6},{1,7},{2,4},{3,5},{4,2},{5,3},{6,0},{7,1},{8,14},{9,15},{10,... | collective-permute-start | bytes 55304 | tf_op jit(solution)/shard_map/ppermute | solution.py:815
  479.2 5.1 collective-permute-start.45
  506.3 20.1 %collective-permute-start.48 = (bf16[64,2048]{1,0:T(8,128)(2,1)S(1)}, bf16[64,2048]{1,0:T(8,128)(2,1)S(1)}, u32[]{:S(2)}, u32[]{:S(2)}) collective-permute-start(bf16[64,2048]{1,0:T(8,128)(2,1)S(1)} %pack.45), channel_id=1, source_target_pairs={{0,16},{1,17},{2,18},{3,19},{4,20},{5,21},{6,22},{7,23},{8,24},{9,... | collective-permute-start | bytes 786440 | tf_op jit(solution)/shard_map/ppermute | solution.py:815
  506.4 20.1 %collective-permute-start.49 = (bf16[64,2048]{1,0:T(8,128)(2,1)S(1)}, bf16[64,2048]{1,0:T(8,128)(2,1)}, u32[]{:S(2)}, u32[]{:S(2)}) collective-permute-start(bf16[64,2048]{1,0:T(8,128)(2,1)S(1)} %pack.46), channel_id=1, source_target_pairs={{0,8},{1,9},{2,10},{3,11},{4,12},{5,13},{6,14},{7,15},{8,0},{9,1},... | collective-permute-start | bytes 786440 | tf_op jit(solution)/shard_map/ppermute | solution.py:815
  507.5 19.0 %collective-permute-start.50 = (bf16[64,2048]{1,0:T(8,128)(2,1)S(1)}, bf16[64,2048]{1,0:T(8,128)(2,1)}, u32[]{:S(2)}, u32[]{:S(2)}) collective-permute-start(bf16[64,2048]{1,0:T(8,128)(2,1)S(1)} %pack.47), channel_id=1, source_target_pairs={{0,24},{1,25},{2,26},{3,27},{4,28},{5,29},{6,30},{7,31},{8,16},{9,... | collective-permute-start | bytes 786440 | tf_op jit(solution)/shard_map/ppermute | solution.py:815
  511.4 15.1 %collective-permute-start.51 = (f32[2,18,64]{2,1,0:T(8,128)}, f32[2,18,64]{2,1,0:T(8,128)}, u32[]{:S(2)}, u32[]{:S(2)}) collective-permute-start(f32[2,18,64]{2,1,0:T(8,128)} %slice_add_fusion.3), channel_id=1, source_target_pairs={{0,8},{1,9},{2,10},{3,11},{4,12},{5,13},{6,14},{7,15},{8,0},{9,1},... | collective-permute-start | bytes 27656 | tf_op jit(solution)/shard_map/ppermute | solution.py:815
  514.9 11.5 %collective-permute-start.47 = (bf16[256,1024]{1,0:T(8,128)(2,1)S(1)}, bf16[256,1024]{1,0:T(8,128)(2,1)S(1)}, u32[]{:S(2)}, u32[]{:S(2)}) collective-permute-start(bf16[256,1024]{1,0:T(8,128)(2,1)S(1)} %pack.48), channel_id=1, source_target_pairs={{0,4},{1,3},{2,6},{3,1},{4,0},{5,7},{6,2},{7,5},{8,12},{9,11},{10,... | collective-permute-start | bytes 1572872 | tf_op jit(solution)/shard_map/ppermute | solution.py:815
  532.4 17.3 %collective-permute-start.52 = (bf16[64,1024]{1,0:T(8,128)(2,1)S(1)}, bf16[64,1024]{1,0:T(8,128)(2,1)S(1)}, u32[]{:S(2)}, u32[]{:S(2)}) collective-permute-start(bf16[64,1024]{1,0:T(8,128)(2,1)S(1)} %pack.49), channel_id=1, source_target_pairs={{0,16},{1,17},{2,18},{3,19},{4,20},{5,21},{6,22},{7,23},{8,24},{9,... | collective-permute-start | bytes 393224 | tf_op jit(solution)/shard_map/ppermute | solution.py:815
  537.8 11.9 %collective-permute-start.53 = (bf16[64,1024]{1,0:T(8,128)(2,1)S(1)}, bf16[64,1024]{1,0:T(8,128)(2,1)S(1)}, u32[]{:S(2)}, u32[]{:S(2)}) collective-permute-start(bf16[64,1024]{1,0:T(8,128)(2,1)S(1)} %pack.50), channel_id=1, source_target_pairs={{0,8},{1,9},{2,10},{3,11},{4,12},{5,13},{6,14},{7,15},{8,0},{9,1},... | collective-permute-start | bytes 393224 | tf_op jit(solution)/shard_map/ppermute | solution.py:815
  537.9 11.9 %collective-permute-start.54 = (bf16[64,1024]{1,0:T(8,128)(2,1)S(1)}, bf16[64,1024]{1,0:T(8,128)(2,1)S(1)}, u32[]{:S(2)}, u32[]{:S(2)}) collective-permute-start(bf16[64,1024]{1,0:T(8,128)(2,1)S(1)} %pack.51), channel_id=1, source_target_pairs={{0,24},{1,25},{2,26},{3,27},{4,28},{5,29},{6,30},{7,31},{8,16},{9,... | collective-permute-start | bytes 393224 | tf_op jit(solution)/shard_map/ppermute | solution.py:815
  540.1 9.6 %collective-permute-start.55 = (f32[1,18,64]{2,1,0:T(8,128)S(1)}, f32[1,18,64]{2,1,0:T(8,128)S(1)}, u32[]{:S(2)}, u32[]{:S(2)}) collective-permute-start(f32[1,18,64]{2,1,0:T(8,128)S(1)} %slice_add_fusion.4), channel_id=1, source_target_pairs={{0,16},{1,17},{2,18},{3,19},{4,20},{5,21},{6,22},{7,23},{8,24},{9,... | collective-permute-start | bytes 13832 | tf_op jit(solution)/shard_map/ppermute | solution.py:815
  (78 other events, 705.2 us)

commit v5 on v4

--- a/solution.py
+++ b/solution.py
@@ -51,18 +51,21 @@
     out = jnp.zeros((PAD, GROUP), F32)
     ex_all = jnp.zeros((PAD, 16), F32)
     il_all = jnp.zeros((PAD, 16), F32)
+    lane_v = lax.broadcasted_iota(jnp.int32, (2 * MAIN, GROUP), 1) // HD
+    ones = jnp.ones((2 * MAIN, GROUP), BF16)
     for h in range(HEADS_IN_GROUP):
         qh = jnp.where(lane == h, q, jnp.zeros_like(q))
         s = _dot(qh, k_s[...], ((1,), (1,)))
         sxh = jnp.where(slot == h, sx, -jnp.inf)
         top = jnp.maximum(jnp.max(s, axis=1, keepdims=True), jnp.max(sxh, axis=1, keepdims=True))
-        e = jnp.exp(s - top)
+        low = jnp.exp(s - top).astype(BF16)
+        e_ref[h] = low
         exh = jnp.exp(sxh - top)
-        total = jnp.sum(e, axis=1, keepdims=True) + jnp.sum(exh, axis=1, keepdims=True)
+        other = (h + 1) % HEADS_IN_GROUP
+        summed = _dot(low, jnp.where(lane_v == h, v_s[...], ones), ((1,), (0,)))
+        total = summed[:, other * HD : other * HD + 1] + jnp.sum(exh, axis=1, keepdims=True)
         inverse = 1.0 / total
-        low = e.astype(BF16)
-        e_ref[h] = low
-        out = out + jnp.where(lane == h, _dot(low, v_s[...], ((1,), (0,))) * inverse, 0.0)
+        out = out + jnp.where(lane == h, summed * inverse, 0.0)
         ex_all = ex_all + exh
         il_all = il_all + jnp.where(slot == h, inverse, 0.0)
     out = out + _dot((ex_all * il_all).astype(BF16), vx, ((1,), (0,)))
@@ -925,11 +928,12 @@
     )
     skip_parts = localize(skips.transpose(1, 0, 2), core)
 
+    skip_parts = [skip_parts[:, layer] for layer in range(layers)]
     rows0 = localize(inputs, core)
     weights["up_peer"] = swap_cores(after(up_weight, skip_peer, qkv_peer, skip_parts, rows0))
 
     def enter(layer, residual):
-        skip_rows = skip_parts[:, layer]
+        skip_rows = skip_parts[layer]
         hidden, normed, q, kv = entry_forward(
             layer, coords, residual, skip_rows, skip_weight, skip_peer, skip_bias, attn_norm_gain, attn_norm_bias,
             qkv_turned, qkv_peer,

time: 560 us -> 560 us (level)
  no operation moved by 1% of the time
where the time goes in v5:
time: 560 us; the launch traced here: 555 us
  Pallas kernels  345 us (62%)
  waiting for transfers between devices  88.1 us (16%)
  local copies, waits for them, and re-layouts  50.8 us (9%)
  starting transfers between devices  49.6 us (9%)
  other arithmetic  18.9 us (3%)
    pallas_call x5, Pallas kernels, mlp(): pl.pallas_call(functools.partial(_mlp_kernel, (*names, *out_names, *scrat...  110 us
    ppermute x31, waiting for transfers between devices, swap_bits(): return lax.ppermute(value, ('dp', 'tensor'), pairs)  63.6 us
    pallas_call x26, Pallas kernels, pack(): pl.pallas_call(functools.partial(_pack_kernel, tuple((len(arrays) for arr...  60.6 us
    pallas_call x2, Pallas kernels, attn_backward(): pl.pallas_call(_attn_bwd_kernel, grid=(groups,), in_specs=[near(0), near(...  46.7 us
    ppermute x31, starting transfers between devices, swap_bits(): return lax.ppermute(value, ('dp', 'tensor'), pairs)  44.3 us
    pallas_call x2, Pallas kernels, attn_forward(): pl.pallas_call(_attn_fwd_kernel, grid=(groups,), in_specs=[near(0), near(...  37.6 us
    pallas_call x2, Pallas kernels, entry_backward(): pl.pallas_call(functools.partial(_entry_back_kernel, layer, pieces, order...  34.5 us
    unnamed x142, local copies, waits for them, and re-layouts  33 us
  transfers between devices with their start and end apart: 56, of which 20 were waited for; matrix products, arithmetic and copies ran while one was open for 6% of the time, Pallas kernels for 41%

profile of v5, /device:TPU:0, one launch (start us, length us, event | category | flops | bytes accessed | tf_op | source)
XLA Modules:
  0.0 554.9 jit_solution(17163861720334122254)
XLA Ops:
  1.9 3.0 constant_dynamic-slice_fusion.2
  10.6 6.7 %collective-permute-done.wb_ref = bf16[2,1,1024,1024]{3,2,1,0:T(8,128)(2,1)} collective-permute-done((bf16[2,1,1024,1024]{3,2,1,0:T(8,128)(2,1)}, bf16[2,1,1024,1024]{3,2,1,0:T(8,128)(2,1)}, u32[]{:S(2)}, u32[]{:S(2)}) %collective-permute-start) | collective-permute-done | bytes 4194336 | tf_op jit(solution)/shard_map/ppermute | solution.py:806
  17.8 14.0 %entry_forward.2 = (f32[528,1024]{1,0:T(8,128)}, bf16[528,1024]{1,0:T(8,128)(2,1)}, bf16[528,1024]{1,0:T(8,128)(2,1)}, bf16[528,2048]{1,0:T(8,128)(2,1)}) custom-call(s32[2]{0:T(128)S(1)} %pad_add_fusion.coords_ref, bf16[528,1024]{1,0:T(8,128)(2,1)S(1)} %get-tuple-element.601.xa_ref, bf16[528,1024]{1,0:T(8,128)(2,1)S(1)} %get-tuple-element.583.xb_ref, ...), custom_call_target="tpu_custom_call" | custom-call | flops 1 | bytes 4900000 | tf_op jit(solution)/shard_map/entry_forward/pallas_call | solution.py:332
  32.3 3.5 collective-permute-done.4.refs_10_.refs_11_
  38.8 18.8 %attn_forward.2 = (bf16[528,1024]{1,0:T(8,128)(2,1)}, f32[528,1024]{1,0:T(8,128)}, bf16[16,528,1024]{2,1,0:T(8,128)(2,1)}, f32[4,528,16]{2,1,0:T(8,128)}, f32[4,528,16]{2,1,0:T(8,128)}) custom-call(bf16[528,1024]{1,0:T(8,128)(2,1)S(1)} %copy-done.12, bf16[528,2048]{1,0:T(8,128)(2,1)} %get-tuple-element.285.km_ref.vm_ref, ...), custom_call_target="tpu_custom_call" | custom-call | flops 1 | bytes 6650000 | tf_op jit(solution)/shard_map/attn_forward/pallas_call | solution.py:94
  57.6 3.3 copy-done.49
  62.1 24.6 %mlp_f_peer_own.1 = (f32[528,1024]{1,0:T(8,128)}, bf16[528,1024]{1,0:T(8,128)(2,1)}, bf16[528,1024]{1,0:T(8,128)(2,1)S(1)}, bf16[528,2048]{1,0:T(8,128)(2,1)}, b...) custom-call(s32[2]{0:T(128)S(1)} %pad_add_fusion.coords_ref, ...), custom_call_target="tpu_custom_call" | custom-call | flops 1 | bytes 9800000 | tf_op jit(solution)/shard_map/mlp_f_peer_own/pallas_call | solution.py:556
  86.7 13.6 %entry_forward.3 = (f32[528,1024]{1,0:T(8,128)}, bf16[528,1024]{1,0:T(8,128)(2,1)}, bf16[528,1024]{1,0:T(8,128)(2,1)}, bf16[528,2048]{1,0:T(8,128)(2,1)}) custom-call(s32[2]{0:T(128)S(1)} %pad_add_fusion.coords_ref, bf16[528,1024]{1,0:T(8,128)(2,1)S(1)} %get-tuple-element.291.xa_ref, bf16[528,1024]{1,0:T(8,128)(2,1)S(1)} %copy-done.1, ...), custom_call_target="tpu_custom_call" | custom-call | flops 1 | bytes 4900000 | tf_op jit(solution)/shard_map/entry_forward/pallas_call | solution.py:332
  100.4 4.3 collective-permute-done.7.ko_ref.vo_ref
  107.4 18.8 %attn_forward.3 = (bf16[528,1024]{1,0:T(8,128)(2,1)}, f32[528,1024]{1,0:T(8,128)}, bf16[16,528,1024]{2,1,0:T(8,128)(2,1)}, f32[4,528,16]{2,1,0:T(8,128)}, f32[4,528,16]{2,1,0:T(8,128)}) custom-call(bf16[528,1024]{1,0:T(8,128)(2,1)S(1)} %copy-done.13, bf16[528,2048]{1,0:T(8,128)(2,1)} %get-tuple-element.294.km_ref.vm_ref, ...), custom_call_target="tpu_custom_call" | custom-call | flops 1 | bytes 6650000 | tf_op jit(solution)/shard_map/attn_forward/pallas_call | solution.py:94
  127.4 25.8 %mlp_fb_peer.1 = (f32[528,1024]{1,0:T(8,128)}, bf16[528,1024]{1,0:T(8,128)(2,1)}, f32[528,1024]{1,0:T(8,128)S(1)}, f32[528,1024]{1,0:T(8,128)}, bf16[1024,2048]{...) custom-call(s32[2]{0:T(128)S(1)} %pad_add_fusion.coords_ref, ...), custom_call_target="tpu_custom_call" | custom-call | flops 1 | bytes 11200000 | tf_op jit(solution)/shard_map/mlp_fb_peer/pallas_call | solution.py:556
  156.3 27.3 %mlp_fb_own.1 = (bf16[528,1024]{1,0:T(8,128)(2,1)S(1)}, f32[8,1024]{1,0:T(8,128)S(1)}, f32[528,1024]{1,0:T(8,128)}, bf16[528,1024]{1,0:T(8,128)(2,1)S(1)}, bf16[...) custom-call(s32[2]{0:T(128)S(1)} %pad_add_fusion.coords_ref, bf16[528,1024]{1,0:T(8,128)(2,1)S(1)} %copy-done.22, ...), custom_call_target="tpu_custom_call" | custom-call | flops 1 | bytes 11200000 | tf_op jit(solution)/shard_map/mlp_fb_own/pallas_call | solution.py:556
  184.6 4.4 pack.26
  189.1 2.7 collective-permute-start.12
  191.8 23.4 %attn_backward.2 = (bf16[528,1024]{1,0:T(8,128)(2,1)S(1)}, bf16[528,1024]{1,0:T(8,128)(2,1)S(1)}, bf16[528,1024]{1,0:T(8,128)(2,1)S(1)}, bf16[528,1024]{1,0:T(8,128)(2,1)S(1)}, bf16[528,1024]{1,0:T(8,128)(2,1)S(1)}) custom-call(bf16[528,1024]{1,0:T(8,128)(2,1)} %get-tuple-element.293.q_ref, bf16[528,2048]{1,0:T(8,128)(2,1)} %get-tuple-element.294.km_ref.vm_ref, ...), custom_call_target="tpu_custom_call" | custom-call | flops 1 | bytes 8050000 | tf_op jit(solution)/shard_map/attn_backward/pallas_call | solution.py:195
  219.5 8.7 %head_gradients.2 = (bf16[1024,2048]{1,0:T(8,128)(2,1)}, bf16[1024,2048]{1,0:T(8,128)(2,1)}, bf16[528,2048]{1,0:T(8,128)(2,1)S(1)}) custom-call(s32[2]{0:T(128)S(1)} %pad_add_fusion.coords_ref, bf16[528,1024]{1,0:T(8,128)(2,1)S(1)} %get-tuple-element.315.dq_ref, bf16[528,1024]{1,0:T(8,128)(2,1)S(1)} %get-tuple-element.316.dk_ref, ...), custom_call_target="tpu_custom_call" | custom-call | flops 1 | bytes 4550000 | tf_op jit(solution)/shard_map/head_gradients/pallas_call | solution.py:614
  228.2 10.1 %collective-permute-done.12.refs_3_ = bf16[2,512,2048]{2,1,0:T(8,128)(2,1)S(1)} collective-permute-done((bf16[2,512,2048]{2,1,0:T(8,128)(2,1)S(1)}, bf16[2,512,2048]{2,1,0:T(8,128)(2,1)S(1)}, u32[]{:S(2)}, u32[]{:S(2)}) %collective-permute-start.12) | collective-permute-done | bytes 4194336 | tf_op jit(solution)/shard_map/ppermute | solution.py:818
  240.2 3.3 pack.27
  247.3 16.9 %entry_backward.2 = (bf16[1024,1024]{1,0:T(8,128)(2,1)}, bf16[1024,1024]{1,0:T(8,128)(2,1)}, f32[528,1024]{1,0:T(8,128)S(1)}, bf16[528,1024]{1,0:T(8,128)(2,1)S(1)}, f32[8,1024]{1,0:T(8,128)S(1)}) custom-call(s32[2]{0:T(128)S(1)} %pad_add_fusion.coords_ref, bf16[528,1024]{1,0:T(8,128)(2,1)S(1)} %get-tuple-element.315.dq_ref, ...), custom_call_target="tpu_custom_call" | custom-call | flops 1 | bytes 7000000 | tf_op jit(solution)/shard_map/entry_backward/pallas_call | solution.py:700
  264.2 3.5 pack.28
  271.0 2.7 pack.29
  277.5 14.8 %mlp_b_peer.1 = (f32[528,1024]{1,0:T(8,128)S(1)}, bf16[1024,2048]{1,0:T(8,128)(2,1)}, bf16[1024,2048]{1,0:T(8,128)(2,1)S(1)}, f32[1,2048]{1,0:T(1,128)S(1)}) custom-call(s32[2]{0:T(128)S(1)} %pad_add_fusion.coords_ref, bf16[528,1024]{1,0:T(8,128)(2,1)S(1)} %copy-done.11, f32[528,1024]{1,0:T(8,128)S(1)} %get-tuple-element.343.refs_1_, ...), custom_call_target="tpu_custom_call" | custom-call | flops 1 | bytes 6300000 | tf_op jit(solution)/shard_map/mlp_b_peer/pallas_call | solution.py:556
  296.7 4.4 collective-permute-done.17.refs_5_
  309.1 2.6 collective-permute-start.22
  311.7 17.5 %mlp_b_own.1 = (f32[8,1024]{1,0:T(8,128)S(1)}, f32[528,1024]{1,0:T(8,128)S(1)}, bf16[528,1024]{1,0:T(8,128)(2,1)S(1)}, bf16[2,1024,2048]{2,1,0:T(8,128)(2,1)}, f32[1,2048]{1,0:T(1,128)S(1)}) custom-call(s32[2]{0:T(128)S(1)} %pad_add_fusion.coords_ref, bf16[528,1024]{1,0:T(8,128)(2,1)S(1)} %copy-done.11, f32[528,1024]{1,0:T(8,128)S(1)} %get-tuple-element.343.refs_1_, ...), custom_call_target="tpu_custom_call" | custom-call | flops 1 | bytes 6300000 | tf_op jit(solution)/shard_map/mlp_b_own/pallas_call | solution.py:556
  329.8 5.2 pack.33
  341.4 2.8 convert_add_fusion.1
  344.2 23.3 %attn_backward.3 = (bf16[528,1024]{1,0:T(8,128)(2,1)S(1)}, bf16[528,1024]{1,0:T(8,128)(2,1)S(1)}, bf16[528,1024]{1,0:T(8,128)(2,1)S(1)}, bf16[528,1024]{1,0:T(8,128)(2,1)S(1)}, bf16[528,1024]{1,0:T(8,128)(2,1)S(1)}) custom-call(bf16[528,1024]{1,0:T(8,128)(2,1)} %get-tuple-element.284.q_ref, bf16[528,2048]{1,0:T(8,128)(2,1)} %get-tuple-element.285.km_ref.vm_ref, ...), custom_call_target="tpu_custom_call" | custom-call | flops 1 | bytes 8050000 | tf_op jit(solution)/shard_map/attn_backward/pallas_call | solution.py:195
  371.9 8.6 %head_gradients.3 = (bf16[1024,2048]{1,0:T(8,128)(2,1)}, bf16[1024,2048]{1,0:T(8,128)(2,1)}, bf16[528,2048]{1,0:T(8,128)(2,1)S(1)}) custom-call(s32[2]{0:T(128)S(1)} %pad_add_fusion.coords_ref, bf16[528,1024]{1,0:T(8,128)(2,1)S(1)} %get-tuple-element.399.dq_ref, bf16[528,1024]{1,0:T(8,128)(2,1)S(1)} %get-tuple-element.400.dk_ref, ...), custom_call_target="tpu_custom_call" | custom-call | flops 1 | bytes 4550000 | tf_op jit(solution)/shard_map/head_gradients/pallas_call | solution.py:614
  380.5 2.5 collective-permute-done.27.refs_3_
  383.0 6.3 %collective-permute-done.25.refs_3_ = bf16[2,512,2048]{2,1,0:T(8,128)(2,1)S(1)} collective-permute-done((bf16[2,512,2048]{2,1,0:T(8,128)(2,1)S(1)}, bf16[2,512,2048]{2,1,0:T(8,128)(2,1)S(1)}, u32[]{:S(2)}, u32[]{:S(2)}) %collective-permute-start.25) | collective-permute-done | bytes 4194336 | tf_op jit(solution)/shard_map/ppermute | solution.py:818
  389.3 2.8 pack.38
  392.1 4.2 pack.36
  409.8 17.6 %entry_backward.3 = (bf16[1024,1024]{1,0:T(8,128)(2,1)}, bf16[1024,1024]{1,0:T(8,128)(2,1)}, bf16[528,1024]{1,0:T(8,128)(2,1)}, bf16[528,1024]{1,0:T(8,128)(2,1)}, f32[8,1024]{1,0:T(8,128)S(1)}) custom-call(s32[2]{0:T(128)S(1)} %pad_add_fusion.coords_ref, bf16[528,1024]{1,0:T(8,128)(2,1)S(1)} %get-tuple-element.399.dq_ref, bf16[528,2048]{1,0:T(8,128)(2,1)S(1)} %copy-done.15, ...), custom_call_target="tpu_custom_call" | custom-call | flops 1 | bytes 7000000 | tf_op jit(solution)/shard_map/entry_backward/pallas_call | solution.py:700
  427.4 3.3 pack.39
  432.1 2.8 pack.40
  441.4 4.8 collective-permute-done.34.refs_3_
  446.9 3.2 gather_rows.3
  450.1 6.3 %gather_rows.4 = bf16[1026,2,1024]{2,1,0:T(2,128)(2,1)} custom-call(s32[1]{0:T(128)} %bitcast.core_ref, bf16[528,1024]{1,0:T(8,128)(2,1)} %get-tuple-element.446.refs_0_, bf16[528,1024]{1,0:T(8,128)(2,1)} %collective-permute-done.33.refs_1_, bf16[528,1024]{1,0:T(8,128)(2,1)S(1)} %copy-done.24, bf16[528,1024]{1,0:T(8,128)(2,1)S(1)} %collective-permute-done.34.refs_3_), custom_call_target="tpu_custom_call" | custom-call | flops 1 | bytes 1050000 | tf_op jit(solution)/shard_map/gather_rows/pallas_call | solution.py:749
  460.7 6.5 %collective-permute-done.40 = bf16[64,1024]{1,0:T(8,128)(2,1)S(1)} collective-permute-done((bf16[64,1024]{1,0:T(8,128)(2,1)S(1)}, bf16[64,1024]{1,0:T(8,128)(2,1)S(1)}, u32[]{:S(2)}, u32[]{:S(2)}) %collective-permute-start.40) | collective-permute-done | bytes 131104 | tf_op jit(solution)/shard_map/ppermute | solution.py:818
  469.3 2.4 pack.44
  480.1 2.9 collective-permute-done.46
  484.3 3.4 collective-permute-done.44
  487.7 13.6 %collective-permute-done.42 = bf16[2,64,2048]{2,1,0:T(8,128)(2,1)S(1)} collective-permute-done((bf16[2,64,2048]{2,1,0:T(8,128)(2,1)S(1)}, bf16[2,64,2048]{2,1,0:T(8,128)(2,1)S(1)}, u32[]{:S(2)}, u32[]{:S(2)}) %collective-permute-start.42) | collective-permute-done | bytes 524320 | tf_op jit(solution)/shard_map/ppermute | solution.py:818
  507.5 3.3 collective-permute-start.50
  522.0 4.5 collective-permute-done.51
  532.4 5.4 collective-permute-start.52
  544.5 5.2 collective-permute-done.55
  (319 shorter events, 133.1 us)
Async XLA Ops:
  0.6 16.6 %collective-permute-start.1 = (bf16[2,3,1024,512]{3,2,1,0:T(8,128)(2,1)}, bf16[2,3,1024,512]{3,2,1,0:T(8,128)(2,1)}, u32[]{:S(2)}, u32[]{:S(2)}) collective-permute-start(bf16[2,3,1024,512]{3,2,1,0:T(8,128)(2,1)} %bitcast.55), channel_id=1, source_target_pairs={{0,1},{1,0},{2,3},{3,2},{4,5},{5,4},{6,7},{7,6},{8,9},{9,8},{10,11... | collective-permute-start | bytes 18874376 | tf_op jit(solution)/shard_map/ppermute | solution.py:806
  1.2 16.1 %collective-permute-start = (bf16[2,1,1024,1024]{3,2,1,0:T(8,128)(2,1)}, bf16[2,1,1024,1024]{3,2,1,0:T(8,128)(2,1)}, u32[]{:S(2)}, u32[]{:S(2)}) collective-permute-start(bf16[2,1,1024,1024]{3,2,1,0:T(8,128)(2,1)} %wa_ref.7), channel_id=1, source_target_pairs={{0,1},{1,0},{2,3},{3,2},{4,5},{5,4},{6,7},{7,6},{8,9},{9,8},{10,11... | collective-permute-start | bytes 12582920 | tf_op jit(solution)/shard_map/ppermute | solution.py:806
  17.3 18.9 %collective-permute-start.3 = (bf16[2,1024,2048]{2,1,0:T(8,128)(2,1)}, bf16[2,1024,2048]{2,1,0:T(8,128)(2,1)}, u32[]{:S(2)}, u32[]{:S(2)}) collective-permute-start(bf16[2,1024,2048]{2,1,0:T(8,128)(2,1)} %refs_7_.7), channel_id=1, source_target_pairs={{0,1},{1,0},{2,3},{3,2},{4,5},{5,4},{6,7},{7,6},{8,9},{9,8},{10,11... | collective-permute-start | bytes 25165832 | tf_op jit(solution)/shard_map/ppermute | solution.py:806
  36.2 21.4 %collective-permute-start.6 = (bf16[2,1024,2048]{2,1,0:T(8,128)(2,1)}, bf16[2,1024,2048]{2,1,0:T(8,128)(2,1)S(1)}, u32[]{:S(2)}, u32[]{:S(2)}) collective-permute-start(bf16[2,1024,2048]{2,1,0:T(8,128)(2,1)} %refs_8_.3), channel_id=1, source_target_pairs={{0,1},{1,0},{2,3},{3,2},{4,5},{5,4},{6,7},{7,6},{8,9},{9,8},{10,11... | collective-permute-start | bytes 25165832 | tf_op jit(solution)/shard_map/ppermute | solution.py:806
  36.4 21.2 %collective-permute-start.5 = (bf16[2,1024,512]{2,1,0:T(8,128)(2,1)S(1)}, bf16[2,1024,512]{2,1,0:T(8,128)(2,1)S(1)}, u32[]{:S(2)}, u32[]{:S(2)}) collective-permute-start(bf16[2,1024,512]{2,1,0:T(8,128)(2,1)S(1)} %copy-done), channel_id=1, source_target_pairs={{0,1},{1,0},{2,3},{3,2},{4,5},{5,4},{6,7},{7,6},{8,9},{9,8},{10,11... | collective-permute-start | bytes 6291464 | tf_op jit(solution)/shard_map/ppermute | solution.py:806
  154.6 29.1 %collective-permute-start.8 = (bf16[1024,2048]{1,0:T(8,128)(2,1)}, bf16[1024,2048]{1,0:T(8,128)(2,1)}, u32[]{:S(2)}, u32[]{:S(2)}) collective-permute-start(bf16[1024,2048]{1,0:T(8,128)(2,1)} %get-tuple-element.303), channel_id=1, source_target_pairs={{0,1},{1,0},{2,3},{3,2},{4,5},{5,4},{6,7},{7,6},{8,9},{9,8},{10,11... | collective-permute-start | bytes 12582920 | tf_op jit(solution)/shard_map/ppermute | solution.py:806
  154.7 28.9 %collective-permute-start.9 = (bf16[1024,2048]{1,0:T(8,128)(2,1)}, bf16[1024,2048]{1,0:T(8,128)(2,1)}, u32[]{:S(2)}, u32[]{:S(2)}) collective-permute-start(bf16[1024,2048]{1,0:T(8,128)(2,1)} %get-tuple-element.304), channel_id=1, source_target_pairs={{0,1},{1,0},{2,3},{3,2},{4,5},{5,4},{6,7},{7,6},{8,9},{9,8},{10,11... | collective-permute-start | bytes 12582920 | tf_op jit(solution)/shard_map/ppermute | solution.py:806
  189.1 49.2 %collective-permute-start.12 = (bf16[2,512,2048]{2,1,0:T(8,128)(2,1)S(1)}, bf16[2,512,2048]{2,1,0:T(8,128)(2,1)S(1)}, u32[]{:S(2)}, u32[]{:S(2)}) collective-permute-start(bf16[2,512,2048]{2,1,0:T(8,128)(2,1)S(1)} %pack.26), channel_id=1, source_target_pairs={{0,2},{1,5},{2,0},{3,7},{4,6},{5,1},{6,4},{7,3},{8,10},{9,13},{10,... | collective-permute-start | bytes 12582920 | tf_op jit(solution)/shard_map/ppermute | solution.py:818
  243.5 20.7 %collective-permute-start.13 = (bf16[1024,2048]{1,0:T(8,128)(2,1)}, bf16[1024,2048]{1,0:T(8,128)(2,1)}, u32[]{:S(2)}, u32[]{:S(2)}) collective-permute-start(bf16[1024,2048]{1,0:T(8,128)(2,1)} %get-tuple-element.331), channel_id=1, source_target_pairs={{0,1},{1,0},{2,3},{3,2},{4,5},{5,4},{6,7},{7,6},{8,9},{9,8},{10,11... | collective-permute-start | bytes 12582920 | tf_op jit(solution)/shard_map/ppermute | solution.py:806
  243.6 26.1 %collective-permute-start.14 = (bf16[2,256,2048]{2,1,0:T(8,128)(2,1)S(1)}, bf16[2,256,2048]{2,1,0:T(8,128)(2,1)S(1)}, u32[]{:S(2)}, u32[]{:S(2)}) collective-permute-start(bf16[2,256,2048]{2,1,0:T(8,128)(2,1)S(1)} %pack.27), channel_id=1, source_target_pairs={{0,4},{1,3},{2,6},{3,1},{4,0},{5,7},{6,2},{7,5},{8,12},{9,11},{10,... | collective-permute-start | bytes 6291464 | tf_op jit(solution)/shard_map/ppermute | solution.py:818
  273.7 20.6 %collective-permute-start.15 = (bf16[1024,1024]{1,0:T(8,128)(2,1)}, bf16[1024,1024]{1,0:T(8,128)(2,1)}, u32[]{:S(2)}, u32[]{:S(2)}) collective-permute-start(bf16[1024,1024]{1,0:T(8,128)(2,1)} %get-tuple-element.348), channel_id=1, source_target_pairs={{0,1},{1,0},{2,3},{3,2},{4,5},{5,4},{6,7},{7,6},{8,9},{9,8},{10,11... | collective-permute-start | bytes 6291464 | tf_op jit(solution)/shard_map/ppermute | solution.py:806
  273.8 28.3 %collective-permute-start.16 = (bf16[512,2048]{1,0:T(8,128)(2,1)S(1)}, bf16[512,2048]{1,0:T(8,128)(2,1)}, u32[]{:S(2)}, u32[]{:S(2)}) collective-permute-start(bf16[512,2048]{1,0:T(8,128)(2,1)S(1)} %pack.28), channel_id=1, source_target_pairs={{0,2},{1,5},{2,0},{3,7},{4,6},{5,1},{6,4},{7,3},{8,10},{9,13},{10,... | collective-permute-start | bytes 6291464 | tf_op jit(solution)/shard_map/ppermute | solution.py:818
  275.9 25.2 %collective-permute-start.17 = (bf16[2,128,2048]{2,1,0:T(8,128)(2,1)S(1)}, bf16[2,128,2048]{2,1,0:T(8,128)(2,1)S(1)}, u32[]{:S(2)}, u32[]{:S(2)}) collective-permute-start(bf16[2,128,2048]{2,1,0:T(8,128)(2,1)S(1)} %pack.29), channel_id=1, source_target_pairs={{0,8},{1,9},{2,10},{3,11},{4,12},{5,13},{6,14},{7,15},{8,0},{9,1},... | collective-permute-start | bytes 3145736 | tf_op jit(solution)/shard_map/ppermute | solution.py:818
  306.3 23.5 %collective-permute-start.18 = (bf16[1024,2048]{1,0:T(8,128)(2,1)}, bf16[1024,2048]{1,0:T(8,128)(2,1)}, u32[]{:S(2)}, u32[]{:S(2)}) collective-permute-start(bf16[1024,2048]{1,0:T(8,128)(2,1)} %get-tuple-element.370), channel_id=1, source_target_pairs={{0,1},{1,0},{2,3},{3,2},{4,5},{5,4},{6,7},{7,6},{8,9},{9,8},{10,11... | collective-permute-start | bytes 12582920 | tf_op jit(solution)/shard_map/ppermute | solution.py:806
  307.1 22.7 %collective-permute-start.19 = (bf16[1024,2048]{1,0:T(8,128)(2,1)S(1)}, bf16[1024,2048]{1,0:T(8,128)(2,1)}, u32[]{:S(2)}, u32[]{:S(2)}) collective-permute-start(bf16[1024,2048]{1,0:T(8,128)(2,1)S(1)} %copy-done.48), channel_id=1, source_target_pairs={{0,1},{1,0},{2,3},{3,2},{4,5},{5,4},{6,7},{7,6},{8,9},{9,8},{10,11... | collective-permute-start | bytes 12582920 | tf_op jit(solution)/shard_map/ppermute | solution.py:806
  307.1 28.0 %collective-permute-start.20 = (bf16[512,1024]{1,0:T(8,128)(2,1)S(1)}, bf16[512,1024]{1,0:T(8,128)(2,1)S(1)}, u32[]{:S(2)}, u32[]{:S(2)}) collective-permute-start(bf16[512,1024]{1,0:T(8,128)(2,1)S(1)} %pack.30), channel_id=1, source_target_pairs={{0,2},{1,5},{2,0},{3,7},{4,6},{5,1},{6,4},{7,3},{8,10},{9,13},{10,... | collective-permute-start | bytes 3145736 | tf_op jit(solution)/shard_map/ppermute | solution.py:818
  308.1 27.0 %collective-permute-start.21 = (bf16[256,2048]{1,0:T(8,128)(2,1)S(1)}, bf16[256,2048]{1,0:T(8,128)(2,1)}, u32[]{:S(2)}, u32[]{:S(2)}) collective-permute-start(bf16[256,2048]{1,0:T(8,128)(2,1)S(1)} %pack.31), channel_id=1, source_target_pairs={{0,4},{1,3},{2,6},{3,1},{4,0},{5,7},{6,2},{7,5},{8,12},{9,11},{10,... | collective-permute-start | bytes 3145736 | tf_op jit(solution)/shard_map/ppermute | solution.py:818
  309.1 26.0 %collective-permute-start.22 = (bf16[2,64,2048]{2,1,0:T(8,128)(2,1)S(1)}, bf16[2,64,2048]{2,1,0:T(8,128)(2,1)S(1)}, u32[]{:S(2)}, u32[]{:S(2)}) collective-permute-start(bf16[2,64,2048]{2,1,0:T(8,128)(2,1)S(1)} %pack.32), channel_id=1, source_target_pairs={{0,16},{1,17},{2,18},{3,19},{4,20},{5,21},{6,22},{7,23},{8,24},{9,... | collective-permute-start | bytes 1572872 | tf_op jit(solution)/shard_map/ppermute | solution.py:818
  335.1 54.2 %collective-permute-start.25 = (bf16[2,512,2048]{2,1,0:T(8,128)(2,1)S(1)}, bf16[2,512,2048]{2,1,0:T(8,128)(2,1)S(1)}, u32[]{:S(2)}, u32[]{:S(2)}) collective-permute-start(bf16[2,512,2048]{2,1,0:T(8,128)(2,1)S(1)} %pack.33), channel_id=1, source_target_pairs={{0,2},{1,5},{2,0},{3,7},{4,6},{5,1},{6,4},{7,3},{8,10},{9,13},{10,... | collective-permute-start | bytes 12582920 | tf_op jit(solution)/shard_map/ppermute | solution.py:818
  368.1 14.9 %collective-permute-start.27 = (bf16[256,1024]{1,0:T(8,128)(2,1)S(1)}, bf16[256,1024]{1,0:T(8,128)(2,1)S(1)}, u32[]{:S(2)}, u32[]{:S(2)}) collective-permute-start(bf16[256,1024]{1,0:T(8,128)(2,1)S(1)} %pack.35), channel_id=1, source_target_pairs={{0,4},{1,3},{2,6},{3,1},{4,0},{5,7},{6,2},{7,5},{8,12},{9,11},{10,... | collective-permute-start | bytes 1572872 | tf_op jit(solution)/shard_map/ppermute | solution.py:818
  369.4 13.6 %collective-permute-start.26 = (bf16[128,2048]{1,0:T(8,128)(2,1)S(1)}, bf16[128,2048]{1,0:T(8,128)(2,1)S(1)}, u32[]{:S(2)}, u32[]{:S(2)}) collective-permute-start(bf16[128,2048]{1,0:T(8,128)(2,1)S(1)} %pack.34), channel_id=1, source_target_pairs={{0,8},{1,9},{2,10},{3,11},{4,12},{5,13},{6,14},{7,15},{8,0},{9,1},... | collective-permute-start | bytes 1572872 | tf_op jit(solution)/shard_map/ppermute | solution.py:818
  397.7 29.7 %collective-permute-start.28 = (bf16[1024,2048]{1,0:T(8,128)(2,1)}, bf16[1024,2048]{1,0:T(8,128)(2,1)}, u32[]{:S(2)}, u32[]{:S(2)}) collective-permute-start(bf16[1024,2048]{1,0:T(8,128)(2,1)} %get-tuple-element.426), channel_id=1, source_target_pairs={{0,1},{1,0},{2,3},{3,2},{4,5},{5,4},{6,7},{7,6},{8,9},{9,8},{10,11... | collective-permute-start | bytes 12582920 | tf_op jit(solution)/shard_map/ppermute | solution.py:806
  397.8 33.0 %collective-permute-start.29 = (bf16[2,256,2048]{2,1,0:T(8,128)(2,1)}, bf16[2,256,2048]{2,1,0:T(8,128)(2,1)}, u32[]{:S(2)}, u32[]{:S(2)}) collective-permute-start(bf16[2,256,2048]{2,1,0:T(8,128)(2,1)} %pack.36), channel_id=1, source_target_pairs={{0,4},{1,3},{2,6},{3,1},{4,0},{5,7},{6,2},{7,5},{8,12},{9,11},{10,... | collective-permute-start | bytes 6291464 | tf_op jit(solution)/shard_map/ppermute | solution.py:818
  399.2 31.6 %collective-permute-start.31 = (bf16[128,1024]{1,0:T(8,128)(2,1)}, bf16[128,1024]{1,0:T(8,128)(2,1)}, u32[]{:S(2)}, u32[]{:S(2)}) collective-permute-start(bf16[128,1024]{1,0:T(8,128)(2,1)} %pack.38), channel_id=1, source_target_pairs={{0,8},{1,9},{2,10},{3,11},{4,12},{5,13},{6,14},{7,15},{8,0},{9,1},... | collective-permute-start | bytes 786440 | tf_op jit(solution)/shard_map/ppermute | solution.py:818
  400.8 30.0 %collective-permute-start.30 = (bf16[64,2048]{1,0:T(8,128)(2,1)S(1)}, bf16[64,2048]{1,0:T(8,128)(2,1)}, u32[]{:S(2)}, u32[]{:S(2)}) collective-permute-start(bf16[64,2048]{1,0:T(8,128)(2,1)S(1)} %pack.37), channel_id=1, source_target_pairs={{0,16},{1,17},{2,18},{3,19},{4,20},{5,21},{6,22},{7,23},{8,24},{9,... | collective-permute-start | bytes 786440 | tf_op jit(solution)/shard_map/ppermute | solution.py:818
  435.9 5.3 collective-permute-start.32
  435.9 5.4 collective-permute-start.33
  437.1 32.2 %collective-permute-start.38 = (bf16[512,2048]{1,0:T(8,128)(2,1)S(1)}, bf16[512,2048]{1,0:T(8,128)(2,1)}, u32[]{:S(2)}, u32[]{:S(2)}) collective-permute-start(bf16[512,2048]{1,0:T(8,128)(2,1)S(1)} %pack.39), channel_id=1, source_target_pairs={{0,2},{1,5},{2,0},{3,7},{4,6},{5,1},{6,4},{7,3},{8,10},{9,13},{10,... | collective-permute-start | bytes 6291464 | tf_op jit(solution)/shard_map/ppermute | solution.py:818
  438.0 19.9 %collective-permute-start.36 = (bf16[1024,1024]{1,0:T(8,128)(2,1)}, bf16[1024,1024]{1,0:T(8,128)(2,1)}, u32[]{:S(2)}, u32[]{:S(2)}) collective-permute-start(bf16[1024,1024]{1,0:T(8,128)(2,1)} %get-tuple-element.453), channel_id=1, source_target_pairs={{0,1},{1,0},{2,3},{3,2},{4,5},{5,4},{6,7},{7,6},{8,9},{9,8},{10,11... | collective-permute-start | bytes 6291464 | tf_op jit(solution)/shard_map/ppermute | solution.py:806
  440.5 5.7 %collective-permute-start.34 = (bf16[528,1024]{1,0:T(8,128)(2,1)S(1)}, bf16[528,1024]{1,0:T(8,128)(2,1)S(1)}, u32[]{:S(2)}, u32[]{:S(2)}) collective-permute-start(bf16[528,1024]{1,0:T(8,128)(2,1)S(1)} %copy-done.24), channel_id=1, source_target_pairs={{0,1},{1,0},{2,3},{3,2},{4,5},{5,4},{6,7},{7,6},{8,9},{9,8},{10,11... | collective-permute-start | bytes 3244040 | tf_op jit(solution)/shard_map/ppermute | solution.py:806
  441.1 28.2 %collective-permute-start.39 = (bf16[2,128,2048]{2,1,0:T(8,128)(2,1)}, bf16[2,128,2048]{2,1,0:T(8,128)(2,1)S(1)}, u32[]{:S(2)}, u32[]{:S(2)}) collective-permute-start(bf16[2,128,2048]{2,1,0:T(8,128)(2,1)} %copy-done.29), channel_id=1, source_target_pairs={{0,8},{1,9},{2,10},{3,11},{4,12},{5,13},{6,14},{7,15},{8,0},{9,1},... | collective-permute-start | bytes 3145736 | tf_op jit(solution)/shard_map/ppermute | solution.py:818
  441.2 15.2 %collective-permute-start.35 = (bf16[528,1024]{1,0:T(8,128)(2,1)}, bf16[528,1024]{1,0:T(8,128)(2,1)S(1)}, u32[]{:S(2)}, u32[]{:S(2)}) collective-permute-start(bf16[528,1024]{1,0:T(8,128)(2,1)} %copy-done.27), channel_id=1, source_target_pairs={{0,1},{1,0},{2,3},{3,2},{4,5},{5,4},{6,7},{7,6},{8,9},{9,8},{10,11... | collective-permute-start | bytes 3244040 | tf_op jit(solution)/shard_map/ppermute | solution.py:806
  446.2 20.9 %collective-permute-start.40 = (bf16[64,1024]{1,0:T(8,128)(2,1)S(1)}, bf16[64,1024]{1,0:T(8,128)(2,1)S(1)}, u32[]{:S(2)}, u32[]{:S(2)}) collective-permute-start(bf16[64,1024]{1,0:T(8,128)(2,1)S(1)} %pack.41), channel_id=1, source_target_pairs={{0,16},{1,17},{2,18},{3,19},{4,20},{5,21},{6,22},{7,23},{8,24},{9,... | collective-permute-start | bytes 393224 | tf_op jit(solution)/shard_map/ppermute | solution.py:818
  460.4 41.0 %collective-permute-start.37 = (bf16[512,1024]{1,0:T(8,128)(2,1)S(1)}, bf16[512,1024]{1,0:T(8,128)(2,1)S(1)}, u32[]{:S(2)}, u32[]{:S(2)}) collective-permute-start(bf16[512,1024]{1,0:T(8,128)(2,1)S(1)} %pack.42), channel_id=1, source_target_pairs={{0,2},{1,5},{2,0},{3,7},{4,6},{5,1},{6,4},{7,3},{8,10},{9,13},{10,... | collective-permute-start | bytes 3145736 | tf_op jit(solution)/shard_map/ppermute | solution.py:818
  471.8 29.6 %collective-permute-start.43 = (bf16[256,2048]{1,0:T(8,128)(2,1)S(1)}, bf16[256,2048]{1,0:T(8,128)(2,1)S(1)}, u32[]{:S(2)}, u32[]{:S(2)}) collective-permute-start(bf16[256,2048]{1,0:T(8,128)(2,1)S(1)} %pack.44), channel_id=1, source_target_pairs={{0,4},{1,3},{2,6},{3,1},{4,0},{5,7},{6,2},{7,5},{8,12},{9,11},{10,... | collective-permute-start | bytes 3145736 | tf_op jit(solution)/shard_map/ppermute | solution.py:818
  474.8 26.5 %collective-permute-start.42 = (bf16[2,64,2048]{2,1,0:T(8,128)(2,1)S(1)}, bf16[2,64,2048]{2,1,0:T(8,128)(2,1)S(1)}, u32[]{:S(2)}, u32[]{:S(2)}) collective-permute-start(bf16[2,64,2048]{2,1,0:T(8,128)(2,1)S(1)} %pack.43), channel_id=1, source_target_pairs={{0,16},{1,17},{2,18},{3,19},{4,20},{5,21},{6,22},{7,23},{8,24},{9,... | collective-permute-start | bytes 1572872 | tf_op jit(solution)/shard_map/ppermute | solution.py:818
  477.4 5.6 %collective-permute-start.46 = (f32[4,18,64]{2,1,0:T(8,128)S(1)}, f32[4,18,64]{2,1,0:T(8,128)S(1)}, u32[]{:S(2)}, u32[]{:S(2)}) collective-permute-start(f32[4,18,64]{2,1,0:T(8,128)S(1)} %get-tuple-element.588), channel_id=1, source_target_pairs={{0,6},{1,7},{2,4},{3,5},{4,2},{5,3},{6,0},{7,1},{8,14},{9,15},{10,... | collective-permute-start | bytes 55304 | tf_op jit(solution)/shard_map/ppermute | solution.py:818
  479.2 5.1 collective-permute-start.45
  483.0 4.6 collective-permute-start.44
  506.3 20.1 %collective-permute-start.48 = (bf16[64,2048]{1,0:T(8,128)(2,1)S(1)}, bf16[64,2048]{1,0:T(8,128)(2,1)S(1)}, u32[]{:S(2)}, u32[]{:S(2)}) collective-permute-start(bf16[64,2048]{1,0:T(8,128)(2,1)S(1)} %pack.45), channel_id=1, source_target_pairs={{0,16},{1,17},{2,18},{3,19},{4,20},{5,21},{6,22},{7,23},{8,24},{9,... | collective-permute-start | bytes 786440 | tf_op jit(solution)/shard_map/ppermute | solution.py:818
  506.4 20.1 %collective-permute-start.49 = (bf16[64,2048]{1,0:T(8,128)(2,1)S(1)}, bf16[64,2048]{1,0:T(8,128)(2,1)}, u32[]{:S(2)}, u32[]{:S(2)}) collective-permute-start(bf16[64,2048]{1,0:T(8,128)(2,1)S(1)} %pack.46), channel_id=1, source_target_pairs={{0,8},{1,9},{2,10},{3,11},{4,12},{5,13},{6,14},{7,15},{8,0},{9,1},... | collective-permute-start | bytes 786440 | tf_op jit(solution)/shard_map/ppermute | solution.py:818
  507.5 19.0 %collective-permute-start.50 = (bf16[64,2048]{1,0:T(8,128)(2,1)S(1)}, bf16[64,2048]{1,0:T(8,128)(2,1)}, u32[]{:S(2)}, u32[]{:S(2)}) collective-permute-start(bf16[64,2048]{1,0:T(8,128)(2,1)S(1)} %pack.47), channel_id=1, source_target_pairs={{0,24},{1,25},{2,26},{3,27},{4,28},{5,29},{6,30},{7,31},{8,16},{9,... | collective-permute-start | bytes 786440 | tf_op jit(solution)/shard_map/ppermute | solution.py:818
  511.4 15.1 %collective-permute-start.51 = (f32[2,18,64]{2,1,0:T(8,128)}, f32[2,18,64]{2,1,0:T(8,128)}, u32[]{:S(2)}, u32[]{:S(2)}) collective-permute-start(f32[2,18,64]{2,1,0:T(8,128)} %slice_add_fusion.3), channel_id=1, source_target_pairs={{0,8},{1,9},{2,10},{3,11},{4,12},{5,13},{6,14},{7,15},{8,0},{9,1},... | collective-permute-start | bytes 27656 | tf_op jit(solution)/shard_map/ppermute | solution.py:818
  514.9 11.5 %collective-permute-start.47 = (bf16[256,1024]{1,0:T(8,128)(2,1)S(1)}, bf16[256,1024]{1,0:T(8,128)(2,1)S(1)}, u32[]{:S(2)}, u32[]{:S(2)}) collective-permute-start(bf16[256,1024]{1,0:T(8,128)(2,1)S(1)} %pack.48), channel_id=1, source_target_pairs={{0,4},{1,3},{2,6},{3,1},{4,0},{5,7},{6,2},{7,5},{8,12},{9,11},{10,... | collective-permute-start | bytes 1572872 | tf_op jit(solution)/shard_map/ppermute | solution.py:818
  532.4 17.3 %collective-permute-start.52 = (bf16[64,1024]{1,0:T(8,128)(2,1)S(1)}, bf16[64,1024]{1,0:T(8,128)(2,1)S(1)}, u32[]{:S(2)}, u32[]{:S(2)}) collective-permute-start(bf16[64,1024]{1,0:T(8,128)(2,1)S(1)} %pack.49), channel_id=1, source_target_pairs={{0,16},{1,17},{2,18},{3,19},{4,20},{5,21},{6,22},{7,23},{8,24},{9,... | collective-permute-start | bytes 393224 | tf_op jit(solution)/shard_map/ppermute | solution.py:818
  537.9 11.9 %collective-permute-start.53 = (bf16[64,1024]{1,0:T(8,128)(2,1)S(1)}, bf16[64,1024]{1,0:T(8,128)(2,1)S(1)}, u32[]{:S(2)}, u32[]{:S(2)}) collective-permute-start(bf16[64,1024]{1,0:T(8,128)(2,1)S(1)} %pack.50), channel_id=1, source_target_pairs={{0,8},{1,9},{2,10},{3,11},{4,12},{5,13},{6,14},{7,15},{8,0},{9,1},... | collective-permute-start | bytes 393224 | tf_op jit(solution)/shard_map/ppermute | solution.py:818
  537.9 11.9 %collective-permute-start.54 = (bf16[64,1024]{1,0:T(8,128)(2,1)S(1)}, bf16[64,1024]{1,0:T(8,128)(2,1)S(1)}, u32[]{:S(2)}, u32[]{:S(2)}) collective-permute-start(bf16[64,1024]{1,0:T(8,128)(2,1)S(1)} %pack.51), channel_id=1, source_target_pairs={{0,24},{1,25},{2,26},{3,27},{4,28},{5,29},{6,30},{7,31},{8,16},{9,... | collective-permute-start | bytes 393224 | tf_op jit(solution)/shard_map/ppermute | solution.py:818
  540.2 9.6 %collective-permute-start.55 = (f32[1,18,64]{2,1,0:T(8,128)S(1)}, f32[1,18,64]{2,1,0:T(8,128)S(1)}, u32[]{:S(2)}, u32[]{:S(2)}) collective-permute-start(f32[1,18,64]{2,1,0:T(8,128)S(1)} %slice_add_fusion.4), channel_id=1, source_target_pairs={{0,16},{1,17},{2,18},{3,19},{4,20},{5,21},{6,22},{7,23},{8,24},{9,... | collective-permute-start | bytes 13832 | tf_op jit(solution)/shard_map/ppermute | solution.py:818
  (78 other events, 725.7 us)
